TPU v7x, 32 devices: a whole 2x2x4 slice. The times are simulated.
32 devices in a mesh: groups: 2 (over x), rows: 8 (over z, y), fsdp: 2 (over core).
Axes of the slice: x: 2, y: 2, z: 4, core: 2. Of those that a mesh axis runs over, the one named last changes fastest.
Arguments:
- image: bfloat16 [32, 256, 512], P(('groups', 'rows'), 'fsdp'), parts along dimension 0, may hold values from -81 to 81
- deconv_weight: bfloat16 [4, 4, 512, 256], P(None, None, None, 'fsdp'), may hold values from -0.125 to 0.125
- norm_gain: float32 [256], replicated, may hold values from 0.1 to 1.9
- norm_shift: float32 [256], replicated, may hold values from -3 to 3
- first_weight: bfloat16 [3, 3, 256, 256], P(None, None, None, 'fsdp'), may hold values from -0.125 to 0.125
- first_bias: float32 [256], replicated, may hold values from -3 to 3
- second_weight: bfloat16 [3, 3, 256, 256], P(None, None, None, 'fsdp'), may hold values from -0.125 to 0.125
- second_bias: float32 [256], replicated, may hold values from -3 to 3
Outputs:
- result: bfloat16 [64, 512, 256], P(('groups', 'rows'), 'fsdp'), parts along dimension 0
There are 2 independent parts, one for each index of `groups`. A program takes and returns all parts, laid end to end along the dimension named above; an argument that names none is the same for every part. Nothing has to cross between parts.
All inputs are finite; a program needn't handle non-finite values.
Results may differ from a plain program's by a relative error of at most 0.0055.
Values may be sent and summed in bfloat16 or wider, within the bound.
No kernel may reach another device: no remote copies, remote signals or barrier semaphores. Data moves between devices by JAX's collectives and lax.ppermute only.
A program may use at most 64 MiB of HBM per device.

v0:
```python
import jax
import jax.numpy as jnp
from jax import lax
from jax.sharding import PartitionSpec as P

NORM_GROUPS = 32


TAP_TABLE = (((0, 3), (1, 1)), ((1, 2), (2, 0)))


def padded_2(cells, sides, width):
    for axis, dim in sides:
        count = lax.axis_size(axis)
        ends = count - 1
        head = lax.slice_in_dim(cells, 0, width, axis=dim)
        tail = lax.slice_in_dim(cells, cells.shape[dim] - width, cells.shape[dim], axis=dim)
        cells = jnp.concatenate(
            [
                lax.ppermute(tail, axis, [(i, (i + 1) % count) for i in range(ends)]),
                cells,
                lax.ppermute(head, axis, [((i + 1) % count, i) for i in range(ends)]),
            ],
            axis=dim,
        )
    return cells


def upsample(padded, weight):
    height = padded.shape[0] - 2
    breadth = padded.shape[1] - 2
    inputs = padded.shape[2]
    outputs = weight.shape[3]
    phases = []
    for phase_row in range(2):
        line = []
        for phase_col in range(2):
            total = jnp.zeros((height * breadth, outputs), jnp.float32)
            for row_off, row_tap in TAP_TABLE[phase_row]:
                for col_off, col_tap in TAP_TABLE[phase_col]:
                    patch = padded[row_off : row_off + height, col_off : col_off + breadth].reshape(
                        height * breadth, inputs
                    )
                    total = total + jnp.dot(
                        patch, weight[row_tap, col_tap], preferred_element_type=jnp.float32
                    )
            line.append(total.reshape(height, breadth, outputs))
        phases.append(jnp.stack(line, axis=2))
    stacked = jnp.stack(phases, axis=1)
    return stacked.reshape(2 * height, 2 * breadth, outputs)


def convolve(padded, weight):
    height = padded.shape[0] - 2
    breadth = padded.shape[1] - 2
    inputs = padded.shape[2]
    outputs = weight.shape[3]
    total = jnp.zeros((height * breadth, outputs), jnp.float32)
    for row_tap in range(3):
        for col_tap in range(3):
            patch = padded[row_tap : row_tap + height, col_tap : col_tap + breadth].reshape(
                height * breadth, inputs
            )
            total = total + jnp.dot(
                patch, weight[row_tap, col_tap], preferred_element_type=jnp.float32
            )
    return total.reshape(height, breadth, outputs)


def group_totals(values, width):
    return jnp.sum(values, axis=(0, 1)).reshape(NORM_GROUPS, width).sum(axis=1)


def local(
    image,
    deconv_weight,
    norm_gain,
    norm_shift,
    first_weight,
    first_bias,
    second_weight,
    second_bias,
):
    rimmed = padded_2(image, (("rows", 0), ("fsdp", 1)), 1)
    upsampled = upsample(rimmed, lax.all_gather(deconv_weight, "fsdp", axis=3, tiled=True)).astype(
        jnp.bfloat16
    )
    values = upsampled.astype(jnp.float32)
    width = values.shape[2] // NORM_GROUPS
    count = (
        values.shape[0] * values.shape[1] * lax.axis_size("rows") * lax.axis_size("fsdp") * width
    )
    sums = group_totals(values, width)
    squares = group_totals(values * values, width)
    total, total_sq = lax.psum((sums, squares), ("rows", "fsdp"))
    mean = total / count
    spread = total_sq / count - mean * mean
    scale = jnp.repeat(lax.rsqrt(spread + 1e-05), width) * norm_gain
    shift = norm_shift - jnp.repeat(mean, width) * scale
    hidden = jax.nn.silu(values * scale + shift).astype(jnp.bfloat16)
    first_rimmed = padded_2(hidden, (("rows", 0), ("fsdp", 1)), 1)
    first = (
        convolve(first_rimmed, lax.all_gather(first_weight, "fsdp", axis=3, tiled=True))
        + first_bias
    )
    activated = jax.nn.silu(first).astype(jnp.bfloat16)
    second_rimmed = padded_2(activated, (("rows", 0), ("fsdp", 1)), 1)
    second = (
        convolve(second_rimmed, lax.all_gather(second_weight, "fsdp", axis=3, tiled=True))
        + second_bias
    )
    return second.astype(jnp.bfloat16)


def solution(mesh):
    placed = (
        P(("groups", "rows"), "fsdp", None),
        P(None, None, None, "fsdp"),
        P(),
        P(),
        P(None, None, None, "fsdp"),
        P(),
        P(None, None, None, "fsdp"),
        P(),
    )
    return jax.shard_map(
        local,
        mesh=mesh,
        in_specs=placed,
        out_specs=P(("groups", "rows"), "fsdp", None),
        check_vma=False,
    )
```

profile of v0, /device:TPU:0, one launch (start us, length us, event | category | flops | bytes accessed | tf_op | source)
XLA Modules:
  0.0 113.9 jit_solution(777925448147219815)
XLA Ops:
  8.1 4.9 %collective-permute-start = (bf16[1,128,512]{2,1,0:T(8,128)(2,1)S(1)}, bf16[1,128,512]{2,1,0:T(8,128)(2,1)S(1)}, u32[]{:S(2)}, u32[]{:S(2)}) collective-permute-start(bf16[1,128,512]{2,1,0:T(8,128)(2,1)S(1)} %get-tuple-element.55), channel_id=1, source_target_pairs={{0,2},{2,4},{4,6},{6,8},{8,10},{10,12},{12,14},{1,3},{3,5},{5,7},{... | collective-permute-start | bytes 393224 | tf_op jit(solution)/shard_map/ppermute | solution.py:20
  13.0 1.3 %collective-permute-start.1 = (bf16[1,128,512]{2,1,0:T(8,128)(2,1)S(1)}, bf16[1,128,512]{2,1,0:T(8,128)(2,1)S(1)}, u32[]{:S(2)}, u32[]{:S(2)}) collective-permute-start(bf16[1,128,512]{2,1,0:T(8,128)(2,1)S(1)} %get-tuple-element.54), channel_id=1, source_target_pairs={{2,0},{4,2},{6,4},{8,6},{10,8},{12,10},{14,12},{3,1},{5,3},{7,5},{... | collective-permute-start | bytes 393224 | tf_op jit(solution)/shard_map/ppermute | solution.py:22
  14.3 1.4 %collective-permute-done = bf16[1,128,512]{2,1,0:T(8,128)(2,1)S(1)} collective-permute-done((bf16[1,128,512]{2,1,0:T(8,128)(2,1)S(1)}, bf16[1,128,512]{2,1,0:T(8,128)(2,1)S(1)}, u32[]{:S(2)}, u32[]{:S(2)}) %collective-permute-start) | collective-permute-done | bytes 131104 | tf_op jit(solution)/shard_map/ppermute | solution.py:20
  15.7 4.1 %collective-permute-done.1 = bf16[1,128,512]{2,1,0:T(8,128)(2,1)S(1)} collective-permute-done((bf16[1,128,512]{2,1,0:T(8,128)(2,1)S(1)}, bf16[1,128,512]{2,1,0:T(8,128)(2,1)S(1)}, u32[]{:S(2)}, u32[]{:S(2)}) %collective-permute-start.1) | collective-permute-done | bytes 131104 | tf_op jit(solution)/shard_map/ppermute | solution.py:22
  20.0 1.3 %collective-permute-start.2 = (bf16[4,1,512]{2,1,0:T(2,128)(2,1)S(1)}, bf16[4,1,512]{2,1,0:T(2,128)(2,1)S(1)}, u32[]{:S(2)}, u32[]{:S(2)}) collective-permute-start(bf16[4,1,512]{2,1,0:T(2,128)(2,1)S(1)} %get-tuple-element.49), channel_id=1, source_target_pairs={{0,1},{2,3},{4,5},{6,7},{8,9},{10,11},{12,13},{14,15},{16,17},{18,... | collective-permute-start | bytes 12296 | tf_op jit(solution)/shard_map/ppermute | solution.py:20
  21.3 1.3 %collective-permute-start.3 = (bf16[4,1,512]{2,1,0:T(2,128)(2,1)S(1)}, bf16[4,1,512]{2,1,0:T(2,128)(2,1)S(1)}, u32[]{:S(2)}, u32[]{:S(2)}) collective-permute-start(bf16[4,1,512]{2,1,0:T(2,128)(2,1)S(1)} %get-tuple-element.50), channel_id=1, source_target_pairs={{1,0},{3,2},{5,4},{7,6},{9,8},{11,10},{13,12},{15,14},{17,16},{19,... | collective-permute-start | bytes 12296 | tf_op jit(solution)/shard_map/ppermute | solution.py:22
  22.6 1.7 %collective-permute-done.3 = bf16[4,1,512]{2,1,0:T(2,128)(2,1)S(1)} collective-permute-done((bf16[4,1,512]{2,1,0:T(2,128)(2,1)S(1)}, bf16[4,1,512]{2,1,0:T(2,128)(2,1)S(1)}, u32[]{:S(2)}, u32[]{:S(2)}) %collective-permute-start.3) | collective-permute-done | bytes 4128 | tf_op jit(solution)/shard_map/ppermute | solution.py:22
  24.6 1.3 %fusion.15 = f32[256,256]{1,0:T(8,128)S(1)} fusion(bf16[256,512]{1,0:T(8,128)(2,1)S(1)} %bitcast.170, bf16[4,4,512,256]{3,2,1,0:T(8,128)(2,1)} %all-gather.4.cloned.1.call-done), kind=kOutput, calls=%fused_computation.74 | convolution fusion | flops 67108864 | bytes 786432 | tf_op jit(solution)/shard_map/dot_general | solution.py:44
  27.2 1.2 %convolution_add_fusion.17 = f32[256,256]{1,0:T(8,128)S(1)} fusion(f32[256,256]{1,0:T(8,128)S(1)} %fusion.15, bf16[256,512]{1,0:T(8,128)(2,1)S(1)} %bitcast.182, bf16[4,4,512,256]{3,2,1,0:T(8,128)(2,1)} %all-gather.4.cloned.1.call-done), kind=kOutput, calls=%fused_computation.21 | convolution fusion | flops 67174400 | bytes 1048576 | tf_op jit(solution)/shard_map/dot_general | solution.py:44
  35.8 33.9 %all-reduce = (f32[32]{0:T(128)S(1)}, f32[32]{0:T(128)S(1)}) all-reduce(f32[32]{0:T(128)S(1)} %reduce_sum.39, f32[32]{0:T(128)S(1)} %reduce_sum.37), channel_id=1, replica_groups=mesh['groups'=2,'rows'=8,'fsdp'=2] {'rows','fsdp'}, use_global_device_ids=true, to_apply=%region_5.0 | all-reduce | flops 64 | bytes 512 | tf_op jit(solution)/shard_map/psum | solution.py:95
  70.6 1.3 %collective-permute-start.4 = (bf16[1,256,256]{2,1,0:T(8,128)(2,1)S(1)}, bf16[1,256,256]{2,1,0:T(8,128)(2,1)S(1)}, u32[]{:S(2)}, u32[]{:S(2)}) collective-permute-start(bf16[1,256,256]{2,1,0:T(8,128)(2,1)S(1)} %get-tuple-element.44), channel_id=1, source_target_pairs={{0,2},{2,4},{4,6},{6,8},{8,10},{10,12},{12,14},{1,3},{3,5},{5,7},{... | collective-permute-start | bytes 393224 | tf_op jit(solution)/shard_map/ppermute | solution.py:20
  71.9 1.3 %collective-permute-start.5 = (bf16[1,256,256]{2,1,0:T(8,128)(2,1)S(1)}, bf16[1,256,256]{2,1,0:T(8,128)(2,1)S(1)}, u32[]{:S(2)}, u32[]{:S(2)}) collective-permute-start(bf16[1,256,256]{2,1,0:T(8,128)(2,1)S(1)} %get-tuple-element.45), channel_id=1, source_target_pairs={{2,0},{4,2},{6,4},{8,6},{10,8},{12,10},{14,12},{3,1},{5,3},{7,5},{... | collective-permute-start | bytes 393224 | tf_op jit(solution)/shard_map/ppermute | solution.py:22
  73.2 1.2 %fusion.5 = bf16[2,2,128,2,256]{4,3,2,1,0:T(2,128)(2,1)S(1)} fusion(bf16[2,2,128,2,256]{4,3,2,1,0:T(2,128)(2,1)S(1)} %get-tuple-element.11, f32[256]{0:T(256)S(1)} %get-tuple-element.9, f32[256]{0:T(256)S(1)} %get-tuple-element.10), kind=kLoop, calls=%fused_computation.35 | loop fusion | flops 2097152 | bytes 1050624 | tf_op jit(solution)/shard_map/convert_element_type | solution.py:100
  75.8 3.0 %collective-permute-done.5 = bf16[1,256,256]{2,1,0:T(8,128)(2,1)S(1)} collective-permute-done((bf16[1,256,256]{2,1,0:T(8,128)(2,1)S(1)}, bf16[1,256,256]{2,1,0:T(8,128)(2,1)S(1)}, u32[]{:S(2)}, u32[]{:S(2)}) %collective-permute-start.5) | collective-permute-done | bytes 131104 | tf_op jit(solution)/shard_map/ppermute | solution.py:22
  78.8 1.3 %collective-permute-start.6 = (bf16[6,1,256]{2,1,0:T(2,128)(2,1)S(1)}, bf16[6,1,256]{2,1,0:T(2,128)(2,1)S(1)}, u32[]{:S(2)}, u32[]{:S(2)}) collective-permute-start(bf16[6,1,256]{2,1,0:T(2,128)(2,1)S(1)} %get-tuple-element.30), channel_id=1, source_target_pairs={{0,1},{2,3},{4,5},{6,7},{8,9},{10,11},{12,13},{14,15},{16,17},{18,... | collective-permute-start | bytes 9224 | tf_op jit(solution)/shard_map/ppermute | solution.py:20
  80.1 1.3 %collective-permute-start.7 = (bf16[6,1,256]{2,1,0:T(2,128)(2,1)S(1)}, bf16[6,1,256]{2,1,0:T(2,128)(2,1)S(1)}, u32[]{:S(2)}, u32[]{:S(2)}) collective-permute-start(bf16[6,1,256]{2,1,0:T(2,128)(2,1)S(1)} %get-tuple-element.31), channel_id=1, source_target_pairs={{1,0},{3,2},{5,4},{7,6},{9,8},{11,10},{13,12},{15,14},{17,16},{19,... | collective-permute-start | bytes 9224 | tf_op jit(solution)/shard_map/ppermute | solution.py:22
  81.5 1.2 %fusion.22 = f32[1024,256]{1,0:T(8,128)S(1)} fusion(bf16[1024,256]{1,0:T(8,128)(2,1)S(1)} %bitcast.184, bf16[3,3,256,256]{3,2,1,0:T(8,128)(2,1)} %all-gather.6.cloned.1.call-done), kind=kOutput, calls=%fused_computation.108 | convolution fusion | flops 134217728 | bytes 1703936 | tf_op jit(solution)/shard_map/dot_general | solution.py:64
  87.9 1.5 %collective-permute-start.8 = (bf16[1,256,256]{2,1,0:T(8,128)(2,1)S(1)}, bf16[1,256,256]{2,1,0:T(8,128)(2,1)S(1)}, u32[]{:S(2)}, u32[]{:S(2)}) collective-permute-start(bf16[1,256,256]{2,1,0:T(8,128)(2,1)S(1)} %get-tuple-element.40), channel_id=1, source_target_pairs={{0,2},{2,4},{4,6},{6,8},{8,10},{10,12},{12,14},{1,3},{3,5},{5,7},{... | collective-permute-start | bytes 393224 | tf_op jit(solution)/shard_map/ppermute | solution.py:20
  89.4 1.5 %collective-permute-start.9 = (bf16[1,256,256]{2,1,0:T(8,128)(2,1)S(1)}, bf16[1,256,256]{2,1,0:T(8,128)(2,1)S(1)}, u32[]{:S(2)}, u32[]{:S(2)}) collective-permute-start(bf16[1,256,256]{2,1,0:T(8,128)(2,1)S(1)} %get-tuple-element.41), channel_id=1, source_target_pairs={{2,0},{4,2},{6,4},{8,6},{10,8},{12,10},{14,12},{3,1},{5,3},{7,5},{... | collective-permute-start | bytes 393224 | tf_op jit(solution)/shard_map/ppermute | solution.py:22
  90.8 2.4 %collective-permute-done.8 = bf16[1,256,256]{2,1,0:T(8,128)(2,1)S(1)} collective-permute-done((bf16[1,256,256]{2,1,0:T(8,128)(2,1)S(1)}, bf16[1,256,256]{2,1,0:T(8,128)(2,1)S(1)}, u32[]{:S(2)}, u32[]{:S(2)}) %collective-permute-start.8) | collective-permute-done | bytes 131104 | tf_op jit(solution)/shard_map/ppermute | solution.py:20
  93.2 4.0 %collective-permute-done.9 = bf16[1,256,256]{2,1,0:T(8,128)(2,1)S(1)} collective-permute-done((bf16[1,256,256]{2,1,0:T(8,128)(2,1)S(1)}, bf16[1,256,256]{2,1,0:T(8,128)(2,1)S(1)}, u32[]{:S(2)}, u32[]{:S(2)}) %collective-permute-start.9) | collective-permute-done | bytes 131104 | tf_op jit(solution)/shard_map/ppermute | solution.py:22
  97.2 1.7 %collective-permute-start.10 = (bf16[6,1,256]{2,1,0:T(2,128)(2,1)S(1)}, bf16[6,1,256]{2,1,0:T(2,128)(2,1)S(1)}, u32[]{:S(2)}, u32[]{:S(2)}) collective-permute-start(bf16[6,1,256]{2,1,0:T(2,128)(2,1)S(1)} %get-tuple-element.26), channel_id=1, source_target_pairs={{0,1},{2,3},{4,5},{6,7},{8,9},{10,11},{12,13},{14,15},{16,17},{18,... | collective-permute-start | bytes 9224 | tf_op jit(solution)/shard_map/ppermute | solution.py:20
  98.9 1.3 %collective-permute-start.11 = (bf16[6,1,256]{2,1,0:T(2,128)(2,1)S(1)}, bf16[6,1,256]{2,1,0:T(2,128)(2,1)S(1)}, u32[]{:S(2)}, u32[]{:S(2)}) collective-permute-start(bf16[6,1,256]{2,1,0:T(2,128)(2,1)S(1)} %get-tuple-element.27), channel_id=1, source_target_pairs={{1,0},{3,2},{5,4},{7,6},{9,8},{11,10},{13,12},{15,14},{17,16},{19,... | collective-permute-start | bytes 9224 | tf_op jit(solution)/shard_map/ppermute | solution.py:22
  100.3 1.2 %fusion.20 = f32[1024,256]{1,0:T(8,128)S(1)} fusion(bf16[1024,256]{1,0:T(8,128)(2,1)S(1)} %bitcast.185, bf16[3,3,256,256]{3,2,1,0:T(8,128)(2,1)} %all-gather.8.cloned.1.call-done), kind=kOutput, calls=%fused_computation.97 | convolution fusion | flops 134217728 | bytes 1703936 | tf_op jit(solution)/shard_map/dot_general | solution.py:64
  (100 shorter events, 23.7 us)
Async XLA Ops:
  6.5 1.5 %copy-start = (bf16[2,128,512]{2,1,0:T(8,128)(2,1)S(1)}, bf16[2,128,512]{2,1,0:T(8,128)(2,1)}, u32[]{:S(2)}) copy-start(bf16[2,128,512]{2,1,0:T(8,128)(2,1)} %param.8) | copy-start | bytes 786436
  6.5 18.1 %all-gather.4.cloned.1.call-start = ((), (), s32[]{:S(2)}) async-start(), calls=%async_computation | async-start | bytes 6291456 | tf_op jit(solution)/shard_map/all_gather | solution.py:85
  7.3 74.2 %all-gather.6.cloned.1.call-start = ((), (), s32[]{:S(2)}) async-start(), calls=%async_computation.1 | async-start | bytes 1769472 | tf_op jit(solution)/shard_map/all_gather | solution.py:103
  8.0 92.3 %all-gather.8.cloned.1.call-start = ((), (), s32[]{:S(2)}) async-start(), calls=%async_computation.2 | async-start | bytes 1769472 | tf_op jit(solution)/shard_map/all_gather | solution.py:109
  8.1 7.6 %collective-permute-start = (bf16[1,128,512]{2,1,0:T(8,128)(2,1)S(1)}, bf16[1,128,512]{2,1,0:T(8,128)(2,1)S(1)}, u32[]{:S(2)}, u32[]{:S(2)}) collective-permute-start(bf16[1,128,512]{2,1,0:T(8,128)(2,1)S(1)} %get-tuple-element.55), channel_id=1, source_target_pairs={{0,2},{2,4},{4,6},{6,8},{8,10},{10,12},{12,14},{1,3},{3,5},{5,7},{... | collective-permute-start | bytes 393224 | tf_op jit(solution)/shard_map/ppermute | solution.py:20
  13.0 6.9 %collective-permute-start.1 = (bf16[1,128,512]{2,1,0:T(8,128)(2,1)S(1)}, bf16[1,128,512]{2,1,0:T(8,128)(2,1)S(1)}, u32[]{:S(2)}, u32[]{:S(2)}) collective-permute-start(bf16[1,128,512]{2,1,0:T(8,128)(2,1)S(1)} %get-tuple-element.54), channel_id=1, source_target_pairs={{2,0},{4,2},{6,4},{8,6},{10,8},{12,10},{14,12},{3,1},{5,3},{7,5},{... | collective-permute-start | bytes 393224 | tf_op jit(solution)/shard_map/ppermute | solution.py:22
  20.0 2.6 %collective-permute-start.2 = (bf16[4,1,512]{2,1,0:T(2,128)(2,1)S(1)}, bf16[4,1,512]{2,1,0:T(2,128)(2,1)S(1)}, u32[]{:S(2)}, u32[]{:S(2)}) collective-permute-start(bf16[4,1,512]{2,1,0:T(2,128)(2,1)S(1)} %get-tuple-element.49), channel_id=1, source_target_pairs={{0,1},{2,3},{4,5},{6,7},{8,9},{10,11},{12,13},{14,15},{16,17},{18,... | collective-permute-start | bytes 12296 | tf_op jit(solution)/shard_map/ppermute | solution.py:20
  21.3 3.1 %collective-permute-start.3 = (bf16[4,1,512]{2,1,0:T(2,128)(2,1)S(1)}, bf16[4,1,512]{2,1,0:T(2,128)(2,1)S(1)}, u32[]{:S(2)}, u32[]{:S(2)}) collective-permute-start(bf16[4,1,512]{2,1,0:T(2,128)(2,1)S(1)} %get-tuple-element.50), channel_id=1, source_target_pairs={{1,0},{3,2},{5,4},{7,6},{9,8},{11,10},{13,12},{15,14},{17,16},{19,... | collective-permute-start | bytes 12296 | tf_op jit(solution)/shard_map/ppermute | solution.py:22
  24.6 5.1 %copy-start.1 = (bf16[4,4,512,256]{3,2,1,0:T(8,128)(2,1)S(1)}, bf16[4,4,512,256]{3,2,1,0:T(8,128)(2,1)}, u32[]{:S(2)}) copy-start(bf16[4,4,512,256]{3,2,1,0:T(8,128)(2,1)} %all-gather.4.cloned.1.call-done) | copy-start | bytes 12582916
  34.3 35.9 %copy-start.4 = (f32[256]{0:T(256)S(1)}, f32[256]{0:T(256)}, u32[]{:S(2)}) copy-start(f32[256]{0:T(256)} %param.11) | copy-start | bytes 3076
  34.3 35.9 %copy-start.5 = (f32[256]{0:T(256)S(1)}, f32[256]{0:T(256)}, u32[]{:S(2)}) copy-start(f32[256]{0:T(256)} %param.10) | copy-start | bytes 3076
  70.6 5.2 %collective-permute-start.4 = (bf16[1,256,256]{2,1,0:T(8,128)(2,1)S(1)}, bf16[1,256,256]{2,1,0:T(8,128)(2,1)S(1)}, u32[]{:S(2)}, u32[]{:S(2)}) collective-permute-start(bf16[1,256,256]{2,1,0:T(8,128)(2,1)S(1)} %get-tuple-element.44), channel_id=1, source_target_pairs={{0,2},{2,4},{4,6},{6,8},{8,10},{10,12},{12,14},{1,3},{3,5},{5,7},{... | collective-permute-start | bytes 393224 | tf_op jit(solution)/shard_map/ppermute | solution.py:20
  71.9 6.9 %collective-permute-start.5 = (bf16[1,256,256]{2,1,0:T(8,128)(2,1)S(1)}, bf16[1,256,256]{2,1,0:T(8,128)(2,1)S(1)}, u32[]{:S(2)}, u32[]{:S(2)}) collective-permute-start(bf16[1,256,256]{2,1,0:T(8,128)(2,1)S(1)} %get-tuple-element.45), channel_id=1, source_target_pairs={{2,0},{4,2},{6,4},{8,6},{10,8},{12,10},{14,12},{3,1},{5,3},{7,5},{... | collective-permute-start | bytes 393224 | tf_op jit(solution)/shard_map/ppermute | solution.py:22
  78.8 3.9 %collective-permute-start.6 = (bf16[6,1,256]{2,1,0:T(2,128)(2,1)S(1)}, bf16[6,1,256]{2,1,0:T(2,128)(2,1)S(1)}, u32[]{:S(2)}, u32[]{:S(2)}) collective-permute-start(bf16[6,1,256]{2,1,0:T(2,128)(2,1)S(1)} %get-tuple-element.30), channel_id=1, source_target_pairs={{0,1},{2,3},{4,5},{6,7},{8,9},{10,11},{12,13},{14,15},{16,17},{18,... | collective-permute-start | bytes 9224 | tf_op jit(solution)/shard_map/ppermute | solution.py:20
  80.1 3.1 %collective-permute-start.7 = (bf16[6,1,256]{2,1,0:T(2,128)(2,1)S(1)}, bf16[6,1,256]{2,1,0:T(2,128)(2,1)S(1)}, u32[]{:S(2)}, u32[]{:S(2)}) collective-permute-start(bf16[6,1,256]{2,1,0:T(2,128)(2,1)S(1)} %get-tuple-element.31), channel_id=1, source_target_pairs={{1,0},{3,2},{5,4},{7,6},{9,8},{11,10},{13,12},{15,14},{17,16},{19,... | collective-permute-start | bytes 9224 | tf_op jit(solution)/shard_map/ppermute | solution.py:22
  83.5 1.3 %copy-start.2 = (bf16[3,3,256,256]{3,2,1,0:T(8,128)(2,1)S(1)}, bf16[3,3,256,256]{3,2,1,0:T(8,128)(2,1)}, u32[]{:S(2)}) copy-start(bf16[3,3,256,256]{3,2,1,0:T(8,128)(2,1)} %all-gather.6.cloned.1.call-done) | copy-start | bytes 3538948
  86.9 0.7 copy-start.6
  87.9 5.3 %collective-permute-start.8 = (bf16[1,256,256]{2,1,0:T(8,128)(2,1)S(1)}, bf16[1,256,256]{2,1,0:T(8,128)(2,1)S(1)}, u32[]{:S(2)}, u32[]{:S(2)}) collective-permute-start(bf16[1,256,256]{2,1,0:T(8,128)(2,1)S(1)} %get-tuple-element.40), channel_id=1, source_target_pairs={{0,2},{2,4},{4,6},{6,8},{8,10},{10,12},{12,14},{1,3},{3,5},{5,7},{... | collective-permute-start | bytes 393224 | tf_op jit(solution)/shard_map/ppermute | solution.py:20
  89.4 7.8 %collective-permute-start.9 = (bf16[1,256,256]{2,1,0:T(8,128)(2,1)S(1)}, bf16[1,256,256]{2,1,0:T(8,128)(2,1)S(1)}, u32[]{:S(2)}, u32[]{:S(2)}) collective-permute-start(bf16[1,256,256]{2,1,0:T(8,128)(2,1)S(1)} %get-tuple-element.41), channel_id=1, source_target_pairs={{2,0},{4,2},{6,4},{8,6},{10,8},{12,10},{14,12},{3,1},{5,3},{7,5},{... | collective-permute-start | bytes 393224 | tf_op jit(solution)/shard_map/ppermute | solution.py:22
  97.2 4.3 %collective-permute-start.10 = (bf16[6,1,256]{2,1,0:T(2,128)(2,1)S(1)}, bf16[6,1,256]{2,1,0:T(2,128)(2,1)S(1)}, u32[]{:S(2)}, u32[]{:S(2)}) collective-permute-start(bf16[6,1,256]{2,1,0:T(2,128)(2,1)S(1)} %get-tuple-element.26), channel_id=1, source_target_pairs={{0,1},{2,3},{4,5},{6,7},{8,9},{10,11},{12,13},{14,15},{16,17},{18,... | collective-permute-start | bytes 9224 | tf_op jit(solution)/shard_map/ppermute | solution.py:20
  98.9 3.1 %collective-permute-start.11 = (bf16[6,1,256]{2,1,0:T(2,128)(2,1)S(1)}, bf16[6,1,256]{2,1,0:T(2,128)(2,1)S(1)}, u32[]{:S(2)}, u32[]{:S(2)}) collective-permute-start(bf16[6,1,256]{2,1,0:T(2,128)(2,1)S(1)} %get-tuple-element.27), channel_id=1, source_target_pairs={{1,0},{3,2},{5,4},{7,6},{9,8},{11,10},{13,12},{15,14},{17,16},{19,... | collective-permute-start | bytes 9224 | tf_op jit(solution)/shard_map/ppermute | solution.py:22
  102.3 1.3 %copy-start.3 = (bf16[3,3,256,256]{3,2,1,0:T(8,128)(2,1)S(1)}, bf16[3,3,256,256]{3,2,1,0:T(8,128)(2,1)}, u32[]{:S(2)}) copy-start(bf16[3,3,256,256]{3,2,1,0:T(8,128)(2,1)} %all-gather.8.cloned.1.call-done) | copy-start | bytes 3538948
  105.8 0.7 copy-start.7
Sparse Core Ops, SparseCore 0:
  8.9 15.6 all-gather.3
  26.2 10.3 all-gather.5
  38.1 10.3 all-gather.7
where the time goes:
time: 115 us; the launch traced here: 114 us
  blocking collectives  33.9 us (29%)
  waiting for transfers between devices  20.1 us (17%)
  starting transfers between devices  19.9 us (17%)
  matrix products  14.9 us (13%)
  between operations  13.8 us (12%)
  other arithmetic  6.14 us (5%)
  local copies, waits for them, and re-layouts  5.25 us (5%)
    psum x1, blocking collectives, local(): total, total_sq = lax.psum((sums, squares), ('rows', 'fsdp'))  33.9 us
    ppermute x6, waiting for transfers between devices, padded_2(): lax.ppermute(head, axis, [((i + 1) % count, i) for i in range(ends)])  13.7 us
    ppermute x6, starting transfers between devices, padded_2(): lax.ppermute(tail, axis, [(i, (i + 1) % count) for i in range(ends)])  11.9 us
    ppermute x6, starting transfers between devices, padded_2(): lax.ppermute(head, axis, [((i + 1) % count, i) for i in range(ends)])  7.93 us
    dot_general x16, matrix products, upsample(): jnp.dot(patch, weight[row_tap, col_tap], preferred_element_type=jnp.float32)  7.6 us
    dot_general x18, matrix products, convolve(): jnp.dot(patch, weight[row_tap, col_tap], preferred_element_type=jnp.float32)  7.26 us
    ppermute x6, waiting for transfers between devices, padded_2(): lax.ppermute(tail, axis, [(i, (i + 1) % count) for i in range(ends)])  4.92 us
    unnamed x17, local copies, waits for them, and re-layouts  2.87 us
  transfers between devices with their start and end apart: 15, of which 9 were waited for; matrix products, arithmetic and copies ran while one was open for 17% of the time, Pallas kernels for 0%

commit v1 on v0

v1 whole, which is shorter than its diff:
```python
import functools

import jax
import jax.numpy as jnp
from jax import lax
from jax.experimental import pallas as pl
from jax.experimental.pallas import tpu as pltpu
from jax.sharding import PartitionSpec as P

NORM_GROUPS = 32
HALO = 2
EDGE = 16
VMEM_BYTES = 40 * 2**20


def silu(v):
    h = 0.5 * v
    return h + h * jnp.tanh(h)


def edge_mask(width):
    column = lax.axis_index("fsdp")
    last = lax.axis_size("fsdp") - 1
    cell = lax.broadcasted_iota(jnp.int32, (width + EDGE, 1), 0) - width
    right = (cell < EDGE // 2) & (column < last)
    left = (cell >= EDGE // 2) & (column > 0)
    return (cell < 0) | right | left


def deconv_kernel(own_ref, up_ref, down_ref, edge_ref, own_w, other_w, u_ref, stats_ref, xs, wd, sems):
    rows, width, cin = own_ref.shape
    lanes = own_w.shape[-1]
    taps = own_w.shape[0]
    column = lax.axis_index("fsdp")
    copies = []
    for kr in range(taps):
        for phase in range(2):
            for side, ref in enumerate((own_w, other_w)):
                place = column if side == 0 else 1 - column
                copies.append(
                    pltpu.make_async_copy(
                        ref.at[kr, :, 1 - phase],
                        wd.at[kr, phase, :, :, pl.ds(pl.multiple_of(place * lanes, lanes), lanes)],
                        sems.at[kr, phase, side],
                    )
                )
    for copy in copies:
        copy.start()

    cell = lax.broadcasted_iota(jnp.int32, (EDGE, 1), 0)
    keep = jnp.where(column == 0, cell, EDGE - 1 - cell) < EDGE // 2
    for row in range(rows + 2 * HALO):
        if row < HALO:
            main = up_ref[row]
        elif row < HALO + rows:
            main = own_ref[row - HALO]
        else:
            main = down_ref[row - HALO - rows]
        edge = jnp.where(keep, edge_ref[row].astype(jnp.float32), 0.0)
        line = jnp.concatenate([main.astype(jnp.float32), edge], axis=0)
        total = width + EDGE
        xs[row, :, 0:cin] = pltpu.roll(line, total - 1, 0).astype(jnp.bfloat16)
        xs[row, :, cin : 2 * cin] = line.astype(jnp.bfloat16)
        xs[row, :, 2 * cin : 3 * cin] = pltpu.roll(line, 1, 0).astype(jnp.bfloat16)
    for copy in copies:
        copy.wait()

    total = width + EDGE
    lines = rows + 2
    cout = u_ref.shape[-1]
    sums = jnp.zeros((1, cout), jnp.float32)
    squares = jnp.zeros((1, cout), jnp.float32)
    for phase_row in range(2):
        first, second = ((3, 1), (2, 0))[phase_row]
        for phase in range(2):
            low = (1 - phase) * cin
            part = slice(low, low + 2 * cin)
            acc = jnp.dot(
                xs[phase_row : phase_row + lines, :, part].reshape(lines * total, 2 * cin),
                wd[first, phase].reshape(2 * cin, cout),
                preferred_element_type=jnp.float32,
            ) + jnp.dot(
                xs[phase_row + 1 : phase_row + 1 + lines, :, part].reshape(lines * total, 2 * cin),
                wd[second, phase].reshape(2 * cin, cout),
                preferred_element_type=jnp.float32,
            )
            acc = acc.astype(jnp.bfloat16).reshape(lines, total, cout)
            for line in range(lines):
                u_ref[2 * line + phase_row, phase] = acc[line]
                if 1 <= line < 1 + rows:
                    values = acc[line, :width].astype(jnp.float32)
                    sums += jnp.sum(values, axis=0, keepdims=True)
                    squares += jnp.sum(values * values, axis=0, keepdims=True)
    half = cout // 2
    block = jnp.concatenate(
        [sums[:, :half], sums[:, half:], squares[:, :half], squares[:, half:]]
        + [jnp.zeros((4, half), jnp.float32)],
        axis=0,
    )
    for peer in range(stats_ref.shape[0]):
        stats_ref[peer] = block


def group_sum(v, width):
    lane = lax.broadcasted_iota(jnp.int32, v.shape, 1)
    size = v.shape[1]
    step = 1
    while step < width:
        v = v + jnp.where(
            (lane & step) == 0, pltpu.roll(v, size - step, 1), pltpu.roll(v, step, 1)
        )
        step *= 2
    return v


def fill(ref, row, even, odd):
    total, channels = even.shape
    ref[row, :, 0:channels] = pltpu.roll(odd, 1, 0).astype(jnp.bfloat16)
    ref[row, :, channels : 2 * channels] = even.astype(jnp.bfloat16)
    ref[row, :, 2 * channels : 3 * channels] = odd.astype(jnp.bfloat16)
    ref[row, :, 3 * channels : 4 * channels] = pltpu.roll(even, total - 1, 0).astype(jnp.bfloat16)


def conv_kernel(count, u_ref, stats_ref, params_ref, w1_ref, w2_ref, out_ref, g, act, w1, w2, mixed, sems):
    lines, _, total, cout = u_ref.shape
    width = total - EDGE
    lanes = w1_ref.shape[-1]
    copies = []
    for index, (src, dst) in enumerate(((w1_ref, w1), (w2_ref, w2))):
        for side in range(src.shape[0]):
            copies.append(
                pltpu.make_async_copy(
                    src.at[side],
                    dst.at[:, :, :, side * lanes : (side + 1) * lanes],
                    sems.at[index, side],
                )
            )
    for copy in copies:
        copy.start()

    block = stats_ref[0]
    for peer in range(1, stats_ref.shape[0]):
        block += stats_ref[peer]
    width_group = cout // NORM_GROUPS
    sums = jnp.concatenate([block[0:1], block[1:2]], axis=1)
    squares = jnp.concatenate([block[2:3], block[3:4]], axis=1)
    mean = group_sum(sums, width_group) / count
    spread = group_sum(squares, width_group) / count - mean * mean
    scale = lax.rsqrt(spread + 1e-05) * params_ref[0:1]
    shift = params_ref[1:2] - mean * scale

    mask = edge_mask(width)
    place = lax.axis_index("rows")
    last = lax.axis_size("rows") - 1

    def inside(row, beyond):
        if row < beyond:
            return mask & (place > 0)
        if row >= lines - 2 * HALO + beyond:
            return mask & (place < last)
        return mask

    for row in range(lines):
        seen = inside(row, HALO)
        pair = [
            jnp.where(seen, silu(u_ref[row, phase].astype(jnp.float32) * scale + shift), 0.0)
            for phase in range(2)
        ]
        fill(g, row, *pair)
    for copy in copies[:2]:
        copy.wait()
    bias = params_ref[2:3]
    chunk = 2
    for start in range(0, lines - 2, chunk):
        results = []
        for phase in range(2):
            acc = bias
            for a in range(3):
                acc = acc + jnp.dot(
                    g[start + a : start + a + chunk, :, phase * cout : (phase + 3) * cout].reshape(
                        chunk * total, 3 * cout
                    ),
                    w1[a].reshape(3 * cout, cout),
                    preferred_element_type=jnp.float32,
                )
            results.append(silu(acc).reshape(chunk, total, cout))
        for row in range(chunk):
            seen = inside(start + row, 1)
            fill(act, start + row, *[jnp.where(seen, r[row], 0.0) for r in results])
    for copy in copies[2:]:
        copy.wait()
    bias = params_ref[3:4]
    for start in range(0, lines - 4, chunk):
        for phase in range(2):
            acc = bias
            for a in range(3):
                acc = acc + jnp.dot(
                    act[start + a : start + a + chunk, 0:width, phase * cout : (phase + 3) * cout].reshape(
                        chunk * width, 3 * cout
                    ),
                    w2[a].reshape(3 * cout, cout),
                    preferred_element_type=jnp.float32,
                )
            acc = acc.reshape(chunk, width, cout)
            for row in range(chunk):
                for side in range(0, cout, 128):
                    mixed[side // 128, start + row, pl.ds(phase, width, stride=2), :] = acc[row, :, side : side + 128]
    for row in range(lines - 4):
        for side in range(0, cout, 128):
            out_ref[row, :, side : side + 128] = mixed[side // 128, row].astype(jnp.bfloat16)


def local(image, deconv_weight, norm_gain, norm_shift, first_weight, first_bias, second_weight, second_bias):
    rows, width, cin = image.shape
    taps, _, _, lanes = deconv_weight.shape
    columns = lax.axis_size("fsdp")
    cout = lanes * columns
    assert columns == 2 and rows >= HALO and width % EDGE == 0
    n_rows = lax.axis_size("rows")
    n = n_rows * columns
    count = float(2 * rows * n_rows * 2 * width * columns * (cout // NORM_GROUPS))
    swap = [(0, 1), (1, 0)]

    up = lax.ppermute(image[rows - HALO :], "rows", [(i, i + 1) for i in range(n_rows - 1)])
    down = lax.ppermute(image[:HALO], "rows", [(i + 1, i) for i in range(n_rows - 1)])
    other_w = lax.ppermute(deconv_weight, "fsdp", swap)
    first_all = lax.all_gather(first_weight, "fsdp")
    second_all = lax.all_gather(second_weight, "fsdp")
    rimmed = jnp.concatenate([up, image, down], axis=0)
    sent = jnp.where(lax.axis_index("fsdp") == 0, rimmed[:, width - EDGE :], rimmed[:, :EDGE])
    edge = lax.ppermute(sent, "fsdp", swap)

    total = width + EDGE
    any_spec = pl.BlockSpec(memory_space=pl.ANY)
    vmem = pl.BlockSpec(memory_space=pltpu.VMEM)
    shape_w = (taps, taps // 2, 2, cin, lanes)
    u, stats = pl.pallas_call(
        deconv_kernel,
        out_shape=(
            jax.ShapeDtypeStruct((2 * rows + 2 * HALO, 2, total, cout), jnp.bfloat16),
            jax.ShapeDtypeStruct((n, 8, cout // 2), jnp.float32),
        ),
        in_specs=[vmem] * 4 + [any_spec] * 2,
        out_specs=(vmem, vmem),
        scratch_shapes=[
            pltpu.VMEM((rows + 2 * HALO, total, 3 * cin), jnp.bfloat16),
            pltpu.VMEM((taps, 2, taps // 2, cin, cout), jnp.bfloat16),
            pltpu.SemaphoreType.DMA((taps, 2, 2)),
        ],
        compiler_params=pltpu.CompilerParams(vmem_limit_bytes=VMEM_BYTES),
        name="deconv",
    )(image, up, down, edge, deconv_weight.reshape(shape_w), other_w.reshape(shape_w))

    gathered = lax.all_to_all(stats, ("rows", "fsdp"), split_axis=0, concat_axis=0)
    params = jnp.stack([norm_gain, norm_shift, first_bias, second_bias])
    out = pl.pallas_call(
        functools.partial(conv_kernel, count),
        out_shape=jax.ShapeDtypeStruct((2 * rows, 2 * width, cout), jnp.bfloat16),
        in_specs=[vmem] * 3 + [any_spec] * 2,
        out_specs=vmem,
        scratch_shapes=[
            pltpu.VMEM((2 * rows + 2 * HALO, total, 4 * cout), jnp.bfloat16),
            pltpu.VMEM((2 * rows + 2, total, 4 * cout), jnp.bfloat16),
            pltpu.VMEM((3, 3, cout, cout), jnp.bfloat16),
            pltpu.VMEM((3, 3, cout, cout), jnp.bfloat16),
            pltpu.VMEM((cout // 128, 2 * rows, 2 * width, 128), jnp.float32),
            pltpu.SemaphoreType.DMA((2, 2)),
        ],
        compiler_params=pltpu.CompilerParams(vmem_limit_bytes=VMEM_BYTES),
        name="convs",
    )(u, gathered, params, first_all, second_all)
    return out


def solution(mesh):
    placed = (
        P(("groups", "rows"), "fsdp", None),
        P(None, None, None, "fsdp"),
        P(),
        P(),
        P(None, None, None, "fsdp"),
        P(),
        P(None, None, None, "fsdp"),
        P(),
    )
    return jax.shard_map(
        local,
        mesh=mesh,
        in_specs=placed,
        out_specs=P(("groups", "rows"), "fsdp", None),
        check_vma=False,
    )
```

time: 115 us -> 62.5 us (0.54)
  blocking collectives: 33.9 us -> 0 us
  matrix products: 14.9 us -> 0 us
  Pallas kernels: 0 us -> 10.7 us
  starting transfers between devices: 19.9 us -> 13.7 us
  other arithmetic: 6.14 us -> 0.03 us
  waiting for transfers between devices: 20.1 us -> 18.9 us
    psum x1 -> x0, blocking collectives: 33.9 us -> none  [local(): total, total_sq = lax.psum((sums, squares), ('rows', 'fsdp'))]
    dot_general x34 -> x0, matrix products: 14.9 us -> none  [the longest x16 7.6 us: upsample(): jnp.dot(patch, weight[row_tap, col_tap], preferred_element_type=jnp.float32)]
    ppermute x12 -> x4, starting transfers between devices: 19.9 us -> 6.77 us  [the longest x1 4.89 us: local(): lax.ppermute(image[rows - HALO:], 'rows', [(i, i + 1) for i in range(n_ro...]
    pallas_call x0 -> x2, Pallas kernels: none -> 10.7 us  [the longest x1 6.33 us: local(): pl.pallas_call(functools.partial(conv_kernel, count), out_shape=jax.Shape...]
    ppermute x12 -> x4, waiting for transfers between devices: 18.6 us -> 11.2 us  [the longest x1 9.9 us: local(): lax.ppermute(image[rows - HALO:], 'rows', [(i, i + 1) for i in range(n_ro...]
    all_to_all x0 -> x1, starting transfers between devices: none -> 6.93 us  [local(): lax.all_to_all(stats, ('rows', 'fsdp'), split_axis=0, concat_axis=0)]
    all_to_all x0 -> x1, waiting for transfers between devices: none -> 6.78 us  [local(): lax.all_to_all(stats, ('rows', 'fsdp'), split_axis=0, concat_axis=0)]
    convert_element_type x4 -> x0, other arithmetic: 2.71 us -> none  [the longest x2 1.55 us: local(): hidden = jax.nn.silu(values * scale + shift).astype(jnp.bfloat16)]
  transfers between devices with their start and end apart: 15 -> 7, of which waited for: 9 -> 3; matrix products, arithmetic and copies ran while one was open for 17% -> 0% of each run, Pallas kernels for 0% -> 7%
where the time goes in v1:
time: 62.5 us; the launch traced here: 62.1 us
  waiting for transfers between devices  18.9 us (30%)
  starting transfers between devices  13.7 us (22%)
  between operations  13.6 us (22%)
  Pallas kernels  10.7 us (17%)
  local copies, waits for them, and re-layouts  5.15 us (8%)
    ppermute x1, waiting for transfers between devices, local(): lax.ppermute(image[rows - HALO:], 'rows', [(i, i + 1) for i in range(n_ro...  9.9 us
    all_to_all x1, starting transfers between devices, local(): lax.all_to_all(stats, ('rows', 'fsdp'), split_axis=0, concat_axis=0)  6.93 us
    all_to_all x1, waiting for transfers between devices, local(): lax.all_to_all(stats, ('rows', 'fsdp'), split_axis=0, concat_axis=0)  6.78 us
    pallas_call x1, Pallas kernels, local(): pl.pallas_call(functools.partial(conv_kernel, count), out_shape=jax.Shape...  6.33 us
    unnamed x28, local copies, waits for them, and re-layouts  5.13 us
    ppermute x1, starting transfers between devices, local(): lax.ppermute(image[rows - HALO:], 'rows', [(i, i + 1) for i in range(n_ro...  4.89 us
    pallas_call x1, Pallas kernels, local(): pl.pallas_call(deconv_kernel, out_shape=(jax.ShapeDtypeStruct((2 * rows +...  4.38 us
    ppermute x1, starting transfers between devices, local(): lax.ppermute(image[:HALO], 'rows', [(i + 1, i) for i in range(n_rows - 1)])  1.29 us
  transfers between devices with their start and end apart: 7, of which 3 were waited for; matrix products, arithmetic and copies ran while one was open for 0% of the time, Pallas kernels for 7%

profile of v1, /device:TPU:0, one launch (start us, length us, event | category | flops | bytes accessed | tf_op | source)
XLA Modules:
  0.0 62.1 jit_solution(7592441775244021091)
XLA Ops:
  6.5 0.7 %all-gather.5.cloned.1.call-update = ((bf16[3,3,256,128]{3,2,1,0:T(8,128)(2,1)}), bf16[6,3,256,128]{3,2,1,0:T(8,128)(2,1)}) async-update(((), (), s32[]{:S(2)}) %all-gather.5.cloned.1.call-start, bf16[3,3,256,128]{3,2,1,0:T(8,128)(2,1)} %param.12) | async-update | bytes 2359320
  7.3 0.0 all-gather.7.cloned.1.call-start
  7.3 0.5 collective-permute-start.3
  7.8 0.2 all-gather.7.cloned.1.call-update
  8.0 4.9 %collective-permute-start = (bf16[2,128,512]{2,1,0:T(8,128)(2,1)S(1)}, bf16[2,128,512]{2,1,0:T(8,128)(2,1)S(1)}, u32[]{:S(2)}, u32[]{:S(2)}) collective-permute-start(bf16[2,128,512]{2,1,0:T(8,128)(2,1)S(1)} %copy-done.3), channel_id=1, source_target_pairs={{0,2},{2,4},{4,6},{6,8},{8,10},{10,12},{12,14},{1,3},{3,5},{5,7},{... | collective-permute-start | bytes 786440 | tf_op jit(solution)/shard_map/ppermute | solution.py:224
  12.9 1.3 %collective-permute-start.1 = (bf16[2,128,512]{2,1,0:T(8,128)(2,1)S(1)}, bf16[2,128,512]{2,1,0:T(8,128)(2,1)S(1)}, u32[]{:S(2)}, u32[]{:S(2)}) collective-permute-start(bf16[2,128,512]{2,1,0:T(8,128)(2,1)S(1)} %copy-done.3), channel_id=1, source_target_pairs={{2,0},{4,2},{6,4},{8,6},{10,8},{12,10},{14,12},{3,1},{5,3},{7,5},{... | collective-permute-start | bytes 786440 | tf_op jit(solution)/shard_map/ppermute | solution.py:225
  14.2 9.9 %collective-permute-done.up_ref = bf16[2,128,512]{2,1,0:T(8,128)(2,1)S(1)} collective-permute-done((bf16[2,128,512]{2,1,0:T(8,128)(2,1)S(1)}, bf16[2,128,512]{2,1,0:T(8,128)(2,1)S(1)}, u32[]{:S(2)}, u32[]{:S(2)}) %collective-permute-start) | collective-permute-done | bytes 262176 | tf_op jit(solution)/shard_map/ppermute | solution.py:224
  24.2 0.0 collective-permute-done.1.down_ref
  24.3 0.1 collective-permute-start.2
  24.3 1.3 %collective-permute-done.2.edge_ref = bf16[6,16,512]{2,1,0:T(8,128)(2,1)S(1)} collective-permute-done((bf16[6,16,512]{2,1,0:T(8,128)(2,1)S(1)}, bf16[6,16,512]{2,1,0:T(8,128)(2,1)S(1)}, u32[]{:S(2)}, u32[]{:S(2)}) %collective-permute-start.2) | collective-permute-done | bytes 98336 | tf_op jit(solution)/shard_map/ppermute | solution.py:231
  25.6 0.0 collective-permute-done.3
  25.6 0.0 copy-start.5
  25.7 0.9 %copy-done.5 = bf16[2,128,512]{2,1,0:T(8,128)(2,1)S(1)} copy-done((bf16[2,128,512]{2,1,0:T(8,128)(2,1)S(1)}, bf16[2,128,512]{2,1,0:T(8,128)(2,1)}, u32[]{:S(2)}) %copy-start.5) | copy-done | bytes 262168
  26.6 0.9 %copy-done.7 = bf16[2,128,512]{2,1,0:T(8,128)(2,1)S(1)} copy-done((bf16[2,128,512]{2,1,0:T(8,128)(2,1)S(1)}, bf16[2,128,512]{2,1,0:T(8,128)(2,1)}, u32[]{:S(2)}) %copy-start.7) | copy-done | bytes 262168
  27.6 4.4 %deconv.1 = (bf16[8,2,144,256]{3,2,1,0:T(8,128)(2,1)S(1)}, f32[16,8,128]{2,1,0:T(8,128)S(1)}) custom-call(bf16[2,128,512]{2,1,0:T(8,128)(2,1)S(1)} %copy-done.3, bf16[2,128,512]{2,1,0:T(8,128)(2,1)S(1)} %copy-done.5, bf16[2,128,512]{2,1,0:T(8,128)(2,1)S(1)} %copy-done.7, bf16[6,16,512]{2,1,0:T(8,128)(2,1)S(1)} %collective-permute-done.2.edge_ref, ...), custom_call_target="tpu_custom_call" | custom-call | tf_op jit(solution)/shard_map/deconv/pallas_call | solution.py:237
  31.9 0.0 copy-start.8
  32.0 0.6 copy-done.8
  32.6 6.9 %all-to-all-start = ((f32[16,8,128]{2,1,0:T(8,128)}), f32[16,8,128]{2,1,0:T(8,128)S(1)}, u32[]{:S(2)}, u32[]{:S(2)}) async-start(f32[16,8,128]{2,1,0:T(8,128)} %copy-done.8), calls=%async_computation | async-start | bytes 131072 | tf_op jit(solution)/shard_map/all_to_all | solution.py:254
  39.6 0.0 all-gather.5.cloned.1.call-done
  39.6 0.0 all-gather.7.cloned.1.call-done
  39.6 6.8 %all-to-all-done.stats_ref = f32[16,8,128]{2,1,0:T(8,128)S(1)} async-done(((f32[16,8,128]{2,1,0:T(8,128)}), f32[16,8,128]{2,1,0:T(8,128)S(1)}, u32[]{:S(2)}, u32[]{:S(2)}) %all-to-all-start) | async-done | bytes 65568 | tf_op jit(solution)/shard_map/all_to_all | solution.py:254
  46.4 1.3 %copy-done.1 = bf16[6,3,256,128]{3,2,1,0:T(8,128)(2,1)S(1)} copy-done((bf16[6,3,256,128]{3,2,1,0:T(8,128)(2,1)S(1)}, bf16[6,3,256,128]{3,2,1,0:T(8,128)(2,1)}, u32[]{:S(2)}) %copy-start.1) | copy-done | bytes 1179672
  47.7 1.3 %copy-done.2 = bf16[6,3,256,128]{3,2,1,0:T(8,128)(2,1)S(1)} copy-done((bf16[6,3,256,128]{3,2,1,0:T(8,128)(2,1)S(1)}, bf16[6,3,256,128]{3,2,1,0:T(8,128)(2,1)}, u32[]{:S(2)}) %copy-start.2) | copy-done | bytes 1179672
  48.9 6.3 %convs.1 = bf16[4,256,256]{2,1,0:T(8,128)(2,1)} custom-call(bf16[8,2,144,256]{3,2,1,0:T(8,128)(2,1)S(1)} %get-tuple-element.7.u_ref, f32[16,8,128]{2,1,0:T(8,128)S(1)} %all-to-all-done.stats_ref, f32[4,256]{1,0:T(4,128)S(1)} %pad_maximum_fusion.params_ref, bf16[2,3,3,256,128]{4,3,2,1,0:T(8,128)(2,1)S(1)} %bitcast.9, bf16[2,3,3,256,128]{4,3,2,1,0:T(8,128)(2,1)S(1)} %bitcast.10), custom_call_target="tpu_custom_call" | custom-call | tf_op jit(solution)/shard_map/convs/pallas_call | solution.py:256
  (25 shorter events, 0.1 us)
Async XLA Ops:
  6.5 1.5 %copy-start.3 = (bf16[2,128,512]{2,1,0:T(8,128)(2,1)S(1)}, bf16[2,128,512]{2,1,0:T(8,128)(2,1)}, u32[]{:S(2)}) copy-start(bf16[2,128,512]{2,1,0:T(8,128)(2,1)} %own_ref.1) | copy-start | bytes 786436
  6.5 33.1 %all-gather.5.cloned.1.call-start = ((), (), s32[]{:S(2)}) async-start(), calls=%async_computation.1 | async-start | bytes 1769472 | tf_op jit(solution)/shard_map/all_gather | solution.py:227
  7.3 18.4 %copy-start = (bf16[4,4,512,128]{3,2,1,0:T(8,128)(2,1)S(1)}, bf16[4,4,512,128]{3,2,1,0:T(8,128)(2,1)}, u32[]{:S(2)}) copy-start(bf16[4,4,512,128]{3,2,1,0:T(8,128)(2,1)} %param.9) | copy-start | bytes 6291460
  7.3 32.3 %all-gather.7.cloned.1.call-start = ((), (), s32[]{:S(2)}) async-start(), calls=%async_computation.2 | async-start | bytes 1769472 | tf_op jit(solution)/shard_map/all_gather | solution.py:228
  7.3 18.3 %collective-permute-start.3 = (bf16[4,4,512,128]{3,2,1,0:T(8,128)(2,1)}, bf16[4,4,512,128]{3,2,1,0:T(8,128)(2,1)}, u32[]{:S(2)}, u32[]{:S(2)}) collective-permute-start(bf16[4,4,512,128]{3,2,1,0:T(8,128)(2,1)} %param.9), channel_id=1, source_target_pairs={{0,1},{1,0},{2,3},{3,2},{4,5},{5,4},{6,7},{7,6},{8,9},{9,8},{10,11... | collective-permute-start | bytes 6291464 | tf_op jit(solution)/shard_map/ppermute | solution.py:226
  8.0 16.1 %collective-permute-start = (bf16[2,128,512]{2,1,0:T(8,128)(2,1)S(1)}, bf16[2,128,512]{2,1,0:T(8,128)(2,1)S(1)}, u32[]{:S(2)}, u32[]{:S(2)}) collective-permute-start(bf16[2,128,512]{2,1,0:T(8,128)(2,1)S(1)} %copy-done.3), channel_id=1, source_target_pairs={{0,2},{2,4},{4,6},{6,8},{8,10},{10,12},{12,14},{1,3},{3,5},{5,7},{... | collective-permute-start | bytes 786440 | tf_op jit(solution)/shard_map/ppermute | solution.py:224
  12.9 11.3 %collective-permute-start.1 = (bf16[2,128,512]{2,1,0:T(8,128)(2,1)S(1)}, bf16[2,128,512]{2,1,0:T(8,128)(2,1)S(1)}, u32[]{:S(2)}, u32[]{:S(2)}) collective-permute-start(bf16[2,128,512]{2,1,0:T(8,128)(2,1)S(1)} %copy-done.3), channel_id=1, source_target_pairs={{2,0},{4,2},{6,4},{8,6},{10,8},{12,10},{14,12},{3,1},{5,3},{7,5},{... | collective-permute-start | bytes 786440 | tf_op jit(solution)/shard_map/ppermute | solution.py:225
  24.1 1.5 %copy-start.4 = (bf16[2,128,512]{2,1,0:T(8,128)(2,1)}, bf16[2,128,512]{2,1,0:T(8,128)(2,1)S(1)}, u32[]{:S(2)}) copy-start(bf16[2,128,512]{2,1,0:T(8,128)(2,1)S(1)} %collective-permute-done.up_ref) | copy-start | bytes 786436
  24.2 1.4 %copy-start.6 = (bf16[2,128,512]{2,1,0:T(8,128)(2,1)}, bf16[2,128,512]{2,1,0:T(8,128)(2,1)S(1)}, u32[]{:S(2)}) copy-start(bf16[2,128,512]{2,1,0:T(8,128)(2,1)S(1)} %collective-permute-done.1.down_ref) | copy-start | bytes 786436
  24.3 1.4 %collective-permute-start.2 = (bf16[6,16,512]{2,1,0:T(8,128)(2,1)S(1)}, bf16[6,16,512]{2,1,0:T(8,128)(2,1)S(1)}, u32[]{:S(2)}, u32[]{:S(2)}) collective-permute-start(bf16[6,16,512]{2,1,0:T(8,128)(2,1)S(1)} %slice_select_fusion), channel_id=1, source_target_pairs={{0,1},{1,0},{2,3},{3,2},{4,5},{5,4},{6,7},{7,6},{8,9},{9,8},{10,11... | collective-permute-start | bytes 294920 | tf_op jit(solution)/shard_map/ppermute | solution.py:231
  25.6 1.0 %copy-start.5 = (bf16[2,128,512]{2,1,0:T(8,128)(2,1)S(1)}, bf16[2,128,512]{2,1,0:T(8,128)(2,1)}, u32[]{:S(2)}) copy-start(bf16[2,128,512]{2,1,0:T(8,128)(2,1)} %copy-done.4) | copy-start | bytes 786436
  26.6 0.9 %copy-start.7 = (bf16[2,128,512]{2,1,0:T(8,128)(2,1)S(1)}, bf16[2,128,512]{2,1,0:T(8,128)(2,1)}, u32[]{:S(2)}) copy-start(bf16[2,128,512]{2,1,0:T(8,128)(2,1)} %copy-done.6) | copy-start | bytes 786436
  27.5 12.0 %copy-start.9 = (f32[256]{0:T(256)S(1)}, f32[256]{0:T(256)}, u32[]{:S(2)}) copy-start(f32[256]{0:T(256)} %param.15) | copy-start | bytes 3076
  27.5 12.0 %copy-start.10 = (f32[256]{0:T(256)S(1)}, f32[256]{0:T(256)}, u32[]{:S(2)}) copy-start(f32[256]{0:T(256)} %param.13) | copy-start | bytes 3076
  27.5 12.0 %copy-start.11 = (f32[256]{0:T(256)S(1)}, f32[256]{0:T(256)}, u32[]{:S(2)}) copy-start(f32[256]{0:T(256)} %param.11) | copy-start | bytes 3076
  27.6 12.0 %copy-start.12 = (f32[256]{0:T(256)S(1)}, f32[256]{0:T(256)}, u32[]{:S(2)}) copy-start(f32[256]{0:T(256)} %param.10) | copy-start | bytes 3076
  31.9 0.6 %copy-start.8 = (f32[16,8,128]{2,1,0:T(8,128)}, f32[16,8,128]{2,1,0:T(8,128)S(1)}, u32[]{:S(2)}) copy-start(f32[16,8,128]{2,1,0:T(8,128)S(1)} %get-tuple-element.8) | copy-start | bytes 196612
  32.6 13.8 %all-to-all-start = ((f32[16,8,128]{2,1,0:T(8,128)}), f32[16,8,128]{2,1,0:T(8,128)S(1)}, u32[]{:S(2)}, u32[]{:S(2)}) async-start(f32[16,8,128]{2,1,0:T(8,128)} %copy-done.8), calls=%async_computation | async-start | bytes 131072 | tf_op jit(solution)/shard_map/all_to_all | solution.py:254
  46.4 1.3 %copy-start.1 = (bf16[6,3,256,128]{3,2,1,0:T(8,128)(2,1)S(1)}, bf16[6,3,256,128]{3,2,1,0:T(8,128)(2,1)}, u32[]{:S(2)}) copy-start(bf16[6,3,256,128]{3,2,1,0:T(8,128)(2,1)} %all-gather.5.cloned.1.call-done) | copy-start | bytes 3538948
  47.7 1.3 %copy-start.2 = (bf16[6,3,256,128]{3,2,1,0:T(8,128)(2,1)S(1)}, bf16[6,3,256,128]{3,2,1,0:T(8,128)(2,1)}, u32[]{:S(2)}) copy-start(bf16[6,3,256,128]{3,2,1,0:T(8,128)(2,1)} %all-gather.7.cloned.1.call-done) | copy-start | bytes 3538948
Sparse Core Ops, SparseCore 0:
  8.9 11.9 all-gather.4
  22.4 10.3 all-gather.6

commit v2 on v1

v2 whole, which is shorter than its diff:
```python
import functools

import jax
import jax.numpy as jnp
from jax import lax
from jax.experimental import pallas as pl
from jax.experimental.pallas import tpu as pltpu
from jax.sharding import PartitionSpec as P

NORM_GROUPS = 32
HALO = 2
EDGE = 16
VMEM_BYTES = 40 * 2**20


def silu(v):
    h = 0.5 * v
    return h + h * jnp.tanh(h)


def edge_mask(width):
    column = lax.axis_index("fsdp")
    last = lax.axis_size("fsdp") - 1
    cell = lax.broadcasted_iota(jnp.int32, (width + EDGE, 1), 0) - width
    right = (cell < EDGE // 2) & (column < last)
    left = (cell >= EDGE // 2) & (column > 0)
    return (cell < 0) | right | left


def load_deconv(own_w, other_w, wd, sems):
    lanes = own_w.shape[-1]
    column = lax.axis_index("fsdp")
    copies = []
    for kr in range(own_w.shape[0]):
        for phase in range(2):
            for side, ref in enumerate((own_w, other_w)):
                place = column if side == 0 else 1 - column
                copies.append(
                    pltpu.make_async_copy(
                        ref.at[kr, :, 1 - phase],
                        wd.at[kr, phase, :, :, pl.ds(pl.multiple_of(place * lanes, lanes), lanes)],
                        sems.at[kr, phase, side],
                    )
                )
    for copy in copies:
        copy.start()
    return copies


def spread_line(xs, index, main, edge):
    cin = main.shape[-1]
    cell = lax.broadcasted_iota(jnp.int32, (EDGE, 1), 0)
    keep = jnp.where(lax.axis_index("fsdp") == 0, cell, EDGE - 1 - cell) < EDGE // 2
    edge = jnp.where(keep, edge.astype(jnp.float32), 0.0)
    line = jnp.concatenate([main.astype(jnp.float32), edge], axis=0)
    xs[index, :, 0:cin] = pltpu.roll(line, line.shape[0] - 1, 0).astype(jnp.bfloat16)
    xs[index, :, cin : 2 * cin] = line.astype(jnp.bfloat16)
    xs[index, :, 2 * cin : 3 * cin] = pltpu.roll(line, 1, 0).astype(jnp.bfloat16)


def tap_dot(xs, lines, phase, weight):
    _, total, lanes = xs.shape
    cin = lanes // 3
    low = (1 - phase) * cin
    part = xs[lines, :, low : low + 2 * cin]
    count = part.shape[0]
    out = jnp.dot(
        part.reshape(count * total, 2 * cin),
        weight.reshape(2 * cin, weight.shape[-1]),
        preferred_element_type=jnp.float32,
    )
    return out.reshape(count, total, weight.shape[-1])


def main_kernel(own_ref, edge_ref, next_ref, next_edge_ref, own_w, other_w, u_ref, part_ref, stats_ref, xs, wd, sems):
    rows, width, cin = own_ref.shape
    cout = u_ref.shape[-1]
    copies = load_deconv(own_w, other_w, wd, sems)
    for row in range(rows):
        spread_line(xs, row, own_ref[row], edge_ref[row])
    spread_line(xs, rows, next_ref[0], next_edge_ref[0])
    for copy in copies:
        copy.wait()

    place = lax.axis_index("rows")
    first_here = place == 0
    last_here = place == lax.axis_size("rows") - 1
    sums = jnp.zeros((1, cout), jnp.float32)
    squares = jnp.zeros((1, cout), jnp.float32)
    for phase in range(2):
        upper = tap_dot(xs, slice(0, rows + 1), phase, wd[1, phase])
        even = upper[1:] + tap_dot(xs, slice(0, rows), phase, wd[3, phase])
        part_ref[phase] = upper[0]
        odd = tap_dot(xs, slice(0, rows), phase, wd[2, phase]) + tap_dot(
            xs, slice(1, rows + 1), phase, wd[0, phase]
        )
        lines = []
        for row in range(rows):
            lines += [odd[row].astype(jnp.bfloat16), even[row].astype(jnp.bfloat16)]
        for row, line in enumerate(lines):
            u_ref[row, phase] = line
        edge_line = jnp.where(first_here, upper[0].astype(jnp.bfloat16).astype(jnp.float32), 0.0)
        final_line = jnp.where(last_here, 0.0, lines[-1].astype(jnp.float32))
        for line in lines[:-1] + [edge_line, final_line]:
            values = line[:width].astype(jnp.float32)
            sums += jnp.sum(values, axis=0, keepdims=True)
            squares += jnp.sum(values * values, axis=0, keepdims=True)
    half = cout // 2
    stats_ref[...] = jnp.concatenate(
        [sums[:, :half], sums[:, half:], squares[:, :half], squares[:, half:]]
        + [jnp.zeros((4, half), jnp.float32)],
        axis=0,
    )


def halo_kernel(above_ref, own_ref, edge_ref, next_ref, next_edge_ref, below_ref, part_ref, own_w, other_w, u_ref, xs, wd, sems):
    rows, width, cin = own_ref.shape
    copies = load_deconv(own_w, other_w, wd, sems)
    spread_line(xs, 0, above_ref[0, :width], above_ref[0, width:])
    spread_line(xs, 1, above_ref[1, :width], above_ref[1, width:])
    spread_line(xs, 2, next_ref[0], next_edge_ref[0])
    spread_line(xs, 3, own_ref[0], edge_ref[0])
    spread_line(xs, 4, below_ref[0, :width], below_ref[0, width:])
    for copy in copies:
        copy.wait()
    for phase in range(2):
        outer = tap_dot(xs, slice(0, 2), phase, wd[3, phase])
        u_ref[0, phase] = (outer[0] + tap_dot(xs, slice(1, 2), phase, wd[1, phase])[0]).astype(jnp.bfloat16)
        u_ref[2, phase] = (outer[1] + part_ref[phase]).astype(jnp.bfloat16)
        odd = tap_dot(xs, slice(1, 3), phase, wd[2, phase]) + tap_dot(xs, slice(3, 5), phase, wd[0, phase])
        u_ref[1, phase] = odd[0].astype(jnp.bfloat16)
        u_ref[3, phase] = odd[1].astype(jnp.bfloat16)


def group_sum(v, width):
    lane = lax.broadcasted_iota(jnp.int32, v.shape, 1)
    size = v.shape[1]
    step = 1
    while step < width:
        v = v + jnp.where(
            (lane & step) == 0, pltpu.roll(v, size - step, 1), pltpu.roll(v, step, 1)
        )
        step *= 2
    return v


def fill(ref, row, even, odd):
    total, channels = even.shape
    ref[row, :, 0:channels] = pltpu.roll(odd, 1, 0).astype(jnp.bfloat16)
    ref[row, :, channels : 2 * channels] = even.astype(jnp.bfloat16)
    ref[row, :, 2 * channels : 3 * channels] = odd.astype(jnp.bfloat16)
    ref[row, :, 3 * channels : 4 * channels] = pltpu.roll(even, total - 1, 0).astype(jnp.bfloat16)


def conv_kernel(
    count, u_ref, halo_ref, stats_ref, params_ref, own_w1, other_w1, own_w2, other_w2, out_ref, g, act, w1, w2, mixed, sems
):
    main, _, total, cout = u_ref.shape
    lines = main + 2 * HALO
    width = total - EDGE
    lanes = own_w1.shape[-1]
    column = lax.axis_index("fsdp")
    copies = []
    for index, (own, other, dst) in enumerate(((own_w1, other_w1, w1), (own_w2, other_w2, w2))):
        for side, src in enumerate((own, other)):
            place = column if side == 0 else 1 - column
            copies.append(
                pltpu.make_async_copy(
                    src,
                    dst.at[:, :, :, pl.ds(pl.multiple_of(place * lanes, lanes), lanes)],
                    sems.at[index, side],
                )
            )
    for copy in copies:
        copy.start()

    block = stats_ref[...]
    width_group = cout // NORM_GROUPS
    sums = jnp.concatenate([block[0:1], block[1:2]], axis=1)
    squares = jnp.concatenate([block[2:3], block[3:4]], axis=1)
    mean = group_sum(sums, width_group) / count
    spread = group_sum(squares, width_group) / count - mean * mean
    scale = lax.rsqrt(spread + 1e-05) * params_ref[0:1]
    shift = params_ref[1:2] - mean * scale

    mask = edge_mask(width)
    place = lax.axis_index("rows")
    last = lax.axis_size("rows") - 1

    def inside(row, beyond):
        if row < beyond:
            return mask & (place > 0)
        if row >= lines - 2 * HALO + beyond:
            return mask & (place < last)
        return mask

    for row in range(lines):
        seen = inside(row, HALO)
        if row < 3:
            source = halo_ref.at[row]
        elif row < 3 + main:
            source = u_ref.at[row - 3]
        else:
            source = halo_ref.at[3]
        pair = [
            jnp.where(seen, silu(source[phase].astype(jnp.float32) * scale + shift), 0.0)
            for phase in range(2)
        ]
        fill(g, row, *pair)
    for copy in copies[:2]:
        copy.wait()
    bias = params_ref[2:3]
    chunk = 2
    for start in range(0, lines - 2, chunk):
        results = []
        for phase in range(2):
            acc = bias
            for a in range(3):
                acc = acc + jnp.dot(
                    g[start + a : start + a + chunk, :, phase * cout : (phase + 3) * cout].reshape(
                        chunk * total, 3 * cout
                    ),
                    w1[a].reshape(3 * cout, cout),
                    preferred_element_type=jnp.float32,
                )
            results.append(silu(acc).reshape(chunk, total, cout))
        for row in range(chunk):
            seen = inside(start + row, 1)
            fill(act, start + row, *[jnp.where(seen, r[row], 0.0) for r in results])
    for copy in copies[2:]:
        copy.wait()
    bias = params_ref[3:4]
    for start in range(0, lines - 4, chunk):
        for phase in range(2):
            acc = bias
            for a in range(3):
                acc = acc + jnp.dot(
                    act[start + a : start + a + chunk, 0:width, phase * cout : (phase + 3) * cout].reshape(
                        chunk * width, 3 * cout
                    ),
                    w2[a].reshape(3 * cout, cout),
                    preferred_element_type=jnp.float32,
                )
            acc = acc.reshape(chunk, width, cout)
            for row in range(chunk):
                for side in range(0, cout, 128):
                    mixed[side // 128, start + row, pl.ds(phase, width, stride=2), :] = acc[row, :, side : side + 128]
    for row in range(lines - 4):
        for side in range(0, cout, 128):
            out_ref[row, :, side : side + 128] = mixed[side // 128, row].astype(jnp.bfloat16)


def total_over(block, axes):
    for axis in axes:
        size = lax.axis_size(axis)
        if size & (size - 1):
            block = lax.psum(block, axis)
            continue
        step = 1
        while step < size:
            block = block + lax.ppermute(block, axis, [(i, i ^ step) for i in range(size)])
            step *= 2
    return block


def local(image, deconv_weight, norm_gain, norm_shift, first_weight, first_bias, second_weight, second_bias):
    rows, width, cin = image.shape
    taps, _, _, lanes = deconv_weight.shape
    columns = lax.axis_size("fsdp")
    cout = lanes * columns
    assert columns == 2 and rows >= HALO and width % EDGE == 0
    n_rows = lax.axis_size("rows")
    count = float(2 * rows * n_rows * 2 * width * columns * (cout // NORM_GROUPS))
    swap = [(0, 1), (1, 0)]
    to_next = [(i, i + 1) for i in range(n_rows - 1)]
    to_previous = [(i + 1, i) for i in range(n_rows - 1)]
    to_previous_swapped = [(2 * i + 2 + k, 2 * i + 1 - k) for i in range(n_rows - 1) for k in range(2)]

    edges = jnp.where(lax.axis_index("fsdp") == 0, image[:, width - EDGE :], image[:, :EDGE])
    following = lax.ppermute(image[:1], "rows", to_previous)
    following_edge = lax.ppermute(edges[:1], ("rows", "fsdp"), to_previous_swapped)
    edge = lax.ppermute(edges, "fsdp", swap)
    other_w = lax.ppermute(deconv_weight, "fsdp", swap)
    first_other = lax.ppermute(first_weight, "fsdp", swap)
    second_other = lax.ppermute(second_weight, "fsdp", swap)

    total = width + EDGE
    hbm = pl.BlockSpec(memory_space=pltpu.HBM)
    vmem = pl.BlockSpec(memory_space=pltpu.VMEM)
    shape_w = (taps, taps // 2, 2, cin, lanes)
    own_w, other_w = deconv_weight.reshape(shape_w), other_w.reshape(shape_w)
    deconv_scratch = [
        pltpu.VMEM((taps, 2, taps // 2, cin, cout), jnp.bfloat16),
        pltpu.SemaphoreType.DMA((taps, 2, 2)),
    ]
    u, part, stats = pl.pallas_call(
        main_kernel,
        out_shape=(
            jax.ShapeDtypeStruct((2 * rows, 2, total, cout), jnp.bfloat16),
            jax.ShapeDtypeStruct((2, total, cout), jnp.float32),
            jax.ShapeDtypeStruct((8, cout // 2), jnp.float32),
        ),
        in_specs=[vmem] * 4 + [hbm] * 2,
        out_specs=(vmem, vmem, vmem),
        scratch_shapes=[pltpu.VMEM((rows + 1, total, 3 * cin), jnp.bfloat16)] + deconv_scratch,
        compiler_params=pltpu.CompilerParams(vmem_limit_bytes=VMEM_BYTES),
        cost_estimate=pl.CostEstimate(flops=2 * 2 * (2 * rows) * total * 4 * cin * cout, bytes_accessed=2**22, transcendentals=0),
        name="deconv_main",
    )(image, edge, following, following_edge, own_w, other_w)

    lines, _ = lax.optimization_barrier((jnp.concatenate([image, edge], axis=1), following))
    above = lax.ppermute(lines[rows - HALO :], "rows", to_next)
    below = lax.ppermute(lines[1:HALO], "rows", to_previous)
    halo = pl.pallas_call(
        halo_kernel,
        out_shape=jax.ShapeDtypeStruct((4, 2, total, cout), jnp.bfloat16),
        in_specs=[vmem] * 7 + [hbm] * 2,
        out_specs=vmem,
        scratch_shapes=[pltpu.VMEM((5, total, 3 * cin), jnp.bfloat16)] + deconv_scratch,
        compiler_params=pltpu.CompilerParams(vmem_limit_bytes=VMEM_BYTES),
        cost_estimate=pl.CostEstimate(flops=2 * 2 * 4 * total * 4 * cin * cout, bytes_accessed=2**22, transcendentals=0),
        name="deconv_halo",
    )(above, image, edge, following, following_edge, below, part, own_w, other_w)

    totals = total_over(stats, ("fsdp", "rows"))
    params = jnp.stack([norm_gain, norm_shift, first_bias, second_bias])
    out = pl.pallas_call(
        functools.partial(conv_kernel, count),
        out_shape=jax.ShapeDtypeStruct((2 * rows, 2 * width, cout), jnp.bfloat16),
        in_specs=[vmem] * 4 + [hbm] * 4,
        out_specs=vmem,
        scratch_shapes=[
            pltpu.VMEM((2 * rows + 2 * HALO, total, 4 * cout), jnp.bfloat16),
            pltpu.VMEM((2 * rows + 2, total, 4 * cout), jnp.bfloat16),
            pltpu.VMEM((3, 3, cout, cout), jnp.bfloat16),
            pltpu.VMEM((3, 3, cout, cout), jnp.bfloat16),
            pltpu.VMEM((cout // 128, 2 * rows, 2 * width, 128), jnp.float32),
            pltpu.SemaphoreType.DMA((2, 2)),
        ],
        compiler_params=pltpu.CompilerParams(vmem_limit_bytes=VMEM_BYTES),
        cost_estimate=pl.CostEstimate(flops=5 * 10**9, bytes_accessed=2**22, transcendentals=0),
        name="convs",
    )(u, halo, totals, params, first_weight, first_other, second_weight, second_other)
    return out


def solution(mesh):
    placed = (
        P(("groups", "rows"), "fsdp", None),
        P(None, None, None, "fsdp"),
        P(),
        P(),
        P(None, None, None, "fsdp"),
        P(),
        P(None, None, None, "fsdp"),
        P(),
    )
    return jax.shard_map(
        local,
        mesh=mesh,
        in_specs=placed,
        out_specs=P(("groups", "rows"), "fsdp", None),
        check_vma=False,
    )
```

time: 62.5 us -> 50.2 us (0.80)
  between operations: 13.6 us -> 0.18 us
  starting transfers between devices: 13.7 us -> 18.6 us
  waiting for transfers between devices: 18.9 us -> 14.3 us
  other arithmetic: 0.03 us -> 1.78 us
  local copies, waits for them, and re-layouts: 5.15 us -> 3.49 us
  Pallas kernels: 10.7 us -> 11.5 us
    ppermute x3 -> x11, starting transfers between devices: 6.25 us -> 18.1 us  [the longest x4 9.13 us: total_over(): lax.ppermute(block, axis, [(i, i ^ step) for i in range(size)])]
    all_to_all x1 -> x0, starting transfers between devices: 6.93 us -> none  [local(): lax.all_to_all(stats, ('rows', 'fsdp'), split_axis=0, concat_axis=0)]
    all_to_all x1 -> x0, waiting for transfers between devices: 6.78 us -> none  [local(): lax.all_to_all(stats, ('rows', 'fsdp'), split_axis=0, concat_axis=0)]
    ppermute x3 -> x11, waiting for transfers between devices: 11.2 us -> 14.3 us  [the longest x1 5.95 us: local(): following = lax.ppermute(image[:1], 'rows', to_previous)]
    unnamed x28 -> x16, local copies, waits for them, and re-layouts: 5.13 us -> 2.56 us
    concatenate x0 -> x1, other arithmetic: none -> 0.97 us  [local(): jnp.concatenate([image, edge], axis=1)]
    slice x0 -> x3, local copies, waits for them, and re-layouts: none -> 0.93 us  [the longest x1 0.91 us: local(): following = lax.ppermute(image[:1], 'rows', to_previous)]
    unnamed x2 -> x0, waiting for transfers between devices: 0.89 us -> none
  transfers between devices with their start and end apart: 7 -> 12, of which waited for: 3 -> 6; matrix products, arithmetic and copies ran while one was open for 0% -> 5% of each run, Pallas kernels for 7% -> 10%
where the time goes in v2:
time: 50.2 us; the launch traced here: 49.8 us
  starting transfers between devices  18.6 us (37%)
  waiting for transfers between devices  14.3 us (28%)
  Pallas kernels  11.5 us (23%)
  local copies, waits for them, and re-layouts  3.49 us (7%)
  other arithmetic  1.78 us (4%)
    ppermute x4, starting transfers between devices, total_over(): lax.ppermute(block, axis, [(i, i ^ step) for i in range(size)])  9.13 us
    pallas_call x1, Pallas kernels, local(): pl.pallas_call(functools.partial(conv_kernel, count), out_shape=jax.Shape...  6.32 us
    ppermute x1, waiting for transfers between devices, local(): following = lax.ppermute(image[:1], 'rows', to_previous)  5.95 us
    ppermute x1, starting transfers between devices, local(): above = lax.ppermute(lines[rows - HALO:], 'rows', to_next)  4.54 us
    ppermute x4, waiting for transfers between devices, total_over(): lax.ppermute(block, axis, [(i, i ^ step) for i in range(size)])  4.29 us
    ppermute x1, waiting for transfers between devices, local(): lax.ppermute(edges[:1], ('rows', 'fsdp'), to_previous_swapped)  3.74 us
    pallas_call x1, Pallas kernels, local(): pl.pallas_call(main_kernel, out_shape=(jax.ShapeDtypeStruct((2 * rows, 2,...  2.69 us
    unnamed x16, local copies, waits for them, and re-layouts  2.56 us
  transfers between devices with their start and end apart: 12, of which 6 were waited for; matrix products, arithmetic and copies ran while one was open for 5% of the time, Pallas kernels for 10%

profile of v2, /device:TPU:0, one launch (start us, length us, event | category | flops | bytes accessed | tf_op | source)
XLA Modules:
  0.0 49.8 jit_solution(1695065041032302628)
XLA Ops:
  0.0 0.5 collective-permute-start.3
  0.5 0.5 collective-permute-start.11
  1.0 0.8 %slice_select_fusion = bf16[2,16,512]{2,1,0:T(8,128)(2,1)S(1)} fusion(bf16[2,128,512]{2,1,0:T(8,128)(2,1)} %own_ref.3, pred[]{:T(512)S(6)} %eq.3), kind=kLoop, calls=%fused_computation.1 | loop fusion | flops 16384 | bytes 98305 | tf_op jit(solution)/shard_map/jit(_where)/select_n | solution.py:279
  1.8 0.9 %slice.17 = bf16[1,128,512]{2,1,0:T(8,128)(2,1)S(1)} slice(bf16[2,128,512]{2,1,0:T(8,128)(2,1)} %own_ref.3), slice={[0:1], [0:128], [0:512]} | slice | bytes 262144 | tf_op jit(solution)/shard_map/slice | solution.py:280
  2.7 1.3 %collective-permute-start.1 = (bf16[1,128,512]{2,1,0:T(8,128)(2,1)S(1)}, bf16[1,128,512]{2,1,0:T(8,128)(2,1)S(1)}, u32[]{:S(2)}, u32[]{:S(2)}) collective-permute-start(bf16[1,128,512]{2,1,0:T(8,128)(2,1)S(1)} %slice.17), channel_id=1, source_target_pairs={{2,0},{4,2},{6,4},{8,6},{10,8},{12,10},{14,12},{3,1},{5,3},{7,5},{... | collective-permute-start | bytes 393224 | tf_op jit(solution)/shard_map/ppermute | solution.py:280
  4.0 0.3 collective-permute-done.edge_ref
  4.3 1.0 %pad_maximum_fusion = bf16[2,144,512]{2,1,0:T(8,128)(2,1)S(1)} fusion(bf16[2,16,512]{2,1,0:T(8,128)(2,1)S(1)} %collective-permute-done.edge_ref, bf16[2,128,512]{2,1,0:T(8,128)(2,1)} %own_ref.3), kind=kLoop, calls=%fused_computation | loop fusion | flops 589824 | bytes 589824 | tf_op jit(solution)/shard_map/concatenate | solution.py:311
  5.3 6.0 %collective-permute-done.1.next_ref = bf16[1,128,512]{2,1,0:T(8,128)(2,1)S(1)} collective-permute-done((bf16[1,128,512]{2,1,0:T(8,128)(2,1)S(1)}, bf16[1,128,512]{2,1,0:T(8,128)(2,1)S(1)}, u32[]{:S(2)}, u32[]{:S(2)}) %collective-permute-start.1) | collective-permute-done | bytes 131104 | tf_op jit(solution)/shard_map/ppermute | solution.py:280
  11.3 4.5 %collective-permute-start.4 = (bf16[2,144,512]{2,1,0:T(8,128)(2,1)S(1)}, bf16[2,144,512]{2,1,0:T(8,128)(2,1)S(1)}, u32[]{:S(2)}, u32[]{:S(2)}) collective-permute-start(bf16[2,144,512]{2,1,0:T(8,128)(2,1)S(1)} %pad_maximum_fusion), channel_id=1, source_target_pairs={{0,2},{2,4},{4,6},{6,8},{8,10},{10,12},{12,14},{1,3},{3,5},{5,7},{... | collective-permute-start | bytes 884744 | tf_op jit(solution)/shard_map/ppermute | solution.py:312
  15.8 1.3 %collective-permute-start.2 = (bf16[1,16,512]{2,1,0:T(8,128)(2,1)S(1)}, bf16[1,16,512]{2,1,0:T(8,128)(2,1)S(1)}, u32[]{:S(2)}, u32[]{:S(2)}) collective-permute-start(bf16[1,16,512]{2,1,0:T(8,128)(2,1)S(1)} %slice.20), channel_id=1, source_target_pairs={{2,1},{3,0},{4,3},{5,2},{6,5},{7,4},{8,7},{9,6},{10,9},{11,8},{12,... | collective-permute-start | bytes 49160 | tf_op jit(solution)/shard_map/ppermute | solution.py:281
  17.1 3.7 %collective-permute-done.2.next_edge_ref = bf16[1,16,512]{2,1,0:T(8,128)(2,1)S(1)} collective-permute-done((bf16[1,16,512]{2,1,0:T(8,128)(2,1)S(1)}, bf16[1,16,512]{2,1,0:T(8,128)(2,1)S(1)}, u32[]{:S(2)}, u32[]{:S(2)}) %collective-permute-start.2) | collective-permute-done | bytes 16416 | tf_op jit(solution)/shard_map/ppermute | solution.py:281
  20.9 1.3 %collective-permute-start.5 = (bf16[1,144,512]{2,1,0:T(8,128)(2,1)S(1)}, bf16[1,144,512]{2,1,0:T(8,128)(2,1)S(1)}, u32[]{:S(2)}, u32[]{:S(2)}) collective-permute-start(bf16[1,144,512]{2,1,0:T(8,128)(2,1)S(1)} %slice.19), channel_id=1, source_target_pairs={{2,0},{4,2},{6,4},{8,6},{10,8},{12,10},{14,12},{3,1},{5,3},{7,5},{... | collective-permute-start | bytes 442376 | tf_op jit(solution)/shard_map/ppermute | solution.py:313
  22.2 1.6 %copy-done = bf16[4,4,512,128]{3,2,1,0:T(8,128)(2,1)S(1)} copy-done((bf16[4,4,512,128]{3,2,1,0:T(8,128)(2,1)S(1)}, bf16[4,4,512,128]{3,2,1,0:T(8,128)(2,1)}, u32[]{:S(2)}) %copy-start) | copy-done | bytes 2097176
  23.8 0.9 %copy-done.1 = bf16[2,128,512]{2,1,0:T(8,128)(2,1)S(1)} copy-done((bf16[2,128,512]{2,1,0:T(8,128)(2,1)S(1)}, bf16[2,128,512]{2,1,0:T(8,128)(2,1)}, u32[]{:S(2)}) %copy-start.1) | copy-done | bytes 262168
  24.7 2.7 %deconv_main.1 = (bf16[4,2,144,256]{3,2,1,0:T(8,128)(2,1)S(1)}, f32[2,144,256]{2,1,0:T(8,128)S(1)}, f32[8,128]{1,0:T(8,128)S(1)}) custom-call(bf16[2,128,512]{2,1,0:T(8,128)(2,1)S(1)} %copy-done.1, bf16[2,16,512]{2,1,0:T(8,128)(2,1)S(1)} %collective-permute-done.edge_ref, bf16[1,128,512]{2,1,0:T(8,128)(2,1)S(1)} %collective-permute-done.1.next_ref, ...), custom_call_target="tpu_custom_call" | custom-call | flops 1207959552 | bytes 4194304 | tf_op jit(solution)/shard_map/deconv_main/pallas_call | solution.py:296
  27.4 0.1 collective-permute-start.6
  27.5 1.2 %collective-permute-done.6 = f32[8,128]{1,0:T(8,128)S(1)} collective-permute-done((f32[8,128]{1,0:T(8,128)S(1)}, f32[8,128]{1,0:T(8,128)S(1)}, u32[]{:S(2)}, u32[]{:S(2)}) %collective-permute-start.6) | collective-permute-done | bytes 4128 | tf_op jit(solution)/shard_map/ppermute | solution.py:261
  28.7 2.6 %collective-permute-start.7 = (f32[8,128]{1,0:T(8,128)S(1)}, f32[8,128]{1,0:T(8,128)S(1)}, u32[]{:S(2)}, u32[]{:S(2)}) collective-permute-start(f32[8,128]{1,0:T(8,128)S(1)} %add.12), channel_id=1, source_target_pairs={{0,2},{2,0},{4,6},{6,4},{8,10},{10,8},{12,14},{14,12},{1,3},{3,1},... | collective-permute-start | bytes 12296 | tf_op jit(solution)/shard_map/ppermute | solution.py:261
  31.3 1.6 %collective-permute-done.7 = f32[8,128]{1,0:T(8,128)S(1)} collective-permute-done((f32[8,128]{1,0:T(8,128)S(1)}, f32[8,128]{1,0:T(8,128)S(1)}, u32[]{:S(2)}, u32[]{:S(2)}) %collective-permute-start.7) | collective-permute-done | bytes 4128 | tf_op jit(solution)/shard_map/ppermute | solution.py:261
  32.9 3.4 %collective-permute-start.8 = (f32[8,128]{1,0:T(8,128)S(1)}, f32[8,128]{1,0:T(8,128)S(1)}, u32[]{:S(2)}, u32[]{:S(2)}) collective-permute-start(f32[8,128]{1,0:T(8,128)S(1)} %add.13), channel_id=1, source_target_pairs={{0,4},{2,6},{4,0},{6,2},{8,12},{10,14},{12,8},{14,10},{1,5},{3,7},... | collective-permute-start | bytes 12296 | tf_op jit(solution)/shard_map/ppermute | solution.py:261
  36.3 1.6 %collective-permute-done.8 = f32[8,128]{1,0:T(8,128)S(1)} collective-permute-done((f32[8,128]{1,0:T(8,128)S(1)}, f32[8,128]{1,0:T(8,128)S(1)}, u32[]{:S(2)}, u32[]{:S(2)}) %collective-permute-start.8) | collective-permute-done | bytes 4128 | tf_op jit(solution)/shard_map/ppermute | solution.py:261
  37.9 3.0 %collective-permute-start.9 = (f32[8,128]{1,0:T(8,128)S(1)}, f32[8,128]{1,0:T(8,128)S(1)}, u32[]{:S(2)}, u32[]{:S(2)}) collective-permute-start(f32[8,128]{1,0:T(8,128)S(1)} %add.14), channel_id=1, source_target_pairs={{0,8},{2,10},{4,12},{6,14},{8,0},{10,2},{12,4},{14,6},{1,9},{3,11}... | collective-permute-start | bytes 12296 | tf_op jit(solution)/shard_map/ppermute | solution.py:261
  40.9 2.5 %deconv_halo.1.halo_ref = bf16[4,2,144,256]{3,2,1,0:T(8,128)(2,1)S(1)} custom-call(bf16[2,144,512]{2,1,0:T(8,128)(2,1)S(1)} %collective-permute-done.4.above_ref, bf16[2,128,512]{2,1,0:T(8,128)(2,1)S(1)} %copy-done.1, bf16[2,16,512]{2,1,0:T(8,128)(2,1)S(1)} %collective-permute-done.edge_ref, bf16[1,128,512]{2,1,0:T(8,128)(2,1)S(1)} %collective-permute-done.1.next_ref, ...), custom_call_target="tpu_custom_call" | custom-call | flops 1207959552 | bytes 4194304 | tf_op jit(solution)/shard_map/deconv_halo/pallas_call | solution.py:314
  43.5 6.3 %convs.1 = bf16[4,256,256]{2,1,0:T(8,128)(2,1)} custom-call(bf16[4,2,144,256]{3,2,1,0:T(8,128)(2,1)S(1)} %get-tuple-element.9.u_ref, bf16[4,2,144,256]{3,2,1,0:T(8,128)(2,1)S(1)} %deconv_halo.1.halo_ref, f32[8,128]{1,0:T(8,128)S(1)} %add.15.stats_ref, f32[4,256]{1,0:T(4,128)S(1)} %pad_maximum_fusion.1.params_ref, bf16[3,3,256,128]{3,2,1,0:T(8,128)(2,1)S(1)} %copy-done.2, ...), custom_call_target="tpu_custom_call" | custom-call | flops 5000000000 | bytes 4194304 | tf_op jit(solution)/shard_map/convs/pallas_call | solution.py:327
  (29 shorter events, 0.2 us)
Async XLA Ops:
  0.0 22.2 %collective-permute-start.3 = (bf16[4,4,512,128]{3,2,1,0:T(8,128)(2,1)}, bf16[4,4,512,128]{3,2,1,0:T(8,128)(2,1)S(1)}, u32[]{:S(2)}, u32[]{:S(2)}) collective-permute-start(bf16[4,4,512,128]{3,2,1,0:T(8,128)(2,1)} %param.9), channel_id=1, source_target_pairs={{0,1},{1,0},{2,3},{3,2},{4,5},{5,4},{6,7},{7,6},{8,9},{9,8},{10,11... | collective-permute-start | bytes 6291464 | tf_op jit(solution)/shard_map/ppermute | solution.py:283
  0.5 43.0 %collective-permute-start.10 = (bf16[3,3,256,128]{3,2,1,0:T(8,128)(2,1)}, bf16[3,3,256,128]{3,2,1,0:T(8,128)(2,1)S(1)}, u32[]{:S(2)}, u32[]{:S(2)}) collective-permute-start(bf16[3,3,256,128]{3,2,1,0:T(8,128)(2,1)} %own_w1.1), channel_id=1, source_target_pairs={{0,1},{1,0},{2,3},{3,2},{4,5},{5,4},{6,7},{7,6},{8,9},{9,8},{10,11... | collective-permute-start | bytes 1769480 | tf_op jit(solution)/shard_map/ppermute | solution.py:284
  0.5 42.9 %collective-permute-start.11 = (bf16[3,3,256,128]{3,2,1,0:T(8,128)(2,1)}, bf16[3,3,256,128]{3,2,1,0:T(8,128)(2,1)S(1)}, u32[]{:S(2)}, u32[]{:S(2)}) collective-permute-start(bf16[3,3,256,128]{3,2,1,0:T(8,128)(2,1)} %own_w2.1), channel_id=1, source_target_pairs={{0,1},{1,0},{2,3},{3,2},{4,5},{5,4},{6,7},{7,6},{8,9},{9,8},{10,11... | collective-permute-start | bytes 1769480 | tf_op jit(solution)/shard_map/ppermute | solution.py:285
  1.7 2.6 %collective-permute-start = (bf16[2,16,512]{2,1,0:T(8,128)(2,1)S(1)}, bf16[2,16,512]{2,1,0:T(8,128)(2,1)S(1)}, u32[]{:S(2)}, u32[]{:S(2)}) collective-permute-start(bf16[2,16,512]{2,1,0:T(8,128)(2,1)S(1)} %slice_select_fusion), channel_id=1, source_target_pairs={{0,1},{1,0},{2,3},{3,2},{4,5},{5,4},{6,7},{7,6},{8,9},{9,8},{10,11... | collective-permute-start | bytes 98312 | tf_op jit(solution)/shard_map/ppermute | solution.py:282
  2.7 8.5 %collective-permute-start.1 = (bf16[1,128,512]{2,1,0:T(8,128)(2,1)S(1)}, bf16[1,128,512]{2,1,0:T(8,128)(2,1)S(1)}, u32[]{:S(2)}, u32[]{:S(2)}) collective-permute-start(bf16[1,128,512]{2,1,0:T(8,128)(2,1)S(1)} %slice.17), channel_id=1, source_target_pairs={{2,0},{4,2},{6,4},{8,6},{10,8},{12,10},{14,12},{3,1},{5,3},{7,5},{... | collective-permute-start | bytes 393224 | tf_op jit(solution)/shard_map/ppermute | solution.py:280
  11.3 29.6 %collective-permute-start.4 = (bf16[2,144,512]{2,1,0:T(8,128)(2,1)S(1)}, bf16[2,144,512]{2,1,0:T(8,128)(2,1)S(1)}, u32[]{:S(2)}, u32[]{:S(2)}) collective-permute-start(bf16[2,144,512]{2,1,0:T(8,128)(2,1)S(1)} %pad_maximum_fusion), channel_id=1, source_target_pairs={{0,2},{2,4},{4,6},{6,8},{8,10},{10,12},{12,14},{1,3},{3,5},{5,7},{... | collective-permute-start | bytes 884744 | tf_op jit(solution)/shard_map/ppermute | solution.py:312
  15.8 5.1 %collective-permute-start.2 = (bf16[1,16,512]{2,1,0:T(8,128)(2,1)S(1)}, bf16[1,16,512]{2,1,0:T(8,128)(2,1)S(1)}, u32[]{:S(2)}, u32[]{:S(2)}) collective-permute-start(bf16[1,16,512]{2,1,0:T(8,128)(2,1)S(1)} %slice.20), channel_id=1, source_target_pairs={{2,1},{3,0},{4,3},{5,2},{6,5},{7,4},{8,7},{9,6},{10,9},{11,8},{12,... | collective-permute-start | bytes 49160 | tf_op jit(solution)/shard_map/ppermute | solution.py:281
  20.9 20.0 %collective-permute-start.5 = (bf16[1,144,512]{2,1,0:T(8,128)(2,1)S(1)}, bf16[1,144,512]{2,1,0:T(8,128)(2,1)S(1)}, u32[]{:S(2)}, u32[]{:S(2)}) collective-permute-start(bf16[1,144,512]{2,1,0:T(8,128)(2,1)S(1)} %slice.19), channel_id=1, source_target_pairs={{2,0},{4,2},{6,4},{8,6},{10,8},{12,10},{14,12},{3,1},{5,3},{7,5},{... | collective-permute-start | bytes 442376 | tf_op jit(solution)/shard_map/ppermute | solution.py:313
  22.2 1.6 %copy-start = (bf16[4,4,512,128]{3,2,1,0:T(8,128)(2,1)S(1)}, bf16[4,4,512,128]{3,2,1,0:T(8,128)(2,1)}, u32[]{:S(2)}) copy-start(bf16[4,4,512,128]{3,2,1,0:T(8,128)(2,1)} %param.9) | copy-start | bytes 6291460
  23.8 0.9 %copy-start.1 = (bf16[2,128,512]{2,1,0:T(8,128)(2,1)S(1)}, bf16[2,128,512]{2,1,0:T(8,128)(2,1)}, u32[]{:S(2)}) copy-start(bf16[2,128,512]{2,1,0:T(8,128)(2,1)} %own_ref.3) | copy-start | bytes 786436
  24.7 11.6 %copy-start.4 = (f32[256]{0:T(256)S(1)}, f32[256]{0:T(256)}, u32[]{:S(2)}) copy-start(f32[256]{0:T(256)} %param.15) | copy-start | bytes 3076
  24.7 11.6 %copy-start.5 = (f32[256]{0:T(256)S(1)}, f32[256]{0:T(256)}, u32[]{:S(2)}) copy-start(f32[256]{0:T(256)} %param.13) | copy-start | bytes 3076
  24.7 11.6 %copy-start.6 = (f32[256]{0:T(256)S(1)}, f32[256]{0:T(256)}, u32[]{:S(2)}) copy-start(f32[256]{0:T(256)} %param.11) | copy-start | bytes 3076
  24.7 11.6 %copy-start.7 = (f32[256]{0:T(256)S(1)}, f32[256]{0:T(256)}, u32[]{:S(2)}) copy-start(f32[256]{0:T(256)} %param.10) | copy-start | bytes 3076
  27.4 1.2 %collective-permute-start.6 = (f32[8,128]{1,0:T(8,128)S(1)}, f32[8,128]{1,0:T(8,128)S(1)}, u32[]{:S(2)}, u32[]{:S(2)}) collective-permute-start(f32[8,128]{1,0:T(8,128)S(1)} %get-tuple-element.12), channel_id=1, source_target_pairs={{0,1},{1,0},{2,3},{3,2},{4,5},{5,4},{6,7},{7,6},{8,9},{9,8},{10,11... | collective-permute-start | bytes 12296 | tf_op jit(solution)/shard_map/ppermute | solution.py:261
  28.7 4.2 %collective-permute-start.7 = (f32[8,128]{1,0:T(8,128)S(1)}, f32[8,128]{1,0:T(8,128)S(1)}, u32[]{:S(2)}, u32[]{:S(2)}) collective-permute-start(f32[8,128]{1,0:T(8,128)S(1)} %add.12), channel_id=1, source_target_pairs={{0,2},{2,0},{4,6},{6,4},{8,10},{10,8},{12,14},{14,12},{1,3},{3,1},... | collective-permute-start | bytes 12296 | tf_op jit(solution)/shard_map/ppermute | solution.py:261
  32.9 5.0 %collective-permute-start.8 = (f32[8,128]{1,0:T(8,128)S(1)}, f32[8,128]{1,0:T(8,128)S(1)}, u32[]{:S(2)}, u32[]{:S(2)}) collective-permute-start(f32[8,128]{1,0:T(8,128)S(1)} %add.13), channel_id=1, source_target_pairs={{0,4},{2,6},{4,0},{6,2},{8,12},{10,14},{12,8},{14,10},{1,5},{3,7},... | collective-permute-start | bytes 12296 | tf_op jit(solution)/shard_map/ppermute | solution.py:261
  37.9 5.6 %collective-permute-start.9 = (f32[8,128]{1,0:T(8,128)S(1)}, f32[8,128]{1,0:T(8,128)S(1)}, u32[]{:S(2)}, u32[]{:S(2)}) collective-permute-start(f32[8,128]{1,0:T(8,128)S(1)} %add.14), channel_id=1, source_target_pairs={{0,8},{2,10},{4,12},{6,14},{8,0},{10,2},{12,4},{14,6},{1,9},{3,11}... | collective-permute-start | bytes 12296 | tf_op jit(solution)/shard_map/ppermute | solution.py:261
  40.9 2.6 %copy-start.2 = (bf16[3,3,256,128]{3,2,1,0:T(8,128)(2,1)S(1)}, bf16[3,3,256,128]{3,2,1,0:T(8,128)(2,1)}, u32[]{:S(2)}) copy-start(bf16[3,3,256,128]{3,2,1,0:T(8,128)(2,1)} %own_w1.1) | copy-start | bytes 1769476
  40.9 2.6 %copy-start.3 = (bf16[3,3,256,128]{3,2,1,0:T(8,128)(2,1)S(1)}, bf16[3,3,256,128]{3,2,1,0:T(8,128)(2,1)}, u32[]{:S(2)}) copy-start(bf16[3,3,256,128]{3,2,1,0:T(8,128)(2,1)} %own_w2.1) | copy-start | bytes 1769476

commit v3 on v2

v3 whole, which is shorter than its diff:
```python
import functools

import jax
import jax.numpy as jnp
from jax import lax
from jax.experimental import pallas as pl
from jax.experimental.pallas import tpu as pltpu
from jax.sharding import PartitionSpec as P

NORM_GROUPS = 32
HALO = 2
EDGE = 16
LANES = 128
VMEM_BYTES = 24 * 2**20


def silu(v):
    h = 0.5 * v
    return h + h * jnp.tanh(h)


def edge_mask(width):
    column = lax.axis_index("fsdp")
    last = lax.axis_size("fsdp") - 1
    cell = lax.broadcasted_iota(jnp.int32, (width + EDGE, 1), 0) - width
    right = (cell < EDGE // 2) & (column < last)
    left = (cell >= EDGE // 2) & (column > 0)
    return (cell < 0) | right | left


def cut_kernel(image_ref, line_ref, edges_ref, sems):
    width = image_ref.shape[1]
    start = pl.multiple_of((1 - lax.axis_index("fsdp")) * (width - EDGE), EDGE)
    copies = [
        pltpu.make_async_copy(image_ref.at[0:1], line_ref, sems.at[0]),
        pltpu.make_async_copy(image_ref.at[:, pl.ds(start, EDGE), :], edges_ref, sems.at[1]),
    ]
    for copy in copies:
        copy.start()
    for copy in copies:
        copy.wait()


def spread_line(out, main, edge):
    cin = main.shape[-1]
    cell = lax.broadcasted_iota(jnp.int32, (EDGE, 1), 0)
    keep = jnp.where(lax.axis_index("fsdp") == 0, cell, EDGE - 1 - cell) < EDGE // 2
    edge = jnp.where(keep, edge.astype(jnp.float32), 0.0)
    line = jnp.concatenate([main.astype(jnp.float32), edge], axis=0)
    out[:, 0:cin] = pltpu.roll(line, line.shape[0] - 1, 0).astype(jnp.bfloat16)
    out[:, cin : 2 * cin] = line.astype(jnp.bfloat16)
    out[:, 2 * cin : 3 * cin] = pltpu.roll(line, 1, 0).astype(jnp.bfloat16)


def own_kernel(image_ref, edge_ref, weight_ref, xs_ref, lines_ref, own_w_ref, held, sems):
    rows, width, _ = image_ref.shape
    copies = [
        pltpu.make_async_copy(image_ref, held, sems.at[0]),
        pltpu.make_async_copy(weight_ref, own_w_ref, sems.at[1]),
    ]
    for copy in copies:
        copy.start()
    copies[0].wait()
    for row in range(rows):
        spread_line(xs_ref.at[row], held[row], edge_ref[row])
        lines_ref[row, :width] = held[row]
        lines_ref[row, width:] = edge_ref[row]
    copies[1].wait()


def tap_dot(lines, phase, kr, own_w, other_w):
    count, total, lanes = lines.shape
    cin = lanes // 3
    low = (1 - phase) * cin
    weight = jnp.concatenate(
        [ref[kr, :, 1 - phase].reshape(2 * cin, ref.shape[-1]) for ref in (own_w, other_w)], axis=1
    )
    out = jnp.dot(
        lines[:, :, low : low + 2 * cin].reshape(count * total, 2 * cin),
        weight,
        preferred_element_type=jnp.float32,
    )
    return out.reshape(count, total, weight.shape[-1])


def main_kernel(xs_ref, next_ref, next_edge_ref, own_w, other_w, u_ref, part_ref, xs_next_ref, stats_ref):
    rows, total, _ = xs_ref.shape
    width = total - EDGE
    cout = u_ref.shape[-1]
    spread_line(xs_next_ref.at[0], next_ref[0], next_edge_ref[0])
    column = lax.axis_index("fsdp")
    place = lax.axis_index("rows")
    first_here = place == 0
    last_here = place == lax.axis_size("rows") - 1
    sums = jnp.zeros((1, cout), jnp.float32)
    squares = jnp.zeros((1, cout), jnp.float32)
    for phase in range(2):
        dot = functools.partial(tap_dot, phase=phase, own_w=own_w, other_w=other_w)
        upper = dot(xs_ref[...], kr=1)
        lower = dot(xs_ref[...], kr=3)
        part_ref[phase] = upper[0]
        even = [upper[row + 1] + lower[row] for row in range(rows - 1)]
        even.append(lower[rows - 1] + dot(xs_next_ref[...], kr=1)[0])
        upper = dot(xs_ref[...], kr=2)
        lower = dot(xs_ref[1:], kr=0)
        odd = [upper[row] + lower[row] for row in range(rows - 1)]
        odd.append(upper[rows - 1] + dot(xs_next_ref[...], kr=0)[0])
        lines = []
        for row in range(rows):
            lines += [odd[row].astype(jnp.bfloat16), even[row].astype(jnp.bfloat16)]
        for row, line in enumerate(lines):
            u_ref[row, phase] = line
        edge_line = jnp.where(first_here, part_ref[phase].astype(jnp.bfloat16).astype(jnp.float32), 0.0)
        final_line = jnp.where(last_here, 0.0, lines[-1].astype(jnp.float32))
        for line in lines[:-1] + [edge_line, final_line]:
            values = line[:width].astype(jnp.float32)
            sums += jnp.sum(values, axis=0, keepdims=True)
            squares += jnp.sum(values * values, axis=0, keepdims=True)
    half = cout // 2
    halves = []
    for row in (sums, squares):
        own, other = row[:, :half], row[:, half:]
        halves += [jnp.where(column == 0, own, other), jnp.where(column == 0, other, own)]
    stats_ref[...] = jnp.concatenate(halves + [jnp.zeros((4, half), jnp.float32)], axis=0)


def halo_kernel(above_ref, below_ref, xs_ref, xs_next_ref, part_ref, own_w, other_w, u_ref, xs_above, xs_below):
    width = above_ref.shape[1] - EDGE
    for row in range(HALO):
        spread_line(xs_above.at[row], above_ref[row, :width], above_ref[row, width:])
    spread_line(xs_below.at[0], below_ref[0, :width], below_ref[0, width:])
    for phase in range(2):
        dot = functools.partial(tap_dot, phase=phase, own_w=own_w, other_w=other_w)
        outer = dot(xs_above[...], kr=3)
        u_ref[0, phase] = (outer[0] + dot(xs_above[1:2], kr=1)[0]).astype(jnp.bfloat16)
        u_ref[2, phase] = (outer[1] + part_ref[phase]).astype(jnp.bfloat16)
        u_ref[1, phase] = (dot(xs_above[1:2], kr=2)[0] + dot(xs_ref[0:1], kr=0)[0]).astype(jnp.bfloat16)
        u_ref[3, phase] = (dot(xs_next_ref[...], kr=2)[0] + dot(xs_below[...], kr=0)[0]).astype(jnp.bfloat16)


def group_sum(v, width):
    lane = lax.broadcasted_iota(jnp.int32, v.shape, 1)
    size = v.shape[1]
    step = 1
    while step < width:
        v = v + jnp.where(
            (lane & step) == 0, pltpu.roll(v, size - step, 1), pltpu.roll(v, step, 1)
        )
        step *= 2
    return v


def fill(ref, row, even, odd):
    total, channels = even.shape
    ref[row, :, 0:channels] = pltpu.roll(odd, 1, 0).astype(jnp.bfloat16)
    ref[row, :, channels : 2 * channels] = even.astype(jnp.bfloat16)
    ref[row, :, 2 * channels : 3 * channels] = odd.astype(jnp.bfloat16)
    ref[row, :, 3 * channels : 4 * channels] = pltpu.roll(even, total - 1, 0).astype(jnp.bfloat16)


def conv_kernel(
    count, u_ref, halo_ref, stats_ref, params_ref, own_w1, other_w1, own_w2, other_w2, out_ref, g, act, mixed
):
    main, _, total, cout = u_ref.shape
    lines = main + 2 * HALO
    width = total - EDGE
    half = own_w1.shape[-1]
    column = lax.axis_index("fsdp")
    own_at = pl.multiple_of(column * half, half)
    other_at = pl.multiple_of((1 - column) * half, half)

    def own_first(row):
        low, high = row[:, :half], row[:, half:]
        return jnp.concatenate([jnp.where(column == 0, low, high), jnp.where(column == 0, high, low)], axis=1)

    def kernel_row(a, own, other):
        return jnp.concatenate(
            [
                jnp.concatenate([ref[a, b, pl.ds(at, half), :] for b in range(3) for at in (own_at, other_at)], axis=0)
                for ref in (own, other)
            ],
            axis=1,
        )

    block = stats_ref[...]
    width_group = cout // NORM_GROUPS
    sums = jnp.concatenate([block[0:1], block[1:2]], axis=1)
    squares = jnp.concatenate([block[2:3], block[3:4]], axis=1)
    mean = group_sum(sums, width_group) / count
    spread = group_sum(squares, width_group) / count - mean * mean
    scale = lax.rsqrt(spread + 1e-05) * params_ref[0:1]
    shift = own_first(params_ref[1:2] - mean * scale)
    scale = own_first(scale)

    mask = edge_mask(width)
    place = lax.axis_index("rows")
    last = lax.axis_size("rows") - 1

    def inside(row, beyond):
        if row < beyond:
            return mask & (place > 0)
        if row >= lines - 2 * HALO + beyond:
            return mask & (place < last)
        return mask

    def hidden(row):
        if row < 3:
            source = halo_ref.at[row]
        elif row < 3 + main:
            source = u_ref.at[row - 3]
        else:
            source = halo_ref.at[3]
        seen = inside(row, HALO)
        fill(
            g,
            row,
            *[jnp.where(seen, silu(source[phase].astype(jnp.float32) * scale + shift), 0.0) for phase in range(2)],
        )

    def conv(source, start, size, cells, phase, own, other, bias):
        acc = bias
        for a in range(3):
            acc = acc + jnp.dot(
                source[start + a : start + a + size, 0:cells, phase * cout : (phase + 3) * cout].reshape(
                    size * cells, 3 * cout
                ),
                kernel_row(a, own, other),
                preferred_element_type=jnp.float32,
            )
        return acc.reshape(size, cells, cout)

    chunk = 2
    bias1 = own_first(params_ref[2:3])
    bias2 = own_first(params_ref[3:4])

    def first(start):
        results = [silu(conv(g, start, chunk, total, phase, own_w1, other_w1, bias1)) for phase in range(2)]
        for row in range(chunk):
            seen = inside(start + row, 1)
            fill(act, start + row, *[jnp.where(seen, r[row], 0.0) for r in results])

    def second(start):
        for phase in range(2):
            acc = conv(act, start, chunk, width, phase, own_w2, other_w2, bias2)
            for row in range(chunk):
                for side in range(2):
                    mixed[side, start + row, pl.ds(phase, width, stride=2), :] = acc[
                        row, :, side * half : (side + 1) * half
                    ]
        for row in range(start, start + chunk):
            out_ref[row, :, pl.ds(own_at, half)] = mixed[0, row].astype(jnp.bfloat16)
            out_ref[row, :, pl.ds(other_at, half)] = mixed[1, row].astype(jnp.bfloat16)

    for row in range(chunk):
        hidden(row)
    for start in range(0, lines - 2, chunk):
        for row in range(start + chunk, start + 2 * chunk):
            hidden(row)
        first(start)
        if start >= chunk:
            second(start - chunk)


def total_over(block, axis, done=1):
    size = lax.axis_size(axis)
    if size & (size - 1):
        return lax.psum(block, axis)
    step = 1
    if (size.bit_length() - 1) % 2:
        block = block + lax.ppermute(block, axis, [(i, i ^ 1) for i in range(size)])
        step = 2
    while step < size:
        block = block + sum(
            lax.ppermute(block, axis, [(i, i ^ (step * d)) for i in range(size)]) for d in (1, 2, 3)
        )
        step *= 4
    return block


def after(value, *others):
    return lax.optimization_barrier((value, *others))[0]


def local(image, deconv_weight, norm_gain, norm_shift, first_weight, first_bias, second_weight, second_bias):
    rows, width, cin = image.shape
    taps, _, _, lanes = deconv_weight.shape
    columns = lax.axis_size("fsdp")
    cout = lanes * columns
    assert columns == 2 and rows == HALO and width % EDGE == 0 and lanes == LANES
    n_rows = lax.axis_size("rows")
    count = float(2 * rows * n_rows * 2 * width * columns * (cout // NORM_GROUPS))
    swap = [(0, 1), (1, 0)]
    to_next = [(i, i + 1) for i in range(n_rows - 1)]
    to_previous = [(i + 1, i) for i in range(n_rows - 1)]
    to_previous_swapped = [(2 * i + 2 + k, 2 * i + 1 - k) for i in range(n_rows - 1) for k in range(2)]
    total = width + EDGE
    hbm = pl.BlockSpec(memory_space=pltpu.HBM)
    vmem = pl.BlockSpec(memory_space=pltpu.VMEM)
    bf16, f32 = jnp.bfloat16, jnp.float32

    def call(kernel, ins, outs, scratch, name, flops=0):
        return pl.pallas_call(
            kernel,
            out_shape=tuple(jax.ShapeDtypeStruct(*o) for o in outs),
            in_specs=ins,
            out_specs=(vmem,) * len(outs),
            scratch_shapes=scratch,
            compiler_params=pltpu.CompilerParams(vmem_limit_bytes=VMEM_BYTES),
            cost_estimate=pl.CostEstimate(flops=flops, bytes_accessed=2**21, transcendentals=0),
            name=name,
        )

    in_hbm = functools.partial(pltpu.with_memory_space_constraint, memory_space=pltpu.HBM)
    line, edges = call(
        cut_kernel,
        [hbm],
        [((1, width, cin), bf16), ((rows, EDGE, cin), bf16)],
        [pltpu.SemaphoreType.DMA((2,))],
        "cut",
    )(in_hbm(image))
    following = lax.ppermute(line, "rows", to_previous)
    following_edge = lax.ppermute(edges[:1], ("rows", "fsdp"), to_previous_swapped)
    edge = lax.ppermute(edges, "fsdp", swap)
    shape_w = (taps, taps // 2, 2, cin, lanes)
    other_w = lax.ppermute(deconv_weight, "fsdp", swap).reshape(shape_w)

    first_other = lax.ppermute(after(first_weight, edge), "fsdp", swap)
    second_other = lax.ppermute(after(second_weight, edge), "fsdp", swap)
    xs, lines, own_w = call(
        own_kernel,
        [hbm, vmem, hbm],
        [((rows, total, 3 * cin), bf16), ((rows, total, cin), bf16), (shape_w, bf16)],
        [pltpu.VMEM(image.shape, bf16), pltpu.SemaphoreType.DMA((2,))],
        "own_lines",
    )(in_hbm(image), edge, in_hbm(deconv_weight.reshape(shape_w)))
    u, part, xs_next, stats = call(
        main_kernel,
        [vmem] * 5,
        [((2 * rows, 2, total, cout), bf16), ((2, total, cout), f32), ((1, total, 3 * cin), bf16), ((8, cout // 2), f32)],
        [],
        "deconv_main",
        flops=2 * 2 * (2 * rows) * total * 4 * cin * cout,
    )(xs, following, following_edge, own_w, other_w)

    lines = after(lines, stats)
    stats = stats + lax.ppermute(stats, "fsdp", swap)
    above = lax.ppermute(lines, "rows", to_next)
    below = lax.ppermute(lines[1:], "rows", to_previous)
    (halo,) = call(
        halo_kernel,
        [vmem] * 7,
        [((4, 2, total, cout), bf16)],
        [pltpu.VMEM((HALO, total, 3 * cin), bf16), pltpu.VMEM((1, total, 3 * cin), bf16)],
        "deconv_halo",
        flops=2 * 2 * 4 * total * 4 * cin * cout,
    )(above, below, xs, xs_next, part, own_w, other_w)

    totals = total_over(stats, "rows")
    params = jnp.stack([norm_gain, norm_shift, first_bias, second_bias])
    (out,) = call(
        functools.partial(conv_kernel, count),
        [vmem] * 8,
        [((2 * rows, 2 * width, cout), bf16)],
        [
            pltpu.VMEM((2 * rows + 2 * HALO, total, 4 * cout), bf16),
            pltpu.VMEM((2 * rows + 2, total, 4 * cout), bf16),
            pltpu.VMEM((2, 2 * rows, 2 * width, lanes), f32),
        ],
        "convs",
        flops=5 * 10**9,
    )(u, halo, totals, params, first_weight, first_other, second_weight, second_other)
    return out


def solution(mesh):
    placed = (
        P(("groups", "rows"), "fsdp", None),
        P(None, None, None, "fsdp"),
        P(),
        P(),
        P(None, None, None, "fsdp"),
        P(),
        P(None, None, None, "fsdp"),
        P(),
    )
    return jax.shard_map(
        local,
        mesh=mesh,
        in_specs=placed,
        out_specs=P(("groups", "rows"), "fsdp", None),
        check_vma=False,
    )
```

time: 50.2 us -> 42 us (0.84)
  the two profiles are of different devices: /device:TPU:0 before, /device:TPU:12 now
where the time goes in v3:
time: 42 us; the launch traced here: 41.8 us
  starting transfers between devices  16.2 us (39%)
  waiting for transfers between devices  15 us (36%)
  Pallas kernels  10.3 us (25%)
    ppermute x1, waiting for transfers between devices, local(): below = lax.ppermute(lines[1:], 'rows', to_previous)  5.98 us
    ppermute x3, starting transfers between devices, total_over(): lax.ppermute(block, axis, [(i, i ^ step * d) for i in range(size)])  5.32 us
    pallas_call x1, Pallas kernels, local(): call(functools.partial(conv_kernel, count), [vmem] * 8, [((2 * rows, 2 *...  4.81 us
    ppermute x3, waiting for transfers between devices, total_over(): lax.ppermute(block, axis, [(i, i ^ step * d) for i in range(size)])  4 us
    ppermute x1, waiting for transfers between devices, total_over(): block = block + lax.ppermute(block, axis, [(i, i ^ 1) for i in range(size)])  3.32 us
    ppermute x1, starting transfers between devices, local(): lax.ppermute(edges[:1], ('rows', 'fsdp'), to_previous_swapped)  3.19 us
    ppermute x1, starting transfers between devices, local(): following = lax.ppermute(line, 'rows', to_previous)  2.41 us
    ppermute x1, starting transfers between devices, local(): above = lax.ppermute(lines, 'rows', to_next)  2.07 us
  transfers between devices with their start and end apart: 13, of which 5 were waited for; matrix products, arithmetic and copies ran while one was open for 0% of the time, Pallas kernels for 13%

profile of v3, /device:TPU:12, one launch (start us, length us, event | category | flops | bytes accessed | tf_op | source)
XLA Modules:
  0.0 41.8 jit_solution(8849635517134519512)
XLA Ops:
  0.0 0.9 %cut.1 = (bf16[1,128,512]{2,1,0:T(8,128)(2,1)S(1)}, bf16[2,16,512]{2,1,0:T(8,128)(2,1)S(1)}) custom-call(bf16[2,128,512]{2,1,0:T(8,128)(2,1)} %image_ref.3), custom_call_target="tpu_custom_call" | custom-call | bytes 2097152 | tf_op jit(solution)/shard_map/cut/pallas_call | solution.py:314
  0.9 2.4 %collective-permute-start.1 = (bf16[1,128,512]{2,1,0:T(8,128)(2,1)S(1)}, bf16[1,128,512]{2,1,0:T(8,128)(2,1)S(1)}, u32[]{:S(2)}, u32[]{:S(2)}) collective-permute-start(bf16[1,128,512]{2,1,0:T(8,128)(2,1)S(1)} %get-tuple-element.19), channel_id=1, source_target_pairs={{2,0},{4,2},{6,4},{8,6},{10,8},{12,10},{14,12},{3,1},{5,3},{7,5},{... | collective-permute-start | bytes 393224 | tf_op jit(solution)/shard_map/ppermute | solution.py:321
  3.4 0.3 collective-permute-start
  3.7 3.2 %collective-permute-start.2 = (bf16[1,16,512]{2,1,0:T(8,128)(2,1)S(1)}, bf16[1,16,512]{2,1,0:T(8,128)(2,1)S(1)}, u32[]{:S(2)}, u32[]{:S(2)}) collective-permute-start(bf16[1,16,512]{2,1,0:T(8,128)(2,1)S(1)} %slice.6), channel_id=1, source_target_pairs={{2,1},{3,0},{4,3},{5,2},{6,5},{7,4},{8,7},{9,6},{10,9},{11,8},{12,... | collective-permute-start | bytes 49160 | tf_op jit(solution)/shard_map/ppermute | solution.py:322
  6.9 0.3 collective-permute-start.11
  7.2 0.3 collective-permute-start.12
  7.4 1.7 %own_lines.1 = (bf16[2,144,1536]{2,1,0:T(8,128)(2,1)S(1)}, bf16[2,144,512]{2,1,0:T(8,128)(2,1)S(1)}, bf16[4,2,2,512,128]{4,3,2,1,0:T(8,128)(2,1)S(1)}) custom-call(bf16[2,128,512]{2,1,0:T(8,128)(2,1)} %image_ref.3, bf16[2,16,512]{2,1,0:T(8,128)(2,1)S(1)} %collective-permute-done.edge_ref, bf16[4,2,2,512,128]{4,3,2,1,0:T(8,128)(2,1)} %bitcast.8), custom_call_target="tpu_custom_call" | custom-call | bytes 2097152 | tf_op jit(solution)/shard_map/own_lines/pallas_call | solution.py:329
  9.1 0.7 %collective-permute-done.2.next_edge_ref = bf16[1,16,512]{2,1,0:T(8,128)(2,1)S(1)} collective-permute-done((bf16[1,16,512]{2,1,0:T(8,128)(2,1)S(1)}, bf16[1,16,512]{2,1,0:T(8,128)(2,1)S(1)}, u32[]{:S(2)}, u32[]{:S(2)}) %collective-permute-start.2) | collective-permute-done | bytes 16416 | tf_op jit(solution)/shard_map/ppermute | solution.py:322
  9.8 0.0 copy-start.3
  9.8 0.0 copy-start.4
  9.9 1.6 %deconv_main.1 = (bf16[4,2,144,256]{3,2,1,0:T(8,128)(2,1)S(1)}, f32[2,144,256]{2,1,0:T(8,128)S(1)}, bf16[1,144,1536]{2,1,0:T(8,128)(2,1)S(1)}, f32[8,128]{1,0:T(8,128)S(1)}) custom-call(bf16[2,144,1536]{2,1,0:T(8,128)(2,1)S(1)} %get-tuple-element.18.xs_ref, bf16[1,128,512]{2,1,0:T(8,128)(2,1)S(1)} %collective-permute-done.1.next_ref, ...), custom_call_target="tpu_custom_call" | custom-call | flops 1207959552 | bytes 2097152 | tf_op jit(solution)/shard_map/deconv_main/pallas_call | solution.py:336
  11.4 0.2 collective-permute-start.6
  11.6 1.1 %collective-permute-done.6 = f32[8,128]{1,0:T(8,128)S(1)} collective-permute-done((f32[8,128]{1,0:T(8,128)S(1)}, f32[8,128]{1,0:T(8,128)S(1)}, u32[]{:S(2)}, u32[]{:S(2)}) %collective-permute-start.6) | collective-permute-done | bytes 4128 | tf_op jit(solution)/shard_map/ppermute | solution.py:346
  12.7 0.3 collective-permute-start.7
  13.0 3.3 %collective-permute-done.7 = f32[8,128]{1,0:T(8,128)S(1)} collective-permute-done((f32[8,128]{1,0:T(8,128)S(1)}, f32[8,128]{1,0:T(8,128)S(1)}, u32[]{:S(2)}, u32[]{:S(2)}) %collective-permute-start.7) | collective-permute-done | bytes 4128 | tf_op jit(solution)/shard_map/ppermute | solution.py:270
  16.3 1.6 %collective-permute-start.10 = (f32[8,128]{1,0:T(8,128)S(1)}, f32[8,128]{1,0:T(8,128)S(1)}, u32[]{:S(2)}, u32[]{:S(2)}) collective-permute-start(f32[8,128]{1,0:T(8,128)S(1)} %add.16), channel_id=1, source_target_pairs={{0,12},{2,14},{4,8},{6,10},{8,4},{10,6},{12,0},{14,2},{1,13},{3,15... | collective-permute-start | bytes 12296 | tf_op jit(solution)/shard_map/ppermute | solution.py:274
  17.9 2.1 %collective-permute-start.4 = (bf16[2,144,512]{2,1,0:T(8,128)(2,1)S(1)}, bf16[2,144,512]{2,1,0:T(8,128)(2,1)S(1)}, u32[]{:S(2)}, u32[]{:S(2)}) collective-permute-start(bf16[2,144,512]{2,1,0:T(8,128)(2,1)S(1)} %get-tuple-element.24), channel_id=1, source_target_pairs={{0,2},{2,4},{4,6},{6,8},{8,10},{10,12},{12,14},{1,3},{3,5},{5,7},{... | collective-permute-start | bytes 884744 | tf_op jit(solution)/shard_map/ppermute | solution.py:347
  19.9 1.7 %collective-permute-start.8 = (f32[8,128]{1,0:T(8,128)S(1)}, f32[8,128]{1,0:T(8,128)S(1)}, u32[]{:S(2)}, u32[]{:S(2)}) collective-permute-start(f32[8,128]{1,0:T(8,128)S(1)} %add.16), channel_id=1, source_target_pairs={{0,4},{2,6},{4,0},{6,2},{8,12},{10,14},{12,8},{14,10},{1,5},{3,7},... | collective-permute-start | bytes 12296 | tf_op jit(solution)/shard_map/ppermute | solution.py:274
  21.7 2.0 %collective-permute-start.9 = (f32[8,128]{1,0:T(8,128)S(1)}, f32[8,128]{1,0:T(8,128)S(1)}, u32[]{:S(2)}, u32[]{:S(2)}) collective-permute-start(f32[8,128]{1,0:T(8,128)S(1)} %add.16), channel_id=1, source_target_pairs={{0,8},{2,10},{4,12},{6,14},{8,0},{10,2},{12,4},{14,6},{1,9},{3,11}... | collective-permute-start | bytes 12296 | tf_op jit(solution)/shard_map/ppermute | solution.py:274
  23.7 4.0 %collective-permute-done.8 = f32[8,128]{1,0:T(8,128)S(1)} collective-permute-done((f32[8,128]{1,0:T(8,128)S(1)}, f32[8,128]{1,0:T(8,128)S(1)}, u32[]{:S(2)}, u32[]{:S(2)}) %collective-permute-start.8) | collective-permute-done | bytes 4128 | tf_op jit(solution)/shard_map/ppermute | solution.py:274
  27.7 1.9 %collective-permute-start.5 = (bf16[1,144,512]{2,1,0:T(8,128)(2,1)S(1)}, bf16[1,144,512]{2,1,0:T(8,128)(2,1)S(1)}, u32[]{:S(2)}, u32[]{:S(2)}) collective-permute-start(bf16[1,144,512]{2,1,0:T(8,128)(2,1)S(1)} %slice.7), channel_id=1, source_target_pairs={{2,0},{4,2},{6,4},{8,6},{10,8},{12,10},{14,12},{3,1},{5,3},{7,5},{... | collective-permute-start | bytes 442376 | tf_op jit(solution)/shard_map/ppermute | solution.py:348
  29.7 6.0 %collective-permute-done.5.below_ref = bf16[1,144,512]{2,1,0:T(8,128)(2,1)S(1)} collective-permute-done((bf16[1,144,512]{2,1,0:T(8,128)(2,1)S(1)}, bf16[1,144,512]{2,1,0:T(8,128)(2,1)S(1)}, u32[]{:S(2)}, u32[]{:S(2)}) %collective-permute-start.5) | collective-permute-done | bytes 147488 | tf_op jit(solution)/shard_map/ppermute | solution.py:348
  35.7 1.2 %deconv_halo.1.halo_ref = bf16[4,2,144,256]{3,2,1,0:T(8,128)(2,1)S(1)} custom-call(bf16[2,144,512]{2,1,0:T(8,128)(2,1)S(1)} %collective-permute-done.4.above_ref, bf16[1,144,512]{2,1,0:T(8,128)(2,1)S(1)} %collective-permute-done.5.below_ref, bf16[2,144,1536]{2,1,0:T(8,128)(2,1)S(1)} %get-tuple-element.18.xs_ref, ...), custom_call_target="tpu_custom_call" | custom-call | flops 1207959552 | bytes 2097152 | tf_op jit(solution)/shard_map/deconv_halo/pallas_call | solution.py:349
  37.0 4.8 %convs.1 = bf16[4,256,256]{2,1,0:T(8,128)(2,1)} custom-call(bf16[4,2,144,256]{3,2,1,0:T(8,128)(2,1)S(1)} %get-tuple-element.21.u_ref, bf16[4,2,144,256]{3,2,1,0:T(8,128)(2,1)S(1)} %deconv_halo.1.halo_ref, f32[8,128]{1,0:T(8,128)S(1)} %add_add_fusion.stats_ref, f32[4,256]{1,0:T(4,128)S(1)} %pad_maximum_fusion.params_ref, ...), custom_call_target="tpu_custom_call" | custom-call | flops 5000000000 | bytes 2097152 | tf_op jit(solution)/shard_map/convs/pallas_call | solution.py:360
  (25 shorter events, 0.1 us)
Async XLA Ops:
  0.0 9.8 %collective-permute-start.3 = (bf16[4,4,512,128]{3,2,1,0:T(8,128)(2,1)}, bf16[4,4,512,128]{3,2,1,0:T(8,128)(2,1)S(1)}, u32[]{:S(2)}, u32[]{:S(2)}) collective-permute-start(bf16[4,4,512,128]{3,2,1,0:T(8,128)(2,1)} %param.9), channel_id=1, source_target_pairs={{0,1},{1,0},{2,3},{3,2},{4,5},{5,4},{6,7},{7,6},{8,9},{9,8},{10,11... | collective-permute-start | bytes 6291464 | tf_op jit(solution)/shard_map/ppermute | solution.py:325
  0.9 8.9 %collective-permute-start.1 = (bf16[1,128,512]{2,1,0:T(8,128)(2,1)S(1)}, bf16[1,128,512]{2,1,0:T(8,128)(2,1)S(1)}, u32[]{:S(2)}, u32[]{:S(2)}) collective-permute-start(bf16[1,128,512]{2,1,0:T(8,128)(2,1)S(1)} %get-tuple-element.19), channel_id=1, source_target_pairs={{2,0},{4,2},{6,4},{8,6},{10,8},{12,10},{14,12},{3,1},{5,3},{7,5},{... | collective-permute-start | bytes 393224 | tf_op jit(solution)/shard_map/ppermute | solution.py:321
  3.4 3.5 %collective-permute-start = (bf16[2,16,512]{2,1,0:T(8,128)(2,1)S(1)}, bf16[2,16,512]{2,1,0:T(8,128)(2,1)S(1)}, u32[]{:S(2)}, u32[]{:S(2)}) collective-permute-start(bf16[2,16,512]{2,1,0:T(8,128)(2,1)S(1)} %get-tuple-element.17), channel_id=1, source_target_pairs={{0,1},{1,0},{2,3},{3,2},{4,5},{5,4},{6,7},{7,6},{8,9},{9,8},{10,11... | collective-permute-start | bytes 98312 | tf_op jit(solution)/shard_map/ppermute | solution.py:323
  3.7 6.2 %collective-permute-start.2 = (bf16[1,16,512]{2,1,0:T(8,128)(2,1)S(1)}, bf16[1,16,512]{2,1,0:T(8,128)(2,1)S(1)}, u32[]{:S(2)}, u32[]{:S(2)}) collective-permute-start(bf16[1,16,512]{2,1,0:T(8,128)(2,1)S(1)} %slice.6), channel_id=1, source_target_pairs={{2,1},{3,0},{4,3},{5,2},{6,5},{7,4},{8,7},{9,6},{10,9},{11,8},{12,... | collective-permute-start | bytes 49160 | tf_op jit(solution)/shard_map/ppermute | solution.py:322
  6.9 30.1 %collective-permute-start.11 = (bf16[3,3,256,128]{3,2,1,0:T(8,128)(2,1)}, bf16[3,3,256,128]{3,2,1,0:T(8,128)(2,1)S(1)}, u32[]{:S(2)}, u32[]{:S(2)}) collective-permute-start(bf16[3,3,256,128]{3,2,1,0:T(8,128)(2,1)} %own_w1.1), channel_id=1, source_target_pairs={{0,1},{1,0},{2,3},{3,2},{4,5},{5,4},{6,7},{7,6},{8,9},{9,8},{10,11... | collective-permute-start | bytes 1769480 | tf_op jit(solution)/shard_map/ppermute | solution.py:327
  7.2 29.8 %collective-permute-start.12 = (bf16[3,3,256,128]{3,2,1,0:T(8,128)(2,1)}, bf16[3,3,256,128]{3,2,1,0:T(8,128)(2,1)S(1)}, u32[]{:S(2)}, u32[]{:S(2)}) collective-permute-start(bf16[3,3,256,128]{3,2,1,0:T(8,128)(2,1)} %own_w2.1), channel_id=1, source_target_pairs={{0,1},{1,0},{2,3},{3,2},{4,5},{5,4},{6,7},{7,6},{8,9},{9,8},{10,11... | collective-permute-start | bytes 1769480 | tf_op jit(solution)/shard_map/ppermute | solution.py:328
  9.8 13.9 %copy-start.2 = (f32[256]{0:T(256)S(1)}, f32[256]{0:T(256)}, u32[]{:S(2)}) copy-start(f32[256]{0:T(256)} %param.15) | copy-start | bytes 3076
  9.8 13.9 %copy-start.3 = (f32[256]{0:T(256)S(1)}, f32[256]{0:T(256)}, u32[]{:S(2)}) copy-start(f32[256]{0:T(256)} %param.13) | copy-start | bytes 3076
  9.8 13.9 %copy-start.4 = (f32[256]{0:T(256)S(1)}, f32[256]{0:T(256)}, u32[]{:S(2)}) copy-start(f32[256]{0:T(256)} %param.11) | copy-start | bytes 3076
  9.8 13.9 %copy-start.5 = (f32[256]{0:T(256)S(1)}, f32[256]{0:T(256)}, u32[]{:S(2)}) copy-start(f32[256]{0:T(256)} %param.10) | copy-start | bytes 3076
  11.4 1.2 %collective-permute-start.6 = (f32[8,128]{1,0:T(8,128)S(1)}, f32[8,128]{1,0:T(8,128)S(1)}, u32[]{:S(2)}, u32[]{:S(2)}) collective-permute-start(f32[8,128]{1,0:T(8,128)S(1)} %get-tuple-element.23), channel_id=1, source_target_pairs={{0,1},{1,0},{2,3},{3,2},{4,5},{5,4},{6,7},{7,6},{8,9},{9,8},{10,11... | collective-permute-start | bytes 12296 | tf_op jit(solution)/shard_map/ppermute | solution.py:346
  12.7 3.6 %collective-permute-start.7 = (f32[8,128]{1,0:T(8,128)S(1)}, f32[8,128]{1,0:T(8,128)S(1)}, u32[]{:S(2)}, u32[]{:S(2)}) collective-permute-start(f32[8,128]{1,0:T(8,128)S(1)} %add.15), channel_id=1, source_target_pairs={{0,2},{2,0},{4,6},{6,4},{8,10},{10,8},{12,14},{14,12},{1,3},{3,1},... | collective-permute-start | bytes 12296 | tf_op jit(solution)/shard_map/ppermute | solution.py:270
  16.3 5.4 %collective-permute-start.10 = (f32[8,128]{1,0:T(8,128)S(1)}, f32[8,128]{1,0:T(8,128)S(1)}, u32[]{:S(2)}, u32[]{:S(2)}) collective-permute-start(f32[8,128]{1,0:T(8,128)S(1)} %add.16), channel_id=1, source_target_pairs={{0,12},{2,14},{4,8},{6,10},{8,4},{10,6},{12,0},{14,2},{1,13},{3,15... | collective-permute-start | bytes 12296 | tf_op jit(solution)/shard_map/ppermute | solution.py:274
  17.9 17.8 %collective-permute-start.4 = (bf16[2,144,512]{2,1,0:T(8,128)(2,1)S(1)}, bf16[2,144,512]{2,1,0:T(8,128)(2,1)S(1)}, u32[]{:S(2)}, u32[]{:S(2)}) collective-permute-start(bf16[2,144,512]{2,1,0:T(8,128)(2,1)S(1)} %get-tuple-element.24), channel_id=1, source_target_pairs={{0,2},{2,4},{4,6},{6,8},{8,10},{10,12},{12,14},{1,3},{3,5},{5,7},{... | collective-permute-start | bytes 884744 | tf_op jit(solution)/shard_map/ppermute | solution.py:347
  19.9 7.8 %collective-permute-start.8 = (f32[8,128]{1,0:T(8,128)S(1)}, f32[8,128]{1,0:T(8,128)S(1)}, u32[]{:S(2)}, u32[]{:S(2)}) collective-permute-start(f32[8,128]{1,0:T(8,128)S(1)} %add.16), channel_id=1, source_target_pairs={{0,4},{2,6},{4,0},{6,2},{8,12},{10,14},{12,8},{14,10},{1,5},{3,7},... | collective-permute-start | bytes 12296 | tf_op jit(solution)/shard_map/ppermute | solution.py:274
  21.7 8.0 %collective-permute-start.9 = (f32[8,128]{1,0:T(8,128)S(1)}, f32[8,128]{1,0:T(8,128)S(1)}, u32[]{:S(2)}, u32[]{:S(2)}) collective-permute-start(f32[8,128]{1,0:T(8,128)S(1)} %add.16), channel_id=1, source_target_pairs={{0,8},{2,10},{4,12},{6,14},{8,0},{10,2},{12,4},{14,6},{1,9},{3,11}... | collective-permute-start | bytes 12296 | tf_op jit(solution)/shard_map/ppermute | solution.py:274
  27.7 7.9 %collective-permute-start.5 = (bf16[1,144,512]{2,1,0:T(8,128)(2,1)S(1)}, bf16[1,144,512]{2,1,0:T(8,128)(2,1)S(1)}, u32[]{:S(2)}, u32[]{:S(2)}) collective-permute-start(bf16[1,144,512]{2,1,0:T(8,128)(2,1)S(1)} %slice.7), channel_id=1, source_target_pairs={{2,0},{4,2},{6,4},{8,6},{10,8},{12,10},{14,12},{3,1},{5,3},{7,5},{... | collective-permute-start | bytes 442376 | tf_op jit(solution)/shard_map/ppermute | solution.py:348
  35.7 1.3 %copy-start = (bf16[3,3,256,128]{3,2,1,0:T(8,128)(2,1)S(1)}, bf16[3,3,256,128]{3,2,1,0:T(8,128)(2,1)}, u32[]{:S(2)}) copy-start(bf16[3,3,256,128]{3,2,1,0:T(8,128)(2,1)} %own_w1.1) | copy-start | bytes 1769476
  35.7 1.3 %copy-start.1 = (bf16[3,3,256,128]{3,2,1,0:T(8,128)(2,1)S(1)}, bf16[3,3,256,128]{3,2,1,0:T(8,128)(2,1)}, u32[]{:S(2)}) copy-start(bf16[3,3,256,128]{3,2,1,0:T(8,128)(2,1)} %own_w2.1) | copy-start | bytes 1769476

commit v4 on v3

--- a/solution.py
+++ b/solution.py
@@ -28,12 +28,12 @@
     return (cell < 0) | right | left
 
 
-def cut_kernel(image_ref, line_ref, edges_ref, sems):
+def cut_kernel(image_ref, near_ref, edges_ref, sems):
     width = image_ref.shape[1]
     start = pl.multiple_of((1 - lax.axis_index("fsdp")) * (width - EDGE), EDGE)
     copies = [
-        pltpu.make_async_copy(image_ref.at[0:1], line_ref, sems.at[0]),
-        pltpu.make_async_copy(image_ref.at[:, pl.ds(start, EDGE), :], edges_ref, sems.at[1]),
+        pltpu.make_async_copy(image_ref.at[:, pl.ds(start, EDGE), :], edges_ref, sems.at[0]),
+        pltpu.make_async_copy(image_ref, near_ref, sems.at[1]),
     ]
     for copy in copies:
         copy.start()
@@ -41,31 +41,23 @@
         copy.wait()
 
 
-def spread_line(out, main, edge):
-    cin = main.shape[-1]
-    cell = lax.broadcasted_iota(jnp.int32, (EDGE, 1), 0)
-    keep = jnp.where(lax.axis_index("fsdp") == 0, cell, EDGE - 1 - cell) < EDGE // 2
-    edge = jnp.where(keep, edge.astype(jnp.float32), 0.0)
-    line = jnp.concatenate([main.astype(jnp.float32), edge], axis=0)
-    out[:, 0:cin] = pltpu.roll(line, line.shape[0] - 1, 0).astype(jnp.bfloat16)
+def near_kernel(weight_ref, near_ref, sem):
+    copy = pltpu.make_async_copy(weight_ref, near_ref, sem)
+    copy.start()
+    copy.wait()
+
+
+def spread_line(out, line):
+    total, cin = line.shape
+    line = jnp.where(edge_mask(total - EDGE), line.astype(jnp.float32), 0.0)
+    out[:, 0:cin] = pltpu.roll(line, total - 1, 0).astype(jnp.bfloat16)
     out[:, cin : 2 * cin] = line.astype(jnp.bfloat16)
     out[:, 2 * cin : 3 * cin] = pltpu.roll(line, 1, 0).astype(jnp.bfloat16)
 
 
-def own_kernel(image_ref, edge_ref, weight_ref, xs_ref, lines_ref, own_w_ref, held, sems):
-    rows, width, _ = image_ref.shape
-    copies = [
-        pltpu.make_async_copy(image_ref, held, sems.at[0]),
-        pltpu.make_async_copy(weight_ref, own_w_ref, sems.at[1]),
-    ]
-    for copy in copies:
-        copy.start()
-    copies[0].wait()
-    for row in range(rows):
-        spread_line(xs_ref.at[row], held[row], edge_ref[row])
-        lines_ref[row, :width] = held[row]
-        lines_ref[row, width:] = edge_ref[row]
-    copies[1].wait()
+def own_kernel(lines_ref, xs_ref):
+    for row in range(lines_ref.shape[0]):
+        spread_line(xs_ref.at[row], lines_ref[row])
 
 
 def tap_dot(lines, phase, kr, own_w, other_w):
@@ -83,11 +75,11 @@
     return out.reshape(count, total, weight.shape[-1])
 
 
-def main_kernel(xs_ref, next_ref, next_edge_ref, own_w, other_w, u_ref, part_ref, xs_next_ref, stats_ref):
+def main_kernel(xs_ref, next_ref, own_w, other_w, u_ref, part_ref, xs_next_ref, stats_ref):
     rows, total, _ = xs_ref.shape
     width = total - EDGE
     cout = u_ref.shape[-1]
-    spread_line(xs_next_ref.at[0], next_ref[0], next_edge_ref[0])
+    spread_line(xs_next_ref.at[0], next_ref[0])
     column = lax.axis_index("fsdp")
     place = lax.axis_index("rows")
     first_here = place == 0
@@ -125,10 +117,9 @@
 
 
 def halo_kernel(above_ref, below_ref, xs_ref, xs_next_ref, part_ref, own_w, other_w, u_ref, xs_above, xs_below):
-    width = above_ref.shape[1] - EDGE
     for row in range(HALO):
-        spread_line(xs_above.at[row], above_ref[row, :width], above_ref[row, width:])
-    spread_line(xs_below.at[0], below_ref[0, :width], below_ref[0, width:])
+        spread_line(xs_above.at[row], above_ref[row])
+    spread_line(xs_below.at[0], below_ref[0])
     for phase in range(2):
         dot = functools.partial(tap_dot, phase=phase, own_w=own_w, other_w=other_w)
         outer = dot(xs_above[...], kr=3)
@@ -261,19 +252,14 @@
             second(start - chunk)
 
 
-def total_over(block, axis, done=1):
+def total_over(block, axis):
     size = lax.axis_size(axis)
     if size & (size - 1):
         return lax.psum(block, axis)
     step = 1
-    if (size.bit_length() - 1) % 2:
-        block = block + lax.ppermute(block, axis, [(i, i ^ 1) for i in range(size)])
-        step = 2
     while step < size:
-        block = block + sum(
-            lax.ppermute(block, axis, [(i, i ^ (step * d)) for i in range(size)]) for d in (1, 2, 3)
-        )
-        step *= 4
+        block = block + lax.ppermute(block, axis, [(i, i ^ step) for i in range(size)])
+        step *= 2
     return block
 
 
@@ -292,7 +278,6 @@
     swap = [(0, 1), (1, 0)]
     to_next = [(i, i + 1) for i in range(n_rows - 1)]
     to_previous = [(i + 1, i) for i in range(n_rows - 1)]
-    to_previous_swapped = [(2 * i + 2 + k, 2 * i + 1 - k) for i in range(n_rows - 1) for k in range(2)]
     total = width + EDGE
     hbm = pl.BlockSpec(memory_space=pltpu.HBM)
     vmem = pl.BlockSpec(memory_space=pltpu.VMEM)
@@ -311,41 +296,35 @@
         )
 
     in_hbm = functools.partial(pltpu.with_memory_space_constraint, memory_space=pltpu.HBM)
-    line, edges = call(
+    shape_w = (taps, taps // 2, 2, cin, lanes)
+    other_w = lax.ppermute(deconv_weight, "fsdp", swap).reshape(shape_w)
+    first_other = lax.ppermute(first_weight, "fsdp", swap)
+    second_other = lax.ppermute(second_weight, "fsdp", swap)
+    near, edges = call(
         cut_kernel,
         [hbm],
-        [((1, width, cin), bf16), ((rows, EDGE, cin), bf16)],
+        [(image.shape, bf16), ((rows, EDGE, cin), bf16)],
         [pltpu.SemaphoreType.DMA((2,))],
         "cut",
     )(in_hbm(image))
-    following = lax.ppermute(line, "rows", to_previous)
-    following_edge = lax.ppermute(edges[:1], ("rows", "fsdp"), to_previous_swapped)
     edge = lax.ppermute(edges, "fsdp", swap)
-    shape_w = (taps, taps // 2, 2, cin, lanes)
-    other_w = lax.ppermute(deconv_weight, "fsdp", swap).reshape(shape_w)
-
-    first_other = lax.ppermute(after(first_weight, edge), "fsdp", swap)
-    second_other = lax.ppermute(after(second_weight, edge), "fsdp", swap)
-    xs, lines, own_w = call(
-        own_kernel,
-        [hbm, vmem, hbm],
-        [((rows, total, 3 * cin), bf16), ((rows, total, cin), bf16), (shape_w, bf16)],
-        [pltpu.VMEM(image.shape, bf16), pltpu.SemaphoreType.DMA((2,))],
-        "own_lines",
-    )(in_hbm(image), edge, in_hbm(deconv_weight.reshape(shape_w)))
+    (own_w,) = call(near_kernel, [hbm], [(shape_w, bf16)], [pltpu.SemaphoreType.DMA(())], "near_weights")(
+        in_hbm(after(deconv_weight, edges).reshape(shape_w))
+    )
+    lines = jnp.concatenate([near, edge], axis=1)
+    following = lax.ppermute(lines[:1], "rows", to_previous)
+    above = lax.ppermute(lines, "rows", to_next)
+    below = lax.ppermute(lines[1:], "rows", to_previous)
+    (xs,) = call(own_kernel, [vmem], [((rows, total, 3 * cin), bf16)], [], "own_lines")(lines)
     u, part, xs_next, stats = call(
         main_kernel,
-        [vmem] * 5,
+        [vmem] * 4,
         [((2 * rows, 2, total, cout), bf16), ((2, total, cout), f32), ((1, total, 3 * cin), bf16), ((8, cout // 2), f32)],
         [],
         "deconv_main",
         flops=2 * 2 * (2 * rows) * total * 4 * cin * cout,
-    )(xs, following, following_edge, own_w, other_w)
-
-    lines = after(lines, stats)
-    stats = stats + lax.ppermute(stats, "fsdp", swap)
-    above = lax.ppermute(lines, "rows", to_next)
-    below = lax.ppermute(lines[1:], "rows", to_previous)
+    )(xs, following, own_w, other_w)
+
     (halo,) = call(
         halo_kernel,
         [vmem] * 7,
@@ -355,7 +334,7 @@
         flops=2 * 2 * 4 * total * 4 * cin * cout,
     )(above, below, xs, xs_next, part, own_w, other_w)
 
-    totals = total_over(stats, "rows")
+    totals = total_over(total_over(stats, "fsdp"), "rows")
     params = jnp.stack([norm_gain, norm_shift, first_bias, second_bias])
     (out,) = call(
         functools.partial(conv_kernel, count),

time: 42 us -> 37.1 us (0.88)
  the two profiles are of different devices: /device:TPU:12 before, /device:TPU:0 now
where the time goes in v4:
time: 37.1 us; the launch traced here: 36.9 us
  starting transfers between devices  18.4 us (50%)
  Pallas kernels  10.4 us (28%)
  waiting for transfers between devices  7.83 us (21%)
    ppermute x4, starting transfers between devices, total_over(): lax.ppermute(block, axis, [(i, i ^ step) for i in range(size)])  9.31 us
    ppermute x1, starting transfers between devices, local(): above = lax.ppermute(lines, 'rows', to_next)  5.44 us
    ppermute x4, waiting for transfers between devices, total_over(): lax.ppermute(block, axis, [(i, i ^ step) for i in range(size)])  5.24 us
    pallas_call x1, Pallas kernels, local(): call(functools.partial(conv_kernel, count), [vmem] * 8, [((2 * rows, 2 *...  4.79 us
    ppermute x1, waiting for transfers between devices, local(): edge = lax.ppermute(edges, 'fsdp', swap)  2.15 us
    pallas_call x1, Pallas kernels, local(): call(near_kernel, [hbm], [(shape_w, bf16)], [pltpu.SemaphoreType.DMA(())]...  1.6 us
    pallas_call x1, Pallas kernels, local(): call(main_kernel, [vmem] * 4, [((2 * rows, 2, total, cout), bf16), ((2, t...  1.57 us
    ppermute x1, starting transfers between devices, local(): following = lax.ppermute(lines[:1], 'rows', to_previous)  1.29 us
  transfers between devices with their start and end apart: 11, of which 6 were waited for; matrix products, arithmetic and copies ran while one was open for 0% of the time, Pallas kernels for 15%

profile of v4, /device:TPU:0, one launch (start us, length us, event | category | flops | bytes accessed | tf_op | source)
XLA Modules:
  0.0 36.9 jit_solution(16025641654570244888)
XLA Ops:
  0.0 0.5 %collective-permute-start.2 = (bf16[4,4,512,128]{3,2,1,0:T(8,128)(2,1)}, bf16[4,4,512,128]{3,2,1,0:T(8,128)(2,1)S(1)}, u32[]{:S(2)}, u32[]{:S(2)}) collective-permute-start(bf16[4,4,512,128]{3,2,1,0:T(8,128)(2,1)} %param.9), channel_id=1, source_target_pairs={{0,1},{1,0},{2,3},{3,2},{4,5},{5,4},{6,7},{7,6},{8,9},{9,8},{10,11... | collective-permute-start | bytes 6291464 | tf_op jit(solution)/shard_map/ppermute | solution.py:300
  0.5 1.0 %cut.1 = (bf16[2,128,512]{2,1,0:T(8,128)(2,1)S(1)}, bf16[2,16,512]{2,1,0:T(8,128)(2,1)S(1)}) custom-call(bf16[2,128,512]{2,1,0:T(8,128)(2,1)} %image_ref.1), custom_call_target="tpu_custom_call" | custom-call | bytes 2097152 | tf_op jit(solution)/shard_map/cut/pallas_call | solution.py:303
  1.5 0.1 collective-permute-start
  1.6 0.5 %collective-permute-start.10 = (bf16[3,3,256,128]{3,2,1,0:T(8,128)(2,1)}, bf16[3,3,256,128]{3,2,1,0:T(8,128)(2,1)S(1)}, u32[]{:S(2)}, u32[]{:S(2)}) collective-permute-start(bf16[3,3,256,128]{3,2,1,0:T(8,128)(2,1)} %own_w2.1), channel_id=1, source_target_pairs={{0,1},{1,0},{2,3},{3,2},{4,5},{5,4},{6,7},{7,6},{8,9},{9,8},{10,11... | collective-permute-start | bytes 1769480 | tf_op jit(solution)/shard_map/ppermute | solution.py:302
  2.1 0.1 collective-permute-start.9
  2.2 2.2 %collective-permute-done = bf16[2,16,512]{2,1,0:T(8,128)(2,1)S(1)} collective-permute-done((bf16[2,16,512]{2,1,0:T(8,128)(2,1)S(1)}, bf16[2,16,512]{2,1,0:T(8,128)(2,1)S(1)}, u32[]{:S(2)}, u32[]{:S(2)}) %collective-permute-start) | collective-permute-done | bytes 32800 | tf_op jit(solution)/shard_map/ppermute | solution.py:310
  4.4 1.3 %collective-permute-start.1 = (bf16[1,144,512]{2,1,0:T(8,128)(2,1)S(1)}, bf16[1,144,512]{2,1,0:T(8,128)(2,1)S(1)}, u32[]{:S(2)}, u32[]{:S(2)}) collective-permute-start(bf16[1,144,512]{2,1,0:T(8,128)(2,1)S(1)} %get-tuple-element.20), channel_id=1, source_target_pairs={{2,0},{4,2},{6,4},{8,6},{10,8},{12,10},{14,12},{3,1},{5,3},{7,5},{... | collective-permute-start | bytes 442376 | tf_op jit(solution)/shard_map/ppermute | solution.py:315
  5.7 5.4 %collective-permute-start.3 = (bf16[2,144,512]{2,1,0:T(8,128)(2,1)S(1)}, bf16[2,144,512]{2,1,0:T(8,128)(2,1)S(1)}, u32[]{:S(2)}, u32[]{:S(2)}) collective-permute-start(bf16[2,144,512]{2,1,0:T(8,128)(2,1)S(1)} %constant_dynamic-update-slice_fusion.lines_ref), channel_id=1, source_target_pairs={{0,2},{2,4},{4,6},{6,8},{8,10},{10,12},{12,14},{1,3},{3,5},{5,7},{... | collective-permute-start | bytes 884744 | tf_op jit(solution)/shard_map/ppermute | solution.py:316
  11.1 1.6 %near_weights.1.own_w = bf16[4,2,2,512,128]{4,3,2,1,0:T(8,128)(2,1)S(1)} custom-call(bf16[4,2,2,512,128]{4,3,2,1,0:T(8,128)(2,1)} %bitcast.8), custom_call_target="tpu_custom_call" | custom-call | bytes 2097152 | tf_op jit(solution)/shard_map/near_weights/pallas_call | solution.py:311
  12.7 0.1 own_lines.1.xs_ref
  12.9 0.4 %collective-permute-done.1.next_ref = bf16[1,144,512]{2,1,0:T(8,128)(2,1)S(1)} collective-permute-done((bf16[1,144,512]{2,1,0:T(8,128)(2,1)S(1)}, bf16[1,144,512]{2,1,0:T(8,128)(2,1)S(1)}, u32[]{:S(2)}, u32[]{:S(2)}) %collective-permute-start.1) | collective-permute-done | bytes 147488 | tf_op jit(solution)/shard_map/ppermute | solution.py:315
  13.3 1.3 %collective-permute-start.4 = (bf16[1,144,512]{2,1,0:T(8,128)(2,1)S(1)}, bf16[1,144,512]{2,1,0:T(8,128)(2,1)S(1)}, u32[]{:S(2)}, u32[]{:S(2)}) collective-permute-start(bf16[1,144,512]{2,1,0:T(8,128)(2,1)S(1)} %get-tuple-element.19), channel_id=1, source_target_pairs={{2,0},{4,2},{6,4},{8,6},{10,8},{12,10},{14,12},{3,1},{5,3},{7,5},{... | collective-permute-start | bytes 442376 | tf_op jit(solution)/shard_map/ppermute | solution.py:317
  14.6 0.0 copy-start.4
  14.6 1.6 %deconv_main.1 = (bf16[4,2,144,256]{3,2,1,0:T(8,128)(2,1)S(1)}, f32[2,144,256]{2,1,0:T(8,128)S(1)}, bf16[1,144,1536]{2,1,0:T(8,128)(2,1)S(1)}, f32[8,128]{1,0:T(8,128)S(1)}) custom-call(bf16[2,144,1536]{2,1,0:T(8,128)(2,1)S(1)} %own_lines.1.xs_ref, bf16[1,144,512]{2,1,0:T(8,128)(2,1)S(1)} %collective-permute-done.1.next_ref, ...), custom_call_target="tpu_custom_call" | custom-call | flops 1207959552 | bytes 2097152 | tf_op jit(solution)/shard_map/deconv_main/pallas_call | solution.py:319
  16.2 0.1 collective-permute-start.5
  16.3 1.2 %collective-permute-done.5 = f32[8,128]{1,0:T(8,128)S(1)} collective-permute-done((f32[8,128]{1,0:T(8,128)S(1)}, f32[8,128]{1,0:T(8,128)S(1)}, u32[]{:S(2)}, u32[]{:S(2)}) %collective-permute-start.5) | collective-permute-done | bytes 4128 | tf_op jit(solution)/shard_map/ppermute | solution.py:261
  17.5 3.4 %collective-permute-start.6 = (f32[8,128]{1,0:T(8,128)S(1)}, f32[8,128]{1,0:T(8,128)S(1)}, u32[]{:S(2)}, u32[]{:S(2)}) collective-permute-start(f32[8,128]{1,0:T(8,128)S(1)} %add.12), channel_id=1, source_target_pairs={{0,2},{2,0},{4,6},{6,4},{8,10},{10,8},{12,14},{14,12},{1,3},{3,1},... | collective-permute-start | bytes 12296 | tf_op jit(solution)/shard_map/ppermute | solution.py:261
  20.8 2.2 %collective-permute-done.6 = f32[8,128]{1,0:T(8,128)S(1)} collective-permute-done((f32[8,128]{1,0:T(8,128)S(1)}, f32[8,128]{1,0:T(8,128)S(1)}, u32[]{:S(2)}, u32[]{:S(2)}) %collective-permute-start.6) | collective-permute-done | bytes 4128 | tf_op jit(solution)/shard_map/ppermute | solution.py:261
  23.0 2.8 %collective-permute-start.7 = (f32[8,128]{1,0:T(8,128)S(1)}, f32[8,128]{1,0:T(8,128)S(1)}, u32[]{:S(2)}, u32[]{:S(2)}) collective-permute-start(f32[8,128]{1,0:T(8,128)S(1)} %add.13), channel_id=1, source_target_pairs={{0,4},{2,6},{4,0},{6,2},{8,12},{10,14},{12,8},{14,10},{1,5},{3,7},... | collective-permute-start | bytes 12296 | tf_op jit(solution)/shard_map/ppermute | solution.py:261
  25.9 1.6 %collective-permute-done.7 = f32[8,128]{1,0:T(8,128)S(1)} collective-permute-done((f32[8,128]{1,0:T(8,128)S(1)}, f32[8,128]{1,0:T(8,128)S(1)}, u32[]{:S(2)}, u32[]{:S(2)}) %collective-permute-start.7) | collective-permute-done | bytes 4128 | tf_op jit(solution)/shard_map/ppermute | solution.py:261
  27.5 3.0 %collective-permute-start.8 = (f32[8,128]{1,0:T(8,128)S(1)}, f32[8,128]{1,0:T(8,128)S(1)}, u32[]{:S(2)}, u32[]{:S(2)}) collective-permute-start(f32[8,128]{1,0:T(8,128)S(1)} %add.14), channel_id=1, source_target_pairs={{0,8},{2,10},{4,12},{6,14},{8,0},{10,2},{12,4},{14,6},{1,9},{3,11}... | collective-permute-start | bytes 12296 | tf_op jit(solution)/shard_map/ppermute | solution.py:261
  30.5 1.2 %deconv_halo.1.halo_ref = bf16[4,2,144,256]{3,2,1,0:T(8,128)(2,1)S(1)} custom-call(bf16[2,144,512]{2,1,0:T(8,128)(2,1)S(1)} %collective-permute-done.3.above_ref, bf16[1,144,512]{2,1,0:T(8,128)(2,1)S(1)} %collective-permute-done.4.below_ref, bf16[2,144,1536]{2,1,0:T(8,128)(2,1)S(1)} %own_lines.1.xs_ref, ...), custom_call_target="tpu_custom_call" | custom-call | flops 1207959552 | bytes 2097152 | tf_op jit(solution)/shard_map/deconv_halo/pallas_call | solution.py:328
  31.8 0.3 collective-permute-done.8
  32.1 4.8 %convs.1 = bf16[4,256,256]{2,1,0:T(8,128)(2,1)} custom-call(bf16[4,2,144,256]{3,2,1,0:T(8,128)(2,1)S(1)} %get-tuple-element.15.u_ref, bf16[4,2,144,256]{3,2,1,0:T(8,128)(2,1)S(1)} %deconv_halo.1.halo_ref, f32[8,128]{1,0:T(8,128)S(1)} %add.15.stats_ref, f32[4,256]{1,0:T(4,128)S(1)} %pad_maximum_fusion.params_ref, bf16[3,3,256,128]{3,2,1,0:T(8,128)(2,1)S(1)} %copy-done, ...), custom_call_target="tpu_custom_call" | custom-call | flops 5000000000 | bytes 2097152 | tf_op jit(solution)/shard_map/convs/pallas_call | solution.py:339
  (24 shorter events, 0.1 us)
Async XLA Ops:
  0.0 14.6 %collective-permute-start.2 = (bf16[4,4,512,128]{3,2,1,0:T(8,128)(2,1)}, bf16[4,4,512,128]{3,2,1,0:T(8,128)(2,1)S(1)}, u32[]{:S(2)}, u32[]{:S(2)}) collective-permute-start(bf16[4,4,512,128]{3,2,1,0:T(8,128)(2,1)} %param.9), channel_id=1, source_target_pairs={{0,1},{1,0},{2,3},{3,2},{4,5},{5,4},{6,7},{7,6},{8,9},{9,8},{10,11... | collective-permute-start | bytes 6291464 | tf_op jit(solution)/shard_map/ppermute | solution.py:300
  1.5 2.8 %collective-permute-start = (bf16[2,16,512]{2,1,0:T(8,128)(2,1)S(1)}, bf16[2,16,512]{2,1,0:T(8,128)(2,1)S(1)}, u32[]{:S(2)}, u32[]{:S(2)}) collective-permute-start(bf16[2,16,512]{2,1,0:T(8,128)(2,1)S(1)} %get-tuple-element.13), channel_id=1, source_target_pairs={{0,1},{1,0},{2,3},{3,2},{4,5},{5,4},{6,7},{7,6},{8,9},{9,8},{10,11... | collective-permute-start | bytes 98312 | tf_op jit(solution)/shard_map/ppermute | solution.py:310
  1.6 30.5 %collective-permute-start.10 = (bf16[3,3,256,128]{3,2,1,0:T(8,128)(2,1)}, bf16[3,3,256,128]{3,2,1,0:T(8,128)(2,1)S(1)}, u32[]{:S(2)}, u32[]{:S(2)}) collective-permute-start(bf16[3,3,256,128]{3,2,1,0:T(8,128)(2,1)} %own_w2.1), channel_id=1, source_target_pairs={{0,1},{1,0},{2,3},{3,2},{4,5},{5,4},{6,7},{7,6},{8,9},{9,8},{10,11... | collective-permute-start | bytes 1769480 | tf_op jit(solution)/shard_map/ppermute | solution.py:302
  2.1 30.0 %collective-permute-start.9 = (bf16[3,3,256,128]{3,2,1,0:T(8,128)(2,1)}, bf16[3,3,256,128]{3,2,1,0:T(8,128)(2,1)S(1)}, u32[]{:S(2)}, u32[]{:S(2)}) collective-permute-start(bf16[3,3,256,128]{3,2,1,0:T(8,128)(2,1)} %own_w1.1), channel_id=1, source_target_pairs={{0,1},{1,0},{2,3},{3,2},{4,5},{5,4},{6,7},{7,6},{8,9},{9,8},{10,11... | collective-permute-start | bytes 1769480 | tf_op jit(solution)/shard_map/ppermute | solution.py:301
  4.4 8.9 %collective-permute-start.1 = (bf16[1,144,512]{2,1,0:T(8,128)(2,1)S(1)}, bf16[1,144,512]{2,1,0:T(8,128)(2,1)S(1)}, u32[]{:S(2)}, u32[]{:S(2)}) collective-permute-start(bf16[1,144,512]{2,1,0:T(8,128)(2,1)S(1)} %get-tuple-element.20), channel_id=1, source_target_pairs={{2,0},{4,2},{6,4},{8,6},{10,8},{12,10},{14,12},{3,1},{5,3},{7,5},{... | collective-permute-start | bytes 442376 | tf_op jit(solution)/shard_map/ppermute | solution.py:315
  5.7 24.9 %collective-permute-start.3 = (bf16[2,144,512]{2,1,0:T(8,128)(2,1)S(1)}, bf16[2,144,512]{2,1,0:T(8,128)(2,1)S(1)}, u32[]{:S(2)}, u32[]{:S(2)}) collective-permute-start(bf16[2,144,512]{2,1,0:T(8,128)(2,1)S(1)} %constant_dynamic-update-slice_fusion.lines_ref), channel_id=1, source_target_pairs={{0,2},{2,4},{4,6},{6,8},{8,10},{10,12},{12,14},{1,3},{3,5},{5,7},{... | collective-permute-start | bytes 884744 | tf_op jit(solution)/shard_map/ppermute | solution.py:316
  13.3 17.2 %collective-permute-start.4 = (bf16[1,144,512]{2,1,0:T(8,128)(2,1)S(1)}, bf16[1,144,512]{2,1,0:T(8,128)(2,1)S(1)}, u32[]{:S(2)}, u32[]{:S(2)}) collective-permute-start(bf16[1,144,512]{2,1,0:T(8,128)(2,1)S(1)} %get-tuple-element.19), channel_id=1, source_target_pairs={{2,0},{4,2},{6,4},{8,6},{10,8},{12,10},{14,12},{3,1},{5,3},{7,5},{... | collective-permute-start | bytes 442376 | tf_op jit(solution)/shard_map/ppermute | solution.py:317
  14.6 11.3 %copy-start.2 = (f32[256]{0:T(256)S(1)}, f32[256]{0:T(256)}, u32[]{:S(2)}) copy-start(f32[256]{0:T(256)} %param.15) | copy-start | bytes 3076
  14.6 11.3 %copy-start.3 = (f32[256]{0:T(256)S(1)}, f32[256]{0:T(256)}, u32[]{:S(2)}) copy-start(f32[256]{0:T(256)} %param.13) | copy-start | bytes 3076
  14.6 11.3 %copy-start.4 = (f32[256]{0:T(256)S(1)}, f32[256]{0:T(256)}, u32[]{:S(2)}) copy-start(f32[256]{0:T(256)} %param.11) | copy-start | bytes 3076
  14.6 11.3 %copy-start.5 = (f32[256]{0:T(256)S(1)}, f32[256]{0:T(256)}, u32[]{:S(2)}) copy-start(f32[256]{0:T(256)} %param.10) | copy-start | bytes 3076
  16.2 1.2 %collective-permute-start.5 = (f32[8,128]{1,0:T(8,128)S(1)}, f32[8,128]{1,0:T(8,128)S(1)}, u32[]{:S(2)}, u32[]{:S(2)}) collective-permute-start(f32[8,128]{1,0:T(8,128)S(1)} %get-tuple-element.18), channel_id=1, source_target_pairs={{0,1},{1,0},{2,3},{3,2},{4,5},{5,4},{6,7},{7,6},{8,9},{9,8},{10,11... | collective-permute-start | bytes 12296 | tf_op jit(solution)/shard_map/ppermute | solution.py:261
  17.5 5.6 %collective-permute-start.6 = (f32[8,128]{1,0:T(8,128)S(1)}, f32[8,128]{1,0:T(8,128)S(1)}, u32[]{:S(2)}, u32[]{:S(2)}) collective-permute-start(f32[8,128]{1,0:T(8,128)S(1)} %add.12), channel_id=1, source_target_pairs={{0,2},{2,0},{4,6},{6,4},{8,10},{10,8},{12,14},{14,12},{1,3},{3,1},... | collective-permute-start | bytes 12296 | tf_op jit(solution)/shard_map/ppermute | solution.py:261
  23.0 4.4 %collective-permute-start.7 = (f32[8,128]{1,0:T(8,128)S(1)}, f32[8,128]{1,0:T(8,128)S(1)}, u32[]{:S(2)}, u32[]{:S(2)}) collective-permute-start(f32[8,128]{1,0:T(8,128)S(1)} %add.13), channel_id=1, source_target_pairs={{0,4},{2,6},{4,0},{6,2},{8,12},{10,14},{12,8},{14,10},{1,5},{3,7},... | collective-permute-start | bytes 12296 | tf_op jit(solution)/shard_map/ppermute | solution.py:261
  27.5 4.6 %collective-permute-start.8 = (f32[8,128]{1,0:T(8,128)S(1)}, f32[8,128]{1,0:T(8,128)S(1)}, u32[]{:S(2)}, u32[]{:S(2)}) collective-permute-start(f32[8,128]{1,0:T(8,128)S(1)} %add.14), channel_id=1, source_target_pairs={{0,8},{2,10},{4,12},{6,14},{8,0},{10,2},{12,4},{14,6},{1,9},{3,11}... | collective-permute-start | bytes 12296 | tf_op jit(solution)/shard_map/ppermute | solution.py:261
  30.5 1.6 %copy-start = (bf16[3,3,256,128]{3,2,1,0:T(8,128)(2,1)S(1)}, bf16[3,3,256,128]{3,2,1,0:T(8,128)(2,1)}, u32[]{:S(2)}) copy-start(bf16[3,3,256,128]{3,2,1,0:T(8,128)(2,1)} %own_w1.1) | copy-start | bytes 1769476
  30.5 1.6 %copy-start.1 = (bf16[3,3,256,128]{3,2,1,0:T(8,128)(2,1)S(1)}, bf16[3,3,256,128]{3,2,1,0:T(8,128)(2,1)}, u32[]{:S(2)}) copy-start(bf16[3,3,256,128]{3,2,1,0:T(8,128)(2,1)} %own_w2.1) | copy-start | bytes 1769476

commit v5 on v4

--- a/solution.py
+++ b/solution.py
@@ -47,17 +47,13 @@
     copy.wait()
 
 
-def spread_line(out, line):
-    total, cin = line.shape
-    line = jnp.where(edge_mask(total - EDGE), line.astype(jnp.float32), 0.0)
-    out[:, 0:cin] = pltpu.roll(line, total - 1, 0).astype(jnp.bfloat16)
+def spread_line(out, main, edge):
+    width, cin = main.shape
+    line = jnp.concatenate([main.astype(jnp.float32), edge.astype(jnp.float32)], axis=0)
+    line = jnp.where(edge_mask(width), line, 0.0)
+    out[:, 0:cin] = pltpu.roll(line, width + EDGE - 1, 0).astype(jnp.bfloat16)
     out[:, cin : 2 * cin] = line.astype(jnp.bfloat16)
     out[:, 2 * cin : 3 * cin] = pltpu.roll(line, 1, 0).astype(jnp.bfloat16)
-
-
-def own_kernel(lines_ref, xs_ref):
-    for row in range(lines_ref.shape[0]):
-        spread_line(xs_ref.at[row], lines_ref[row])
 
 
 def tap_dot(lines, phase, kr, own_w, other_w):
@@ -75,58 +71,73 @@
     return out.reshape(count, total, weight.shape[-1])
 
 
-def main_kernel(xs_ref, next_ref, own_w, other_w, u_ref, part_ref, xs_next_ref, stats_ref):
-    rows, total, _ = xs_ref.shape
+def add_sums(line, width):
+    values = line[:width].astype(jnp.float32)
+    return jnp.concatenate(
+        [jnp.sum(values, axis=0, keepdims=True), jnp.sum(values * values, axis=0, keepdims=True)], axis=0
+    )
+
+
+def own_kernel(lines_ref, own_w, other_w, xs_ref, u_ref, part_ref, tail_ref, sums_ref):
+    rows, total, _ = lines_ref.shape
     width = total - EDGE
-    cout = u_ref.shape[-1]
-    spread_line(xs_next_ref.at[0], next_ref[0])
-    column = lax.axis_index("fsdp")
-    place = lax.axis_index("rows")
-    first_here = place == 0
-    last_here = place == lax.axis_size("rows") - 1
-    sums = jnp.zeros((1, cout), jnp.float32)
-    squares = jnp.zeros((1, cout), jnp.float32)
+    for row in range(rows):
+        spread_line(xs_ref.at[row], lines_ref[row, :width], lines_ref[row, width:])
+    first_here = lax.axis_index("rows") == 0
+    sums = jnp.zeros((2, u_ref.shape[-1]), jnp.float32)
     for phase in range(2):
         dot = functools.partial(tap_dot, phase=phase, own_w=own_w, other_w=other_w)
         upper = dot(xs_ref[...], kr=1)
         lower = dot(xs_ref[...], kr=3)
         part_ref[phase] = upper[0]
-        even = [upper[row + 1] + lower[row] for row in range(rows - 1)]
-        even.append(lower[rows - 1] + dot(xs_next_ref[...], kr=1)[0])
+        tail_ref[phase, 1] = lower[rows - 1]
+        even = [(upper[row + 1] + lower[row]).astype(jnp.bfloat16) for row in range(rows - 1)]
         upper = dot(xs_ref[...], kr=2)
         lower = dot(xs_ref[1:], kr=0)
-        odd = [upper[row] + lower[row] for row in range(rows - 1)]
-        odd.append(upper[rows - 1] + dot(xs_next_ref[...], kr=0)[0])
-        lines = []
-        for row in range(rows):
-            lines += [odd[row].astype(jnp.bfloat16), even[row].astype(jnp.bfloat16)]
-        for row, line in enumerate(lines):
-            u_ref[row, phase] = line
-        edge_line = jnp.where(first_here, part_ref[phase].astype(jnp.bfloat16).astype(jnp.float32), 0.0)
-        final_line = jnp.where(last_here, 0.0, lines[-1].astype(jnp.float32))
-        for line in lines[:-1] + [edge_line, final_line]:
-            values = line[:width].astype(jnp.float32)
-            sums += jnp.sum(values, axis=0, keepdims=True)
-            squares += jnp.sum(values * values, axis=0, keepdims=True)
-    half = cout // 2
+        tail_ref[phase, 0] = upper[rows - 1]
+        odd = [(upper[row] + lower[row]).astype(jnp.bfloat16) for row in range(rows - 1)]
+        for row in range(rows - 1):
+            u_ref[2 * row, phase] = odd[row]
+            u_ref[2 * row + 1, phase] = even[row]
+            sums += add_sums(odd[row], width) + add_sums(even[row], width)
+        sums += jnp.where(first_here, add_sums(part_ref[phase].astype(jnp.bfloat16), width), 0.0)
+    sums_ref[...] = sums
+
+
+def next_kernel(next_ref, edge_ref, tail_ref, sums_ref, own_w, other_w, u_ref, xs_ref, stats_ref):
+    width = next_ref.shape[1]
+    spread_line(xs_ref.at[0], next_ref[0], edge_ref[0])
+    last_here = lax.axis_index("rows") == lax.axis_size("rows") - 1
+    column = lax.axis_index("fsdp")
+    sums = sums_ref[...]
+    for phase in range(2):
+        dot = functools.partial(tap_dot, phase=phase, own_w=own_w, other_w=other_w)
+        odd = (tail_ref[phase, 0] + dot(xs_ref[...], kr=0)[0]).astype(jnp.bfloat16)
+        even = (tail_ref[phase, 1] + dot(xs_ref[...], kr=1)[0]).astype(jnp.bfloat16)
+        u_ref[0, phase] = odd
+        u_ref[1, phase] = even
+        sums += add_sums(odd, width) + jnp.where(last_here, 0.0, add_sums(even, width))
+    half = sums.shape[1] // 2
     halves = []
-    for row in (sums, squares):
-        own, other = row[:, :half], row[:, half:]
+    for row in range(2):
+        own, other = sums[row : row + 1, :half], sums[row : row + 1, half:]
         halves += [jnp.where(column == 0, own, other), jnp.where(column == 0, other, own)]
     stats_ref[...] = jnp.concatenate(halves + [jnp.zeros((4, half), jnp.float32)], axis=0)
 
 
-def halo_kernel(above_ref, below_ref, xs_ref, xs_next_ref, part_ref, own_w, other_w, u_ref, xs_above, xs_below):
+def halo_kernel(above_ref, next_ref, next_edge_ref, xs_ref, part_ref, own_w, other_w, u_ref, xs_above, xs_below):
+    width = next_ref.shape[1]
     for row in range(HALO):
-        spread_line(xs_above.at[row], above_ref[row])
-    spread_line(xs_below.at[0], below_ref[0])
+        spread_line(xs_above.at[row], above_ref[row, :width], above_ref[row, width:])
+    for row in range(HALO):
+        spread_line(xs_below.at[row], next_ref[row], next_edge_ref[row])
     for phase in range(2):
         dot = functools.partial(tap_dot, phase=phase, own_w=own_w, other_w=other_w)
         outer = dot(xs_above[...], kr=3)
         u_ref[0, phase] = (outer[0] + dot(xs_above[1:2], kr=1)[0]).astype(jnp.bfloat16)
         u_ref[2, phase] = (outer[1] + part_ref[phase]).astype(jnp.bfloat16)
         u_ref[1, phase] = (dot(xs_above[1:2], kr=2)[0] + dot(xs_ref[0:1], kr=0)[0]).astype(jnp.bfloat16)
-        u_ref[3, phase] = (dot(xs_next_ref[...], kr=2)[0] + dot(xs_below[...], kr=0)[0]).astype(jnp.bfloat16)
+        u_ref[3, phase] = (dot(xs_below[0:1], kr=2)[0] + dot(xs_below[1:2], kr=0)[0]).astype(jnp.bfloat16)
 
 
 def group_sum(v, width):
@@ -150,9 +161,10 @@
 
 
 def conv_kernel(
-    count, u_ref, halo_ref, stats_ref, params_ref, own_w1, other_w1, own_w2, other_w2, out_ref, g, act, mixed
+    count, u_ref, u_next_ref, halo_ref, stats_ref, params_ref, own_w1, other_w1, own_w2, other_w2, out_ref, g, act, mixed
 ):
-    main, _, total, cout = u_ref.shape
+    early, _, total, cout = u_ref.shape
+    main = early + u_next_ref.shape[0]
     lines = main + 2 * HALO
     width = total - EDGE
     half = own_w1.shape[-1]
@@ -197,8 +209,10 @@
     def hidden(row):
         if row < 3:
             source = halo_ref.at[row]
+        elif row < 3 + early:
+            source = u_ref.at[row - 3]
         elif row < 3 + main:
-            source = u_ref.at[row - 3]
+            source = u_next_ref.at[row - 3 - early]
         else:
             source = halo_ref.at[3]
         seen = inside(row, HALO)
@@ -256,10 +270,9 @@
     size = lax.axis_size(axis)
     if size & (size - 1):
         return lax.psum(block, axis)
-    step = 1
-    while step < size:
+    steps = [2**n for n in range(size.bit_length() - 1)]
+    for step in steps[1:] + steps[:1]:
         block = block + lax.ppermute(block, axis, [(i, i ^ step) for i in range(size)])
-        step *= 2
     return block
 
 
@@ -297,9 +310,8 @@
 
     in_hbm = functools.partial(pltpu.with_memory_space_constraint, memory_space=pltpu.HBM)
     shape_w = (taps, taps // 2, 2, cin, lanes)
-    other_w = lax.ppermute(deconv_weight, "fsdp", swap).reshape(shape_w)
-    first_other = lax.ppermute(first_weight, "fsdp", swap)
-    second_other = lax.ppermute(second_weight, "fsdp", swap)
+    at_left = lax.axis_index("fsdp") == 0
+    following = lax.ppermute(image, "rows", to_previous)
     near, edges = call(
         cut_kernel,
         [hbm],
@@ -308,37 +320,54 @@
         "cut",
     )(in_hbm(image))
     edge = lax.ppermute(edges, "fsdp", swap)
+    other_w = lax.ppermute(deconv_weight, "fsdp", swap).reshape(shape_w)
+    first_other = lax.ppermute(after(first_weight, edges), "fsdp", swap)
+    second_other = lax.ppermute(after(second_weight, edges), "fsdp", swap)
     (own_w,) = call(near_kernel, [hbm], [(shape_w, bf16)], [pltpu.SemaphoreType.DMA(())], "near_weights")(
         in_hbm(after(deconv_weight, edges).reshape(shape_w))
     )
-    lines = jnp.concatenate([near, edge], axis=1)
-    following = lax.ppermute(lines[:1], "rows", to_previous)
-    above = lax.ppermute(lines, "rows", to_next)
-    below = lax.ppermute(lines[1:], "rows", to_previous)
-    (xs,) = call(own_kernel, [vmem], [((rows, total, 3 * cin), bf16)], [], "own_lines")(lines)
-    u, part, xs_next, stats = call(
-        main_kernel,
-        [vmem] * 4,
-        [((2 * rows, 2, total, cout), bf16), ((2, total, cout), f32), ((1, total, 3 * cin), bf16), ((8, cout // 2), f32)],
+    lines = jnp.concatenate([after(near, own_w), edge], axis=1)
+    u_line = (2, total, cout)
+    xs, u, part, tail, sums = call(
+        own_kernel,
+        [vmem] * 3,
+        [
+            ((rows, total, 3 * cin), bf16),
+            ((2 * rows - 2, *u_line), bf16),
+            (u_line, f32),
+            ((2, *u_line), f32),
+            ((2, cout), f32),
+        ],
         [],
-        "deconv_main",
-        flops=2 * 2 * (2 * rows) * total * 4 * cin * cout,
-    )(xs, following, own_w, other_w)
-
+        "deconv_own",
+        flops=2 * 2 * (2 * rows - 1) * total * 4 * cin * cout,
+    )(lines, own_w, other_w)
+    above = lax.ppermute(after(lines, part), "rows", to_next)
+    next_edge = lax.ppermute(
+        jnp.where(at_left, following[:, width - EDGE :], following[:, :EDGE]), "fsdp", swap
+    )
+    u_next, xs_next, stats = call(
+        next_kernel,
+        [vmem] * 6,
+        [((2, *u_line), bf16), ((1, total, 3 * cin), bf16), ((8, cout // 2), f32)],
+        [],
+        "deconv_next",
+        flops=2 * 2 * total * 4 * cin * cout,
+    )(following, next_edge, tail, sums, own_w, other_w)
     (halo,) = call(
         halo_kernel,
         [vmem] * 7,
-        [((4, 2, total, cout), bf16)],
-        [pltpu.VMEM((HALO, total, 3 * cin), bf16), pltpu.VMEM((1, total, 3 * cin), bf16)],
+        [((4, *u_line), bf16)],
+        [pltpu.VMEM((HALO, total, 3 * cin), bf16), pltpu.VMEM((HALO, total, 3 * cin), bf16)],
         "deconv_halo",
         flops=2 * 2 * 4 * total * 4 * cin * cout,
-    )(above, below, xs, xs_next, part, own_w, other_w)
+    )(above, following, next_edge, xs, part, own_w, other_w)
 
     totals = total_over(total_over(stats, "fsdp"), "rows")
     params = jnp.stack([norm_gain, norm_shift, first_bias, second_bias])
     (out,) = call(
         functools.partial(conv_kernel, count),
-        [vmem] * 8,
+        [vmem] * 9,
         [((2 * rows, 2 * width, cout), bf16)],
         [
             pltpu.VMEM((2 * rows + 2 * HALO, total, 4 * cout), bf16),
@@ -347,7 +376,7 @@
         ],
         "convs",
         flops=5 * 10**9,
-    )(u, halo, totals, params, first_weight, first_other, second_weight, second_other)
+    )(u, u_next, halo, totals, params, first_weight, first_other, second_weight, second_other)
     return out
 
 

time: 37.1 us -> 40.1 us (1.081)
  Pallas kernels: 10.4 us -> 16.9 us
  starting transfers between devices: 18.4 us -> 15.3 us
  waiting for transfers between devices: 7.83 us -> 7.3 us
    pallas_call x4, Pallas kernels: 7.74 us -> 14.3 us  [the longest x1 5.85 us: local(): call(functools.partial(conv_kernel, count), [vmem] * 9, [((2 * rows, 2 *...]
    ppermute x1, waiting for transfers between devices: 2.15 us -> 0.01 us  [local(): edge = lax.ppermute(edges, 'fsdp', swap)]
    ppermute x4, starting transfers between devices: 9.31 us -> 7.36 us  [total_over(): lax.ppermute(block, axis, [(i, i ^ step) for i in range(size)])]
    ppermute x5, starting transfers between devices: 8.54 us -> 7.34 us  [the longest x1 5.46 us: local(): above = lax.ppermute(after(lines, part), 'rows', to_next)]
    ppermute x4, waiting for transfers between devices: 5.24 us -> 6.09 us  [total_over(): lax.ppermute(block, axis, [(i, i ^ step) for i in range(size)])]
    ppermute x5, waiting for transfers between devices: 0.44 us -> 1.2 us  [the longest x1 1.19 us: local(): lax.ppermute(jnp.where(at_left, following[:, width - EDGE:], following[:,...]
  transfers between devices with their start and end apart: 11 -> 11, of which waited for: 6 -> 5; matrix products, arithmetic and copies ran while one was open for 0% -> 0% of each run, Pallas kernels for 15% -> 28%
where the time goes in v5:
time: 40.1 us; the launch traced here: 39.7 us
  Pallas kernels  16.9 us (42%)
  starting transfers between devices  15.3 us (38%)
  waiting for transfers between devices  7.3 us (18%)
    ppermute x4, starting transfers between devices, total_over(): lax.ppermute(block, axis, [(i, i ^ step) for i in range(size)])  7.36 us
    ppermute x4, waiting for transfers between devices, total_over(): lax.ppermute(block, axis, [(i, i ^ step) for i in range(size)])  6.09 us
    pallas_call x1, Pallas kernels, local(): call(functools.partial(conv_kernel, count), [vmem] * 9, [((2 * rows, 2 *...  5.85 us
    ppermute x1, starting transfers between devices, local(): above = lax.ppermute(after(lines, part), 'rows', to_next)  5.46 us
    pallas_call x1, Pallas kernels, local(): call(halo_kernel, [vmem] * 7, [((4, *u_line), bf16)], [pltpu.VMEM((HALO,...  2.92 us
    pallas_call x1, Pallas kernels, local(): call(own_kernel, [vmem] * 3, [((rows, total, 3 * cin), bf16), ((2 * rows...  2.84 us
    pallas_call x1, Pallas kernels, local(): call(next_kernel, [vmem] * 6, [((2, *u_line), bf16), ((1, total, 3 * cin)...  2.64 us
    pallas_call x1, Pallas kernels, local(): call(near_kernel, [hbm], [(shape_w, bf16)], [pltpu.SemaphoreType.DMA(())]...  1.6 us
  transfers between devices with their start and end apart: 11, of which 5 were waited for; matrix products, arithmetic and copies ran while one was open for 0% of the time, Pallas kernels for 28%

profile of v5, /device:TPU:0, one launch (start us, length us, event | category | flops | bytes accessed | tf_op | source)
XLA Modules:
  0.0 39.7 jit_solution(12092744895561574534)
XLA Ops:
  0.0 0.5 %collective-permute-start.1 = (bf16[4,4,512,128]{3,2,1,0:T(8,128)(2,1)}, bf16[4,4,512,128]{3,2,1,0:T(8,128)(2,1)}, u32[]{:S(2)}, u32[]{:S(2)}) collective-permute-start(bf16[4,4,512,128]{3,2,1,0:T(8,128)(2,1)} %param.9), channel_id=1, source_target_pairs={{0,1},{1,0},{2,3},{3,2},{4,5},{5,4},{6,7},{7,6},{8,9},{9,8},{10,11... | collective-permute-start | bytes 6291464 | tf_op jit(solution)/shard_map/ppermute | solution.py:323
  0.5 1.3 %collective-permute-start.2 = (bf16[2,128,512]{2,1,0:T(8,128)(2,1)}, bf16[2,128,512]{2,1,0:T(8,128)(2,1)S(1)}, u32[]{:S(2)}, u32[]{:S(2)}) collective-permute-start(bf16[2,128,512]{2,1,0:T(8,128)(2,1)} %image_ref.1), channel_id=1, source_target_pairs={{2,0},{4,2},{6,4},{8,6},{10,8},{12,10},{14,12},{3,1},{5,3},{7,5},{... | collective-permute-start | bytes 786440 | tf_op jit(solution)/shard_map/ppermute | solution.py:314
  1.7 1.1 %cut.1 = (bf16[2,128,512]{2,1,0:T(8,128)(2,1)S(1)}, bf16[2,16,512]{2,1,0:T(8,128)(2,1)S(1)}) custom-call(bf16[2,128,512]{2,1,0:T(8,128)(2,1)} %image_ref.1), custom_call_target="tpu_custom_call" | custom-call | bytes 2097152 | tf_op jit(solution)/shard_map/cut/pallas_call | solution.py:315
  2.8 0.1 collective-permute-start
  2.9 0.5 %collective-permute-start.10 = (bf16[3,3,256,128]{3,2,1,0:T(8,128)(2,1)}, bf16[3,3,256,128]{3,2,1,0:T(8,128)(2,1)S(1)}, u32[]{:S(2)}, u32[]{:S(2)}) collective-permute-start(bf16[3,3,256,128]{3,2,1,0:T(8,128)(2,1)} %own_w2.1), channel_id=1, source_target_pairs={{0,1},{1,0},{2,3},{3,2},{4,5},{5,4},{6,7},{7,6},{8,9},{9,8},{10,11... | collective-permute-start | bytes 1769480 | tf_op jit(solution)/shard_map/ppermute | solution.py:325
  3.4 0.1 collective-permute-start.9
  3.5 1.6 %near_weights.1.own_w = bf16[4,2,2,512,128]{4,3,2,1,0:T(8,128)(2,1)S(1)} custom-call(bf16[4,2,2,512,128]{4,3,2,1,0:T(8,128)(2,1)} %bitcast.6), custom_call_target="tpu_custom_call" | custom-call | bytes 2097152 | tf_op jit(solution)/shard_map/near_weights/pallas_call | solution.py:326
  5.1 0.0 collective-permute-done
  5.1 2.8 %deconv_own.1 = (bf16[2,144,1536]{2,1,0:T(8,128)(2,1)S(1)}, bf16[2,2,144,256]{3,2,1,0:T(8,128)(2,1)S(1)}, f32[2,144,256]{2,1,0:T(8,128)S(1)}, f32[2,2,144,256]{3,2,1,0:T(8,128)S(1)}, f32[2,256]{1,0:T(2,128)S(1)}) custom-call(bf16[2,144,512]{2,1,0:T(8,128)(2,1)S(1)} %constant_dynamic-update-slice_fusion.lines_ref, ...), custom_call_target="tpu_custom_call" | custom-call | flops 905969664 | bytes 2097152 | tf_op jit(solution)/shard_map/deconv_own/pallas_call | solution.py:331
  8.0 5.5 %collective-permute-start.4 = (bf16[2,144,512]{2,1,0:T(8,128)(2,1)S(1)}, bf16[2,144,512]{2,1,0:T(8,128)(2,1)S(1)}, u32[]{:S(2)}, u32[]{:S(2)}) collective-permute-start(bf16[2,144,512]{2,1,0:T(8,128)(2,1)S(1)} %constant_dynamic-update-slice_fusion.lines_ref), channel_id=1, source_target_pairs={{0,2},{2,4},{4,6},{6,8},{8,10},{10,12},{12,14},{1,3},{3,5},{5,7},{... | collective-permute-start | bytes 884744 | tf_op jit(solution)/shard_map/ppermute | solution.py:345
  13.5 0.1 collective-permute-start.3
  13.6 1.2 %collective-permute-done.3.edge_ref.next_edge_ref = bf16[2,16,512]{2,1,0:T(8,128)(2,1)S(1)} collective-permute-done((bf16[2,16,512]{2,1,0:T(8,128)(2,1)S(1)}, bf16[2,16,512]{2,1,0:T(8,128)(2,1)S(1)}, u32[]{:S(2)}, u32[]{:S(2)}) %collective-permute-start.3) | collective-permute-done | bytes 32800 | tf_op jit(solution)/shard_map/ppermute | solution.py:346
  14.8 2.6 %deconv_next.1 = (bf16[2,2,144,256]{3,2,1,0:T(8,128)(2,1)S(1)}, bf16[1,144,1536]{2,1,0:T(8,128)(2,1)}, f32[8,128]{1,0:T(8,128)S(1)}) custom-call(bf16[2,128,512]{2,1,0:T(8,128)(2,1)S(1)} %collective-permute-done.2.next_ref, bf16[2,16,512]{2,1,0:T(8,128)(2,1)S(1)} %collective-permute-done.3.edge_ref.next_edge_ref, ...), custom_call_target="tpu_custom_call" | custom-call | flops 301989888 | bytes 2097152 | tf_op jit(solution)/shard_map/deconv_next/pallas_call | solution.py:349
  17.4 0.2 collective-permute-start.5
  17.6 1.0 %collective-permute-done.5 = f32[8,128]{1,0:T(8,128)S(1)} collective-permute-done((f32[8,128]{1,0:T(8,128)S(1)}, f32[8,128]{1,0:T(8,128)S(1)}, u32[]{:S(2)}, u32[]{:S(2)}) %collective-permute-start.5) | collective-permute-done | bytes 4128 | tf_op jit(solution)/shard_map/ppermute | solution.py:275
  18.6 1.8 %collective-permute-start.6 = (f32[8,128]{1,0:T(8,128)S(1)}, f32[8,128]{1,0:T(8,128)S(1)}, u32[]{:S(2)}, u32[]{:S(2)}) collective-permute-start(f32[8,128]{1,0:T(8,128)S(1)} %add.12), channel_id=1, source_target_pairs={{0,4},{2,6},{4,0},{6,2},{8,12},{10,14},{12,8},{14,10},{1,5},{3,7},... | collective-permute-start | bytes 12296 | tf_op jit(solution)/shard_map/ppermute | solution.py:275
  20.4 1.8 %collective-permute-done.6 = f32[8,128]{1,0:T(8,128)S(1)} collective-permute-done((f32[8,128]{1,0:T(8,128)S(1)}, f32[8,128]{1,0:T(8,128)S(1)}, u32[]{:S(2)}, u32[]{:S(2)}) %collective-permute-start.6) | collective-permute-done | bytes 4128 | tf_op jit(solution)/shard_map/ppermute | solution.py:275
  22.2 2.8 %collective-permute-start.7 = (f32[8,128]{1,0:T(8,128)S(1)}, f32[8,128]{1,0:T(8,128)S(1)}, u32[]{:S(2)}, u32[]{:S(2)}) collective-permute-start(f32[8,128]{1,0:T(8,128)S(1)} %add.13), channel_id=1, source_target_pairs={{0,8},{2,10},{4,12},{6,14},{8,0},{10,2},{12,4},{14,6},{1,9},{3,11}... | collective-permute-start | bytes 12296 | tf_op jit(solution)/shard_map/ppermute | solution.py:275
  25.0 1.7 %collective-permute-done.7 = f32[8,128]{1,0:T(8,128)S(1)} collective-permute-done((f32[8,128]{1,0:T(8,128)S(1)}, f32[8,128]{1,0:T(8,128)S(1)}, u32[]{:S(2)}, u32[]{:S(2)}) %collective-permute-start.7) | collective-permute-done | bytes 4128 | tf_op jit(solution)/shard_map/ppermute | solution.py:275
  26.7 2.6 %collective-permute-start.8 = (f32[8,128]{1,0:T(8,128)S(1)}, f32[8,128]{1,0:T(8,128)S(1)}, u32[]{:S(2)}, u32[]{:S(2)}) collective-permute-start(f32[8,128]{1,0:T(8,128)S(1)} %add.14), channel_id=1, source_target_pairs={{0,2},{2,0},{4,6},{6,4},{8,10},{10,8},{12,14},{14,12},{1,3},{3,1},... | collective-permute-start | bytes 12296 | tf_op jit(solution)/shard_map/ppermute | solution.py:275
  29.4 1.6 %collective-permute-done.8 = f32[8,128]{1,0:T(8,128)S(1)} collective-permute-done((f32[8,128]{1,0:T(8,128)S(1)}, f32[8,128]{1,0:T(8,128)S(1)}, u32[]{:S(2)}, u32[]{:S(2)}) %collective-permute-start.8) | collective-permute-done | bytes 4128 | tf_op jit(solution)/shard_map/ppermute | solution.py:275
  30.9 0.0 copy-start.1
  30.9 2.9 %deconv_halo.1.halo_ref = bf16[4,2,144,256]{3,2,1,0:T(8,128)(2,1)S(1)} custom-call(bf16[2,144,512]{2,1,0:T(8,128)(2,1)S(1)} %collective-permute-done.4.above_ref, bf16[2,128,512]{2,1,0:T(8,128)(2,1)S(1)} %collective-permute-done.2.next_ref, bf16[2,16,512]{2,1,0:T(8,128)(2,1)S(1)} %collective-permute-done.3.edge_ref.next_edge_ref, ...), custom_call_target="tpu_custom_call" | custom-call | flops 1207959552 | bytes 2097152 | tf_op jit(solution)/shard_map/deconv_halo/pallas_call | solution.py:357
  33.9 5.8 %convs.1 = bf16[4,256,256]{2,1,0:T(8,128)(2,1)} custom-call(bf16[2,2,144,256]{3,2,1,0:T(8,128)(2,1)S(1)} %get-tuple-element.23.u_ref, bf16[2,2,144,256]{3,2,1,0:T(8,128)(2,1)S(1)} %get-tuple-element.26.u_next_ref, bf16[4,2,144,256]{3,2,1,0:T(8,128)(2,1)S(1)} %deconv_halo.1.halo_ref, f32[8,128]{1,0:T(8,128)S(1)} %add.15.stats_ref, ...), custom_call_target="tpu_custom_call" | custom-call | flops 5000000000 | bytes 2097152 | tf_op jit(solution)/shard_map/convs/pallas_call | solution.py:368
  (24 shorter events, 0.1 us)
Async XLA Ops:
  0.0 5.1 %collective-permute-start.1 = (bf16[4,4,512,128]{3,2,1,0:T(8,128)(2,1)}, bf16[4,4,512,128]{3,2,1,0:T(8,128)(2,1)}, u32[]{:S(2)}, u32[]{:S(2)}) collective-permute-start(bf16[4,4,512,128]{3,2,1,0:T(8,128)(2,1)} %param.9), channel_id=1, source_target_pairs={{0,1},{1,0},{2,3},{3,2},{4,5},{5,4},{6,7},{7,6},{8,9},{9,8},{10,11... | collective-permute-start | bytes 6291464 | tf_op jit(solution)/shard_map/ppermute | solution.py:323
  0.5 13.0 %collective-permute-start.2 = (bf16[2,128,512]{2,1,0:T(8,128)(2,1)}, bf16[2,128,512]{2,1,0:T(8,128)(2,1)S(1)}, u32[]{:S(2)}, u32[]{:S(2)}) collective-permute-start(bf16[2,128,512]{2,1,0:T(8,128)(2,1)} %image_ref.1), channel_id=1, source_target_pairs={{2,0},{4,2},{6,4},{8,6},{10,8},{12,10},{14,12},{3,1},{5,3},{7,5},{... | collective-permute-start | bytes 786440 | tf_op jit(solution)/shard_map/ppermute | solution.py:314
  2.8 2.3 %collective-permute-start = (bf16[2,16,512]{2,1,0:T(8,128)(2,1)S(1)}, bf16[2,16,512]{2,1,0:T(8,128)(2,1)S(1)}, u32[]{:S(2)}, u32[]{:S(2)}) collective-permute-start(bf16[2,16,512]{2,1,0:T(8,128)(2,1)S(1)} %get-tuple-element.20), channel_id=1, source_target_pairs={{0,1},{1,0},{2,3},{3,2},{4,5},{5,4},{6,7},{7,6},{8,9},{9,8},{10,11... | collective-permute-start | bytes 98312 | tf_op jit(solution)/shard_map/ppermute | solution.py:322
  2.9 30.9 %collective-permute-start.10 = (bf16[3,3,256,128]{3,2,1,0:T(8,128)(2,1)}, bf16[3,3,256,128]{3,2,1,0:T(8,128)(2,1)S(1)}, u32[]{:S(2)}, u32[]{:S(2)}) collective-permute-start(bf16[3,3,256,128]{3,2,1,0:T(8,128)(2,1)} %own_w2.1), channel_id=1, source_target_pairs={{0,1},{1,0},{2,3},{3,2},{4,5},{5,4},{6,7},{7,6},{8,9},{9,8},{10,11... | collective-permute-start | bytes 1769480 | tf_op jit(solution)/shard_map/ppermute | solution.py:325
  3.4 30.5 %collective-permute-start.9 = (bf16[3,3,256,128]{3,2,1,0:T(8,128)(2,1)}, bf16[3,3,256,128]{3,2,1,0:T(8,128)(2,1)}, u32[]{:S(2)}, u32[]{:S(2)}) collective-permute-start(bf16[3,3,256,128]{3,2,1,0:T(8,128)(2,1)} %own_w1.1), channel_id=1, source_target_pairs={{0,1},{1,0},{2,3},{3,2},{4,5},{5,4},{6,7},{7,6},{8,9},{9,8},{10,11... | collective-permute-start | bytes 1769480 | tf_op jit(solution)/shard_map/ppermute | solution.py:324
  8.0 22.9 %collective-permute-start.4 = (bf16[2,144,512]{2,1,0:T(8,128)(2,1)S(1)}, bf16[2,144,512]{2,1,0:T(8,128)(2,1)S(1)}, u32[]{:S(2)}, u32[]{:S(2)}) collective-permute-start(bf16[2,144,512]{2,1,0:T(8,128)(2,1)S(1)} %constant_dynamic-update-slice_fusion.lines_ref), channel_id=1, source_target_pairs={{0,2},{2,4},{4,6},{6,8},{8,10},{10,12},{12,14},{1,3},{3,5},{5,7},{... | collective-permute-start | bytes 884744 | tf_op jit(solution)/shard_map/ppermute | solution.py:345
  13.5 1.3 %collective-permute-start.3 = (bf16[2,16,512]{2,1,0:T(8,128)(2,1)S(1)}, bf16[2,16,512]{2,1,0:T(8,128)(2,1)S(1)}, u32[]{:S(2)}, u32[]{:S(2)}) collective-permute-start(bf16[2,16,512]{2,1,0:T(8,128)(2,1)S(1)} %slice_select_fusion), channel_id=1, source_target_pairs={{0,1},{1,0},{2,3},{3,2},{4,5},{5,4},{6,7},{7,6},{8,9},{9,8},{10,11... | collective-permute-start | bytes 98312 | tf_op jit(solution)/shard_map/ppermute | solution.py:346
  14.7 14.6 %copy-start.2 = (f32[256]{0:T(256)S(1)}, f32[256]{0:T(256)}, u32[]{:S(2)}) copy-start(f32[256]{0:T(256)} %param.15) | copy-start | bytes 3076
  14.7 14.6 %copy-start.3 = (f32[256]{0:T(256)S(1)}, f32[256]{0:T(256)}, u32[]{:S(2)}) copy-start(f32[256]{0:T(256)} %param.13) | copy-start | bytes 3076
  14.8 14.6 %copy-start.4 = (f32[256]{0:T(256)S(1)}, f32[256]{0:T(256)}, u32[]{:S(2)}) copy-start(f32[256]{0:T(256)} %param.11) | copy-start | bytes 3076
  14.8 14.6 %copy-start.5 = (f32[256]{0:T(256)S(1)}, f32[256]{0:T(256)}, u32[]{:S(2)}) copy-start(f32[256]{0:T(256)} %param.10) | copy-start | bytes 3076
  17.4 1.2 %collective-permute-start.5 = (f32[8,128]{1,0:T(8,128)S(1)}, f32[8,128]{1,0:T(8,128)S(1)}, u32[]{:S(2)}, u32[]{:S(2)}) collective-permute-start(f32[8,128]{1,0:T(8,128)S(1)} %get-tuple-element.30), channel_id=1, source_target_pairs={{0,1},{1,0},{2,3},{3,2},{4,5},{5,4},{6,7},{7,6},{8,9},{9,8},{10,11... | collective-permute-start | bytes 12296 | tf_op jit(solution)/shard_map/ppermute | solution.py:275
  18.6 3.6 %collective-permute-start.6 = (f32[8,128]{1,0:T(8,128)S(1)}, f32[8,128]{1,0:T(8,128)S(1)}, u32[]{:S(2)}, u32[]{:S(2)}) collective-permute-start(f32[8,128]{1,0:T(8,128)S(1)} %add.12), channel_id=1, source_target_pairs={{0,4},{2,6},{4,0},{6,2},{8,12},{10,14},{12,8},{14,10},{1,5},{3,7},... | collective-permute-start | bytes 12296 | tf_op jit(solution)/shard_map/ppermute | solution.py:275
  22.2 4.5 %collective-permute-start.7 = (f32[8,128]{1,0:T(8,128)S(1)}, f32[8,128]{1,0:T(8,128)S(1)}, u32[]{:S(2)}, u32[]{:S(2)}) collective-permute-start(f32[8,128]{1,0:T(8,128)S(1)} %add.13), channel_id=1, source_target_pairs={{0,8},{2,10},{4,12},{6,14},{8,0},{10,2},{12,4},{14,6},{1,9},{3,11}... | collective-permute-start | bytes 12296 | tf_op jit(solution)/shard_map/ppermute | solution.py:275
  26.7 4.2 %collective-permute-start.8 = (f32[8,128]{1,0:T(8,128)S(1)}, f32[8,128]{1,0:T(8,128)S(1)}, u32[]{:S(2)}, u32[]{:S(2)}) collective-permute-start(f32[8,128]{1,0:T(8,128)S(1)} %add.14), channel_id=1, source_target_pairs={{0,2},{2,0},{4,6},{6,4},{8,10},{10,8},{12,14},{14,12},{1,3},{3,1},... | collective-permute-start | bytes 12296 | tf_op jit(solution)/shard_map/ppermute | solution.py:275
  30.9 3.0 %copy-start = (bf16[3,3,256,128]{3,2,1,0:T(8,128)(2,1)S(1)}, bf16[3,3,256,128]{3,2,1,0:T(8,128)(2,1)}, u32[]{:S(2)}) copy-start(bf16[3,3,256,128]{3,2,1,0:T(8,128)(2,1)} %own_w1.1) | copy-start | bytes 1769476
  30.9 3.0 %copy-start.1 = (bf16[3,3,256,128]{3,2,1,0:T(8,128)(2,1)S(1)}, bf16[3,3,256,128]{3,2,1,0:T(8,128)(2,1)}, u32[]{:S(2)}) copy-start(bf16[3,3,256,128]{3,2,1,0:T(8,128)(2,1)} %own_w2.1) | copy-start | bytes 1769476

commit v6 on v5

--- a/solution.py
+++ b/solution.py
@@ -104,7 +104,7 @@
     sums_ref[...] = sums
 
 
-def next_kernel(next_ref, edge_ref, tail_ref, sums_ref, own_w, other_w, u_ref, xs_ref, stats_ref):
+def next_kernel(next_ref, edge_ref, tail_ref, sums_ref, own_w, other_w, u_ref, stats_ref, xs_ref):
     width = next_ref.shape[1]
     spread_line(xs_ref.at[0], next_ref[0], edge_ref[0])
     last_here = lax.axis_index("rows") == lax.axis_size("rows") - 1
@@ -185,7 +185,7 @@
             axis=1,
         )
 
-    block = stats_ref[...]
+    block = jnp.sum(stats_ref[...], axis=0)
     width_group = cout // NORM_GROUPS
     sums = jnp.concatenate([block[0:1], block[1:2]], axis=1)
     squares = jnp.concatenate([block[2:3], block[3:4]], axis=1)
@@ -266,16 +266,6 @@
             second(start - chunk)
 
 
-def total_over(block, axis):
-    size = lax.axis_size(axis)
-    if size & (size - 1):
-        return lax.psum(block, axis)
-    steps = [2**n for n in range(size.bit_length() - 1)]
-    for step in steps[1:] + steps[:1]:
-        block = block + lax.ppermute(block, axis, [(i, i ^ step) for i in range(size)])
-    return block
-
-
 def after(value, *others):
     return lax.optimization_barrier((value, *others))[0]
 
@@ -309,6 +299,7 @@
         )
 
     in_hbm = functools.partial(pltpu.with_memory_space_constraint, memory_space=pltpu.HBM)
+    in_vmem = functools.partial(pltpu.with_memory_space_constraint, memory_space=pltpu.VMEM)
     shape_w = (taps, taps // 2, 2, cin, lanes)
     at_left = lax.axis_index("fsdp") == 0
     following = lax.ppermute(image, "rows", to_previous)
@@ -341,19 +332,19 @@
         [],
         "deconv_own",
         flops=2 * 2 * (2 * rows - 1) * total * 4 * cin * cout,
-    )(lines, own_w, other_w)
+    )(lines, own_w, in_vmem(other_w))
     above = lax.ppermute(after(lines, part), "rows", to_next)
     next_edge = lax.ppermute(
         jnp.where(at_left, following[:, width - EDGE :], following[:, :EDGE]), "fsdp", swap
     )
-    u_next, xs_next, stats = call(
+    u_next, stats = call(
         next_kernel,
         [vmem] * 6,
-        [((2, *u_line), bf16), ((1, total, 3 * cin), bf16), ((8, cout // 2), f32)],
-        [],
+        [((2, *u_line), bf16), ((8, cout // 2), f32)],
+        [pltpu.VMEM((1, total, 3 * cin), bf16)],
         "deconv_next",
         flops=2 * 2 * total * 4 * cin * cout,
-    )(following, next_edge, tail, sums, own_w, other_w)
+    )(following, next_edge, tail, sums, own_w, in_vmem(other_w))
     (halo,) = call(
         halo_kernel,
         [vmem] * 7,
@@ -361,9 +352,10 @@
         [pltpu.VMEM((HALO, total, 3 * cin), bf16), pltpu.VMEM((HALO, total, 3 * cin), bf16)],
         "deconv_halo",
         flops=2 * 2 * 4 * total * 4 * cin * cout,
-    )(above, following, next_edge, xs, part, own_w, other_w)
-
-    totals = total_over(total_over(stats, "fsdp"), "rows")
+    )(above, following, next_edge, xs, part, own_w, in_vmem(other_w))
+
+    stats = stats + lax.ppermute(stats, "fsdp", swap)
+    stats = lax.all_to_all(jnp.broadcast_to(stats, (n_rows, *stats.shape)), "rows", split_axis=0, concat_axis=0)
     params = jnp.stack([norm_gain, norm_shift, first_bias, second_bias])
     (out,) = call(
         functools.partial(conv_kernel, count),
@@ -376,7 +368,7 @@
         ],
         "convs",
         flops=5 * 10**9,
-    )(u, u_next, halo, totals, params, first_weight, first_other, second_weight, second_other)
+    )(u, u_next, halo, stats, params, first_weight, in_vmem(first_other), second_weight, in_vmem(second_other))
     return out
 
 

time: 40.1 us -> 44 us (1.097)
  local copies, waits for them, and re-layouts: 0.05 us -> 9.05 us
  waiting for transfers between devices: 7.3 us -> 3.44 us
  starting transfers between devices: 15.3 us -> 14 us
    unnamed x13 -> x33, local copies, waits for them, and re-layouts: 0.04 us -> 8.42 us
    ppermute x4 -> x1, starting transfers between devices: 7.36 us -> 0.17 us  [local(): stats = stats + lax.ppermute(stats, 'fsdp', swap)]
    all_to_all x0 -> x1, starting transfers between devices: none -> 5.25 us  [local(): lax.all_to_all(jnp.broadcast_to(stats, (n_rows, *stats.shape)), 'rows', s...]
    ppermute x4 -> x1, waiting for transfers between devices: 6.09 us -> 0.97 us  [local(): stats = stats + lax.ppermute(stats, 'fsdp', swap)]
    all_to_all x0 -> x1, waiting for transfers between devices: none -> 1.26 us  [local(): lax.all_to_all(jnp.broadcast_to(stats, (n_rows, *stats.shape)), 'rows', s...]
    ppermute x1, starting transfers between devices: 5.46 us -> 6.15 us  [local(): above = lax.ppermute(after(lines, part), 'rows', to_next)]
    broadcast_in_dim x0 -> x1, local copies, waits for them, and re-layouts: none -> 0.62 us  [local(): jnp.broadcast_to(stats, (n_rows, *stats.shape))]
    pallas_call x1, Pallas kernels: 2.64 us -> 2.16 us  [local(): call(next_kernel, [vmem] * 6, [((2, *u_line), bf16), ((8, cout // 2), f32...]
  transfers between devices with their start and end apart: 11 -> 9, of which waited for: 5 -> 3; matrix products, arithmetic and copies ran while one was open for 0% -> 2% of each run, Pallas kernels for 28% -> 24%
where the time goes in v6:
time: 44 us; the launch traced here: 43.3 us
  Pallas kernels  16.6 us (38%)
  starting transfers between devices  14 us (32%)
  local copies, waits for them, and re-layouts  9.05 us (21%)
  waiting for transfers between devices  3.44 us (8%)
    unnamed x33, local copies, waits for them, and re-layouts  8.42 us
    ppermute x1, starting transfers between devices, local(): above = lax.ppermute(after(lines, part), 'rows', to_next)  6.15 us
    pallas_call x1, Pallas kernels, local(): call(functools.partial(conv_kernel, count), [vmem] * 9, [((2 * rows, 2 *...  6.01 us
    all_to_all x1, starting transfers between devices, local(): lax.all_to_all(jnp.broadcast_to(stats, (n_rows, *stats.shape)), 'rows', s...  5.25 us
    pallas_call x1, Pallas kernels, local(): call(halo_kernel, [vmem] * 7, [((4, *u_line), bf16)], [pltpu.VMEM((HALO,...  2.94 us
    pallas_call x1, Pallas kernels, local(): call(own_kernel, [vmem] * 3, [((rows, total, 3 * cin), bf16), ((2 * rows...  2.84 us
    pallas_call x1, Pallas kernels, local(): call(next_kernel, [vmem] * 6, [((2, *u_line), bf16), ((8, cout // 2), f32...  2.16 us
    pallas_call x1, Pallas kernels, local(): call(near_kernel, [hbm], [(shape_w, bf16)], [pltpu.SemaphoreType.DMA(())]...  1.6 us
  transfers between devices with their start and end apart: 9, of which 3 were waited for; matrix products, arithmetic and copies ran while one was open for 2% of the time, Pallas kernels for 24%

profile of v6, /device:TPU:0, one launch (start us, length us, event | category | flops | bytes accessed | tf_op | source)
XLA Modules:
  0.0 43.3 jit_solution(14457436841083209277)
XLA Ops:
  0.0 0.5 %collective-permute-start.1 = (bf16[4,4,512,128]{3,2,1,0:T(8,128)(2,1)}, bf16[4,4,512,128]{3,2,1,0:T(8,128)(2,1)}, u32[]{:S(2)}, u32[]{:S(2)}) collective-permute-start(bf16[4,4,512,128]{3,2,1,0:T(8,128)(2,1)} %param.9), channel_id=1, source_target_pairs={{0,1},{1,0},{2,3},{3,2},{4,5},{5,4},{6,7},{7,6},{8,9},{9,8},{10,11... | collective-permute-start | bytes 6291464 | tf_op jit(solution)/shard_map/ppermute | solution.py:314
  0.5 1.3 %collective-permute-start.2 = (bf16[2,128,512]{2,1,0:T(8,128)(2,1)}, bf16[2,128,512]{2,1,0:T(8,128)(2,1)S(1)}, u32[]{:S(2)}, u32[]{:S(2)}) collective-permute-start(bf16[2,128,512]{2,1,0:T(8,128)(2,1)} %image_ref.1), channel_id=1, source_target_pairs={{2,0},{4,2},{6,4},{8,6},{10,8},{12,10},{14,12},{3,1},{5,3},{7,5},{... | collective-permute-start | bytes 786440 | tf_op jit(solution)/shard_map/ppermute | solution.py:305
  1.7 1.1 %cut.1 = (bf16[2,128,512]{2,1,0:T(8,128)(2,1)S(1)}, bf16[2,16,512]{2,1,0:T(8,128)(2,1)S(1)}) custom-call(bf16[2,128,512]{2,1,0:T(8,128)(2,1)} %image_ref.1), custom_call_target="tpu_custom_call" | custom-call | bytes 2097152 | tf_op jit(solution)/shard_map/cut/pallas_call | solution.py:306
  2.9 0.5 %collective-permute-start.6 = (bf16[3,3,256,128]{3,2,1,0:T(8,128)(2,1)}, bf16[3,3,256,128]{3,2,1,0:T(8,128)(2,1)}, u32[]{:S(2)}, u32[]{:S(2)}) collective-permute-start(bf16[3,3,256,128]{3,2,1,0:T(8,128)(2,1)} %own_w1.1), channel_id=1, source_target_pairs={{0,1},{1,0},{2,3},{3,2},{4,5},{5,4},{6,7},{7,6},{8,9},{9,8},{10,11... | collective-permute-start | bytes 1769480 | tf_op jit(solution)/shard_map/ppermute | solution.py:315
  3.5 1.6 %near_weights.1.own_w = bf16[4,2,2,512,128]{4,3,2,1,0:T(8,128)(2,1)S(1)} custom-call(bf16[4,2,2,512,128]{4,3,2,1,0:T(8,128)(2,1)} %bitcast.6), custom_call_target="tpu_custom_call" | custom-call | bytes 2097152 | tf_op jit(solution)/shard_map/near_weights/pallas_call | solution.py:317
  5.1 2.8 %deconv_own.1 = (bf16[2,144,1536]{2,1,0:T(8,128)(2,1)S(1)}, bf16[2,2,144,256]{3,2,1,0:T(8,128)(2,1)S(1)}, f32[2,144,256]{2,1,0:T(8,128)S(1)}, f32[2,2,144,256]{3,2,1,0:T(8,128)S(1)}, f32[2,256]{1,0:T(2,128)S(1)}) custom-call(bf16[2,144,512]{2,1,0:T(8,128)(2,1)S(1)} %constant_dynamic-update-slice_fusion.lines_ref, ...), custom_call_target="tpu_custom_call" | custom-call | flops 905969664 | bytes 2097152 | tf_op jit(solution)/shard_map/deconv_own/pallas_call | solution.py:322
  8.0 6.2 %collective-permute-start.4 = (bf16[2,144,512]{2,1,0:T(8,128)(2,1)S(1)}, bf16[2,144,512]{2,1,0:T(8,128)(2,1)}, u32[]{:S(2)}, u32[]{:S(2)}) collective-permute-start(bf16[2,144,512]{2,1,0:T(8,128)(2,1)S(1)} %constant_dynamic-update-slice_fusion.lines_ref), channel_id=1, source_target_pairs={{0,2},{2,4},{4,6},{6,8},{8,10},{10,12},{12,14},{1,3},{3,5},{5,7},{... | collective-permute-start | bytes 884744 | tf_op jit(solution)/shard_map/ppermute | solution.py:336
  14.2 1.2 %collective-permute-done.3.edge_ref.next_edge_ref = bf16[2,16,512]{2,1,0:T(8,128)(2,1)S(1)} collective-permute-done((bf16[2,16,512]{2,1,0:T(8,128)(2,1)S(1)}, bf16[2,16,512]{2,1,0:T(8,128)(2,1)S(1)}, u32[]{:S(2)}, u32[]{:S(2)}) %collective-permute-start.3) | collective-permute-done | bytes 32800 | tf_op jit(solution)/shard_map/ppermute | solution.py:337
  15.5 2.2 %deconv_next.1 = (bf16[2,2,144,256]{3,2,1,0:T(8,128)(2,1)S(1)}, f32[8,128]{1,0:T(8,128)S(1)}) custom-call(bf16[2,128,512]{2,1,0:T(8,128)(2,1)S(1)} %collective-permute-done.2.next_ref, bf16[2,16,512]{2,1,0:T(8,128)(2,1)S(1)} %collective-permute-done.3.edge_ref.next_edge_ref, f32[2,2,144,256]{3,2,1,0:T(8,128)S(1)} %get-tuple-element.24.tail_ref, ...), custom_call_target="tpu_custom_call" | custom-call | flops 301989888 | bytes 2097152 | tf_op jit(solution)/shard_map/deconv_next/pallas_call | solution.py:340
  17.7 0.7 %copy-done.10 = bf16[2,2,144,256]{3,2,1,0:T(8,128)(2,1)} copy-done((bf16[2,2,144,256]{3,2,1,0:T(8,128)(2,1)}, bf16[2,2,144,256]{3,2,1,0:T(8,128)(2,1)S(1)}, u32[]{:S(2)}) %copy-start.10) | copy-done | bytes 294936
  18.6 1.0 %collective-permute-done.5 = f32[8,128]{1,0:T(8,128)S(1)} collective-permute-done((f32[8,128]{1,0:T(8,128)S(1)}, f32[8,128]{1,0:T(8,128)S(1)}, u32[]{:S(2)}, u32[]{:S(2)}) %collective-permute-start.5) | collective-permute-done | bytes 4128 | tf_op jit(solution)/shard_map/ppermute | solution.py:357
  19.5 0.6 %broadcast_in_dim.3 = f32[8,8,128]{2,1,0:T(8,128)} broadcast(f32[8,128]{1,0:T(8,128)S(1)} %add.3), dimensions={1,2} | broadcast | bytes 36864 | tf_op jit(solution)/shard_map/broadcast_in_dim | solution.py:358
  20.2 5.3 %all-to-all-start = ((f32[8,8,128]{2,1,0:T(8,128)}), f32[8,8,128]{2,1,0:T(8,128)}, u32[]{:S(2)}, u32[]{:S(2)}) async-start(f32[8,8,128]{2,1,0:T(8,128)} %broadcast_in_dim.3), calls=%async_computation | async-start | bytes 65536 | tf_op jit(solution)/shard_map/all_to_all | solution.py:358
  25.4 1.0 %copy-done.3 = f32[2,144,256]{2,1,0:T(8,128)S(1)} copy-done((f32[2,144,256]{2,1,0:T(8,128)S(1)}, f32[2,144,256]{2,1,0:T(8,128)}, u32[]{:S(2)}) %copy-start.3) | copy-done | bytes 294936
  26.4 0.8 %copy-done.5 = bf16[2,16,512]{2,1,0:T(8,128)(2,1)S(1)} copy-done((bf16[2,16,512]{2,1,0:T(8,128)(2,1)S(1)}, bf16[2,16,512]{2,1,0:T(8,128)(2,1)}, u32[]{:S(2)}) %copy-start.5) | copy-done | bytes 32792
  27.1 2.9 %deconv_halo.1.halo_ref = bf16[4,2,144,256]{3,2,1,0:T(8,128)(2,1)S(1)} custom-call(bf16[2,144,512]{2,1,0:T(8,128)(2,1)} %collective-permute-done.4.above_ref, bf16[2,128,512]{2,1,0:T(8,128)(2,1)S(1)} %collective-permute-done.2.next_ref, bf16[2,16,512]{2,1,0:T(8,128)(2,1)S(1)} %copy-done.5, bf16[2,144,1536]{2,1,0:T(8,128)(2,1)S(1)} %get-tuple-element.29.xs_ref, ...), custom_call_target="tpu_custom_call" | custom-call | flops 1207959552 | bytes 2097152 | tf_op jit(solution)/shard_map/deconv_halo/pallas_call | solution.py:348
  30.1 0.8 %copy-done = bf16[4,2,144,256]{3,2,1,0:T(8,128)(2,1)} copy-done((bf16[4,2,144,256]{3,2,1,0:T(8,128)(2,1)}, bf16[4,2,144,256]{3,2,1,0:T(8,128)(2,1)S(1)}, u32[]{:S(2)}) %copy-start) | copy-done | bytes 589848
  30.9 1.3 %all-to-all-done.stats_ref = f32[8,8,128]{2,1,0:T(8,128)} async-done(((f32[8,8,128]{2,1,0:T(8,128)}), f32[8,8,128]{2,1,0:T(8,128)}, u32[]{:S(2)}, u32[]{:S(2)}) %all-to-all-start) | async-done | bytes 32800 | tf_op jit(solution)/shard_map/all_to_all | solution.py:358
  32.2 1.1 %copy-done.1 = bf16[4,2,144,256]{3,2,1,0:T(8,128)(2,1)S(1)} copy-done((bf16[4,2,144,256]{3,2,1,0:T(8,128)(2,1)S(1)}, bf16[4,2,144,256]{3,2,1,0:T(8,128)(2,1)}, u32[]{:S(2)}) %copy-start.1) | copy-done | bytes 589848
  33.3 1.1 %copy-done.6 = bf16[3,3,256,128]{3,2,1,0:T(8,128)(2,1)S(1)} copy-done((bf16[3,3,256,128]{3,2,1,0:T(8,128)(2,1)S(1)}, bf16[3,3,256,128]{3,2,1,0:T(8,128)(2,1)}, u32[]{:S(2)}) %copy-start.6) | copy-done | bytes 589848
  34.3 1.1 %copy-done.7 = bf16[3,3,256,128]{3,2,1,0:T(8,128)(2,1)S(1)} copy-done((bf16[3,3,256,128]{3,2,1,0:T(8,128)(2,1)S(1)}, bf16[3,3,256,128]{3,2,1,0:T(8,128)(2,1)}, u32[]{:S(2)}) %copy-start.7) | copy-done | bytes 589848
  35.4 1.0 %copy-done.9 = bf16[2,2,144,256]{3,2,1,0:T(8,128)(2,1)S(1)} copy-done((bf16[2,2,144,256]{3,2,1,0:T(8,128)(2,1)S(1)}, bf16[2,2,144,256]{3,2,1,0:T(8,128)(2,1)}, u32[]{:S(2)}) %copy-start.9) | copy-done | bytes 294936
  36.4 1.0 %copy-done.11 = bf16[2,2,144,256]{3,2,1,0:T(8,128)(2,1)S(1)} copy-done((bf16[2,2,144,256]{3,2,1,0:T(8,128)(2,1)S(1)}, bf16[2,2,144,256]{3,2,1,0:T(8,128)(2,1)}, u32[]{:S(2)}) %copy-start.11) | copy-done | bytes 294936
  37.3 6.0 %convs.1 = bf16[4,256,256]{2,1,0:T(8,128)(2,1)} custom-call(bf16[2,2,144,256]{3,2,1,0:T(8,128)(2,1)S(1)} %copy-done.9, bf16[2,2,144,256]{3,2,1,0:T(8,128)(2,1)S(1)} %copy-done.11, bf16[4,2,144,256]{3,2,1,0:T(8,128)(2,1)S(1)} %copy-done.1, f32[8,8,128]{2,1,0:T(8,128)} %all-to-all-done.stats_ref, f32[4,256]{1,0:T(4,128)S(1)} %pad_maximum_fusion.params_ref, ...), custom_call_target="tpu_custom_call" | custom-call | flops 5000000000 | bytes 2097152 | tf_op jit(solution)/shard_map/convs/pallas_call | solution.py:360
  (38 shorter events, 0.5 us)
Async XLA Ops:
  0.0 5.1 %collective-permute-start.1 = (bf16[4,4,512,128]{3,2,1,0:T(8,128)(2,1)}, bf16[4,4,512,128]{3,2,1,0:T(8,128)(2,1)}, u32[]{:S(2)}, u32[]{:S(2)}) collective-permute-start(bf16[4,4,512,128]{3,2,1,0:T(8,128)(2,1)} %param.9), channel_id=1, source_target_pairs={{0,1},{1,0},{2,3},{3,2},{4,5},{5,4},{6,7},{7,6},{8,9},{9,8},{10,11... | collective-permute-start | bytes 6291464 | tf_op jit(solution)/shard_map/ppermute | solution.py:314
  0.5 13.7 %collective-permute-start.2 = (bf16[2,128,512]{2,1,0:T(8,128)(2,1)}, bf16[2,128,512]{2,1,0:T(8,128)(2,1)S(1)}, u32[]{:S(2)}, u32[]{:S(2)}) collective-permute-start(bf16[2,128,512]{2,1,0:T(8,128)(2,1)} %image_ref.1), channel_id=1, source_target_pairs={{2,0},{4,2},{6,4},{8,6},{10,8},{12,10},{14,12},{3,1},{5,3},{7,5},{... | collective-permute-start | bytes 786440 | tf_op jit(solution)/shard_map/ppermute | solution.py:305
  2.8 2.3 %collective-permute-start = (bf16[2,16,512]{2,1,0:T(8,128)(2,1)S(1)}, bf16[2,16,512]{2,1,0:T(8,128)(2,1)S(1)}, u32[]{:S(2)}, u32[]{:S(2)}) collective-permute-start(bf16[2,16,512]{2,1,0:T(8,128)(2,1)S(1)} %get-tuple-element.20), channel_id=1, source_target_pairs={{0,1},{1,0},{2,3},{3,2},{4,5},{5,4},{6,7},{7,6},{8,9},{9,8},{10,11... | collective-permute-start | bytes 98312 | tf_op jit(solution)/shard_map/ppermute | solution.py:313
  2.9 28.0 %collective-permute-start.6 = (bf16[3,3,256,128]{3,2,1,0:T(8,128)(2,1)}, bf16[3,3,256,128]{3,2,1,0:T(8,128)(2,1)}, u32[]{:S(2)}, u32[]{:S(2)}) collective-permute-start(bf16[3,3,256,128]{3,2,1,0:T(8,128)(2,1)} %own_w1.1), channel_id=1, source_target_pairs={{0,1},{1,0},{2,3},{3,2},{4,5},{5,4},{6,7},{7,6},{8,9},{9,8},{10,11... | collective-permute-start | bytes 1769480 | tf_op jit(solution)/shard_map/ppermute | solution.py:315
  3.4 27.6 %collective-permute-start.7 = (bf16[3,3,256,128]{3,2,1,0:T(8,128)(2,1)}, bf16[3,3,256,128]{3,2,1,0:T(8,128)(2,1)}, u32[]{:S(2)}, u32[]{:S(2)}) collective-permute-start(bf16[3,3,256,128]{3,2,1,0:T(8,128)(2,1)} %own_w2.1), channel_id=1, source_target_pairs={{0,1},{1,0},{2,3},{3,2},{4,5},{5,4},{6,7},{7,6},{8,9},{9,8},{10,11... | collective-permute-start | bytes 1769480 | tf_op jit(solution)/shard_map/ppermute | solution.py:316
  8.0 9.7 %copy-start.2 = (f32[2,144,256]{2,1,0:T(8,128)}, f32[2,144,256]{2,1,0:T(8,128)S(1)}, u32[]{:S(2)}) copy-start(f32[2,144,256]{2,1,0:T(8,128)S(1)} %get-tuple-element.27.part_ref) | copy-start | bytes 884740
  8.0 9.7 %copy-start.8 = (bf16[2,2,144,256]{3,2,1,0:T(8,128)(2,1)}, bf16[2,2,144,256]{3,2,1,0:T(8,128)(2,1)S(1)}, u32[]{:S(2)}) copy-start(bf16[2,2,144,256]{3,2,1,0:T(8,128)(2,1)S(1)} %get-tuple-element.23.u_ref) | copy-start | bytes 884740
  8.0 17.4 %collective-permute-start.4 = (bf16[2,144,512]{2,1,0:T(8,128)(2,1)S(1)}, bf16[2,144,512]{2,1,0:T(8,128)(2,1)}, u32[]{:S(2)}, u32[]{:S(2)}) collective-permute-start(bf16[2,144,512]{2,1,0:T(8,128)(2,1)S(1)} %constant_dynamic-update-slice_fusion.lines_ref), channel_id=1, source_target_pairs={{0,2},{2,4},{4,6},{6,8},{8,10},{10,12},{12,14},{1,3},{3,5},{5,7},{... | collective-permute-start | bytes 884744 | tf_op jit(solution)/shard_map/ppermute | solution.py:336
  14.2 1.3 %collective-permute-start.3 = (bf16[2,16,512]{2,1,0:T(8,128)(2,1)S(1)}, bf16[2,16,512]{2,1,0:T(8,128)(2,1)S(1)}, u32[]{:S(2)}, u32[]{:S(2)}) collective-permute-start(bf16[2,16,512]{2,1,0:T(8,128)(2,1)S(1)} %slice_select_fusion), channel_id=1, source_target_pairs={{0,1},{1,0},{2,3},{3,2},{4,5},{5,4},{6,7},{7,6},{8,9},{9,8},{10,11... | collective-permute-start | bytes 98312 | tf_op jit(solution)/shard_map/ppermute | solution.py:337
  15.4 2.2 %copy-start.4 = (bf16[2,16,512]{2,1,0:T(8,128)(2,1)}, bf16[2,16,512]{2,1,0:T(8,128)(2,1)S(1)}, u32[]{:S(2)}) copy-start(bf16[2,16,512]{2,1,0:T(8,128)(2,1)S(1)} %collective-permute-done.3.edge_ref.next_edge_ref) | copy-start | bytes 98308
  15.4 3.1 %copy-start.12 = (f32[256]{0:T(256)S(1)}, f32[256]{0:T(256)}, u32[]{:S(2)}) copy-start(f32[256]{0:T(256)} %param.15) | copy-start | bytes 3076
  15.4 3.1 %copy-start.13 = (f32[256]{0:T(256)S(1)}, f32[256]{0:T(256)}, u32[]{:S(2)}) copy-start(f32[256]{0:T(256)} %param.13) | copy-start | bytes 3076
  15.4 3.1 %copy-start.14 = (f32[256]{0:T(256)S(1)}, f32[256]{0:T(256)}, u32[]{:S(2)}) copy-start(f32[256]{0:T(256)} %param.11) | copy-start | bytes 3076
  15.5 3.1 %copy-start.15 = (f32[256]{0:T(256)S(1)}, f32[256]{0:T(256)}, u32[]{:S(2)}) copy-start(f32[256]{0:T(256)} %param.10) | copy-start | bytes 3076
  18.4 1.2 %collective-permute-start.5 = (f32[8,128]{1,0:T(8,128)S(1)}, f32[8,128]{1,0:T(8,128)S(1)}, u32[]{:S(2)}, u32[]{:S(2)}) collective-permute-start(f32[8,128]{1,0:T(8,128)S(1)} %get-tuple-element.30), channel_id=1, source_target_pairs={{0,1},{1,0},{2,3},{3,2},{4,5},{5,4},{6,7},{7,6},{8,9},{9,8},{10,11... | collective-permute-start | bytes 12296 | tf_op jit(solution)/shard_map/ppermute | solution.py:357
  20.2 12.0 %all-to-all-start = ((f32[8,8,128]{2,1,0:T(8,128)}), f32[8,8,128]{2,1,0:T(8,128)}, u32[]{:S(2)}, u32[]{:S(2)}) async-start(f32[8,8,128]{2,1,0:T(8,128)} %broadcast_in_dim.3), calls=%async_computation | async-start | bytes 65536 | tf_op jit(solution)/shard_map/all_to_all | solution.py:358
  25.4 1.0 %copy-start.3 = (f32[2,144,256]{2,1,0:T(8,128)S(1)}, f32[2,144,256]{2,1,0:T(8,128)}, u32[]{:S(2)}) copy-start(f32[2,144,256]{2,1,0:T(8,128)} %copy-done.2) | copy-start | bytes 884740
  26.4 0.8 %copy-start.5 = (bf16[2,16,512]{2,1,0:T(8,128)(2,1)S(1)}, bf16[2,16,512]{2,1,0:T(8,128)(2,1)}, u32[]{:S(2)}) copy-start(bf16[2,16,512]{2,1,0:T(8,128)(2,1)} %copy-done.4) | copy-start | bytes 98308
  30.1 0.8 %copy-start = (bf16[4,2,144,256]{3,2,1,0:T(8,128)(2,1)}, bf16[4,2,144,256]{3,2,1,0:T(8,128)(2,1)S(1)}, u32[]{:S(2)}) copy-start(bf16[4,2,144,256]{3,2,1,0:T(8,128)(2,1)S(1)} %deconv_halo.1.halo_ref) | copy-start | bytes 1769476
  32.2 1.1 %copy-start.1 = (bf16[4,2,144,256]{3,2,1,0:T(8,128)(2,1)S(1)}, bf16[4,2,144,256]{3,2,1,0:T(8,128)(2,1)}, u32[]{:S(2)}) copy-start(bf16[4,2,144,256]{3,2,1,0:T(8,128)(2,1)} %copy-done) | copy-start | bytes 1769476
  33.3 1.1 %copy-start.6 = (bf16[3,3,256,128]{3,2,1,0:T(8,128)(2,1)S(1)}, bf16[3,3,256,128]{3,2,1,0:T(8,128)(2,1)}, u32[]{:S(2)}) copy-start(bf16[3,3,256,128]{3,2,1,0:T(8,128)(2,1)} %own_w1.1) | copy-start | bytes 1769476
  34.3 1.1 %copy-start.7 = (bf16[3,3,256,128]{3,2,1,0:T(8,128)(2,1)S(1)}, bf16[3,3,256,128]{3,2,1,0:T(8,128)(2,1)}, u32[]{:S(2)}) copy-start(bf16[3,3,256,128]{3,2,1,0:T(8,128)(2,1)} %own_w2.1) | copy-start | bytes 1769476
  35.4 1.0 %copy-start.9 = (bf16[2,2,144,256]{3,2,1,0:T(8,128)(2,1)S(1)}, bf16[2,2,144,256]{3,2,1,0:T(8,128)(2,1)}, u32[]{:S(2)}) copy-start(bf16[2,2,144,256]{3,2,1,0:T(8,128)(2,1)} %copy-done.8) | copy-start | bytes 884740
  36.4 1.0 %copy-start.11 = (bf16[2,2,144,256]{3,2,1,0:T(8,128)(2,1)S(1)}, bf16[2,2,144,256]{3,2,1,0:T(8,128)(2,1)}, u32[]{:S(2)}) copy-start(bf16[2,2,144,256]{3,2,1,0:T(8,128)(2,1)} %copy-done.10) | copy-start | bytes 884740
  (1 other events, 0.7 us)

commit v7 on v4

--- a/solution.py
+++ b/solution.py
@@ -47,17 +47,13 @@
     copy.wait()
 
 
-def spread_line(out, line):
-    total, cin = line.shape
-    line = jnp.where(edge_mask(total - EDGE), line.astype(jnp.float32), 0.0)
-    out[:, 0:cin] = pltpu.roll(line, total - 1, 0).astype(jnp.bfloat16)
+def spread_line(out, main, edge):
+    width, cin = main.shape
+    line = jnp.concatenate([main.astype(jnp.float32), edge.astype(jnp.float32)], axis=0)
+    line = jnp.where(edge_mask(width), line, 0.0)
+    out[:, 0:cin] = pltpu.roll(line, width + EDGE - 1, 0).astype(jnp.bfloat16)
     out[:, cin : 2 * cin] = line.astype(jnp.bfloat16)
     out[:, 2 * cin : 3 * cin] = pltpu.roll(line, 1, 0).astype(jnp.bfloat16)
-
-
-def own_kernel(lines_ref, xs_ref):
-    for row in range(lines_ref.shape[0]):
-        spread_line(xs_ref.at[row], lines_ref[row])
 
 
 def tap_dot(lines, phase, kr, own_w, other_w):
@@ -75,17 +71,29 @@
     return out.reshape(count, total, weight.shape[-1])
 
 
-def main_kernel(xs_ref, next_ref, own_w, other_w, u_ref, part_ref, xs_next_ref, stats_ref):
+def add_sums(line, width):
+    values = line[:width].astype(jnp.float32)
+    return jnp.concatenate(
+        [jnp.sum(values, axis=0, keepdims=True), jnp.sum(values * values, axis=0, keepdims=True)], axis=0
+    )
+
+
+def own_kernel(lines_ref, xs_ref):
+    rows, total, _ = lines_ref.shape
+    width = total - EDGE
+    for row in range(rows):
+        spread_line(xs_ref.at[row], lines_ref[row, :width], lines_ref[row, width:])
+
+
+def main_kernel(xs_ref, next_ref, next_edge_ref, own_w, other_w, u_ref, part_ref, xs_next_ref, stats_ref):
     rows, total, _ = xs_ref.shape
     width = total - EDGE
-    cout = u_ref.shape[-1]
-    spread_line(xs_next_ref.at[0], next_ref[0])
+    spread_line(xs_next_ref.at[0], next_ref[0], next_edge_ref[0])
     column = lax.axis_index("fsdp")
     place = lax.axis_index("rows")
     first_here = place == 0
     last_here = place == lax.axis_size("rows") - 1
-    sums = jnp.zeros((1, cout), jnp.float32)
-    squares = jnp.zeros((1, cout), jnp.float32)
+    sums = jnp.zeros((2, u_ref.shape[-1]), jnp.float32)
     for phase in range(2):
         dot = functools.partial(tap_dot, phase=phase, own_w=own_w, other_w=other_w)
         upper = dot(xs_ref[...], kr=1)
@@ -97,29 +105,28 @@
         lower = dot(xs_ref[1:], kr=0)
         odd = [upper[row] + lower[row] for row in range(rows - 1)]
         odd.append(upper[rows - 1] + dot(xs_next_ref[...], kr=0)[0])
-        lines = []
         for row in range(rows):
-            lines += [odd[row].astype(jnp.bfloat16), even[row].astype(jnp.bfloat16)]
-        for row, line in enumerate(lines):
-            u_ref[row, phase] = line
-        edge_line = jnp.where(first_here, part_ref[phase].astype(jnp.bfloat16).astype(jnp.float32), 0.0)
-        final_line = jnp.where(last_here, 0.0, lines[-1].astype(jnp.float32))
-        for line in lines[:-1] + [edge_line, final_line]:
-            values = line[:width].astype(jnp.float32)
-            sums += jnp.sum(values, axis=0, keepdims=True)
-            squares += jnp.sum(values * values, axis=0, keepdims=True)
-    half = cout // 2
+            odd[row], even[row] = odd[row].astype(jnp.bfloat16), even[row].astype(jnp.bfloat16)
+            u_ref[2 * row, phase] = odd[row]
+            u_ref[2 * row + 1, phase] = even[row]
+            sums += add_sums(odd[row], width)
+            if row < rows - 1:
+                sums += add_sums(even[row], width)
+        sums += jnp.where(last_here, 0.0, add_sums(even[rows - 1], width))
+        sums += jnp.where(first_here, add_sums(part_ref[phase].astype(jnp.bfloat16), width), 0.0)
+    half = sums.shape[1] // 2
     halves = []
-    for row in (sums, squares):
-        own, other = row[:, :half], row[:, half:]
+    for row in range(2):
+        own, other = sums[row : row + 1, :half], sums[row : row + 1, half:]
         halves += [jnp.where(column == 0, own, other), jnp.where(column == 0, other, own)]
     stats_ref[...] = jnp.concatenate(halves + [jnp.zeros((4, half), jnp.float32)], axis=0)
 
 
-def halo_kernel(above_ref, below_ref, xs_ref, xs_next_ref, part_ref, own_w, other_w, u_ref, xs_above, xs_below):
+def halo_kernel(above_ref, next_ref, next_edge_ref, xs_ref, xs_next_ref, part_ref, own_w, other_w, u_ref, xs_above, xs_below):
+    width = next_ref.shape[1]
     for row in range(HALO):
-        spread_line(xs_above.at[row], above_ref[row])
-    spread_line(xs_below.at[0], below_ref[0])
+        spread_line(xs_above.at[row], above_ref[row, :width], above_ref[row, width:])
+    spread_line(xs_below.at[0], next_ref[1], next_edge_ref[1])
     for phase in range(2):
         dot = functools.partial(tap_dot, phase=phase, own_w=own_w, other_w=other_w)
         outer = dot(xs_above[...], kr=3)
@@ -256,10 +263,9 @@
     size = lax.axis_size(axis)
     if size & (size - 1):
         return lax.psum(block, axis)
-    step = 1
-    while step < size:
+    steps = [2**n for n in range(size.bit_length() - 1)]
+    for step in steps[1:] + steps[:1]:
         block = block + lax.ppermute(block, axis, [(i, i ^ step) for i in range(size)])
-        step *= 2
     return block
 
 
@@ -297,9 +303,8 @@
 
     in_hbm = functools.partial(pltpu.with_memory_space_constraint, memory_space=pltpu.HBM)
     shape_w = (taps, taps // 2, 2, cin, lanes)
-    other_w = lax.ppermute(deconv_weight, "fsdp", swap).reshape(shape_w)
-    first_other = lax.ppermute(first_weight, "fsdp", swap)
-    second_other = lax.ppermute(second_weight, "fsdp", swap)
+    at_left = lax.axis_index("fsdp") == 0
+    following = lax.ppermute(image, "rows", to_previous)
     near, edges = call(
         cut_kernel,
         [hbm],
@@ -308,31 +313,35 @@
         "cut",
     )(in_hbm(image))
     edge = lax.ppermute(edges, "fsdp", swap)
+    other_w = lax.ppermute(deconv_weight, "fsdp", swap).reshape(shape_w)
+    first_other = lax.ppermute(after(first_weight, edges), "fsdp", swap)
+    second_other = lax.ppermute(after(second_weight, edges), "fsdp", swap)
     (own_w,) = call(near_kernel, [hbm], [(shape_w, bf16)], [pltpu.SemaphoreType.DMA(())], "near_weights")(
         in_hbm(after(deconv_weight, edges).reshape(shape_w))
     )
-    lines = jnp.concatenate([near, edge], axis=1)
-    following = lax.ppermute(lines[:1], "rows", to_previous)
+    lines = jnp.concatenate([after(near, own_w), edge], axis=1)
     above = lax.ppermute(lines, "rows", to_next)
-    below = lax.ppermute(lines[1:], "rows", to_previous)
     (xs,) = call(own_kernel, [vmem], [((rows, total, 3 * cin), bf16)], [], "own_lines")(lines)
+    next_edge = lax.ppermute(
+        jnp.where(at_left, following[:, width - EDGE :], following[:, :EDGE]), "fsdp", swap
+    )
+    u_line = (2, total, cout)
     u, part, xs_next, stats = call(
         main_kernel,
-        [vmem] * 4,
-        [((2 * rows, 2, total, cout), bf16), ((2, total, cout), f32), ((1, total, 3 * cin), bf16), ((8, cout // 2), f32)],
+        [vmem] * 5,
+        [((2 * rows, *u_line), bf16), (u_line, f32), ((1, total, 3 * cin), bf16), ((8, cout // 2), f32)],
         [],
         "deconv_main",
         flops=2 * 2 * (2 * rows) * total * 4 * cin * cout,
-    )(xs, following, own_w, other_w)
-
+    )(xs, following, next_edge, own_w, other_w)
     (halo,) = call(
         halo_kernel,
-        [vmem] * 7,
-        [((4, 2, total, cout), bf16)],
+        [vmem] * 8,
+        [((4, *u_line), bf16)],
         [pltpu.VMEM((HALO, total, 3 * cin), bf16), pltpu.VMEM((1, total, 3 * cin), bf16)],
         "deconv_halo",
         flops=2 * 2 * 4 * total * 4 * cin * cout,
-    )(above, below, xs, xs_next, part, own_w, other_w)
+    )(above, following, next_edge, xs, xs_next, part, own_w, other_w)
 
     totals = total_over(total_over(stats, "fsdp"), "rows")
     params = jnp.stack([norm_gain, norm_shift, first_bias, second_bias])

time: 37.1 us -> 37.8 us (1.019)
  Pallas kernels: 10.4 us -> 14.8 us
  starting transfers between devices: 18.4 us -> 15.5 us
  waiting for transfers between devices: 7.83 us -> 7.01 us
    pallas_call x2, Pallas kernels: 2.81 us -> 6.13 us  [the longest x1 3.2 us: local(): call(main_kernel, [vmem] * 5, [((2 * rows, *u_line), bf16), (u_line, f32)...]
    ppermute x1, waiting for transfers between devices: 2.15 us -> 0.01 us  [local(): edge = lax.ppermute(edges, 'fsdp', swap)]
    ppermute x4, waiting for transfers between devices: 0.44 us -> 2.51 us  [the longest x1 1.46 us: local(): following = lax.ppermute(image, 'rows', to_previous)]
    ppermute x4, starting transfers between devices: 9.31 us -> 7.56 us  [total_over(): lax.ppermute(block, axis, [(i, i ^ step) for i in range(size)])]
    ppermute x4, starting transfers between devices: 3.1 us -> 1.88 us  [the longest x1 1.28 us: local(): following = lax.ppermute(image, 'rows', to_previous)]
    pallas_call x1, Pallas kernels: 4.79 us -> 5.83 us  [local(): call(functools.partial(conv_kernel, count), [vmem] * 8, [((2 * rows, 2 *...]
    ppermute x4, waiting for transfers between devices: 5.24 us -> 4.49 us  [total_over(): lax.ppermute(block, axis, [(i, i ^ step) for i in range(size)])]
  transfers between devices with their start and end apart: 11 -> 11, of which waited for: 6 -> 5; matrix products, arithmetic and copies ran while one was open for 0% -> 0% of each run, Pallas kernels for 15% -> 24%
where the time goes in v7:
time: 37.8 us; the launch traced here: 37.5 us
  starting transfers between devices  15.5 us (41%)
  Pallas kernels  14.8 us (39%)
  waiting for transfers between devices  7.01 us (19%)
    ppermute x4, starting transfers between devices, total_over(): lax.ppermute(block, axis, [(i, i ^ step) for i in range(size)])  7.56 us
    pallas_call x1, Pallas kernels, local(): call(functools.partial(conv_kernel, count), [vmem] * 8, [((2 * rows, 2 *...  5.83 us
    ppermute x1, starting transfers between devices, local(): above = lax.ppermute(lines, 'rows', to_next)  5.46 us
    ppermute x4, waiting for transfers between devices, total_over(): lax.ppermute(block, axis, [(i, i ^ step) for i in range(size)])  4.49 us
    pallas_call x1, Pallas kernels, local(): call(main_kernel, [vmem] * 5, [((2 * rows, *u_line), bf16), (u_line, f32)...  3.2 us
    pallas_call x1, Pallas kernels, local(): call(halo_kernel, [vmem] * 8, [((4, *u_line), bf16)], [pltpu.VMEM((HALO,...  2.93 us
    pallas_call x1, Pallas kernels, local(): call(near_kernel, [hbm], [(shape_w, bf16)], [pltpu.SemaphoreType.DMA(())]...  1.6 us
    ppermute x1, waiting for transfers between devices, local(): following = lax.ppermute(image, 'rows', to_previous)  1.46 us
  transfers between devices with their start and end apart: 11, of which 5 were waited for; matrix products, arithmetic and copies ran while one was open for 0% of the time, Pallas kernels for 24%

profile of v7, /device:TPU:0, one launch (start us, length us, event | category | flops | bytes accessed | tf_op | source)
XLA Modules:
  0.0 37.5 jit_solution(5661321891988386520)
XLA Ops:
  0.0 0.5 %collective-permute-start.3 = (bf16[4,4,512,128]{3,2,1,0:T(8,128)(2,1)}, bf16[4,4,512,128]{3,2,1,0:T(8,128)(2,1)}, u32[]{:S(2)}, u32[]{:S(2)}) collective-permute-start(bf16[4,4,512,128]{3,2,1,0:T(8,128)(2,1)} %param.9), channel_id=1, source_target_pairs={{0,1},{1,0},{2,3},{3,2},{4,5},{5,4},{6,7},{7,6},{8,9},{9,8},{10,11... | collective-permute-start | bytes 6291464 | tf_op jit(solution)/shard_map/ppermute | solution.py:316
  0.5 1.3 %collective-permute-start.1 = (bf16[2,128,512]{2,1,0:T(8,128)(2,1)}, bf16[2,128,512]{2,1,0:T(8,128)(2,1)S(1)}, u32[]{:S(2)}, u32[]{:S(2)}) collective-permute-start(bf16[2,128,512]{2,1,0:T(8,128)(2,1)} %image_ref.1), channel_id=1, source_target_pairs={{2,0},{4,2},{6,4},{8,6},{10,8},{12,10},{14,12},{3,1},{5,3},{7,5},{... | collective-permute-start | bytes 786440 | tf_op jit(solution)/shard_map/ppermute | solution.py:307
  1.7 1.1 %cut.1 = (bf16[2,128,512]{2,1,0:T(8,128)(2,1)S(1)}, bf16[2,16,512]{2,1,0:T(8,128)(2,1)S(1)}) custom-call(bf16[2,128,512]{2,1,0:T(8,128)(2,1)} %image_ref.1), custom_call_target="tpu_custom_call" | custom-call | bytes 2097152 | tf_op jit(solution)/shard_map/cut/pallas_call | solution.py:308
  2.8 0.1 collective-permute-start
  2.9 0.5 %collective-permute-start.10 = (bf16[3,3,256,128]{3,2,1,0:T(8,128)(2,1)}, bf16[3,3,256,128]{3,2,1,0:T(8,128)(2,1)S(1)}, u32[]{:S(2)}, u32[]{:S(2)}) collective-permute-start(bf16[3,3,256,128]{3,2,1,0:T(8,128)(2,1)} %own_w2.1), channel_id=1, source_target_pairs={{0,1},{1,0},{2,3},{3,2},{4,5},{5,4},{6,7},{7,6},{8,9},{9,8},{10,11... | collective-permute-start | bytes 1769480 | tf_op jit(solution)/shard_map/ppermute | solution.py:318
  3.4 0.1 collective-permute-start.9
  3.5 1.6 %near_weights.1.own_w = bf16[4,2,2,512,128]{4,3,2,1,0:T(8,128)(2,1)S(1)} custom-call(bf16[4,2,2,512,128]{4,3,2,1,0:T(8,128)(2,1)} %bitcast.6), custom_call_target="tpu_custom_call" | custom-call | bytes 2097152 | tf_op jit(solution)/shard_map/near_weights/pallas_call | solution.py:319
  5.1 0.0 collective-permute-done
  5.1 5.5 %collective-permute-start.4 = (bf16[2,144,512]{2,1,0:T(8,128)(2,1)S(1)}, bf16[2,144,512]{2,1,0:T(8,128)(2,1)S(1)}, u32[]{:S(2)}, u32[]{:S(2)}) collective-permute-start(bf16[2,144,512]{2,1,0:T(8,128)(2,1)S(1)} %constant_dynamic-update-slice_fusion.lines_ref), channel_id=1, source_target_pairs={{0,2},{2,4},{4,6},{6,8},{8,10},{10,12},{12,14},{1,3},{3,5},{5,7},{... | collective-permute-start | bytes 884744 | tf_op jit(solution)/shard_map/ppermute | solution.py:323
  10.6 1.5 %collective-permute-done.1.next_ref = bf16[2,128,512]{2,1,0:T(8,128)(2,1)S(1)} collective-permute-done((bf16[2,128,512]{2,1,0:T(8,128)(2,1)}, bf16[2,128,512]{2,1,0:T(8,128)(2,1)S(1)}, u32[]{:S(2)}, u32[]{:S(2)}) %collective-permute-start.1) | collective-permute-done | bytes 262176 | tf_op jit(solution)/shard_map/ppermute | solution.py:307
  12.1 0.1 collective-permute-start.2
  12.1 0.1 own_lines.1.xs_ref
  12.3 1.0 %collective-permute-done.2.next_edge_ref = bf16[2,16,512]{2,1,0:T(8,128)(2,1)S(1)} collective-permute-done((bf16[2,16,512]{2,1,0:T(8,128)(2,1)S(1)}, bf16[2,16,512]{2,1,0:T(8,128)(2,1)S(1)}, u32[]{:S(2)}, u32[]{:S(2)}) %collective-permute-start.2) | collective-permute-done | bytes 32800 | tf_op jit(solution)/shard_map/ppermute | solution.py:325
  13.3 0.0 copy-start.5
  13.4 3.2 %deconv_main.1 = (bf16[4,2,144,256]{3,2,1,0:T(8,128)(2,1)S(1)}, f32[2,144,256]{2,1,0:T(8,128)S(1)}, bf16[1,144,1536]{2,1,0:T(8,128)(2,1)S(1)}, f32[8,128]{1,0:T(8,128)S(1)}) custom-call(bf16[2,144,1536]{2,1,0:T(8,128)(2,1)S(1)} %own_lines.1.xs_ref, bf16[2,128,512]{2,1,0:T(8,128)(2,1)S(1)} %collective-permute-done.1.next_ref, ...), custom_call_target="tpu_custom_call" | custom-call | flops 1207959552 | bytes 2097152 | tf_op jit(solution)/shard_map/deconv_main/pallas_call | solution.py:329
  16.6 0.2 collective-permute-start.5
  16.8 1.0 %collective-permute-done.5 = f32[8,128]{1,0:T(8,128)S(1)} collective-permute-done((f32[8,128]{1,0:T(8,128)S(1)}, f32[8,128]{1,0:T(8,128)S(1)}, u32[]{:S(2)}, u32[]{:S(2)}) %collective-permute-start.5) | collective-permute-done | bytes 4128 | tf_op jit(solution)/shard_map/ppermute | solution.py:268
  17.8 1.8 %collective-permute-start.6 = (f32[8,128]{1,0:T(8,128)S(1)}, f32[8,128]{1,0:T(8,128)S(1)}, u32[]{:S(2)}, u32[]{:S(2)}) collective-permute-start(f32[8,128]{1,0:T(8,128)S(1)} %add.12), channel_id=1, source_target_pairs={{0,4},{2,6},{4,0},{6,2},{8,12},{10,14},{12,8},{14,10},{1,5},{3,7},... | collective-permute-start | bytes 12296 | tf_op jit(solution)/shard_map/ppermute | solution.py:268
  19.6 1.8 %collective-permute-done.6 = f32[8,128]{1,0:T(8,128)S(1)} collective-permute-done((f32[8,128]{1,0:T(8,128)S(1)}, f32[8,128]{1,0:T(8,128)S(1)}, u32[]{:S(2)}, u32[]{:S(2)}) %collective-permute-start.6) | collective-permute-done | bytes 4128 | tf_op jit(solution)/shard_map/ppermute | solution.py:268
  21.4 2.8 %collective-permute-start.7 = (f32[8,128]{1,0:T(8,128)S(1)}, f32[8,128]{1,0:T(8,128)S(1)}, u32[]{:S(2)}, u32[]{:S(2)}) collective-permute-start(f32[8,128]{1,0:T(8,128)S(1)} %add.13), channel_id=1, source_target_pairs={{0,8},{2,10},{4,12},{6,14},{8,0},{10,2},{12,4},{14,6},{1,9},{3,11}... | collective-permute-start | bytes 12296 | tf_op jit(solution)/shard_map/ppermute | solution.py:268
  24.2 1.7 %collective-permute-done.7 = f32[8,128]{1,0:T(8,128)S(1)} collective-permute-done((f32[8,128]{1,0:T(8,128)S(1)}, f32[8,128]{1,0:T(8,128)S(1)}, u32[]{:S(2)}, u32[]{:S(2)}) %collective-permute-start.7) | collective-permute-done | bytes 4128 | tf_op jit(solution)/shard_map/ppermute | solution.py:268
  25.9 2.7 %collective-permute-start.8 = (f32[8,128]{1,0:T(8,128)S(1)}, f32[8,128]{1,0:T(8,128)S(1)}, u32[]{:S(2)}, u32[]{:S(2)}) collective-permute-start(f32[8,128]{1,0:T(8,128)S(1)} %add.14), channel_id=1, source_target_pairs={{0,2},{2,0},{4,6},{6,4},{8,10},{10,8},{12,14},{14,12},{1,3},{3,1},... | collective-permute-start | bytes 12296 | tf_op jit(solution)/shard_map/ppermute | solution.py:268
  28.7 2.9 %deconv_halo.1.halo_ref = bf16[4,2,144,256]{3,2,1,0:T(8,128)(2,1)S(1)} custom-call(bf16[2,144,512]{2,1,0:T(8,128)(2,1)S(1)} %collective-permute-done.4.above_ref, bf16[2,128,512]{2,1,0:T(8,128)(2,1)S(1)} %collective-permute-done.1.next_ref, bf16[2,16,512]{2,1,0:T(8,128)(2,1)S(1)} %collective-permute-done.2.next_edge_ref, ...), custom_call_target="tpu_custom_call" | custom-call | flops 1207959552 | bytes 2097152 | tf_op jit(solution)/shard_map/deconv_halo/pallas_call | solution.py:337
  31.7 5.8 %convs.1 = bf16[4,256,256]{2,1,0:T(8,128)(2,1)} custom-call(bf16[4,2,144,256]{3,2,1,0:T(8,128)(2,1)S(1)} %get-tuple-element.19.u_ref, bf16[4,2,144,256]{3,2,1,0:T(8,128)(2,1)S(1)} %deconv_halo.1.halo_ref, f32[8,128]{1,0:T(8,128)S(1)} %add.15.stats_ref, f32[4,256]{1,0:T(4,128)S(1)} %pad_maximum_fusion.params_ref, bf16[3,3,256,128]{3,2,1,0:T(8,128)(2,1)S(1)} %copy-done, ...), custom_call_target="tpu_custom_call" | custom-call | flops 5000000000 | bytes 2097152 | tf_op jit(solution)/shard_map/convs/pallas_call | solution.py:348
  (24 shorter events, 0.1 us)
Async XLA Ops:
  0.0 13.3 %collective-permute-start.3 = (bf16[4,4,512,128]{3,2,1,0:T(8,128)(2,1)}, bf16[4,4,512,128]{3,2,1,0:T(8,128)(2,1)}, u32[]{:S(2)}, u32[]{:S(2)}) collective-permute-start(bf16[4,4,512,128]{3,2,1,0:T(8,128)(2,1)} %param.9), channel_id=1, source_target_pairs={{0,1},{1,0},{2,3},{3,2},{4,5},{5,4},{6,7},{7,6},{8,9},{9,8},{10,11... | collective-permute-start | bytes 6291464 | tf_op jit(solution)/shard_map/ppermute | solution.py:316
  0.5 11.6 %collective-permute-start.1 = (bf16[2,128,512]{2,1,0:T(8,128)(2,1)}, bf16[2,128,512]{2,1,0:T(8,128)(2,1)S(1)}, u32[]{:S(2)}, u32[]{:S(2)}) collective-permute-start(bf16[2,128,512]{2,1,0:T(8,128)(2,1)} %image_ref.1), channel_id=1, source_target_pairs={{2,0},{4,2},{6,4},{8,6},{10,8},{12,10},{14,12},{3,1},{5,3},{7,5},{... | collective-permute-start | bytes 786440 | tf_op jit(solution)/shard_map/ppermute | solution.py:307
  2.8 2.3 %collective-permute-start = (bf16[2,16,512]{2,1,0:T(8,128)(2,1)S(1)}, bf16[2,16,512]{2,1,0:T(8,128)(2,1)S(1)}, u32[]{:S(2)}, u32[]{:S(2)}) collective-permute-start(bf16[2,16,512]{2,1,0:T(8,128)(2,1)S(1)} %get-tuple-element.16), channel_id=1, source_target_pairs={{0,1},{1,0},{2,3},{3,2},{4,5},{5,4},{6,7},{7,6},{8,9},{9,8},{10,11... | collective-permute-start | bytes 98312 | tf_op jit(solution)/shard_map/ppermute | solution.py:315
  2.9 28.7 %collective-permute-start.10 = (bf16[3,3,256,128]{3,2,1,0:T(8,128)(2,1)}, bf16[3,3,256,128]{3,2,1,0:T(8,128)(2,1)S(1)}, u32[]{:S(2)}, u32[]{:S(2)}) collective-permute-start(bf16[3,3,256,128]{3,2,1,0:T(8,128)(2,1)} %own_w2.1), channel_id=1, source_target_pairs={{0,1},{1,0},{2,3},{3,2},{4,5},{5,4},{6,7},{7,6},{8,9},{9,8},{10,11... | collective-permute-start | bytes 1769480 | tf_op jit(solution)/shard_map/ppermute | solution.py:318
  3.4 28.2 %collective-permute-start.9 = (bf16[3,3,256,128]{3,2,1,0:T(8,128)(2,1)}, bf16[3,3,256,128]{3,2,1,0:T(8,128)(2,1)}, u32[]{:S(2)}, u32[]{:S(2)}) collective-permute-start(bf16[3,3,256,128]{3,2,1,0:T(8,128)(2,1)} %own_w1.1), channel_id=1, source_target_pairs={{0,1},{1,0},{2,3},{3,2},{4,5},{5,4},{6,7},{7,6},{8,9},{9,8},{10,11... | collective-permute-start | bytes 1769480 | tf_op jit(solution)/shard_map/ppermute | solution.py:317
  5.1 23.5 %collective-permute-start.4 = (bf16[2,144,512]{2,1,0:T(8,128)(2,1)S(1)}, bf16[2,144,512]{2,1,0:T(8,128)(2,1)S(1)}, u32[]{:S(2)}, u32[]{:S(2)}) collective-permute-start(bf16[2,144,512]{2,1,0:T(8,128)(2,1)S(1)} %constant_dynamic-update-slice_fusion.lines_ref), channel_id=1, source_target_pairs={{0,2},{2,4},{4,6},{6,8},{8,10},{10,12},{12,14},{1,3},{3,5},{5,7},{... | collective-permute-start | bytes 884744 | tf_op jit(solution)/shard_map/ppermute | solution.py:323
  12.1 1.3 %collective-permute-start.2 = (bf16[2,16,512]{2,1,0:T(8,128)(2,1)S(1)}, bf16[2,16,512]{2,1,0:T(8,128)(2,1)S(1)}, u32[]{:S(2)}, u32[]{:S(2)}) collective-permute-start(bf16[2,16,512]{2,1,0:T(8,128)(2,1)S(1)} %slice_select_fusion), channel_id=1, source_target_pairs={{0,1},{1,0},{2,3},{3,2},{4,5},{5,4},{6,7},{7,6},{8,9},{9,8},{10,11... | collective-permute-start | bytes 98312 | tf_op jit(solution)/shard_map/ppermute | solution.py:325
  13.3 10.9 %copy-start.2 = (f32[256]{0:T(256)S(1)}, f32[256]{0:T(256)}, u32[]{:S(2)}) copy-start(f32[256]{0:T(256)} %param.15) | copy-start | bytes 3076
  13.3 10.9 %copy-start.3 = (f32[256]{0:T(256)S(1)}, f32[256]{0:T(256)}, u32[]{:S(2)}) copy-start(f32[256]{0:T(256)} %param.13) | copy-start | bytes 3076
  13.3 10.9 %copy-start.4 = (f32[256]{0:T(256)S(1)}, f32[256]{0:T(256)}, u32[]{:S(2)}) copy-start(f32[256]{0:T(256)} %param.11) | copy-start | bytes 3076
  13.3 10.9 %copy-start.5 = (f32[256]{0:T(256)S(1)}, f32[256]{0:T(256)}, u32[]{:S(2)}) copy-start(f32[256]{0:T(256)} %param.10) | copy-start | bytes 3076
  16.6 1.2 %collective-permute-start.5 = (f32[8,128]{1,0:T(8,128)S(1)}, f32[8,128]{1,0:T(8,128)S(1)}, u32[]{:S(2)}, u32[]{:S(2)}) collective-permute-start(f32[8,128]{1,0:T(8,128)S(1)} %get-tuple-element.22), channel_id=1, source_target_pairs={{0,1},{1,0},{2,3},{3,2},{4,5},{5,4},{6,7},{7,6},{8,9},{9,8},{10,11... | collective-permute-start | bytes 12296 | tf_op jit(solution)/shard_map/ppermute | solution.py:268
  17.8 3.6 %collective-permute-start.6 = (f32[8,128]{1,0:T(8,128)S(1)}, f32[8,128]{1,0:T(8,128)S(1)}, u32[]{:S(2)}, u32[]{:S(2)}) collective-permute-start(f32[8,128]{1,0:T(8,128)S(1)} %add.12), channel_id=1, source_target_pairs={{0,4},{2,6},{4,0},{6,2},{8,12},{10,14},{12,8},{14,10},{1,5},{3,7},... | collective-permute-start | bytes 12296 | tf_op jit(solution)/shard_map/ppermute | solution.py:268
  21.4 4.5 %collective-permute-start.7 = (f32[8,128]{1,0:T(8,128)S(1)}, f32[8,128]{1,0:T(8,128)S(1)}, u32[]{:S(2)}, u32[]{:S(2)}) collective-permute-start(f32[8,128]{1,0:T(8,128)S(1)} %add.13), channel_id=1, source_target_pairs={{0,8},{2,10},{4,12},{6,14},{8,0},{10,2},{12,4},{14,6},{1,9},{3,11}... | collective-permute-start | bytes 12296 | tf_op jit(solution)/shard_map/ppermute | solution.py:268
  25.9 5.7 %collective-permute-start.8 = (f32[8,128]{1,0:T(8,128)S(1)}, f32[8,128]{1,0:T(8,128)S(1)}, u32[]{:S(2)}, u32[]{:S(2)}) collective-permute-start(f32[8,128]{1,0:T(8,128)S(1)} %add.14), channel_id=1, source_target_pairs={{0,2},{2,0},{4,6},{6,4},{8,10},{10,8},{12,14},{14,12},{1,3},{3,1},... | collective-permute-start | bytes 12296 | tf_op jit(solution)/shard_map/ppermute | solution.py:268
  28.6 3.0 %copy-start = (bf16[3,3,256,128]{3,2,1,0:T(8,128)(2,1)S(1)}, bf16[3,3,256,128]{3,2,1,0:T(8,128)(2,1)}, u32[]{:S(2)}) copy-start(bf16[3,3,256,128]{3,2,1,0:T(8,128)(2,1)} %own_w1.1) | copy-start | bytes 1769476
  28.7 3.0 %copy-start.1 = (bf16[3,3,256,128]{3,2,1,0:T(8,128)(2,1)S(1)}, bf16[3,3,256,128]{3,2,1,0:T(8,128)(2,1)}, u32[]{:S(2)}) copy-start(bf16[3,3,256,128]{3,2,1,0:T(8,128)(2,1)} %own_w2.1) | copy-start | bytes 1769476

commit v8 on v7

--- a/solution.py
+++ b/solution.py
@@ -39,6 +39,19 @@
         copy.start()
     for copy in copies:
         copy.wait()
+
+
+def pick_kernel(lines_ref, edges_ref):
+    width = lines_ref.shape[1]
+    at_left = lax.axis_index("fsdp") == 0
+
+    @pl.when(at_left)
+    def _():
+        edges_ref[...] = lines_ref[:, width - EDGE :]
+
+    @pl.when(jnp.logical_not(at_left))
+    def _():
+        edges_ref[...] = lines_ref[:, :EDGE]
 
 
 def near_kernel(weight_ref, near_ref, sem):
@@ -303,7 +316,6 @@
 
     in_hbm = functools.partial(pltpu.with_memory_space_constraint, memory_space=pltpu.HBM)
     shape_w = (taps, taps // 2, 2, cin, lanes)
-    at_left = lax.axis_index("fsdp") == 0
     following = lax.ppermute(image, "rows", to_previous)
     near, edges = call(
         cut_kernel,
@@ -322,9 +334,8 @@
     lines = jnp.concatenate([after(near, own_w), edge], axis=1)
     above = lax.ppermute(lines, "rows", to_next)
     (xs,) = call(own_kernel, [vmem], [((rows, total, 3 * cin), bf16)], [], "own_lines")(lines)
-    next_edge = lax.ppermute(
-        jnp.where(at_left, following[:, width - EDGE :], following[:, :EDGE]), "fsdp", swap
-    )
+    (next_edges,) = call(pick_kernel, [vmem], [((rows, EDGE, cin), bf16)], [], "next_edges")(following)
+    next_edge = lax.ppermute(next_edges, "fsdp", swap)
     u_line = (2, total, cout)
     u, part, xs_next, stats = call(
         main_kernel,

time: 37.8 us -> 33.6 us (0.89)
  Pallas kernels: 14.8 us -> 10.4 us
    pallas_call x1, Pallas kernels: 2.93 us -> 1.24 us  [local(): call(halo_kernel, [vmem] * 8, [((4, *u_line), bf16)], [pltpu.VMEM((HALO,...]
    pallas_call x1, Pallas kernels: 3.2 us -> 1.57 us  [local(): call(main_kernel, [vmem] * 5, [((2 * rows, *u_line), bf16), (u_line, f32)...]
    pallas_call x1, Pallas kernels: 5.83 us -> 4.8 us  [local(): call(functools.partial(conv_kernel, count), [vmem] * 8, [((2 * rows, 2 *...]
  transfers between devices with their start and end apart: 11 -> 11, of which waited for: 5 -> 6; matrix products, arithmetic and copies ran while one was open for 0% -> 0% of each run, Pallas kernels for 24% -> 17%
where the time goes in v8:
time: 33.6 us; the launch traced here: 33.4 us
  starting transfers between devices  15.4 us (46%)
  Pallas kernels  10.4 us (31%)
  waiting for transfers between devices  7.35 us (22%)
    ppermute x4, starting transfers between devices, total_over(): lax.ppermute(block, axis, [(i, i ^ step) for i in range(size)])  7.56 us
    ppermute x1, starting transfers between devices, local(): above = lax.ppermute(lines, 'rows', to_next)  5.46 us
    ppermute x4, waiting for transfers between devices, total_over(): lax.ppermute(block, axis, [(i, i ^ step) for i in range(size)])  4.82 us
    pallas_call x1, Pallas kernels, local(): call(functools.partial(conv_kernel, count), [vmem] * 8, [((2 * rows, 2 *...  4.8 us
    pallas_call x1, Pallas kernels, local(): call(near_kernel, [hbm], [(shape_w, bf16)], [pltpu.SemaphoreType.DMA(())]...  1.6 us
    pallas_call x1, Pallas kernels, local(): call(main_kernel, [vmem] * 5, [((2 * rows, *u_line), bf16), (u_line, f32)...  1.57 us
    ppermute x1, waiting for transfers between devices, local(): following = lax.ppermute(image, 'rows', to_previous)  1.46 us
    ppermute x1, starting transfers between devices, local(): following = lax.ppermute(image, 'rows', to_previous)  1.28 us
  transfers between devices with their start and end apart: 11, of which 6 were waited for; matrix products, arithmetic and copies ran while one was open for 0% of the time, Pallas kernels for 17%

profile of v8, /device:TPU:0, one launch (start us, length us, event | category | flops | bytes accessed | tf_op | source)
XLA Modules:
  0.0 33.4 jit_solution(3377166595261823593)
XLA Ops:
  0.0 0.5 %collective-permute-start.3 = (bf16[4,4,512,128]{3,2,1,0:T(8,128)(2,1)}, bf16[4,4,512,128]{3,2,1,0:T(8,128)(2,1)S(1)}, u32[]{:S(2)}, u32[]{:S(2)}) collective-permute-start(bf16[4,4,512,128]{3,2,1,0:T(8,128)(2,1)} %param.9), channel_id=1, source_target_pairs={{0,1},{1,0},{2,3},{3,2},{4,5},{5,4},{6,7},{7,6},{8,9},{9,8},{10,11... | collective-permute-start | bytes 6291464 | tf_op jit(solution)/shard_map/ppermute | solution.py:328
  0.5 1.3 %collective-permute-start.1 = (bf16[2,128,512]{2,1,0:T(8,128)(2,1)}, bf16[2,128,512]{2,1,0:T(8,128)(2,1)S(1)}, u32[]{:S(2)}, u32[]{:S(2)}) collective-permute-start(bf16[2,128,512]{2,1,0:T(8,128)(2,1)} %image_ref.1), channel_id=1, source_target_pairs={{2,0},{4,2},{6,4},{8,6},{10,8},{12,10},{14,12},{3,1},{5,3},{7,5},{... | collective-permute-start | bytes 786440 | tf_op jit(solution)/shard_map/ppermute | solution.py:319
  1.7 1.1 %cut.1 = (bf16[2,128,512]{2,1,0:T(8,128)(2,1)S(1)}, bf16[2,16,512]{2,1,0:T(8,128)(2,1)S(1)}) custom-call(bf16[2,128,512]{2,1,0:T(8,128)(2,1)} %image_ref.1), custom_call_target="tpu_custom_call" | custom-call | bytes 2097152 | tf_op jit(solution)/shard_map/cut/pallas_call | solution.py:320
  2.8 0.1 collective-permute-start
  2.9 0.5 %collective-permute-start.10 = (bf16[3,3,256,128]{3,2,1,0:T(8,128)(2,1)}, bf16[3,3,256,128]{3,2,1,0:T(8,128)(2,1)S(1)}, u32[]{:S(2)}, u32[]{:S(2)}) collective-permute-start(bf16[3,3,256,128]{3,2,1,0:T(8,128)(2,1)} %own_w2.1), channel_id=1, source_target_pairs={{0,1},{1,0},{2,3},{3,2},{4,5},{5,4},{6,7},{7,6},{8,9},{9,8},{10,11... | collective-permute-start | bytes 1769480 | tf_op jit(solution)/shard_map/ppermute | solution.py:330
  3.4 0.1 collective-permute-start.9
  3.5 1.6 %near_weights.1.own_w = bf16[4,2,2,512,128]{4,3,2,1,0:T(8,128)(2,1)S(1)} custom-call(bf16[4,2,2,512,128]{4,3,2,1,0:T(8,128)(2,1)} %bitcast.8), custom_call_target="tpu_custom_call" | custom-call | bytes 2097152 | tf_op jit(solution)/shard_map/near_weights/pallas_call | solution.py:331
  5.1 0.0 collective-permute-done
  5.1 5.5 %collective-permute-start.4 = (bf16[2,144,512]{2,1,0:T(8,128)(2,1)S(1)}, bf16[2,144,512]{2,1,0:T(8,128)(2,1)S(1)}, u32[]{:S(2)}, u32[]{:S(2)}) collective-permute-start(bf16[2,144,512]{2,1,0:T(8,128)(2,1)S(1)} %constant_dynamic-update-slice_fusion.lines_ref), channel_id=1, source_target_pairs={{0,2},{2,4},{4,6},{6,8},{8,10},{10,12},{12,14},{1,3},{3,5},{5,7},{... | collective-permute-start | bytes 884744 | tf_op jit(solution)/shard_map/ppermute | solution.py:335
  10.6 1.5 %collective-permute-done.1.lines_ref.next_ref = bf16[2,128,512]{2,1,0:T(8,128)(2,1)S(1)} collective-permute-done((bf16[2,128,512]{2,1,0:T(8,128)(2,1)}, bf16[2,128,512]{2,1,0:T(8,128)(2,1)S(1)}, u32[]{:S(2)}, u32[]{:S(2)}) %collective-permute-start.1) | collective-permute-done | bytes 262176 | tf_op jit(solution)/shard_map/ppermute | solution.py:319
  12.1 0.1 own_lines.1.xs_ref
  12.2 1.1 %collective-permute-done.2.next_edge_ref = bf16[2,16,512]{2,1,0:T(8,128)(2,1)S(1)} collective-permute-done((bf16[2,16,512]{2,1,0:T(8,128)(2,1)S(1)}, bf16[2,16,512]{2,1,0:T(8,128)(2,1)S(1)}, u32[]{:S(2)}, u32[]{:S(2)}) %collective-permute-start.2) | collective-permute-done | bytes 32800 | tf_op jit(solution)/shard_map/ppermute | solution.py:338
  13.3 0.0 copy-start.5
  13.3 1.6 %deconv_main.1 = (bf16[4,2,144,256]{3,2,1,0:T(8,128)(2,1)S(1)}, f32[2,144,256]{2,1,0:T(8,128)S(1)}, bf16[1,144,1536]{2,1,0:T(8,128)(2,1)S(1)}, f32[8,128]{1,0:T(8,128)S(1)}) custom-call(bf16[2,144,1536]{2,1,0:T(8,128)(2,1)S(1)} %own_lines.1.xs_ref, bf16[2,128,512]{2,1,0:T(8,128)(2,1)S(1)} %collective-permute-done.1.lines_ref.next_ref, ...), custom_call_target="tpu_custom_call" | custom-call | flops 1207959552 | bytes 2097152 | tf_op jit(solution)/shard_map/deconv_main/pallas_call | solution.py:340
  14.9 0.2 collective-permute-start.5
  15.1 1.0 %collective-permute-done.5 = f32[8,128]{1,0:T(8,128)S(1)} collective-permute-done((f32[8,128]{1,0:T(8,128)S(1)}, f32[8,128]{1,0:T(8,128)S(1)}, u32[]{:S(2)}, u32[]{:S(2)}) %collective-permute-start.5) | collective-permute-done | bytes 4128 | tf_op jit(solution)/shard_map/ppermute | solution.py:281
  16.1 1.8 %collective-permute-start.6 = (f32[8,128]{1,0:T(8,128)S(1)}, f32[8,128]{1,0:T(8,128)S(1)}, u32[]{:S(2)}, u32[]{:S(2)}) collective-permute-start(f32[8,128]{1,0:T(8,128)S(1)} %add.12), channel_id=1, source_target_pairs={{0,4},{2,6},{4,0},{6,2},{8,12},{10,14},{12,8},{14,10},{1,5},{3,7},... | collective-permute-start | bytes 12296 | tf_op jit(solution)/shard_map/ppermute | solution.py:281
  17.9 1.8 %collective-permute-done.6 = f32[8,128]{1,0:T(8,128)S(1)} collective-permute-done((f32[8,128]{1,0:T(8,128)S(1)}, f32[8,128]{1,0:T(8,128)S(1)}, u32[]{:S(2)}, u32[]{:S(2)}) %collective-permute-start.6) | collective-permute-done | bytes 4128 | tf_op jit(solution)/shard_map/ppermute | solution.py:281
  19.7 2.8 %collective-permute-start.7 = (f32[8,128]{1,0:T(8,128)S(1)}, f32[8,128]{1,0:T(8,128)S(1)}, u32[]{:S(2)}, u32[]{:S(2)}) collective-permute-start(f32[8,128]{1,0:T(8,128)S(1)} %add.13), channel_id=1, source_target_pairs={{0,8},{2,10},{4,12},{6,14},{8,0},{10,2},{12,4},{14,6},{1,9},{3,11}... | collective-permute-start | bytes 12296 | tf_op jit(solution)/shard_map/ppermute | solution.py:281
  22.5 1.7 %collective-permute-done.7 = f32[8,128]{1,0:T(8,128)S(1)} collective-permute-done((f32[8,128]{1,0:T(8,128)S(1)}, f32[8,128]{1,0:T(8,128)S(1)}, u32[]{:S(2)}, u32[]{:S(2)}) %collective-permute-start.7) | collective-permute-done | bytes 4128 | tf_op jit(solution)/shard_map/ppermute | solution.py:281
  24.2 2.7 %collective-permute-start.8 = (f32[8,128]{1,0:T(8,128)S(1)}, f32[8,128]{1,0:T(8,128)S(1)}, u32[]{:S(2)}, u32[]{:S(2)}) collective-permute-start(f32[8,128]{1,0:T(8,128)S(1)} %add.14), channel_id=1, source_target_pairs={{0,2},{2,0},{4,6},{6,4},{8,10},{10,8},{12,14},{14,12},{1,3},{3,1},... | collective-permute-start | bytes 12296 | tf_op jit(solution)/shard_map/ppermute | solution.py:281
  27.0 1.2 %deconv_halo.1.halo_ref = bf16[4,2,144,256]{3,2,1,0:T(8,128)(2,1)S(1)} custom-call(bf16[2,144,512]{2,1,0:T(8,128)(2,1)S(1)} %collective-permute-done.4.above_ref, bf16[2,128,512]{2,1,0:T(8,128)(2,1)S(1)} %collective-permute-done.1.lines_ref.next_ref, bf16[2,16,512]{2,1,0:T(8,128)(2,1)S(1)} %collective-permute-done.2.next_edge_ref, ...), custom_call_target="tpu_custom_call" | custom-call | flops 1207959552 | bytes 2097152 | tf_op jit(solution)/shard_map/deconv_halo/pallas_call | solution.py:348
  28.2 0.3 collective-permute-done.8
  28.6 4.8 %convs.1 = bf16[4,256,256]{2,1,0:T(8,128)(2,1)} custom-call(bf16[4,2,144,256]{3,2,1,0:T(8,128)(2,1)S(1)} %get-tuple-element.19.u_ref, bf16[4,2,144,256]{3,2,1,0:T(8,128)(2,1)S(1)} %deconv_halo.1.halo_ref, f32[8,128]{1,0:T(8,128)S(1)} %add.15.stats_ref, f32[4,256]{1,0:T(4,128)S(1)} %pad_maximum_fusion.params_ref, bf16[3,3,256,128]{3,2,1,0:T(8,128)(2,1)S(1)} %copy-done, ...), custom_call_target="tpu_custom_call" | custom-call | flops 5000000000 | bytes 2097152 | tf_op jit(solution)/shard_map/convs/pallas_call | solution.py:359
  (24 shorter events, 0.1 us)
Async XLA Ops:
  0.0 13.3 %collective-permute-start.3 = (bf16[4,4,512,128]{3,2,1,0:T(8,128)(2,1)}, bf16[4,4,512,128]{3,2,1,0:T(8,128)(2,1)S(1)}, u32[]{:S(2)}, u32[]{:S(2)}) collective-permute-start(bf16[4,4,512,128]{3,2,1,0:T(8,128)(2,1)} %param.9), channel_id=1, source_target_pairs={{0,1},{1,0},{2,3},{3,2},{4,5},{5,4},{6,7},{7,6},{8,9},{9,8},{10,11... | collective-permute-start | bytes 6291464 | tf_op jit(solution)/shard_map/ppermute | solution.py:328
  0.5 11.6 %collective-permute-start.1 = (bf16[2,128,512]{2,1,0:T(8,128)(2,1)}, bf16[2,128,512]{2,1,0:T(8,128)(2,1)S(1)}, u32[]{:S(2)}, u32[]{:S(2)}) collective-permute-start(bf16[2,128,512]{2,1,0:T(8,128)(2,1)} %image_ref.1), channel_id=1, source_target_pairs={{2,0},{4,2},{6,4},{8,6},{10,8},{12,10},{14,12},{3,1},{5,3},{7,5},{... | collective-permute-start | bytes 786440 | tf_op jit(solution)/shard_map/ppermute | solution.py:319
  2.8 2.3 %collective-permute-start = (bf16[2,16,512]{2,1,0:T(8,128)(2,1)S(1)}, bf16[2,16,512]{2,1,0:T(8,128)(2,1)S(1)}, u32[]{:S(2)}, u32[]{:S(2)}) collective-permute-start(bf16[2,16,512]{2,1,0:T(8,128)(2,1)S(1)} %get-tuple-element.16), channel_id=1, source_target_pairs={{0,1},{1,0},{2,3},{3,2},{4,5},{5,4},{6,7},{7,6},{8,9},{9,8},{10,11... | collective-permute-start | bytes 98312 | tf_op jit(solution)/shard_map/ppermute | solution.py:327
  2.9 25.6 %collective-permute-start.10 = (bf16[3,3,256,128]{3,2,1,0:T(8,128)(2,1)}, bf16[3,3,256,128]{3,2,1,0:T(8,128)(2,1)S(1)}, u32[]{:S(2)}, u32[]{:S(2)}) collective-permute-start(bf16[3,3,256,128]{3,2,1,0:T(8,128)(2,1)} %own_w2.1), channel_id=1, source_target_pairs={{0,1},{1,0},{2,3},{3,2},{4,5},{5,4},{6,7},{7,6},{8,9},{9,8},{10,11... | collective-permute-start | bytes 1769480 | tf_op jit(solution)/shard_map/ppermute | solution.py:330
  3.4 25.2 %collective-permute-start.9 = (bf16[3,3,256,128]{3,2,1,0:T(8,128)(2,1)}, bf16[3,3,256,128]{3,2,1,0:T(8,128)(2,1)S(1)}, u32[]{:S(2)}, u32[]{:S(2)}) collective-permute-start(bf16[3,3,256,128]{3,2,1,0:T(8,128)(2,1)} %own_w1.1), channel_id=1, source_target_pairs={{0,1},{1,0},{2,3},{3,2},{4,5},{5,4},{6,7},{7,6},{8,9},{9,8},{10,11... | collective-permute-start | bytes 1769480 | tf_op jit(solution)/shard_map/ppermute | solution.py:329
  5.1 21.8 %collective-permute-start.4 = (bf16[2,144,512]{2,1,0:T(8,128)(2,1)S(1)}, bf16[2,144,512]{2,1,0:T(8,128)(2,1)S(1)}, u32[]{:S(2)}, u32[]{:S(2)}) collective-permute-start(bf16[2,144,512]{2,1,0:T(8,128)(2,1)S(1)} %constant_dynamic-update-slice_fusion.lines_ref), channel_id=1, source_target_pairs={{0,2},{2,4},{4,6},{6,8},{8,10},{10,12},{12,14},{1,3},{3,5},{5,7},{... | collective-permute-start | bytes 884744 | tf_op jit(solution)/shard_map/ppermute | solution.py:335
  12.1 1.2 %collective-permute-start.2 = (bf16[2,16,512]{2,1,0:T(8,128)(2,1)S(1)}, bf16[2,16,512]{2,1,0:T(8,128)(2,1)S(1)}, u32[]{:S(2)}, u32[]{:S(2)}) collective-permute-start(bf16[2,16,512]{2,1,0:T(8,128)(2,1)S(1)} %next_edges.1), channel_id=1, source_target_pairs={{0,1},{1,0},{2,3},{3,2},{4,5},{5,4},{6,7},{7,6},{8,9},{9,8},{10,11... | collective-permute-start | bytes 98312 | tf_op jit(solution)/shard_map/ppermute | solution.py:338
  13.3 9.2 %copy-start.2 = (f32[256]{0:T(256)S(1)}, f32[256]{0:T(256)}, u32[]{:S(2)}) copy-start(f32[256]{0:T(256)} %param.15) | copy-start | bytes 3076
  13.3 9.3 %copy-start.3 = (f32[256]{0:T(256)S(1)}, f32[256]{0:T(256)}, u32[]{:S(2)}) copy-start(f32[256]{0:T(256)} %param.13) | copy-start | bytes 3076
  13.3 9.3 %copy-start.4 = (f32[256]{0:T(256)S(1)}, f32[256]{0:T(256)}, u32[]{:S(2)}) copy-start(f32[256]{0:T(256)} %param.11) | copy-start | bytes 3076
  13.3 9.2 %copy-start.5 = (f32[256]{0:T(256)S(1)}, f32[256]{0:T(256)}, u32[]{:S(2)}) copy-start(f32[256]{0:T(256)} %param.10) | copy-start | bytes 3076
  14.9 1.2 %collective-permute-start.5 = (f32[8,128]{1,0:T(8,128)S(1)}, f32[8,128]{1,0:T(8,128)S(1)}, u32[]{:S(2)}, u32[]{:S(2)}) collective-permute-start(f32[8,128]{1,0:T(8,128)S(1)} %get-tuple-element.22), channel_id=1, source_target_pairs={{0,1},{1,0},{2,3},{3,2},{4,5},{5,4},{6,7},{7,6},{8,9},{9,8},{10,11... | collective-permute-start | bytes 12296 | tf_op jit(solution)/shard_map/ppermute | solution.py:281
  16.1 3.6 %collective-permute-start.6 = (f32[8,128]{1,0:T(8,128)S(1)}, f32[8,128]{1,0:T(8,128)S(1)}, u32[]{:S(2)}, u32[]{:S(2)}) collective-permute-start(f32[8,128]{1,0:T(8,128)S(1)} %add.12), channel_id=1, source_target_pairs={{0,4},{2,6},{4,0},{6,2},{8,12},{10,14},{12,8},{14,10},{1,5},{3,7},... | collective-permute-start | bytes 12296 | tf_op jit(solution)/shard_map/ppermute | solution.py:281
  19.7 4.5 %collective-permute-start.7 = (f32[8,128]{1,0:T(8,128)S(1)}, f32[8,128]{1,0:T(8,128)S(1)}, u32[]{:S(2)}, u32[]{:S(2)}) collective-permute-start(f32[8,128]{1,0:T(8,128)S(1)} %add.13), channel_id=1, source_target_pairs={{0,8},{2,10},{4,12},{6,14},{8,0},{10,2},{12,4},{14,6},{1,9},{3,11}... | collective-permute-start | bytes 12296 | tf_op jit(solution)/shard_map/ppermute | solution.py:281
  24.2 4.3 %collective-permute-start.8 = (f32[8,128]{1,0:T(8,128)S(1)}, f32[8,128]{1,0:T(8,128)S(1)}, u32[]{:S(2)}, u32[]{:S(2)}) collective-permute-start(f32[8,128]{1,0:T(8,128)S(1)} %add.14), channel_id=1, source_target_pairs={{0,2},{2,0},{4,6},{6,4},{8,10},{10,8},{12,14},{14,12},{1,3},{3,1},... | collective-permute-start | bytes 12296 | tf_op jit(solution)/shard_map/ppermute | solution.py:281
  27.0 1.6 %copy-start = (bf16[3,3,256,128]{3,2,1,0:T(8,128)(2,1)S(1)}, bf16[3,3,256,128]{3,2,1,0:T(8,128)(2,1)}, u32[]{:S(2)}) copy-start(bf16[3,3,256,128]{3,2,1,0:T(8,128)(2,1)} %own_w1.1) | copy-start | bytes 1769476
  27.0 1.6 %copy-start.1 = (bf16[3,3,256,128]{3,2,1,0:T(8,128)(2,1)S(1)}, bf16[3,3,256,128]{3,2,1,0:T(8,128)(2,1)}, u32[]{:S(2)}) copy-start(bf16[3,3,256,128]{3,2,1,0:T(8,128)(2,1)} %own_w2.1) | copy-start | bytes 1769476

commit v9 on v5

--- a/solution.py
+++ b/solution.py
@@ -39,6 +39,19 @@
         copy.start()
     for copy in copies:
         copy.wait()
+
+
+def pick_kernel(lines_ref, edges_ref):
+    width = lines_ref.shape[1]
+    at_left = lax.axis_index("fsdp") == 0
+
+    @pl.when(at_left)
+    def _():
+        edges_ref[...] = lines_ref[:, width - EDGE :]
+
+    @pl.when(jnp.logical_not(at_left))
+    def _():
+        edges_ref[...] = lines_ref[:, :EDGE]
 
 
 def near_kernel(weight_ref, near_ref, sem):
@@ -125,19 +138,18 @@
     stats_ref[...] = jnp.concatenate(halves + [jnp.zeros((4, half), jnp.float32)], axis=0)
 
 
-def halo_kernel(above_ref, next_ref, next_edge_ref, xs_ref, part_ref, own_w, other_w, u_ref, xs_above, xs_below):
+def halo_kernel(above_ref, next_ref, next_edge_ref, xs_ref, xs_next_ref, part_ref, own_w, other_w, u_ref, xs_above, xs_below):
     width = next_ref.shape[1]
     for row in range(HALO):
         spread_line(xs_above.at[row], above_ref[row, :width], above_ref[row, width:])
-    for row in range(HALO):
-        spread_line(xs_below.at[row], next_ref[row], next_edge_ref[row])
+    spread_line(xs_below.at[0], next_ref[1], next_edge_ref[1])
     for phase in range(2):
         dot = functools.partial(tap_dot, phase=phase, own_w=own_w, other_w=other_w)
         outer = dot(xs_above[...], kr=3)
         u_ref[0, phase] = (outer[0] + dot(xs_above[1:2], kr=1)[0]).astype(jnp.bfloat16)
         u_ref[2, phase] = (outer[1] + part_ref[phase]).astype(jnp.bfloat16)
         u_ref[1, phase] = (dot(xs_above[1:2], kr=2)[0] + dot(xs_ref[0:1], kr=0)[0]).astype(jnp.bfloat16)
-        u_ref[3, phase] = (dot(xs_below[0:1], kr=2)[0] + dot(xs_below[1:2], kr=0)[0]).astype(jnp.bfloat16)
+        u_ref[3, phase] = (dot(xs_next_ref[...], kr=2)[0] + dot(xs_below[...], kr=0)[0]).astype(jnp.bfloat16)
 
 
 def group_sum(v, width):
@@ -161,7 +173,7 @@
 
 
 def conv_kernel(
-    count, u_ref, u_next_ref, halo_ref, stats_ref, params_ref, own_w1, other_w1, own_w2, other_w2, out_ref, g, act, mixed
+    count, u_ref, u_next_ref, halo_ref, mine_ref, passed_ref, params_ref, own_w1, other_w1, own_w2, other_w2, out_ref, g, act, mixed
 ):
     early, _, total, cout = u_ref.shape
     main = early + u_next_ref.shape[0]
@@ -185,7 +197,7 @@
             axis=1,
         )
 
-    block = stats_ref[...]
+    block = jnp.where(column == 1, mine_ref[...], passed_ref[...])
     width_group = cout // NORM_GROUPS
     sums = jnp.concatenate([block[0:1], block[1:2]], axis=1)
     squares = jnp.concatenate([block[2:3], block[3:4]], axis=1)
@@ -266,14 +278,15 @@
             second(start - chunk)
 
 
-def total_over(block, axis):
-    size = lax.axis_size(axis)
-    if size & (size - 1):
-        return lax.psum(block, axis)
+def total_over(block, last):
+    size = lax.axis_size("rows")
+    block = block + lax.ppermute(block, "fsdp", [(0, 1)])
+    assert size & (size - 1) == 0
     steps = [2**n for n in range(size.bit_length() - 1)]
     for step in steps[1:] + steps[:1]:
-        block = block + lax.ppermute(block, axis, [(i, i ^ step) for i in range(size)])
-    return block
+        pairs = [(2 * i + 1, 2 * (i ^ step) + 1) for i in range(size)]
+        block = block + lax.ppermute(block, ("rows", "fsdp"), pairs)
+    return block, lax.ppermute(after(block, last), "fsdp", [(1, 0)])
 
 
 def after(value, *others):
@@ -310,7 +323,6 @@
 
     in_hbm = functools.partial(pltpu.with_memory_space_constraint, memory_space=pltpu.HBM)
     shape_w = (taps, taps // 2, 2, cin, lanes)
-    at_left = lax.axis_index("fsdp") == 0
     following = lax.ppermute(image, "rows", to_previous)
     near, edges = call(
         cut_kernel,
@@ -327,6 +339,7 @@
         in_hbm(after(deconv_weight, edges).reshape(shape_w))
     )
     lines = jnp.concatenate([after(near, own_w), edge], axis=1)
+    above = lax.ppermute(lines, "rows", to_next)
     u_line = (2, total, cout)
     xs, u, part, tail, sums = call(
         own_kernel,
@@ -342,10 +355,8 @@
         "deconv_own",
         flops=2 * 2 * (2 * rows - 1) * total * 4 * cin * cout,
     )(lines, own_w, other_w)
-    above = lax.ppermute(after(lines, part), "rows", to_next)
-    next_edge = lax.ppermute(
-        jnp.where(at_left, following[:, width - EDGE :], following[:, :EDGE]), "fsdp", swap
-    )
+    (next_edges,) = call(pick_kernel, [vmem], [((rows, EDGE, cin), bf16)], [], "next_edges")(following)
+    next_edge = lax.ppermute(next_edges, "fsdp", swap)
     u_next, xs_next, stats = call(
         next_kernel,
         [vmem] * 6,
@@ -356,18 +367,18 @@
     )(following, next_edge, tail, sums, own_w, other_w)
     (halo,) = call(
         halo_kernel,
-        [vmem] * 7,
+        [vmem] * 8,
         [((4, *u_line), bf16)],
-        [pltpu.VMEM((HALO, total, 3 * cin), bf16), pltpu.VMEM((HALO, total, 3 * cin), bf16)],
+        [pltpu.VMEM((HALO, total, 3 * cin), bf16), pltpu.VMEM((1, total, 3 * cin), bf16)],
         "deconv_halo",
         flops=2 * 2 * 4 * total * 4 * cin * cout,
-    )(above, following, next_edge, xs, part, own_w, other_w)
-
-    totals = total_over(total_over(stats, "fsdp"), "rows")
+    )(above, following, next_edge, xs, xs_next, part, own_w, other_w)
+
+    mine, passed = total_over(stats, halo)
     params = jnp.stack([norm_gain, norm_shift, first_bias, second_bias])
     (out,) = call(
         functools.partial(conv_kernel, count),
-        [vmem] * 9,
+        [vmem] * 10,
         [((2 * rows, 2 * width, cout), bf16)],
         [
             pltpu.VMEM((2 * rows + 2 * HALO, total, 4 * cout), bf16),
@@ -376,7 +387,7 @@
         ],
         "convs",
         flops=5 * 10**9,
-    )(u, u_next, halo, totals, params, first_weight, first_other, second_weight, second_other)
+    )(u, u_next, halo, mine, passed, params, first_weight, first_other, second_weight, second_other)
     return out
 
 

time: 40.1 us -> 39.8 us (level)
  waiting for transfers between devices: 7.3 us -> 15.1 us
  Pallas kernels: 16.9 us -> 10.5 us
  starting transfers between devices: 15.3 us -> 13.5 us
    ppermute x6 -> x7, waiting for transfers between devices: 7.29 us -> 13.6 us  [the longest x1 12.8 us: total_over(): return (block, lax.ppermute(after(block, last), 'fsdp', [(1, 0)]))]
    pallas_call x2 -> x3, Pallas kernels: 8.77 us -> 6.05 us  [the longest x1 4.81 us: local(): call(functools.partial(conv_kernel, count), [vmem] * 10, [((2 * rows, 2 *...]
    pallas_call x1, Pallas kernels: 2.64 us -> 0.53 us  [local(): call(next_kernel, [vmem] * 6, [((2, *u_line), bf16), ((1, total, 3 * cin)...]
    ppermute x6 -> x7, starting transfers between devices: 12.9 us -> 11.1 us  [the longest x1 5.46 us: local(): above = lax.ppermute(lines, 'rows', to_next)]
    pallas_call x1, Pallas kernels: 2.84 us -> 1.26 us  [local(): call(own_kernel, [vmem] * 3, [((rows, total, 3 * cin), bf16), ((2 * rows...]
    ppermute x1, waiting for transfers between devices: 0.01 us -> 1.46 us  [local(): following = lax.ppermute(image, 'rows', to_previous)]
  transfers between devices with their start and end apart: 11 -> 12, of which waited for: 5 -> 3; matrix products, arithmetic and copies ran while one was open for 0% -> 0% of each run, Pallas kernels for 28% -> 14%
where the time goes in v9:
time: 39.8 us; the launch traced here: 39.5 us
  waiting for transfers between devices  15.1 us (38%)
  starting transfers between devices  13.5 us (34%)
  Pallas kernels  10.5 us (26%)
    ppermute x1, waiting for transfers between devices, total_over(): return (block, lax.ppermute(after(block, last), 'fsdp', [(1, 0)]))  12.8 us
    ppermute x1, starting transfers between devices, local(): above = lax.ppermute(lines, 'rows', to_next)  5.46 us
    pallas_call x1, Pallas kernels, local(): call(functools.partial(conv_kernel, count), [vmem] * 10, [((2 * rows, 2 *...  4.81 us
    ppermute x1, starting transfers between devices, total_over(): block = block + lax.ppermute(block, 'fsdp', [(0, 1)])  2.41 us
    ppermute x3, starting transfers between devices, total_over(): block = block + lax.ppermute(block, ('rows', 'fsdp'), pairs)  1.97 us
    pallas_call x1, Pallas kernels, local(): call(near_kernel, [hbm], [(shape_w, bf16)], [pltpu.SemaphoreType.DMA(())]...  1.6 us
    ppermute x1, waiting for transfers between devices, local(): following = lax.ppermute(image, 'rows', to_previous)  1.46 us
    ppermute x1, starting transfers between devices, total_over(): return (block, lax.ppermute(after(block, last), 'fsdp', [(1, 0)]))  1.29 us
  transfers between devices with their start and end apart: 12, of which 3 were waited for; matrix products, arithmetic and copies ran while one was open for 0% of the time, Pallas kernels for 14%

profile of v9, /device:TPU:0, one launch (start us, length us, event | category | flops | bytes accessed | tf_op | source)
XLA Modules:
  0.0 39.5 jit_solution(4726977220552412171)
XLA Ops:
  0.0 0.5 %collective-permute-start.1 = (bf16[4,4,512,128]{3,2,1,0:T(8,128)(2,1)}, bf16[4,4,512,128]{3,2,1,0:T(8,128)(2,1)S(1)}, u32[]{:S(2)}, u32[]{:S(2)}) collective-permute-start(bf16[4,4,512,128]{3,2,1,0:T(8,128)(2,1)} %param.9), channel_id=1, source_target_pairs={{0,1},{1,0},{2,3},{3,2},{4,5},{5,4},{6,7},{7,6},{8,9},{9,8},{10,11... | collective-permute-start | bytes 6291464 | tf_op jit(solution)/shard_map/ppermute | solution.py:335
  0.5 1.3 %collective-permute-start.2 = (bf16[2,128,512]{2,1,0:T(8,128)(2,1)}, bf16[2,128,512]{2,1,0:T(8,128)(2,1)S(1)}, u32[]{:S(2)}, u32[]{:S(2)}) collective-permute-start(bf16[2,128,512]{2,1,0:T(8,128)(2,1)} %image_ref.1), channel_id=1, source_target_pairs={{2,0},{4,2},{6,4},{8,6},{10,8},{12,10},{14,12},{3,1},{5,3},{7,5},{... | collective-permute-start | bytes 786440 | tf_op jit(solution)/shard_map/ppermute | solution.py:326
  1.7 1.1 %cut.1 = (bf16[2,128,512]{2,1,0:T(8,128)(2,1)S(1)}, bf16[2,16,512]{2,1,0:T(8,128)(2,1)S(1)}) custom-call(bf16[2,128,512]{2,1,0:T(8,128)(2,1)} %image_ref.1), custom_call_target="tpu_custom_call" | custom-call | bytes 2097152 | tf_op jit(solution)/shard_map/cut/pallas_call | solution.py:327
  2.8 0.1 collective-permute-start
  2.9 0.5 %collective-permute-start.10 = (bf16[3,3,256,128]{3,2,1,0:T(8,128)(2,1)}, bf16[3,3,256,128]{3,2,1,0:T(8,128)(2,1)S(1)}, u32[]{:S(2)}, u32[]{:S(2)}) collective-permute-start(bf16[3,3,256,128]{3,2,1,0:T(8,128)(2,1)} %own_w1.1), channel_id=1, source_target_pairs={{0,1},{1,0},{2,3},{3,2},{4,5},{5,4},{6,7},{7,6},{8,9},{9,8},{10,11... | collective-permute-start | bytes 1769480 | tf_op jit(solution)/shard_map/ppermute | solution.py:336
  3.4 0.1 collective-permute-start.11
  3.5 1.6 %near_weights.1.own_w = bf16[4,2,2,512,128]{4,3,2,1,0:T(8,128)(2,1)S(1)} custom-call(bf16[4,2,2,512,128]{4,3,2,1,0:T(8,128)(2,1)} %bitcast.9), custom_call_target="tpu_custom_call" | custom-call | bytes 2097152 | tf_op jit(solution)/shard_map/near_weights/pallas_call | solution.py:338
  5.1 5.5 %collective-permute-start.4 = (bf16[2,144,512]{2,1,0:T(8,128)(2,1)S(1)}, bf16[2,144,512]{2,1,0:T(8,128)(2,1)S(1)}, u32[]{:S(2)}, u32[]{:S(2)}) collective-permute-start(bf16[2,144,512]{2,1,0:T(8,128)(2,1)S(1)} %constant_dynamic-update-slice_fusion.lines_ref), channel_id=1, source_target_pairs={{0,2},{2,4},{4,6},{6,8},{8,10},{10,12},{12,14},{1,3},{3,5},{5,7},{... | collective-permute-start | bytes 884744 | tf_op jit(solution)/shard_map/ppermute | solution.py:342
  10.6 1.5 %collective-permute-done.2.lines_ref.next_ref = bf16[2,128,512]{2,1,0:T(8,128)(2,1)S(1)} collective-permute-done((bf16[2,128,512]{2,1,0:T(8,128)(2,1)}, bf16[2,128,512]{2,1,0:T(8,128)(2,1)S(1)}, u32[]{:S(2)}, u32[]{:S(2)}) %collective-permute-start.2) | collective-permute-done | bytes 262176 | tf_op jit(solution)/shard_map/ppermute | solution.py:326
  12.1 1.3 %deconv_own.1 = (bf16[2,144,1536]{2,1,0:T(8,128)(2,1)S(1)}, bf16[2,2,144,256]{3,2,1,0:T(8,128)(2,1)S(1)}, f32[2,144,256]{2,1,0:T(8,128)S(1)}, f32[2,2,144,256]{3,2,1,0:T(8,128)S(1)}, f32[2,256]{1,0:T(2,128)S(1)}) custom-call(bf16[2,144,512]{2,1,0:T(8,128)(2,1)S(1)} %constant_dynamic-update-slice_fusion.lines_ref, ...), custom_call_target="tpu_custom_call" | custom-call | flops 905969664 | bytes 2097152 | tf_op jit(solution)/shard_map/deconv_own/pallas_call | solution.py:344
  13.3 0.5 %deconv_next.1 = (bf16[2,2,144,256]{3,2,1,0:T(8,128)(2,1)S(1)}, bf16[1,144,1536]{2,1,0:T(8,128)(2,1)S(1)}, f32[8,128]{1,0:T(8,128)S(1)}) custom-call(bf16[2,128,512]{2,1,0:T(8,128)(2,1)S(1)} %collective-permute-done.2.lines_ref.next_ref, bf16[2,16,512]{2,1,0:T(8,128)(2,1)S(1)} %collective-permute-done.3.edge_ref.next_edge_ref, ...), custom_call_target="tpu_custom_call" | custom-call | flops 301989888 | bytes 2097152 | tf_op jit(solution)/shard_map/deconv_next/pallas_call | solution.py:360
  13.9 2.4 %collective-permute-start.5 = (f32[8,128]{1,0:T(8,128)S(1)}, f32[8,128]{1,0:T(8,128)S(1)}, u32[]{:S(2)}, u32[]{:S(2)}) collective-permute-start(f32[8,128]{1,0:T(8,128)S(1)} %get-tuple-element.31), channel_id=1, source_target_pairs={{0,1},{2,3},{4,5},{6,7},{8,9},{10,11},{12,13},{14,15},{16,17},{18,... | collective-permute-start | bytes 12296 | tf_op jit(solution)/shard_map/ppermute | solution.py:283
  16.3 0.8 %collective-permute-done.5 = f32[8,128]{1,0:T(8,128)S(1)} collective-permute-done((f32[8,128]{1,0:T(8,128)S(1)}, f32[8,128]{1,0:T(8,128)S(1)}, u32[]{:S(2)}, u32[]{:S(2)}) %collective-permute-start.5) | collective-permute-done | bytes 4128 | tf_op jit(solution)/shard_map/ppermute | solution.py:283
  17.1 0.6 %collective-permute-start.6 = (f32[8,128]{1,0:T(8,128)S(1)}, f32[8,128]{1,0:T(8,128)S(1)}, u32[]{:S(2)}, u32[]{:S(2)}) collective-permute-start(f32[8,128]{1,0:T(8,128)S(1)} %add.12), channel_id=1, source_target_pairs={{1,5},{3,7},{5,1},{7,3},{9,13},{11,15},{13,9},{15,11},{17,21},{19,... | collective-permute-start | bytes 12296 | tf_op jit(solution)/shard_map/ppermute | solution.py:288
  17.8 0.7 %collective-permute-start.7 = (f32[8,128]{1,0:T(8,128)S(1)}, f32[8,128]{1,0:T(8,128)S(1)}, u32[]{:S(2)}, u32[]{:S(2)}) collective-permute-start(f32[8,128]{1,0:T(8,128)S(1)} %add.13), channel_id=1, source_target_pairs={{1,9},{3,11},{5,13},{7,15},{9,1},{11,3},{13,5},{15,7},{17,25},{19,... | collective-permute-start | bytes 12296 | tf_op jit(solution)/shard_map/ppermute | solution.py:288
  18.5 0.7 %collective-permute-start.8 = (f32[8,128]{1,0:T(8,128)S(1)}, f32[8,128]{1,0:T(8,128)S(1)}, u32[]{:S(2)}, u32[]{:S(2)}) collective-permute-start(f32[8,128]{1,0:T(8,128)S(1)} %add.14), channel_id=1, source_target_pairs={{1,3},{3,1},{5,7},{7,5},{9,11},{11,9},{13,15},{15,13},{17,19},{19,... | collective-permute-start | bytes 12296 | tf_op jit(solution)/shard_map/ppermute | solution.py:288
  19.1 0.0 copy-start.2
  19.2 0.0 copy-start.3
  19.2 0.0 copy-start.4
  19.2 0.0 copy-start.5
  19.2 1.2 %deconv_halo.1.halo_ref = bf16[4,2,144,256]{3,2,1,0:T(8,128)(2,1)S(1)} custom-call(bf16[2,144,512]{2,1,0:T(8,128)(2,1)S(1)} %collective-permute-done.4.above_ref, bf16[2,128,512]{2,1,0:T(8,128)(2,1)S(1)} %collective-permute-done.2.lines_ref.next_ref, bf16[2,16,512]{2,1,0:T(8,128)(2,1)S(1)} %collective-permute-done.3.edge_ref.next_edge_ref, ...), custom_call_target="tpu_custom_call" | custom-call | flops 1207959552 | bytes 2097152 | tf_op jit(solution)/shard_map/deconv_halo/pallas_call | solution.py:368
  20.5 1.3 %collective-permute-start.9 = (f32[8,128]{1,0:T(8,128)S(1)}, f32[8,128]{1,0:T(8,128)S(1)}, u32[]{:S(2)}, u32[]{:S(2)}) collective-permute-start(f32[8,128]{1,0:T(8,128)S(1)} %add.15.mine_ref), channel_id=1, source_target_pairs={{1,0},{3,2},{5,4},{7,6},{9,8},{11,10},{13,12},{15,14},{17,16},{19,... | collective-permute-start | bytes 12296 | tf_op jit(solution)/shard_map/ppermute | solution.py:289
  21.9 12.8 %collective-permute-done.9.passed_ref = f32[8,128]{1,0:T(8,128)S(1)} collective-permute-done((f32[8,128]{1,0:T(8,128)S(1)}, f32[8,128]{1,0:T(8,128)S(1)}, u32[]{:S(2)}, u32[]{:S(2)}) %collective-permute-start.9) | collective-permute-done | bytes 4128 | tf_op jit(solution)/shard_map/ppermute | solution.py:289
  34.7 4.8 %convs.1 = bf16[4,256,256]{2,1,0:T(8,128)(2,1)} custom-call(bf16[2,2,144,256]{3,2,1,0:T(8,128)(2,1)S(1)} %get-tuple-element.24.u_ref, bf16[2,2,144,256]{3,2,1,0:T(8,128)(2,1)S(1)} %get-tuple-element.27.u_next_ref, bf16[4,2,144,256]{3,2,1,0:T(8,128)(2,1)S(1)} %deconv_halo.1.halo_ref, f32[8,128]{1,0:T(8,128)S(1)} %add.15.mine_ref, ...), custom_call_target="tpu_custom_call" | custom-call | flops 5000000000 | bytes 2097152 | tf_op jit(solution)/shard_map/convs/pallas_call | solution.py:379
  (26 shorter events, 0.1 us)
Async XLA Ops:
  0.0 12.1 %collective-permute-start.1 = (bf16[4,4,512,128]{3,2,1,0:T(8,128)(2,1)}, bf16[4,4,512,128]{3,2,1,0:T(8,128)(2,1)S(1)}, u32[]{:S(2)}, u32[]{:S(2)}) collective-permute-start(bf16[4,4,512,128]{3,2,1,0:T(8,128)(2,1)} %param.9), channel_id=1, source_target_pairs={{0,1},{1,0},{2,3},{3,2},{4,5},{5,4},{6,7},{7,6},{8,9},{9,8},{10,11... | collective-permute-start | bytes 6291464 | tf_op jit(solution)/shard_map/ppermute | solution.py:335
  0.5 11.6 %collective-permute-start.2 = (bf16[2,128,512]{2,1,0:T(8,128)(2,1)}, bf16[2,128,512]{2,1,0:T(8,128)(2,1)S(1)}, u32[]{:S(2)}, u32[]{:S(2)}) collective-permute-start(bf16[2,128,512]{2,1,0:T(8,128)(2,1)} %image_ref.1), channel_id=1, source_target_pairs={{2,0},{4,2},{6,4},{8,6},{10,8},{12,10},{14,12},{3,1},{5,3},{7,5},{... | collective-permute-start | bytes 786440 | tf_op jit(solution)/shard_map/ppermute | solution.py:326
  2.8 2.3 %collective-permute-start = (bf16[2,16,512]{2,1,0:T(8,128)(2,1)S(1)}, bf16[2,16,512]{2,1,0:T(8,128)(2,1)S(1)}, u32[]{:S(2)}, u32[]{:S(2)}) collective-permute-start(bf16[2,16,512]{2,1,0:T(8,128)(2,1)S(1)} %get-tuple-element.21), channel_id=1, source_target_pairs={{0,1},{1,0},{2,3},{3,2},{4,5},{5,4},{6,7},{7,6},{8,9},{9,8},{10,11... | collective-permute-start | bytes 98312 | tf_op jit(solution)/shard_map/ppermute | solution.py:334
  2.9 18.9 %collective-permute-start.10 = (bf16[3,3,256,128]{3,2,1,0:T(8,128)(2,1)}, bf16[3,3,256,128]{3,2,1,0:T(8,128)(2,1)S(1)}, u32[]{:S(2)}, u32[]{:S(2)}) collective-permute-start(bf16[3,3,256,128]{3,2,1,0:T(8,128)(2,1)} %own_w1.1), channel_id=1, source_target_pairs={{0,1},{1,0},{2,3},{3,2},{4,5},{5,4},{6,7},{7,6},{8,9},{9,8},{10,11... | collective-permute-start | bytes 1769480 | tf_op jit(solution)/shard_map/ppermute | solution.py:336
  3.4 18.5 %collective-permute-start.11 = (bf16[3,3,256,128]{3,2,1,0:T(8,128)(2,1)}, bf16[3,3,256,128]{3,2,1,0:T(8,128)(2,1)S(1)}, u32[]{:S(2)}, u32[]{:S(2)}) collective-permute-start(bf16[3,3,256,128]{3,2,1,0:T(8,128)(2,1)} %own_w2.1), channel_id=1, source_target_pairs={{0,1},{1,0},{2,3},{3,2},{4,5},{5,4},{6,7},{7,6},{8,9},{9,8},{10,11... | collective-permute-start | bytes 1769480 | tf_op jit(solution)/shard_map/ppermute | solution.py:337
  5.1 14.0 %collective-permute-start.4 = (bf16[2,144,512]{2,1,0:T(8,128)(2,1)S(1)}, bf16[2,144,512]{2,1,0:T(8,128)(2,1)S(1)}, u32[]{:S(2)}, u32[]{:S(2)}) collective-permute-start(bf16[2,144,512]{2,1,0:T(8,128)(2,1)S(1)} %constant_dynamic-update-slice_fusion.lines_ref), channel_id=1, source_target_pairs={{0,2},{2,4},{4,6},{6,8},{8,10},{10,12},{12,14},{1,3},{3,5},{5,7},{... | collective-permute-start | bytes 884744 | tf_op jit(solution)/shard_map/ppermute | solution.py:342
  12.1 1.3 %collective-permute-start.3 = (bf16[2,16,512]{2,1,0:T(8,128)(2,1)S(1)}, bf16[2,16,512]{2,1,0:T(8,128)(2,1)S(1)}, u32[]{:S(2)}, u32[]{:S(2)}) collective-permute-start(bf16[2,16,512]{2,1,0:T(8,128)(2,1)S(1)} %next_edges.1), channel_id=1, source_target_pairs={{0,1},{1,0},{2,3},{3,2},{4,5},{5,4},{6,7},{7,6},{8,9},{9,8},{10,11... | collective-permute-start | bytes 98312 | tf_op jit(solution)/shard_map/ppermute | solution.py:359
  13.9 3.2 %collective-permute-start.5 = (f32[8,128]{1,0:T(8,128)S(1)}, f32[8,128]{1,0:T(8,128)S(1)}, u32[]{:S(2)}, u32[]{:S(2)}) collective-permute-start(f32[8,128]{1,0:T(8,128)S(1)} %get-tuple-element.31), channel_id=1, source_target_pairs={{0,1},{2,3},{4,5},{6,7},{8,9},{10,11},{12,13},{14,15},{16,17},{18,... | collective-permute-start | bytes 12296 | tf_op jit(solution)/shard_map/ppermute | solution.py:283
  17.1 0.7 %collective-permute-start.6 = (f32[8,128]{1,0:T(8,128)S(1)}, f32[8,128]{1,0:T(8,128)S(1)}, u32[]{:S(2)}, u32[]{:S(2)}) collective-permute-start(f32[8,128]{1,0:T(8,128)S(1)} %add.12), channel_id=1, source_target_pairs={{1,5},{3,7},{5,1},{7,3},{9,13},{11,15},{13,9},{15,11},{17,21},{19,... | collective-permute-start | bytes 12296 | tf_op jit(solution)/shard_map/ppermute | solution.py:288
  17.8 0.7 %collective-permute-start.7 = (f32[8,128]{1,0:T(8,128)S(1)}, f32[8,128]{1,0:T(8,128)S(1)}, u32[]{:S(2)}, u32[]{:S(2)}) collective-permute-start(f32[8,128]{1,0:T(8,128)S(1)} %add.13), channel_id=1, source_target_pairs={{1,9},{3,11},{5,13},{7,15},{9,1},{11,3},{13,5},{15,7},{17,25},{19,... | collective-permute-start | bytes 12296 | tf_op jit(solution)/shard_map/ppermute | solution.py:288
  18.5 2.0 %collective-permute-start.8 = (f32[8,128]{1,0:T(8,128)S(1)}, f32[8,128]{1,0:T(8,128)S(1)}, u32[]{:S(2)}, u32[]{:S(2)}) collective-permute-start(f32[8,128]{1,0:T(8,128)S(1)} %add.14), channel_id=1, source_target_pairs={{1,3},{3,1},{5,7},{7,5},{9,11},{11,9},{13,15},{15,13},{17,19},{19,... | collective-permute-start | bytes 12296 | tf_op jit(solution)/shard_map/ppermute | solution.py:288
  19.1 2.6 %copy-start.2 = (f32[256]{0:T(256)S(1)}, f32[256]{0:T(256)}, u32[]{:S(2)}) copy-start(f32[256]{0:T(256)} %param.15) | copy-start | bytes 3076
  19.2 2.6 %copy-start.3 = (f32[256]{0:T(256)S(1)}, f32[256]{0:T(256)}, u32[]{:S(2)}) copy-start(f32[256]{0:T(256)} %param.13) | copy-start | bytes 3076
  19.2 2.6 %copy-start.4 = (f32[256]{0:T(256)S(1)}, f32[256]{0:T(256)}, u32[]{:S(2)}) copy-start(f32[256]{0:T(256)} %param.11) | copy-start | bytes 3076
  19.2 2.6 %copy-start.5 = (f32[256]{0:T(256)S(1)}, f32[256]{0:T(256)}, u32[]{:S(2)}) copy-start(f32[256]{0:T(256)} %param.10) | copy-start | bytes 3076
  19.2 15.5 %copy-start = (bf16[3,3,256,128]{3,2,1,0:T(8,128)(2,1)S(1)}, bf16[3,3,256,128]{3,2,1,0:T(8,128)(2,1)}, u32[]{:S(2)}) copy-start(bf16[3,3,256,128]{3,2,1,0:T(8,128)(2,1)} %own_w1.1) | copy-start | bytes 1769476
  19.2 15.5 %copy-start.1 = (bf16[3,3,256,128]{3,2,1,0:T(8,128)(2,1)S(1)}, bf16[3,3,256,128]{3,2,1,0:T(8,128)(2,1)}, u32[]{:S(2)}) copy-start(bf16[3,3,256,128]{3,2,1,0:T(8,128)(2,1)} %own_w2.1) | copy-start | bytes 1769476
  20.5 14.2 %collective-permute-start.9 = (f32[8,128]{1,0:T(8,128)S(1)}, f32[8,128]{1,0:T(8,128)S(1)}, u32[]{:S(2)}, u32[]{:S(2)}) collective-permute-start(f32[8,128]{1,0:T(8,128)S(1)} %add.15.mine_ref), channel_id=1, source_target_pairs={{1,0},{3,2},{5,4},{7,6},{9,8},{11,10},{13,12},{15,14},{17,16},{19,... | collective-permute-start | bytes 12296 | tf_op jit(solution)/shard_map/ppermute | solution.py:289

commit v10 on v9

--- a/solution.py
+++ b/solution.py
@@ -60,10 +60,10 @@
     copy.wait()
 
 
-def spread_line(out, main, edge):
+def spread_line(out, main, edge, inside=True):
     width, cin = main.shape
     line = jnp.concatenate([main.astype(jnp.float32), edge.astype(jnp.float32)], axis=0)
-    line = jnp.where(edge_mask(width), line, 0.0)
+    line = jnp.where(edge_mask(width) & inside, line, 0.0)
     out[:, 0:cin] = pltpu.roll(line, width + EDGE - 1, 0).astype(jnp.bfloat16)
     out[:, cin : 2 * cin] = line.astype(jnp.bfloat16)
     out[:, 2 * cin : 3 * cin] = pltpu.roll(line, 1, 0).astype(jnp.bfloat16)
@@ -119,8 +119,8 @@
 
 def next_kernel(next_ref, edge_ref, tail_ref, sums_ref, own_w, other_w, u_ref, xs_ref, stats_ref):
     width = next_ref.shape[1]
-    spread_line(xs_ref.at[0], next_ref[0], edge_ref[0])
     last_here = lax.axis_index("rows") == lax.axis_size("rows") - 1
+    spread_line(xs_ref.at[0], next_ref[0], edge_ref[0], jnp.logical_not(last_here))
     column = lax.axis_index("fsdp")
     sums = sums_ref[...]
     for phase in range(2):
@@ -140,9 +140,10 @@
 
 def halo_kernel(above_ref, next_ref, next_edge_ref, xs_ref, xs_next_ref, part_ref, own_w, other_w, u_ref, xs_above, xs_below):
     width = next_ref.shape[1]
+    place = lax.axis_index("rows")
     for row in range(HALO):
-        spread_line(xs_above.at[row], above_ref[row, :width], above_ref[row, width:])
-    spread_line(xs_below.at[0], next_ref[1], next_edge_ref[1])
+        spread_line(xs_above.at[row], above_ref[row, :width], above_ref[row, width:], place > 0)
+    spread_line(xs_below.at[0], next_ref[1], next_edge_ref[1], place < lax.axis_size("rows") - 1)
     for phase in range(2):
         dot = functools.partial(tap_dot, phase=phase, own_w=own_w, other_w=other_w)
         outer = dot(xs_above[...], kr=3)
@@ -173,7 +174,7 @@
 
 
 def conv_kernel(
-    count, u_ref, u_next_ref, halo_ref, mine_ref, passed_ref, params_ref, own_w1, other_w1, own_w2, other_w2, out_ref, g, act, mixed
+    count, u_ref, u_next_ref, halo_ref, stats_ref, params_ref, own_w1, other_w1, own_w2, other_w2, out_ref, g, act, mixed
 ):
     early, _, total, cout = u_ref.shape
     main = early + u_next_ref.shape[0]
@@ -197,7 +198,7 @@
             axis=1,
         )
 
-    block = jnp.where(column == 1, mine_ref[...], passed_ref[...])
+    block = stats_ref[...]
     width_group = cout // NORM_GROUPS
     sums = jnp.concatenate([block[0:1], block[1:2]], axis=1)
     squares = jnp.concatenate([block[2:3], block[3:4]], axis=1)
@@ -278,15 +279,14 @@
             second(start - chunk)
 
 
-def total_over(block, last):
-    size = lax.axis_size("rows")
-    block = block + lax.ppermute(block, "fsdp", [(0, 1)])
-    assert size & (size - 1) == 0
+def total_over(block, axis):
+    size = lax.axis_size(axis)
+    if size & (size - 1):
+        return lax.psum(block, axis)
     steps = [2**n for n in range(size.bit_length() - 1)]
     for step in steps[1:] + steps[:1]:
-        pairs = [(2 * i + 1, 2 * (i ^ step) + 1) for i in range(size)]
-        block = block + lax.ppermute(block, ("rows", "fsdp"), pairs)
-    return block, lax.ppermute(after(block, last), "fsdp", [(1, 0)])
+        block = block + lax.ppermute(block, axis, [(i, i ^ step) for i in range(size)])
+    return block
 
 
 def after(value, *others):
@@ -302,8 +302,8 @@
     n_rows = lax.axis_size("rows")
     count = float(2 * rows * n_rows * 2 * width * columns * (cout // NORM_GROUPS))
     swap = [(0, 1), (1, 0)]
-    to_next = [(i, i + 1) for i in range(n_rows - 1)]
-    to_previous = [(i + 1, i) for i in range(n_rows - 1)]
+    to_next = [(i, (i + 1) % n_rows) for i in range(n_rows)]
+    to_previous = [((i + 1) % n_rows, i) for i in range(n_rows)]
     total = width + EDGE
     hbm = pl.BlockSpec(memory_space=pltpu.HBM)
     vmem = pl.BlockSpec(memory_space=pltpu.VMEM)
@@ -374,11 +374,11 @@
         flops=2 * 2 * 4 * total * 4 * cin * cout,
     )(above, following, next_edge, xs, xs_next, part, own_w, other_w)
 
-    mine, passed = total_over(stats, halo)
+    totals = total_over(total_over(stats, "fsdp"), "rows")
     params = jnp.stack([norm_gain, norm_shift, first_bias, second_bias])
     (out,) = call(
         functools.partial(conv_kernel, count),
-        [vmem] * 10,
+        [vmem] * 9,
         [((2 * rows, 2 * width, cout), bf16)],
         [
             pltpu.VMEM((2 * rows + 2 * HALO, total, 4 * cout), bf16),
@@ -387,7 +387,7 @@
         ],
         "convs",
         flops=5 * 10**9,
-    )(u, u_next, halo, mine, passed, params, first_weight, first_other, second_weight, second_other)
+    )(u, u_next, halo, totals, params, first_weight, first_other, second_weight, second_other)
     return out
 
 

time: 39.8 us -> 36.4 us (0.915)
  waiting for transfers between devices: 15.1 us -> 9.28 us
  starting transfers between devices: 13.5 us -> 16.2 us
    ppermute x5 -> x4, waiting for transfers between devices: 13.6 us -> 6.28 us  [total_over(): lax.ppermute(block, axis, [(i, i ^ step) for i in range(size)])]
    ppermute x1, starting transfers between devices: 5.46 us -> 0.06 us  [local(): above = lax.ppermute(lines, 'rows', to_next)]
    ppermute x1, starting transfers between devices: 1.28 us -> 5.55 us  [local(): following = lax.ppermute(image, 'rows', to_previous)]
    ppermute x5 -> x4, starting transfers between devices: 5.67 us -> 9.32 us  [total_over(): lax.ppermute(block, axis, [(i, i ^ step) for i in range(size)])]
    ppermute x1, waiting for transfers between devices: 1.46 us -> 2.98 us  [local(): following = lax.ppermute(image, 'rows', to_previous)]
  transfers between devices with their start and end apart: 12 -> 11, of which waited for: 3 -> 5; matrix products, arithmetic and copies ran while one was open for 0% -> 0% of each run, Pallas kernels for 14% -> 16%
where the time goes in v10:
time: 36.4 us; the launch traced here: 36.2 us
  starting transfers between devices  16.2 us (45%)
  Pallas kernels  10.5 us (29%)
  waiting for transfers between devices  9.28 us (25%)
    ppermute x4, starting transfers between devices, total_over(): lax.ppermute(block, axis, [(i, i ^ step) for i in range(size)])  9.32 us
    ppermute x4, waiting for transfers between devices, total_over(): lax.ppermute(block, axis, [(i, i ^ step) for i in range(size)])  6.28 us
    ppermute x1, starting transfers between devices, local(): following = lax.ppermute(image, 'rows', to_previous)  5.55 us
    pallas_call x1, Pallas kernels, local(): call(functools.partial(conv_kernel, count), [vmem] * 9, [((2 * rows, 2 *...  4.82 us
    ppermute x1, waiting for transfers between devices, local(): following = lax.ppermute(image, 'rows', to_previous)  2.98 us
    pallas_call x1, Pallas kernels, local(): call(near_kernel, [hbm], [(shape_w, bf16)], [pltpu.SemaphoreType.DMA(())]...  1.6 us
    pallas_call x1, Pallas kernels, local(): call(own_kernel, [vmem] * 3, [((rows, total, 3 * cin), bf16), ((2 * rows...  1.26 us
    pallas_call x1, Pallas kernels, local(): call(halo_kernel, [vmem] * 8, [((4, *u_line), bf16)], [pltpu.VMEM((HALO,...  1.24 us
  transfers between devices with their start and end apart: 11, of which 5 were waited for; matrix products, arithmetic and copies ran while one was open for 0% of the time, Pallas kernels for 16%

profile of v10, /device:TPU:0, one launch (start us, length us, event | category | flops | bytes accessed | tf_op | source)
XLA Modules:
  0.0 36.2 jit_solution(4901813403916909828)
XLA Ops:
  0.0 0.5 %collective-permute-start.1 = (bf16[4,4,512,128]{3,2,1,0:T(8,128)(2,1)}, bf16[4,4,512,128]{3,2,1,0:T(8,128)(2,1)S(1)}, u32[]{:S(2)}, u32[]{:S(2)}) collective-permute-start(bf16[4,4,512,128]{3,2,1,0:T(8,128)(2,1)} %param.9), channel_id=1, source_target_pairs={{0,1},{1,0},{2,3},{3,2},{4,5},{5,4},{6,7},{7,6},{8,9},{9,8},{10,11... | collective-permute-start | bytes 6291464 | tf_op jit(solution)/shard_map/ppermute | solution.py:335
  0.5 5.6 %collective-permute-start.2 = (bf16[2,128,512]{2,1,0:T(8,128)(2,1)}, bf16[2,128,512]{2,1,0:T(8,128)(2,1)S(1)}, u32[]{:S(2)}, u32[]{:S(2)}) collective-permute-start(bf16[2,128,512]{2,1,0:T(8,128)(2,1)} %image_ref.1), channel_id=1, source_target_pairs={{2,0},{4,2},{6,4},{8,6},{10,8},{12,10},{14,12},{0,14},{3,1},{5,3},... | collective-permute-start | bytes 786440 | tf_op jit(solution)/shard_map/ppermute | solution.py:326
  6.0 1.0 %cut.1 = (bf16[2,128,512]{2,1,0:T(8,128)(2,1)S(1)}, bf16[2,16,512]{2,1,0:T(8,128)(2,1)S(1)}) custom-call(bf16[2,128,512]{2,1,0:T(8,128)(2,1)} %image_ref.1), custom_call_target="tpu_custom_call" | custom-call | bytes 2097152 | tf_op jit(solution)/shard_map/cut/pallas_call | solution.py:327
  7.1 0.3 collective-permute-start
  7.3 0.3 collective-permute-start.10
  7.6 0.2 collective-permute-start.9
  7.9 1.6 %near_weights.1.own_w = bf16[4,2,2,512,128]{4,3,2,1,0:T(8,128)(2,1)S(1)} custom-call(bf16[4,2,2,512,128]{4,3,2,1,0:T(8,128)(2,1)} %bitcast.9), custom_call_target="tpu_custom_call" | custom-call | bytes 2097152 | tf_op jit(solution)/shard_map/near_weights/pallas_call | solution.py:338
  9.5 0.1 collective-permute-start.4
  9.6 3.0 %collective-permute-done.2.lines_ref.next_ref = bf16[2,128,512]{2,1,0:T(8,128)(2,1)S(1)} collective-permute-done((bf16[2,128,512]{2,1,0:T(8,128)(2,1)}, bf16[2,128,512]{2,1,0:T(8,128)(2,1)S(1)}, u32[]{:S(2)}, u32[]{:S(2)}) %collective-permute-start.2) | collective-permute-done | bytes 262176 | tf_op jit(solution)/shard_map/ppermute | solution.py:326
  12.6 1.3 %deconv_own.1 = (bf16[2,144,1536]{2,1,0:T(8,128)(2,1)S(1)}, bf16[2,2,144,256]{3,2,1,0:T(8,128)(2,1)S(1)}, f32[2,144,256]{2,1,0:T(8,128)S(1)}, f32[2,2,144,256]{3,2,1,0:T(8,128)S(1)}, f32[2,256]{1,0:T(2,128)S(1)}) custom-call(bf16[2,144,512]{2,1,0:T(8,128)(2,1)S(1)} %constant_dynamic-update-slice_fusion.lines_ref, ...), custom_call_target="tpu_custom_call" | custom-call | flops 905969664 | bytes 2097152 | tf_op jit(solution)/shard_map/deconv_own/pallas_call | solution.py:344
  13.9 0.0 copy-start.3
  13.9 0.0 copy-start.4
  13.9 0.5 %deconv_next.1 = (bf16[2,2,144,256]{3,2,1,0:T(8,128)(2,1)S(1)}, bf16[1,144,1536]{2,1,0:T(8,128)(2,1)S(1)}, f32[8,128]{1,0:T(8,128)S(1)}) custom-call(bf16[2,128,512]{2,1,0:T(8,128)(2,1)S(1)} %collective-permute-done.2.lines_ref.next_ref, bf16[2,16,512]{2,1,0:T(8,128)(2,1)S(1)} %collective-permute-done.3.edge_ref.next_edge_ref, ...), custom_call_target="tpu_custom_call" | custom-call | flops 301989888 | bytes 2097152 | tf_op jit(solution)/shard_map/deconv_next/pallas_call | solution.py:360
  14.4 0.6 %collective-permute-start.5 = (f32[8,128]{1,0:T(8,128)S(1)}, f32[8,128]{1,0:T(8,128)S(1)}, u32[]{:S(2)}, u32[]{:S(2)}) collective-permute-start(f32[8,128]{1,0:T(8,128)S(1)} %get-tuple-element.30), channel_id=1, source_target_pairs={{0,1},{1,0},{2,3},{3,2},{4,5},{5,4},{6,7},{7,6},{8,9},{9,8},{10,11... | collective-permute-start | bytes 12296 | tf_op jit(solution)/shard_map/ppermute | solution.py:288
  15.0 0.8 %collective-permute-done.5 = f32[8,128]{1,0:T(8,128)S(1)} collective-permute-done((f32[8,128]{1,0:T(8,128)S(1)}, f32[8,128]{1,0:T(8,128)S(1)}, u32[]{:S(2)}, u32[]{:S(2)}) %collective-permute-start.5) | collective-permute-done | bytes 4128 | tf_op jit(solution)/shard_map/ppermute | solution.py:288
  15.8 5.7 %collective-permute-start.6 = (f32[8,128]{1,0:T(8,128)S(1)}, f32[8,128]{1,0:T(8,128)S(1)}, u32[]{:S(2)}, u32[]{:S(2)}) collective-permute-start(f32[8,128]{1,0:T(8,128)S(1)} %add.12), channel_id=1, source_target_pairs={{0,4},{2,6},{4,0},{6,2},{8,12},{10,14},{12,8},{14,10},{1,5},{3,7},... | collective-permute-start | bytes 12296 | tf_op jit(solution)/shard_map/ppermute | solution.py:288
  21.5 1.6 %collective-permute-done.6 = f32[8,128]{1,0:T(8,128)S(1)} collective-permute-done((f32[8,128]{1,0:T(8,128)S(1)}, f32[8,128]{1,0:T(8,128)S(1)}, u32[]{:S(2)}, u32[]{:S(2)}) %collective-permute-start.6) | collective-permute-done | bytes 4128 | tf_op jit(solution)/shard_map/ppermute | solution.py:288
  23.1 3.0 %collective-permute-start.7 = (f32[8,128]{1,0:T(8,128)S(1)}, f32[8,128]{1,0:T(8,128)S(1)}, u32[]{:S(2)}, u32[]{:S(2)}) collective-permute-start(f32[8,128]{1,0:T(8,128)S(1)} %add.13), channel_id=1, source_target_pairs={{0,8},{2,10},{4,12},{6,14},{8,0},{10,2},{12,4},{14,6},{1,9},{3,11}... | collective-permute-start | bytes 12296 | tf_op jit(solution)/shard_map/ppermute | solution.py:288
  26.2 1.6 %collective-permute-done.7 = f32[8,128]{1,0:T(8,128)S(1)} collective-permute-done((f32[8,128]{1,0:T(8,128)S(1)}, f32[8,128]{1,0:T(8,128)S(1)}, u32[]{:S(2)}, u32[]{:S(2)}) %collective-permute-start.7) | collective-permute-done | bytes 4128 | tf_op jit(solution)/shard_map/ppermute | solution.py:288
  27.8 0.0 copy-start
  27.8 0.0 copy-start.1
  27.8 1.2 %deconv_halo.1.halo_ref = bf16[4,2,144,256]{3,2,1,0:T(8,128)(2,1)S(1)} custom-call(bf16[2,144,512]{2,1,0:T(8,128)(2,1)S(1)} %collective-permute-done.4.above_ref, bf16[2,128,512]{2,1,0:T(8,128)(2,1)S(1)} %collective-permute-done.2.lines_ref.next_ref, bf16[2,16,512]{2,1,0:T(8,128)(2,1)S(1)} %collective-permute-done.3.edge_ref.next_edge_ref, ...), custom_call_target="tpu_custom_call" | custom-call | flops 1207959552 | bytes 2097152 | tf_op jit(solution)/shard_map/deconv_halo/pallas_call | solution.py:368
  29.0 2.3 %collective-permute-done.8 = f32[8,128]{1,0:T(8,128)S(1)} collective-permute-done((f32[8,128]{1,0:T(8,128)S(1)}, f32[8,128]{1,0:T(8,128)S(1)}, u32[]{:S(2)}, u32[]{:S(2)}) %collective-permute-start.8) | collective-permute-done | bytes 4128 | tf_op jit(solution)/shard_map/ppermute | solution.py:288
  31.4 4.8 %convs.1 = bf16[4,256,256]{2,1,0:T(8,128)(2,1)} custom-call(bf16[2,2,144,256]{3,2,1,0:T(8,128)(2,1)S(1)} %get-tuple-element.23.u_ref, bf16[2,2,144,256]{3,2,1,0:T(8,128)(2,1)S(1)} %get-tuple-element.26.u_next_ref, bf16[4,2,144,256]{3,2,1,0:T(8,128)(2,1)S(1)} %deconv_halo.1.halo_ref, f32[8,128]{1,0:T(8,128)S(1)} %add.15.stats_ref, ...), custom_call_target="tpu_custom_call" | custom-call | flops 5000000000 | bytes 2097152 | tf_op jit(solution)/shard_map/convs/pallas_call | solution.py:379
  (24 shorter events, 0.1 us)
Async XLA Ops:
  0.0 12.6 %collective-permute-start.1 = (bf16[4,4,512,128]{3,2,1,0:T(8,128)(2,1)}, bf16[4,4,512,128]{3,2,1,0:T(8,128)(2,1)S(1)}, u32[]{:S(2)}, u32[]{:S(2)}) collective-permute-start(bf16[4,4,512,128]{3,2,1,0:T(8,128)(2,1)} %param.9), channel_id=1, source_target_pairs={{0,1},{1,0},{2,3},{3,2},{4,5},{5,4},{6,7},{7,6},{8,9},{9,8},{10,11... | collective-permute-start | bytes 6291464 | tf_op jit(solution)/shard_map/ppermute | solution.py:335
  0.5 12.1 %collective-permute-start.2 = (bf16[2,128,512]{2,1,0:T(8,128)(2,1)}, bf16[2,128,512]{2,1,0:T(8,128)(2,1)S(1)}, u32[]{:S(2)}, u32[]{:S(2)}) collective-permute-start(bf16[2,128,512]{2,1,0:T(8,128)(2,1)} %image_ref.1), channel_id=1, source_target_pairs={{2,0},{4,2},{6,4},{8,6},{10,8},{12,10},{14,12},{0,14},{3,1},{5,3},... | collective-permute-start | bytes 786440 | tf_op jit(solution)/shard_map/ppermute | solution.py:326
  7.1 2.4 %collective-permute-start = (bf16[2,16,512]{2,1,0:T(8,128)(2,1)S(1)}, bf16[2,16,512]{2,1,0:T(8,128)(2,1)S(1)}, u32[]{:S(2)}, u32[]{:S(2)}) collective-permute-start(bf16[2,16,512]{2,1,0:T(8,128)(2,1)S(1)} %get-tuple-element.20), channel_id=1, source_target_pairs={{0,1},{1,0},{2,3},{3,2},{4,5},{5,4},{6,7},{7,6},{8,9},{9,8},{10,11... | collective-permute-start | bytes 98312 | tf_op jit(solution)/shard_map/ppermute | solution.py:334
  7.3 24.0 %collective-permute-start.10 = (bf16[3,3,256,128]{3,2,1,0:T(8,128)(2,1)}, bf16[3,3,256,128]{3,2,1,0:T(8,128)(2,1)S(1)}, u32[]{:S(2)}, u32[]{:S(2)}) collective-permute-start(bf16[3,3,256,128]{3,2,1,0:T(8,128)(2,1)} %own_w2.1), channel_id=1, source_target_pairs={{0,1},{1,0},{2,3},{3,2},{4,5},{5,4},{6,7},{7,6},{8,9},{9,8},{10,11... | collective-permute-start | bytes 1769480 | tf_op jit(solution)/shard_map/ppermute | solution.py:337
  7.6 23.7 %collective-permute-start.9 = (bf16[3,3,256,128]{3,2,1,0:T(8,128)(2,1)}, bf16[3,3,256,128]{3,2,1,0:T(8,128)(2,1)S(1)}, u32[]{:S(2)}, u32[]{:S(2)}) collective-permute-start(bf16[3,3,256,128]{3,2,1,0:T(8,128)(2,1)} %own_w1.1), channel_id=1, source_target_pairs={{0,1},{1,0},{2,3},{3,2},{4,5},{5,4},{6,7},{7,6},{8,9},{9,8},{10,11... | collective-permute-start | bytes 1769480 | tf_op jit(solution)/shard_map/ppermute | solution.py:336
  9.5 18.3 %collective-permute-start.4 = (bf16[2,144,512]{2,1,0:T(8,128)(2,1)S(1)}, bf16[2,144,512]{2,1,0:T(8,128)(2,1)S(1)}, u32[]{:S(2)}, u32[]{:S(2)}) collective-permute-start(bf16[2,144,512]{2,1,0:T(8,128)(2,1)S(1)} %constant_dynamic-update-slice_fusion.lines_ref), channel_id=1, source_target_pairs={{0,2},{2,4},{4,6},{6,8},{8,10},{10,12},{12,14},{14,0},{1,3},{3,5},... | collective-permute-start | bytes 884744 | tf_op jit(solution)/shard_map/ppermute | solution.py:342
  12.6 1.3 %collective-permute-start.3 = (bf16[2,16,512]{2,1,0:T(8,128)(2,1)S(1)}, bf16[2,16,512]{2,1,0:T(8,128)(2,1)S(1)}, u32[]{:S(2)}, u32[]{:S(2)}) collective-permute-start(bf16[2,16,512]{2,1,0:T(8,128)(2,1)S(1)} %next_edges.1), channel_id=1, source_target_pairs={{0,1},{1,0},{2,3},{3,2},{4,5},{5,4},{6,7},{7,6},{8,9},{9,8},{10,11... | collective-permute-start | bytes 98312 | tf_op jit(solution)/shard_map/ppermute | solution.py:359
  13.9 12.3 %copy-start.2 = (f32[256]{0:T(256)S(1)}, f32[256]{0:T(256)}, u32[]{:S(2)}) copy-start(f32[256]{0:T(256)} %param.15) | copy-start | bytes 3076
  13.9 12.3 %copy-start.3 = (f32[256]{0:T(256)S(1)}, f32[256]{0:T(256)}, u32[]{:S(2)}) copy-start(f32[256]{0:T(256)} %param.13) | copy-start | bytes 3076
  13.9 12.3 %copy-start.4 = (f32[256]{0:T(256)S(1)}, f32[256]{0:T(256)}, u32[]{:S(2)}) copy-start(f32[256]{0:T(256)} %param.11) | copy-start | bytes 3076
  13.9 12.3 %copy-start.5 = (f32[256]{0:T(256)S(1)}, f32[256]{0:T(256)}, u32[]{:S(2)}) copy-start(f32[256]{0:T(256)} %param.10) | copy-start | bytes 3076
  14.4 1.4 %collective-permute-start.5 = (f32[8,128]{1,0:T(8,128)S(1)}, f32[8,128]{1,0:T(8,128)S(1)}, u32[]{:S(2)}, u32[]{:S(2)}) collective-permute-start(f32[8,128]{1,0:T(8,128)S(1)} %get-tuple-element.30), channel_id=1, source_target_pairs={{0,1},{1,0},{2,3},{3,2},{4,5},{5,4},{6,7},{7,6},{8,9},{9,8},{10,11... | collective-permute-start | bytes 12296 | tf_op jit(solution)/shard_map/ppermute | solution.py:288
  15.8 7.3 %collective-permute-start.6 = (f32[8,128]{1,0:T(8,128)S(1)}, f32[8,128]{1,0:T(8,128)S(1)}, u32[]{:S(2)}, u32[]{:S(2)}) collective-permute-start(f32[8,128]{1,0:T(8,128)S(1)} %add.12), channel_id=1, source_target_pairs={{0,4},{2,6},{4,0},{6,2},{8,12},{10,14},{12,8},{14,10},{1,5},{3,7},... | collective-permute-start | bytes 12296 | tf_op jit(solution)/shard_map/ppermute | solution.py:288
  23.1 4.6 %collective-permute-start.7 = (f32[8,128]{1,0:T(8,128)S(1)}, f32[8,128]{1,0:T(8,128)S(1)}, u32[]{:S(2)}, u32[]{:S(2)}) collective-permute-start(f32[8,128]{1,0:T(8,128)S(1)} %add.13), channel_id=1, source_target_pairs={{0,8},{2,10},{4,12},{6,14},{8,0},{10,2},{12,4},{14,6},{1,9},{3,11}... | collective-permute-start | bytes 12296 | tf_op jit(solution)/shard_map/ppermute | solution.py:288
  27.8 3.6 %collective-permute-start.8 = (f32[8,128]{1,0:T(8,128)S(1)}, f32[8,128]{1,0:T(8,128)S(1)}, u32[]{:S(2)}, u32[]{:S(2)}) collective-permute-start(f32[8,128]{1,0:T(8,128)S(1)} %add.14), channel_id=1, source_target_pairs={{0,2},{2,0},{4,6},{6,4},{8,10},{10,8},{12,14},{14,12},{1,3},{3,1},... | collective-permute-start | bytes 12296 | tf_op jit(solution)/shard_map/ppermute | solution.py:288
  27.8 3.6 %copy-start = (bf16[3,3,256,128]{3,2,1,0:T(8,128)(2,1)S(1)}, bf16[3,3,256,128]{3,2,1,0:T(8,128)(2,1)}, u32[]{:S(2)}) copy-start(bf16[3,3,256,128]{3,2,1,0:T(8,128)(2,1)} %own_w1.1) | copy-start | bytes 1769476
  27.8 3.6 %copy-start.1 = (bf16[3,3,256,128]{3,2,1,0:T(8,128)(2,1)S(1)}, bf16[3,3,256,128]{3,2,1,0:T(8,128)(2,1)}, u32[]{:S(2)}) copy-start(bf16[3,3,256,128]{3,2,1,0:T(8,128)(2,1)} %own_w2.1) | copy-start | bytes 1769476

commit v11 on v10

--- a/solution.py
+++ b/solution.py
@@ -339,7 +339,7 @@
         in_hbm(after(deconv_weight, edges).reshape(shape_w))
     )
     lines = jnp.concatenate([after(near, own_w), edge], axis=1)
-    above = lax.ppermute(lines, "rows", to_next)
+    above = lax.ppermute(after(lines, following), "rows", to_next)
     u_line = (2, total, cout)
     xs, u, part, tail, sums = call(
         own_kernel,

time: 36.4 us -> 33.9 us (0.931)
  waiting for transfers between devices: 9.28 us -> 7.8 us
  starting transfers between devices: 16.2 us -> 15.2 us
    ppermute x4, waiting for transfers between devices: 6.28 us -> 4.74 us  [total_over(): lax.ppermute(block, axis, [(i, i ^ step) for i in range(size)])]
    ppermute x4, starting transfers between devices: 9.32 us -> 8.2 us  [total_over(): lax.ppermute(block, axis, [(i, i ^ step) for i in range(size)])]
  transfers between devices with their start and end apart: 11 -> 11, of which waited for: 5 -> 5; matrix products, arithmetic and copies ran while one was open for 0% -> 0% of each run, Pallas kernels for 16% -> 17%
where the time goes in v11:
time: 33.9 us; the launch traced here: 33.8 us
  starting transfers between devices  15.2 us (45%)
  Pallas kernels  10.5 us (31%)
  waiting for transfers between devices  7.8 us (23%)
    ppermute x4, starting transfers between devices, total_over(): lax.ppermute(block, axis, [(i, i ^ step) for i in range(size)])  8.2 us
    ppermute x1, starting transfers between devices, local(): following = lax.ppermute(image, 'rows', to_previous)  5.55 us
    pallas_call x1, Pallas kernels, local(): call(functools.partial(conv_kernel, count), [vmem] * 9, [((2 * rows, 2 *...  4.82 us
    ppermute x4, waiting for transfers between devices, total_over(): lax.ppermute(block, axis, [(i, i ^ step) for i in range(size)])  4.74 us
    ppermute x1, waiting for transfers between devices, local(): following = lax.ppermute(image, 'rows', to_previous)  3.04 us
    pallas_call x1, Pallas kernels, local(): call(near_kernel, [hbm], [(shape_w, bf16)], [pltpu.SemaphoreType.DMA(())]...  1.6 us
    pallas_call x1, Pallas kernels, local(): call(own_kernel, [vmem] * 3, [((rows, total, 3 * cin), bf16), ((2 * rows...  1.27 us
    pallas_call x1, Pallas kernels, local(): call(halo_kernel, [vmem] * 8, [((4, *u_line), bf16)], [pltpu.VMEM((HALO,...  1.24 us
  transfers between devices with their start and end apart: 11, of which 5 were waited for; matrix products, arithmetic and copies ran while one was open for 0% of the time, Pallas kernels for 17%

profile of v11, /device:TPU:0, one launch (start us, length us, event | category | flops | bytes accessed | tf_op | source)
XLA Modules:
  0.0 33.8 jit_solution(7055374667362339134)
XLA Ops:
  0.0 0.5 %collective-permute-start.1 = (bf16[4,4,512,128]{3,2,1,0:T(8,128)(2,1)}, bf16[4,4,512,128]{3,2,1,0:T(8,128)(2,1)S(1)}, u32[]{:S(2)}, u32[]{:S(2)}) collective-permute-start(bf16[4,4,512,128]{3,2,1,0:T(8,128)(2,1)} %param.9), channel_id=1, source_target_pairs={{0,1},{1,0},{2,3},{3,2},{4,5},{5,4},{6,7},{7,6},{8,9},{9,8},{10,11... | collective-permute-start | bytes 6291464 | tf_op jit(solution)/shard_map/ppermute | solution.py:335
  0.5 5.6 %collective-permute-start.2 = (bf16[2,128,512]{2,1,0:T(8,128)(2,1)}, bf16[2,128,512]{2,1,0:T(8,128)(2,1)S(1)}, u32[]{:S(2)}, u32[]{:S(2)}) collective-permute-start(bf16[2,128,512]{2,1,0:T(8,128)(2,1)} %image_ref.1), channel_id=1, source_target_pairs={{2,0},{4,2},{6,4},{8,6},{10,8},{12,10},{14,12},{0,14},{3,1},{5,3},... | collective-permute-start | bytes 786440 | tf_op jit(solution)/shard_map/ppermute | solution.py:326
  6.0 1.0 %cut.1 = (bf16[2,128,512]{2,1,0:T(8,128)(2,1)S(1)}, bf16[2,16,512]{2,1,0:T(8,128)(2,1)S(1)}) custom-call(bf16[2,128,512]{2,1,0:T(8,128)(2,1)} %image_ref.1), custom_call_target="tpu_custom_call" | custom-call | bytes 2097152 | tf_op jit(solution)/shard_map/cut/pallas_call | solution.py:327
  7.1 0.3 collective-permute-start
  7.3 0.3 collective-permute-start.10
  7.6 0.2 collective-permute-start.9
  7.9 1.6 %near_weights.1.own_w = bf16[4,2,2,512,128]{4,3,2,1,0:T(8,128)(2,1)S(1)} custom-call(bf16[4,2,2,512,128]{4,3,2,1,0:T(8,128)(2,1)} %bitcast.9), custom_call_target="tpu_custom_call" | custom-call | bytes 2097152 | tf_op jit(solution)/shard_map/near_weights/pallas_call | solution.py:338
  9.5 3.0 %collective-permute-done.2.lines_ref.next_ref = bf16[2,128,512]{2,1,0:T(8,128)(2,1)S(1)} collective-permute-done((bf16[2,128,512]{2,1,0:T(8,128)(2,1)}, bf16[2,128,512]{2,1,0:T(8,128)(2,1)S(1)}, u32[]{:S(2)}, u32[]{:S(2)}) %collective-permute-start.2) | collective-permute-done | bytes 262176 | tf_op jit(solution)/shard_map/ppermute | solution.py:326
  12.6 0.2 collective-permute-start.4
  12.8 1.3 %deconv_own.1 = (bf16[2,144,1536]{2,1,0:T(8,128)(2,1)S(1)}, bf16[2,2,144,256]{3,2,1,0:T(8,128)(2,1)S(1)}, f32[2,144,256]{2,1,0:T(8,128)S(1)}, f32[2,2,144,256]{3,2,1,0:T(8,128)S(1)}, f32[2,256]{1,0:T(2,128)S(1)}) custom-call(bf16[2,144,512]{2,1,0:T(8,128)(2,1)S(1)} %constant_dynamic-update-slice_fusion.lines_ref, ...), custom_call_target="tpu_custom_call" | custom-call | flops 905969664 | bytes 2097152 | tf_op jit(solution)/shard_map/deconv_own/pallas_call | solution.py:344
  14.1 0.0 copy-start.2
  14.1 0.0 copy-start.3
  14.1 0.0 copy-start.4
  14.1 0.5 %deconv_next.1 = (bf16[2,2,144,256]{3,2,1,0:T(8,128)(2,1)S(1)}, bf16[1,144,1536]{2,1,0:T(8,128)(2,1)S(1)}, f32[8,128]{1,0:T(8,128)S(1)}) custom-call(bf16[2,128,512]{2,1,0:T(8,128)(2,1)S(1)} %collective-permute-done.2.lines_ref.next_ref, bf16[2,16,512]{2,1,0:T(8,128)(2,1)S(1)} %collective-permute-done.3.edge_ref.next_edge_ref, ...), custom_call_target="tpu_custom_call" | custom-call | flops 301989888 | bytes 2097152 | tf_op jit(solution)/shard_map/deconv_next/pallas_call | solution.py:360
  14.7 0.6 %collective-permute-start.5 = (f32[8,128]{1,0:T(8,128)S(1)}, f32[8,128]{1,0:T(8,128)S(1)}, u32[]{:S(2)}, u32[]{:S(2)}) collective-permute-start(f32[8,128]{1,0:T(8,128)S(1)} %get-tuple-element.32), channel_id=1, source_target_pairs={{0,1},{1,0},{2,3},{3,2},{4,5},{5,4},{6,7},{7,6},{8,9},{9,8},{10,11... | collective-permute-start | bytes 12296 | tf_op jit(solution)/shard_map/ppermute | solution.py:288
  15.2 0.8 %collective-permute-done.5 = f32[8,128]{1,0:T(8,128)S(1)} collective-permute-done((f32[8,128]{1,0:T(8,128)S(1)}, f32[8,128]{1,0:T(8,128)S(1)}, u32[]{:S(2)}, u32[]{:S(2)}) %collective-permute-start.5) | collective-permute-done | bytes 4128 | tf_op jit(solution)/shard_map/ppermute | solution.py:288
  16.1 1.6 %collective-permute-start.6 = (f32[8,128]{1,0:T(8,128)S(1)}, f32[8,128]{1,0:T(8,128)S(1)}, u32[]{:S(2)}, u32[]{:S(2)}) collective-permute-start(f32[8,128]{1,0:T(8,128)S(1)} %add.12), channel_id=1, source_target_pairs={{0,4},{2,6},{4,0},{6,2},{8,12},{10,14},{12,8},{14,10},{1,5},{3,7},... | collective-permute-start | bytes 12296 | tf_op jit(solution)/shard_map/ppermute | solution.py:288
  17.6 2.0 %collective-permute-done.6 = f32[8,128]{1,0:T(8,128)S(1)} collective-permute-done((f32[8,128]{1,0:T(8,128)S(1)}, f32[8,128]{1,0:T(8,128)S(1)}, u32[]{:S(2)}, u32[]{:S(2)}) %collective-permute-start.6) | collective-permute-done | bytes 4128 | tf_op jit(solution)/shard_map/ppermute | solution.py:288
  19.7 3.9 %collective-permute-start.7 = (f32[8,128]{1,0:T(8,128)S(1)}, f32[8,128]{1,0:T(8,128)S(1)}, u32[]{:S(2)}, u32[]{:S(2)}) collective-permute-start(f32[8,128]{1,0:T(8,128)S(1)} %add.13), channel_id=1, source_target_pairs={{0,8},{2,10},{4,12},{6,14},{8,0},{10,2},{12,4},{14,6},{1,9},{3,11}... | collective-permute-start | bytes 12296 | tf_op jit(solution)/shard_map/ppermute | solution.py:288
  23.7 1.6 %collective-permute-done.7 = f32[8,128]{1,0:T(8,128)S(1)} collective-permute-done((f32[8,128]{1,0:T(8,128)S(1)}, f32[8,128]{1,0:T(8,128)S(1)}, u32[]{:S(2)}, u32[]{:S(2)}) %collective-permute-start.7) | collective-permute-done | bytes 4128 | tf_op jit(solution)/shard_map/ppermute | solution.py:288
  25.2 2.1 %collective-permute-start.8 = (f32[8,128]{1,0:T(8,128)S(1)}, f32[8,128]{1,0:T(8,128)S(1)}, u32[]{:S(2)}, u32[]{:S(2)}) collective-permute-start(f32[8,128]{1,0:T(8,128)S(1)} %add.14), channel_id=1, source_target_pairs={{0,2},{2,0},{4,6},{6,4},{8,10},{10,8},{12,14},{14,12},{1,3},{3,1},... | collective-permute-start | bytes 12296 | tf_op jit(solution)/shard_map/ppermute | solution.py:288
  27.3 1.2 %deconv_halo.1.halo_ref = bf16[4,2,144,256]{3,2,1,0:T(8,128)(2,1)S(1)} custom-call(bf16[2,144,512]{2,1,0:T(8,128)(2,1)S(1)} %collective-permute-done.4.above_ref, bf16[2,128,512]{2,1,0:T(8,128)(2,1)S(1)} %collective-permute-done.2.lines_ref.next_ref, bf16[2,16,512]{2,1,0:T(8,128)(2,1)S(1)} %collective-permute-done.3.edge_ref.next_edge_ref, ...), custom_call_target="tpu_custom_call" | custom-call | flops 1207959552 | bytes 2097152 | tf_op jit(solution)/shard_map/deconv_halo/pallas_call | solution.py:368
  28.6 0.3 collective-permute-done.8
  29.0 4.8 %convs.1 = bf16[4,256,256]{2,1,0:T(8,128)(2,1)} custom-call(bf16[2,2,144,256]{3,2,1,0:T(8,128)(2,1)S(1)} %get-tuple-element.24.u_ref, bf16[2,2,144,256]{3,2,1,0:T(8,128)(2,1)S(1)} %get-tuple-element.27.u_next_ref, bf16[4,2,144,256]{3,2,1,0:T(8,128)(2,1)S(1)} %deconv_halo.1.halo_ref, f32[8,128]{1,0:T(8,128)S(1)} %add.15.stats_ref, ...), custom_call_target="tpu_custom_call" | custom-call | flops 5000000000 | bytes 2097152 | tf_op jit(solution)/shard_map/convs/pallas_call | solution.py:379
  (24 shorter events, 0.1 us)
Async XLA Ops:
  0.0 12.8 %collective-permute-start.1 = (bf16[4,4,512,128]{3,2,1,0:T(8,128)(2,1)}, bf16[4,4,512,128]{3,2,1,0:T(8,128)(2,1)S(1)}, u32[]{:S(2)}, u32[]{:S(2)}) collective-permute-start(bf16[4,4,512,128]{3,2,1,0:T(8,128)(2,1)} %param.9), channel_id=1, source_target_pairs={{0,1},{1,0},{2,3},{3,2},{4,5},{5,4},{6,7},{7,6},{8,9},{9,8},{10,11... | collective-permute-start | bytes 6291464 | tf_op jit(solution)/shard_map/ppermute | solution.py:335
  0.5 12.1 %collective-permute-start.2 = (bf16[2,128,512]{2,1,0:T(8,128)(2,1)}, bf16[2,128,512]{2,1,0:T(8,128)(2,1)S(1)}, u32[]{:S(2)}, u32[]{:S(2)}) collective-permute-start(bf16[2,128,512]{2,1,0:T(8,128)(2,1)} %image_ref.1), channel_id=1, source_target_pairs={{2,0},{4,2},{6,4},{8,6},{10,8},{12,10},{14,12},{0,14},{3,1},{5,3},... | collective-permute-start | bytes 786440 | tf_op jit(solution)/shard_map/ppermute | solution.py:326
  7.1 2.4 %collective-permute-start = (bf16[2,16,512]{2,1,0:T(8,128)(2,1)S(1)}, bf16[2,16,512]{2,1,0:T(8,128)(2,1)S(1)}, u32[]{:S(2)}, u32[]{:S(2)}) collective-permute-start(bf16[2,16,512]{2,1,0:T(8,128)(2,1)S(1)} %get-tuple-element.21), channel_id=1, source_target_pairs={{0,1},{1,0},{2,3},{3,2},{4,5},{5,4},{6,7},{7,6},{8,9},{9,8},{10,11... | collective-permute-start | bytes 98312 | tf_op jit(solution)/shard_map/ppermute | solution.py:334
  7.3 21.6 %collective-permute-start.10 = (bf16[3,3,256,128]{3,2,1,0:T(8,128)(2,1)}, bf16[3,3,256,128]{3,2,1,0:T(8,128)(2,1)S(1)}, u32[]{:S(2)}, u32[]{:S(2)}) collective-permute-start(bf16[3,3,256,128]{3,2,1,0:T(8,128)(2,1)} %own_w2.1), channel_id=1, source_target_pairs={{0,1},{1,0},{2,3},{3,2},{4,5},{5,4},{6,7},{7,6},{8,9},{9,8},{10,11... | collective-permute-start | bytes 1769480 | tf_op jit(solution)/shard_map/ppermute | solution.py:337
  7.6 21.3 %collective-permute-start.9 = (bf16[3,3,256,128]{3,2,1,0:T(8,128)(2,1)}, bf16[3,3,256,128]{3,2,1,0:T(8,128)(2,1)S(1)}, u32[]{:S(2)}, u32[]{:S(2)}) collective-permute-start(bf16[3,3,256,128]{3,2,1,0:T(8,128)(2,1)} %own_w1.1), channel_id=1, source_target_pairs={{0,1},{1,0},{2,3},{3,2},{4,5},{5,4},{6,7},{7,6},{8,9},{9,8},{10,11... | collective-permute-start | bytes 1769480 | tf_op jit(solution)/shard_map/ppermute | solution.py:336
  12.6 14.8 %collective-permute-start.4 = (bf16[2,144,512]{2,1,0:T(8,128)(2,1)S(1)}, bf16[2,144,512]{2,1,0:T(8,128)(2,1)S(1)}, u32[]{:S(2)}, u32[]{:S(2)}) collective-permute-start(bf16[2,144,512]{2,1,0:T(8,128)(2,1)S(1)} %constant_dynamic-update-slice_fusion.lines_ref), channel_id=1, source_target_pairs={{0,2},{2,4},{4,6},{6,8},{8,10},{10,12},{12,14},{14,0},{1,3},{3,5},... | collective-permute-start | bytes 884744 | tf_op jit(solution)/shard_map/ppermute | solution.py:342
  12.8 1.3 %collective-permute-start.3 = (bf16[2,16,512]{2,1,0:T(8,128)(2,1)S(1)}, bf16[2,16,512]{2,1,0:T(8,128)(2,1)S(1)}, u32[]{:S(2)}, u32[]{:S(2)}) collective-permute-start(bf16[2,16,512]{2,1,0:T(8,128)(2,1)S(1)} %next_edges.1), channel_id=1, source_target_pairs={{0,1},{1,0},{2,3},{3,2},{4,5},{5,4},{6,7},{7,6},{8,9},{9,8},{10,11... | collective-permute-start | bytes 98312 | tf_op jit(solution)/shard_map/ppermute | solution.py:359
  14.1 9.5 %copy-start.2 = (f32[256]{0:T(256)S(1)}, f32[256]{0:T(256)}, u32[]{:S(2)}) copy-start(f32[256]{0:T(256)} %param.15) | copy-start | bytes 3076
  14.1 9.5 %copy-start.3 = (f32[256]{0:T(256)S(1)}, f32[256]{0:T(256)}, u32[]{:S(2)}) copy-start(f32[256]{0:T(256)} %param.13) | copy-start | bytes 3076
  14.1 9.5 %copy-start.4 = (f32[256]{0:T(256)S(1)}, f32[256]{0:T(256)}, u32[]{:S(2)}) copy-start(f32[256]{0:T(256)} %param.11) | copy-start | bytes 3076
  14.1 9.5 %copy-start.5 = (f32[256]{0:T(256)S(1)}, f32[256]{0:T(256)}, u32[]{:S(2)}) copy-start(f32[256]{0:T(256)} %param.10) | copy-start | bytes 3076
  14.7 1.4 %collective-permute-start.5 = (f32[8,128]{1,0:T(8,128)S(1)}, f32[8,128]{1,0:T(8,128)S(1)}, u32[]{:S(2)}, u32[]{:S(2)}) collective-permute-start(f32[8,128]{1,0:T(8,128)S(1)} %get-tuple-element.32), channel_id=1, source_target_pairs={{0,1},{1,0},{2,3},{3,2},{4,5},{5,4},{6,7},{7,6},{8,9},{9,8},{10,11... | collective-permute-start | bytes 12296 | tf_op jit(solution)/shard_map/ppermute | solution.py:288
  16.1 3.6 %collective-permute-start.6 = (f32[8,128]{1,0:T(8,128)S(1)}, f32[8,128]{1,0:T(8,128)S(1)}, u32[]{:S(2)}, u32[]{:S(2)}) collective-permute-start(f32[8,128]{1,0:T(8,128)S(1)} %add.12), channel_id=1, source_target_pairs={{0,4},{2,6},{4,0},{6,2},{8,12},{10,14},{12,8},{14,10},{1,5},{3,7},... | collective-permute-start | bytes 12296 | tf_op jit(solution)/shard_map/ppermute | solution.py:288
  19.7 5.5 %collective-permute-start.7 = (f32[8,128]{1,0:T(8,128)S(1)}, f32[8,128]{1,0:T(8,128)S(1)}, u32[]{:S(2)}, u32[]{:S(2)}) collective-permute-start(f32[8,128]{1,0:T(8,128)S(1)} %add.13), channel_id=1, source_target_pairs={{0,8},{2,10},{4,12},{6,14},{8,0},{10,2},{12,4},{14,6},{1,9},{3,11}... | collective-permute-start | bytes 12296 | tf_op jit(solution)/shard_map/ppermute | solution.py:288
  25.2 3.7 %collective-permute-start.8 = (f32[8,128]{1,0:T(8,128)S(1)}, f32[8,128]{1,0:T(8,128)S(1)}, u32[]{:S(2)}, u32[]{:S(2)}) collective-permute-start(f32[8,128]{1,0:T(8,128)S(1)} %add.14), channel_id=1, source_target_pairs={{0,2},{2,0},{4,6},{6,4},{8,10},{10,8},{12,14},{14,12},{1,3},{3,1},... | collective-permute-start | bytes 12296 | tf_op jit(solution)/shard_map/ppermute | solution.py:288
  27.3 1.6 %copy-start = (bf16[3,3,256,128]{3,2,1,0:T(8,128)(2,1)S(1)}, bf16[3,3,256,128]{3,2,1,0:T(8,128)(2,1)}, u32[]{:S(2)}) copy-start(bf16[3,3,256,128]{3,2,1,0:T(8,128)(2,1)} %own_w1.1) | copy-start | bytes 1769476
  27.3 1.6 %copy-start.1 = (bf16[3,3,256,128]{3,2,1,0:T(8,128)(2,1)S(1)}, bf16[3,3,256,128]{3,2,1,0:T(8,128)(2,1)}, u32[]{:S(2)}) copy-start(bf16[3,3,256,128]{3,2,1,0:T(8,128)(2,1)} %own_w2.1) | copy-start | bytes 1769476

commit v12 on v11

--- a/solution.py
+++ b/solution.py
@@ -174,7 +174,7 @@
 
 
 def conv_kernel(
-    count, u_ref, u_next_ref, halo_ref, stats_ref, params_ref, own_w1, other_w1, own_w2, other_w2, out_ref, g, act, mixed
+    count, u_ref, u_next_ref, halo_ref, mine_ref, passed_ref, params_ref, own_w1, other_w1, own_w2, other_w2, out_ref, g, act, mixed
 ):
     early, _, total, cout = u_ref.shape
     main = early + u_next_ref.shape[0]
@@ -198,7 +198,7 @@
             axis=1,
         )
 
-    block = stats_ref[...]
+    block = jnp.where(column == 1, mine_ref[...], passed_ref[...])
     width_group = cout // NORM_GROUPS
     sums = jnp.concatenate([block[0:1], block[1:2]], axis=1)
     squares = jnp.concatenate([block[2:3], block[3:4]], axis=1)
@@ -279,14 +279,15 @@
             second(start - chunk)
 
 
-def total_over(block, axis):
-    size = lax.axis_size(axis)
-    if size & (size - 1):
-        return lax.psum(block, axis)
+def total_over(block, last):
+    size = lax.axis_size("rows")
+    assert size & (size - 1) == 0
+    block = block + lax.ppermute(block, "fsdp", [(0, 1), (1, 0)])
     steps = [2**n for n in range(size.bit_length() - 1)]
     for step in steps[1:] + steps[:1]:
-        block = block + lax.ppermute(block, axis, [(i, i ^ step) for i in range(size)])
-    return block
+        pairs = [(2 * i, 2 * i) for i in range(size)] + [(2 * i + 1, 2 * (i ^ step) + 1) for i in range(size)]
+        block = block + lax.ppermute(block, ("rows", "fsdp"), pairs)
+    return block, lax.ppermute(after(block, last), "fsdp", [(0, 1), (1, 0)])
 
 
 def after(value, *others):
@@ -374,11 +375,11 @@
         flops=2 * 2 * 4 * total * 4 * cin * cout,
     )(above, following, next_edge, xs, xs_next, part, own_w, other_w)
 
-    totals = total_over(total_over(stats, "fsdp"), "rows")
+    mine, passed = total_over(stats, halo)
     params = jnp.stack([norm_gain, norm_shift, first_bias, second_bias])
     (out,) = call(
         functools.partial(conv_kernel, count),
-        [vmem] * 9,
+        [vmem] * 10,
         [((2 * rows, 2 * width, cout), bf16)],
         [
             pltpu.VMEM((2 * rows + 2 * HALO, total, 4 * cout), bf16),
@@ -387,7 +388,7 @@
         ],
         "convs",
         flops=5 * 10**9,
-    )(u, u_next, halo, totals, params, first_weight, first_other, second_weight, second_other)
+    )(u, u_next, halo, mine, passed, params, first_weight, first_other, second_weight, second_other)
     return out
 
 

time: 33.9 us -> 37.7 us (1.11)
  waiting for transfers between devices: 7.8 us -> 11.2 us
  starting transfers between devices: 15.2 us -> 15.6 us
    ppermute x1, waiting for transfers between devices: 0.01 us -> 6.52 us  [local(): above = lax.ppermute(after(lines, following), 'rows', to_next)]
    ppermute x4 -> x5, waiting for transfers between devices: 4.74 us -> 1.6 us  [the longest x1 0.82 us: total_over(): block = block + lax.ppermute(block, 'fsdp', [(0, 1), (1, 0)])]
    ppermute x4 -> x5, starting transfers between devices: 8.2 us -> 8.52 us  [the longest x1 5.99 us: total_over(): return (block, lax.ppermute(after(block, last), 'fsdp', [(0, 1), (1, 0)]))]
  transfers between devices with their start and end apart: 11 -> 12, of which waited for: 5 -> 4; matrix products, arithmetic and copies ran while one was open for 0% -> 0% of each run, Pallas kernels for 17% -> 15%
where the time goes in v12:
time: 37.7 us; the launch traced here: 37.5 us
  starting transfers between devices  15.6 us (41%)
  waiting for transfers between devices  11.2 us (30%)
  Pallas kernels  10.5 us (28%)
    ppermute x1, waiting for transfers between devices, local(): above = lax.ppermute(after(lines, following), 'rows', to_next)  6.52 us
    ppermute x1, starting transfers between devices, total_over(): return (block, lax.ppermute(after(block, last), 'fsdp', [(0, 1), (1, 0)]))  5.99 us
    ppermute x1, starting transfers between devices, local(): following = lax.ppermute(image, 'rows', to_previous)  5.55 us
    pallas_call x1, Pallas kernels, local(): call(functools.partial(conv_kernel, count), [vmem] * 10, [((2 * rows, 2 *...  4.81 us
    ppermute x1, waiting for transfers between devices, local(): following = lax.ppermute(image, 'rows', to_previous)  3.04 us
    ppermute x3, starting transfers between devices, total_over(): block = block + lax.ppermute(block, ('rows', 'fsdp'), pairs)  1.97 us
    pallas_call x1, Pallas kernels, local(): call(near_kernel, [hbm], [(shape_w, bf16)], [pltpu.SemaphoreType.DMA(())]...  1.6 us
    pallas_call x1, Pallas kernels, local(): call(own_kernel, [vmem] * 3, [((rows, total, 3 * cin), bf16), ((2 * rows...  1.27 us
  transfers between devices with their start and end apart: 12, of which 4 were waited for; matrix products, arithmetic and copies ran while one was open for 0% of the time, Pallas kernels for 15%

profile of v12, /device:TPU:0, one launch (start us, length us, event | category | flops | bytes accessed | tf_op | source)
XLA Modules:
  0.0 37.5 jit_solution(9734191181384898519)
XLA Ops:
  0.0 0.5 %collective-permute-start.1 = (bf16[4,4,512,128]{3,2,1,0:T(8,128)(2,1)}, bf16[4,4,512,128]{3,2,1,0:T(8,128)(2,1)S(1)}, u32[]{:S(2)}, u32[]{:S(2)}) collective-permute-start(bf16[4,4,512,128]{3,2,1,0:T(8,128)(2,1)} %param.9), channel_id=1, source_target_pairs={{0,1},{1,0},{2,3},{3,2},{4,5},{5,4},{6,7},{7,6},{8,9},{9,8},{10,11... | collective-permute-start | bytes 6291464 | tf_op jit(solution)/shard_map/ppermute | solution.py:336
  0.5 5.6 %collective-permute-start.2 = (bf16[2,128,512]{2,1,0:T(8,128)(2,1)}, bf16[2,128,512]{2,1,0:T(8,128)(2,1)S(1)}, u32[]{:S(2)}, u32[]{:S(2)}) collective-permute-start(bf16[2,128,512]{2,1,0:T(8,128)(2,1)} %image_ref.1), channel_id=1, source_target_pairs={{2,0},{4,2},{6,4},{8,6},{10,8},{12,10},{14,12},{0,14},{3,1},{5,3},... | collective-permute-start | bytes 786440 | tf_op jit(solution)/shard_map/ppermute | solution.py:327
  6.0 1.0 %cut.1 = (bf16[2,128,512]{2,1,0:T(8,128)(2,1)S(1)}, bf16[2,16,512]{2,1,0:T(8,128)(2,1)S(1)}) custom-call(bf16[2,128,512]{2,1,0:T(8,128)(2,1)} %image_ref.1), custom_call_target="tpu_custom_call" | custom-call | bytes 2097152 | tf_op jit(solution)/shard_map/cut/pallas_call | solution.py:328
  7.1 0.3 collective-permute-start
  7.3 0.3 collective-permute-start.10
  7.6 0.2 collective-permute-start.11
  7.9 1.6 %near_weights.1.own_w = bf16[4,2,2,512,128]{4,3,2,1,0:T(8,128)(2,1)S(1)} custom-call(bf16[4,2,2,512,128]{4,3,2,1,0:T(8,128)(2,1)} %bitcast.9), custom_call_target="tpu_custom_call" | custom-call | bytes 2097152 | tf_op jit(solution)/shard_map/near_weights/pallas_call | solution.py:339
  9.5 0.0 collective-permute-done
  9.5 3.0 %collective-permute-done.2.lines_ref.next_ref = bf16[2,128,512]{2,1,0:T(8,128)(2,1)S(1)} collective-permute-done((bf16[2,128,512]{2,1,0:T(8,128)(2,1)}, bf16[2,128,512]{2,1,0:T(8,128)(2,1)S(1)}, u32[]{:S(2)}, u32[]{:S(2)}) %collective-permute-start.2) | collective-permute-done | bytes 262176 | tf_op jit(solution)/shard_map/ppermute | solution.py:327
  12.6 0.2 collective-permute-start.4
  12.8 1.3 %deconv_own.1 = (bf16[2,144,1536]{2,1,0:T(8,128)(2,1)S(1)}, bf16[2,2,144,256]{3,2,1,0:T(8,128)(2,1)S(1)}, f32[2,144,256]{2,1,0:T(8,128)S(1)}, f32[2,2,144,256]{3,2,1,0:T(8,128)S(1)}, f32[2,256]{1,0:T(2,128)S(1)}) custom-call(bf16[2,144,512]{2,1,0:T(8,128)(2,1)S(1)} %constant_dynamic-update-slice_fusion.lines_ref, ...), custom_call_target="tpu_custom_call" | custom-call | flops 905969664 | bytes 2097152 | tf_op jit(solution)/shard_map/deconv_own/pallas_call | solution.py:345
  14.1 0.5 %deconv_next.1 = (bf16[2,2,144,256]{3,2,1,0:T(8,128)(2,1)S(1)}, bf16[1,144,1536]{2,1,0:T(8,128)(2,1)S(1)}, f32[8,128]{1,0:T(8,128)S(1)}) custom-call(bf16[2,128,512]{2,1,0:T(8,128)(2,1)S(1)} %collective-permute-done.2.lines_ref.next_ref, bf16[2,16,512]{2,1,0:T(8,128)(2,1)S(1)} %collective-permute-done.3.edge_ref.next_edge_ref, ...), custom_call_target="tpu_custom_call" | custom-call | flops 301989888 | bytes 2097152 | tf_op jit(solution)/shard_map/deconv_next/pallas_call | solution.py:361
  14.6 0.6 %collective-permute-start.5 = (f32[8,128]{1,0:T(8,128)S(1)}, f32[8,128]{1,0:T(8,128)S(1)}, u32[]{:S(2)}, u32[]{:S(2)}) collective-permute-start(f32[8,128]{1,0:T(8,128)S(1)} %get-tuple-element.33), channel_id=1, source_target_pairs={{0,1},{1,0},{2,3},{3,2},{4,5},{5,4},{6,7},{7,6},{8,9},{9,8},{10,11... | collective-permute-start | bytes 12296 | tf_op jit(solution)/shard_map/ppermute | solution.py:285
  15.2 0.8 %collective-permute-done.5 = f32[8,128]{1,0:T(8,128)S(1)} collective-permute-done((f32[8,128]{1,0:T(8,128)S(1)}, f32[8,128]{1,0:T(8,128)S(1)}, u32[]{:S(2)}, u32[]{:S(2)}) %collective-permute-start.5) | collective-permute-done | bytes 4128 | tf_op jit(solution)/shard_map/ppermute | solution.py:285
  16.0 0.6 %collective-permute-start.6 = (f32[8,128]{1,0:T(8,128)S(1)}, f32[8,128]{1,0:T(8,128)S(1)}, u32[]{:S(2)}, u32[]{:S(2)}) collective-permute-start(f32[8,128]{1,0:T(8,128)S(1)} %add.12), channel_id=1, source_target_pairs={{0,0},{2,2},{4,4},{6,6},{8,8},{10,10},{12,12},{14,14},{1,5},{3,7},... | collective-permute-start | bytes 12296 | tf_op jit(solution)/shard_map/ppermute | solution.py:289
  16.7 0.7 %collective-permute-start.7 = (f32[8,128]{1,0:T(8,128)S(1)}, f32[8,128]{1,0:T(8,128)S(1)}, u32[]{:S(2)}, u32[]{:S(2)}) collective-permute-start(f32[8,128]{1,0:T(8,128)S(1)} %add.13), channel_id=1, source_target_pairs={{0,0},{2,2},{4,4},{6,6},{8,8},{10,10},{12,12},{14,14},{1,9},{3,11}... | collective-permute-start | bytes 12296 | tf_op jit(solution)/shard_map/ppermute | solution.py:289
  17.4 0.7 %collective-permute-start.8 = (f32[8,128]{1,0:T(8,128)S(1)}, f32[8,128]{1,0:T(8,128)S(1)}, u32[]{:S(2)}, u32[]{:S(2)}) collective-permute-start(f32[8,128]{1,0:T(8,128)S(1)} %add.14), channel_id=1, source_target_pairs={{0,0},{2,2},{4,4},{6,6},{8,8},{10,10},{12,12},{14,14},{1,3},{3,1},... | collective-permute-start | bytes 12296 | tf_op jit(solution)/shard_map/ppermute | solution.py:289
  18.1 6.5 %collective-permute-done.4.above_ref = bf16[2,144,512]{2,1,0:T(8,128)(2,1)S(1)} collective-permute-done((bf16[2,144,512]{2,1,0:T(8,128)(2,1)S(1)}, bf16[2,144,512]{2,1,0:T(8,128)(2,1)S(1)}, u32[]{:S(2)}, u32[]{:S(2)}) %collective-permute-start.4) | collective-permute-done | bytes 294944 | tf_op jit(solution)/shard_map/ppermute | solution.py:343
  24.6 0.0 copy-start
  24.6 0.0 copy-start.1
  24.6 1.3 %deconv_halo.1.halo_ref = bf16[4,2,144,256]{3,2,1,0:T(8,128)(2,1)S(1)} custom-call(bf16[2,144,512]{2,1,0:T(8,128)(2,1)S(1)} %collective-permute-done.4.above_ref, bf16[2,128,512]{2,1,0:T(8,128)(2,1)S(1)} %collective-permute-done.2.lines_ref.next_ref, bf16[2,16,512]{2,1,0:T(8,128)(2,1)S(1)} %collective-permute-done.3.edge_ref.next_edge_ref, ...), custom_call_target="tpu_custom_call" | custom-call | flops 1207959552 | bytes 2097152 | tf_op jit(solution)/shard_map/deconv_halo/pallas_call | solution.py:369
  25.9 6.0 %collective-permute-start.9 = (f32[8,128]{1,0:T(8,128)S(1)}, f32[8,128]{1,0:T(8,128)S(1)}, u32[]{:S(2)}, u32[]{:S(2)}) collective-permute-start(f32[8,128]{1,0:T(8,128)S(1)} %add.15.mine_ref), channel_id=1, source_target_pairs={{0,1},{1,0},{2,3},{3,2},{4,5},{5,4},{6,7},{7,6},{8,9},{9,8},{10,11... | collective-permute-start | bytes 12296 | tf_op jit(solution)/shard_map/ppermute | solution.py:290
  31.9 0.8 %collective-permute-done.9.passed_ref = f32[8,128]{1,0:T(8,128)S(1)} collective-permute-done((f32[8,128]{1,0:T(8,128)S(1)}, f32[8,128]{1,0:T(8,128)S(1)}, u32[]{:S(2)}, u32[]{:S(2)}) %collective-permute-start.9) | collective-permute-done | bytes 4128 | tf_op jit(solution)/shard_map/ppermute | solution.py:290
  32.7 4.8 %convs.1 = bf16[4,256,256]{2,1,0:T(8,128)(2,1)} custom-call(bf16[2,2,144,256]{3,2,1,0:T(8,128)(2,1)S(1)} %get-tuple-element.25.u_ref, bf16[2,2,144,256]{3,2,1,0:T(8,128)(2,1)S(1)} %get-tuple-element.28.u_next_ref, bf16[4,2,144,256]{3,2,1,0:T(8,128)(2,1)S(1)} %deconv_halo.1.halo_ref, f32[8,128]{1,0:T(8,128)S(1)} %add.15.mine_ref, ...), custom_call_target="tpu_custom_call" | custom-call | flops 5000000000 | bytes 2097152 | tf_op jit(solution)/shard_map/convs/pallas_call | solution.py:380
  (26 shorter events, 0.1 us)
Async XLA Ops:
  0.0 12.8 %collective-permute-start.1 = (bf16[4,4,512,128]{3,2,1,0:T(8,128)(2,1)}, bf16[4,4,512,128]{3,2,1,0:T(8,128)(2,1)S(1)}, u32[]{:S(2)}, u32[]{:S(2)}) collective-permute-start(bf16[4,4,512,128]{3,2,1,0:T(8,128)(2,1)} %param.9), channel_id=1, source_target_pairs={{0,1},{1,0},{2,3},{3,2},{4,5},{5,4},{6,7},{7,6},{8,9},{9,8},{10,11... | collective-permute-start | bytes 6291464 | tf_op jit(solution)/shard_map/ppermute | solution.py:336
  0.5 12.1 %collective-permute-start.2 = (bf16[2,128,512]{2,1,0:T(8,128)(2,1)}, bf16[2,128,512]{2,1,0:T(8,128)(2,1)S(1)}, u32[]{:S(2)}, u32[]{:S(2)}) collective-permute-start(bf16[2,128,512]{2,1,0:T(8,128)(2,1)} %image_ref.1), channel_id=1, source_target_pairs={{2,0},{4,2},{6,4},{8,6},{10,8},{12,10},{14,12},{0,14},{3,1},{5,3},... | collective-permute-start | bytes 786440 | tf_op jit(solution)/shard_map/ppermute | solution.py:327
  7.1 2.4 %collective-permute-start = (bf16[2,16,512]{2,1,0:T(8,128)(2,1)S(1)}, bf16[2,16,512]{2,1,0:T(8,128)(2,1)S(1)}, u32[]{:S(2)}, u32[]{:S(2)}) collective-permute-start(bf16[2,16,512]{2,1,0:T(8,128)(2,1)S(1)} %get-tuple-element.22), channel_id=1, source_target_pairs={{0,1},{1,0},{2,3},{3,2},{4,5},{5,4},{6,7},{7,6},{8,9},{9,8},{10,11... | collective-permute-start | bytes 98312 | tf_op jit(solution)/shard_map/ppermute | solution.py:335
  7.3 24.6 %collective-permute-start.10 = (bf16[3,3,256,128]{3,2,1,0:T(8,128)(2,1)}, bf16[3,3,256,128]{3,2,1,0:T(8,128)(2,1)S(1)}, u32[]{:S(2)}, u32[]{:S(2)}) collective-permute-start(bf16[3,3,256,128]{3,2,1,0:T(8,128)(2,1)} %own_w1.1), channel_id=1, source_target_pairs={{0,1},{1,0},{2,3},{3,2},{4,5},{5,4},{6,7},{7,6},{8,9},{9,8},{10,11... | collective-permute-start | bytes 1769480 | tf_op jit(solution)/shard_map/ppermute | solution.py:337
  7.6 24.3 %collective-permute-start.11 = (bf16[3,3,256,128]{3,2,1,0:T(8,128)(2,1)}, bf16[3,3,256,128]{3,2,1,0:T(8,128)(2,1)S(1)}, u32[]{:S(2)}, u32[]{:S(2)}) collective-permute-start(bf16[3,3,256,128]{3,2,1,0:T(8,128)(2,1)} %own_w2.1), channel_id=1, source_target_pairs={{0,1},{1,0},{2,3},{3,2},{4,5},{5,4},{6,7},{7,6},{8,9},{9,8},{10,11... | collective-permute-start | bytes 1769480 | tf_op jit(solution)/shard_map/ppermute | solution.py:338
  12.6 12.0 %collective-permute-start.4 = (bf16[2,144,512]{2,1,0:T(8,128)(2,1)S(1)}, bf16[2,144,512]{2,1,0:T(8,128)(2,1)S(1)}, u32[]{:S(2)}, u32[]{:S(2)}) collective-permute-start(bf16[2,144,512]{2,1,0:T(8,128)(2,1)S(1)} %constant_dynamic-update-slice_fusion.lines_ref), channel_id=1, source_target_pairs={{0,2},{2,4},{4,6},{6,8},{8,10},{10,12},{12,14},{14,0},{1,3},{3,5},... | collective-permute-start | bytes 884744 | tf_op jit(solution)/shard_map/ppermute | solution.py:343
  12.8 1.3 %collective-permute-start.3 = (bf16[2,16,512]{2,1,0:T(8,128)(2,1)S(1)}, bf16[2,16,512]{2,1,0:T(8,128)(2,1)S(1)}, u32[]{:S(2)}, u32[]{:S(2)}) collective-permute-start(bf16[2,16,512]{2,1,0:T(8,128)(2,1)S(1)} %next_edges.1), channel_id=1, source_target_pairs={{0,1},{1,0},{2,3},{3,2},{4,5},{5,4},{6,7},{7,6},{8,9},{9,8},{10,11... | collective-permute-start | bytes 98312 | tf_op jit(solution)/shard_map/ppermute | solution.py:360
  14.6 1.4 %collective-permute-start.5 = (f32[8,128]{1,0:T(8,128)S(1)}, f32[8,128]{1,0:T(8,128)S(1)}, u32[]{:S(2)}, u32[]{:S(2)}) collective-permute-start(f32[8,128]{1,0:T(8,128)S(1)} %get-tuple-element.33), channel_id=1, source_target_pairs={{0,1},{1,0},{2,3},{3,2},{4,5},{5,4},{6,7},{7,6},{8,9},{9,8},{10,11... | collective-permute-start | bytes 12296 | tf_op jit(solution)/shard_map/ppermute | solution.py:285
  16.0 0.7 %collective-permute-start.6 = (f32[8,128]{1,0:T(8,128)S(1)}, f32[8,128]{1,0:T(8,128)S(1)}, u32[]{:S(2)}, u32[]{:S(2)}) collective-permute-start(f32[8,128]{1,0:T(8,128)S(1)} %add.12), channel_id=1, source_target_pairs={{0,0},{2,2},{4,4},{6,6},{8,8},{10,10},{12,12},{14,14},{1,5},{3,7},... | collective-permute-start | bytes 12296 | tf_op jit(solution)/shard_map/ppermute | solution.py:289
  16.7 0.7 %collective-permute-start.7 = (f32[8,128]{1,0:T(8,128)S(1)}, f32[8,128]{1,0:T(8,128)S(1)}, u32[]{:S(2)}, u32[]{:S(2)}) collective-permute-start(f32[8,128]{1,0:T(8,128)S(1)} %add.13), channel_id=1, source_target_pairs={{0,0},{2,2},{4,4},{6,6},{8,8},{10,10},{12,12},{14,14},{1,9},{3,11}... | collective-permute-start | bytes 12296 | tf_op jit(solution)/shard_map/ppermute | solution.py:289
  17.4 8.5 %collective-permute-start.8 = (f32[8,128]{1,0:T(8,128)S(1)}, f32[8,128]{1,0:T(8,128)S(1)}, u32[]{:S(2)}, u32[]{:S(2)}) collective-permute-start(f32[8,128]{1,0:T(8,128)S(1)} %add.14), channel_id=1, source_target_pairs={{0,0},{2,2},{4,4},{6,6},{8,8},{10,10},{12,12},{14,14},{1,3},{3,1},... | collective-permute-start | bytes 12296 | tf_op jit(solution)/shard_map/ppermute | solution.py:289
  24.6 7.3 %copy-start.2 = (f32[256]{0:T(256)S(1)}, f32[256]{0:T(256)}, u32[]{:S(2)}) copy-start(f32[256]{0:T(256)} %param.15) | copy-start | bytes 3076
  24.6 7.3 %copy-start.3 = (f32[256]{0:T(256)S(1)}, f32[256]{0:T(256)}, u32[]{:S(2)}) copy-start(f32[256]{0:T(256)} %param.13) | copy-start | bytes 3076
  24.6 7.3 %copy-start.4 = (f32[256]{0:T(256)S(1)}, f32[256]{0:T(256)}, u32[]{:S(2)}) copy-start(f32[256]{0:T(256)} %param.11) | copy-start | bytes 3076
  24.6 7.3 %copy-start.5 = (f32[256]{0:T(256)S(1)}, f32[256]{0:T(256)}, u32[]{:S(2)}) copy-start(f32[256]{0:T(256)} %param.10) | copy-start | bytes 3076
  24.6 8.1 %copy-start = (bf16[3,3,256,128]{3,2,1,0:T(8,128)(2,1)S(1)}, bf16[3,3,256,128]{3,2,1,0:T(8,128)(2,1)}, u32[]{:S(2)}) copy-start(bf16[3,3,256,128]{3,2,1,0:T(8,128)(2,1)} %own_w1.1) | copy-start | bytes 1769476
  24.6 8.1 %copy-start.1 = (bf16[3,3,256,128]{3,2,1,0:T(8,128)(2,1)S(1)}, bf16[3,3,256,128]{3,2,1,0:T(8,128)(2,1)}, u32[]{:S(2)}) copy-start(bf16[3,3,256,128]{3,2,1,0:T(8,128)(2,1)} %own_w2.1) | copy-start | bytes 1769476
  25.9 6.8 %collective-permute-start.9 = (f32[8,128]{1,0:T(8,128)S(1)}, f32[8,128]{1,0:T(8,128)S(1)}, u32[]{:S(2)}, u32[]{:S(2)}) collective-permute-start(f32[8,128]{1,0:T(8,128)S(1)} %add.15.mine_ref), channel_id=1, source_target_pairs={{0,1},{1,0},{2,3},{3,2},{4,5},{5,4},{6,7},{7,6},{8,9},{9,8},{10,11... | collective-permute-start | bytes 12296 | tf_op jit(solution)/shard_map/ppermute | solution.py:290

commit v13 on v10

--- a/solution.py
+++ b/solution.py
@@ -60,10 +60,10 @@
     copy.wait()
 
 
-def spread_line(out, main, edge, inside=True):
+def spread_line(out, main, edge):
     width, cin = main.shape
     line = jnp.concatenate([main.astype(jnp.float32), edge.astype(jnp.float32)], axis=0)
-    line = jnp.where(edge_mask(width) & inside, line, 0.0)
+    line = jnp.where(edge_mask(width), line, 0.0)
     out[:, 0:cin] = pltpu.roll(line, width + EDGE - 1, 0).astype(jnp.bfloat16)
     out[:, cin : 2 * cin] = line.astype(jnp.bfloat16)
     out[:, 2 * cin : 3 * cin] = pltpu.roll(line, 1, 0).astype(jnp.bfloat16)
@@ -120,7 +120,7 @@
 def next_kernel(next_ref, edge_ref, tail_ref, sums_ref, own_w, other_w, u_ref, xs_ref, stats_ref):
     width = next_ref.shape[1]
     last_here = lax.axis_index("rows") == lax.axis_size("rows") - 1
-    spread_line(xs_ref.at[0], next_ref[0], edge_ref[0], jnp.logical_not(last_here))
+    spread_line(xs_ref.at[0], next_ref[0], edge_ref[0])
     column = lax.axis_index("fsdp")
     sums = sums_ref[...]
     for phase in range(2):
@@ -140,10 +140,9 @@
 
 def halo_kernel(above_ref, next_ref, next_edge_ref, xs_ref, xs_next_ref, part_ref, own_w, other_w, u_ref, xs_above, xs_below):
     width = next_ref.shape[1]
-    place = lax.axis_index("rows")
     for row in range(HALO):
-        spread_line(xs_above.at[row], above_ref[row, :width], above_ref[row, width:], place > 0)
-    spread_line(xs_below.at[0], next_ref[1], next_edge_ref[1], place < lax.axis_size("rows") - 1)
+        spread_line(xs_above.at[row], above_ref[row, :width], above_ref[row, width:])
+    spread_line(xs_below.at[0], next_ref[1], next_edge_ref[1])
     for phase in range(2):
         dot = functools.partial(tap_dot, phase=phase, own_w=own_w, other_w=other_w)
         outer = dot(xs_above[...], kr=3)
@@ -302,8 +301,8 @@
     n_rows = lax.axis_size("rows")
     count = float(2 * rows * n_rows * 2 * width * columns * (cout // NORM_GROUPS))
     swap = [(0, 1), (1, 0)]
-    to_next = [(i, (i + 1) % n_rows) for i in range(n_rows)]
-    to_previous = [((i + 1) % n_rows, i) for i in range(n_rows)]
+    to_next = [(i, i + 1) for i in range(n_rows - 1)]
+    to_previous = [(i + 1, i) for i in range(n_rows - 1)]
     total = width + EDGE
     hbm = pl.BlockSpec(memory_space=pltpu.HBM)
     vmem = pl.BlockSpec(memory_space=pltpu.VMEM)

time: 36.4 us -> 32.8 us (0.901)
  waiting for transfers between devices: 9.28 us -> 6.11 us
  starting transfers between devices: 16.2 us -> 15.7 us
    ppermute x1, starting transfers between devices: 0.06 us -> 5.46 us  [local(): above = lax.ppermute(lines, 'rows', to_next)]
    ppermute x1, starting transfers between devices: 5.55 us -> 1.28 us  [local(): following = lax.ppermute(image, 'rows', to_previous)]
    ppermute x4, waiting for transfers between devices: 6.28 us -> 4.63 us  [total_over(): lax.ppermute(block, axis, [(i, i ^ step) for i in range(size)])]
    ppermute x1, waiting for transfers between devices: 2.98 us -> 1.46 us  [local(): following = lax.ppermute(image, 'rows', to_previous)]
    ppermute x4, starting transfers between devices: 9.32 us -> 7.9 us  [total_over(): lax.ppermute(block, axis, [(i, i ^ step) for i in range(size)])]
  transfers between devices with their start and end apart: 11 -> 11, of which waited for: 5 -> 5; matrix products, arithmetic and copies ran while one was open for 0% -> 0% of each run, Pallas kernels for 16% -> 17%
where the time goes in v13:
time: 32.8 us; the launch traced here: 32.6 us
  starting transfers between devices  15.7 us (48%)
  Pallas kernels  10.5 us (32%)
  waiting for transfers between devices  6.11 us (19%)
    ppermute x4, starting transfers between devices, total_over(): lax.ppermute(block, axis, [(i, i ^ step) for i in range(size)])  7.9 us
    ppermute x1, starting transfers between devices, local(): above = lax.ppermute(lines, 'rows', to_next)  5.46 us
    pallas_call x1, Pallas kernels, local(): call(functools.partial(conv_kernel, count), [vmem] * 9, [((2 * rows, 2 *...  4.82 us
    ppermute x4, waiting for transfers between devices, total_over(): lax.ppermute(block, axis, [(i, i ^ step) for i in range(size)])  4.63 us
    pallas_call x1, Pallas kernels, local(): call(near_kernel, [hbm], [(shape_w, bf16)], [pltpu.SemaphoreType.DMA(())]...  1.6 us
    ppermute x1, waiting for transfers between devices, local(): following = lax.ppermute(image, 'rows', to_previous)  1.46 us
    ppermute x1, starting transfers between devices, local(): following = lax.ppermute(image, 'rows', to_previous)  1.28 us
    pallas_call x1, Pallas kernels, local(): call(own_kernel, [vmem] * 3, [((rows, total, 3 * cin), bf16), ((2 * rows...  1.26 us
  transfers between devices with their start and end apart: 11, of which 5 were waited for; matrix products, arithmetic and copies ran while one was open for 0% of the time, Pallas kernels for 17%

profile of v13, /device:TPU:0, one launch (start us, length us, event | category | flops | bytes accessed | tf_op | source)
XLA Modules:
  0.0 32.6 jit_solution(3322588700247320089)
XLA Ops:
  0.0 0.5 %collective-permute-start.1 = (bf16[4,4,512,128]{3,2,1,0:T(8,128)(2,1)}, bf16[4,4,512,128]{3,2,1,0:T(8,128)(2,1)S(1)}, u32[]{:S(2)}, u32[]{:S(2)}) collective-permute-start(bf16[4,4,512,128]{3,2,1,0:T(8,128)(2,1)} %param.9), channel_id=1, source_target_pairs={{0,1},{1,0},{2,3},{3,2},{4,5},{5,4},{6,7},{7,6},{8,9},{9,8},{10,11... | collective-permute-start | bytes 6291464 | tf_op jit(solution)/shard_map/ppermute | solution.py:334
  0.5 1.3 %collective-permute-start.2 = (bf16[2,128,512]{2,1,0:T(8,128)(2,1)}, bf16[2,128,512]{2,1,0:T(8,128)(2,1)S(1)}, u32[]{:S(2)}, u32[]{:S(2)}) collective-permute-start(bf16[2,128,512]{2,1,0:T(8,128)(2,1)} %image_ref.1), channel_id=1, source_target_pairs={{2,0},{4,2},{6,4},{8,6},{10,8},{12,10},{14,12},{3,1},{5,3},{7,5},{... | collective-permute-start | bytes 786440 | tf_op jit(solution)/shard_map/ppermute | solution.py:325
  1.7 1.1 %cut.1 = (bf16[2,128,512]{2,1,0:T(8,128)(2,1)S(1)}, bf16[2,16,512]{2,1,0:T(8,128)(2,1)S(1)}) custom-call(bf16[2,128,512]{2,1,0:T(8,128)(2,1)} %image_ref.1), custom_call_target="tpu_custom_call" | custom-call | bytes 2097152 | tf_op jit(solution)/shard_map/cut/pallas_call | solution.py:326
  2.8 0.1 collective-permute-start
  2.9 0.5 %collective-permute-start.10 = (bf16[3,3,256,128]{3,2,1,0:T(8,128)(2,1)}, bf16[3,3,256,128]{3,2,1,0:T(8,128)(2,1)S(1)}, u32[]{:S(2)}, u32[]{:S(2)}) collective-permute-start(bf16[3,3,256,128]{3,2,1,0:T(8,128)(2,1)} %own_w2.1), channel_id=1, source_target_pairs={{0,1},{1,0},{2,3},{3,2},{4,5},{5,4},{6,7},{7,6},{8,9},{9,8},{10,11... | collective-permute-start | bytes 1769480 | tf_op jit(solution)/shard_map/ppermute | solution.py:336
  3.4 0.1 collective-permute-start.9
  3.5 1.6 %near_weights.1.own_w = bf16[4,2,2,512,128]{4,3,2,1,0:T(8,128)(2,1)S(1)} custom-call(bf16[4,2,2,512,128]{4,3,2,1,0:T(8,128)(2,1)} %bitcast.9), custom_call_target="tpu_custom_call" | custom-call | bytes 2097152 | tf_op jit(solution)/shard_map/near_weights/pallas_call | solution.py:337
  5.1 5.5 %collective-permute-start.4 = (bf16[2,144,512]{2,1,0:T(8,128)(2,1)S(1)}, bf16[2,144,512]{2,1,0:T(8,128)(2,1)S(1)}, u32[]{:S(2)}, u32[]{:S(2)}) collective-permute-start(bf16[2,144,512]{2,1,0:T(8,128)(2,1)S(1)} %constant_dynamic-update-slice_fusion.lines_ref), channel_id=1, source_target_pairs={{0,2},{2,4},{4,6},{6,8},{8,10},{10,12},{12,14},{1,3},{3,5},{5,7},{... | collective-permute-start | bytes 884744 | tf_op jit(solution)/shard_map/ppermute | solution.py:341
  10.6 1.5 %collective-permute-done.2.lines_ref.next_ref = bf16[2,128,512]{2,1,0:T(8,128)(2,1)S(1)} collective-permute-done((bf16[2,128,512]{2,1,0:T(8,128)(2,1)}, bf16[2,128,512]{2,1,0:T(8,128)(2,1)S(1)}, u32[]{:S(2)}, u32[]{:S(2)}) %collective-permute-start.2) | collective-permute-done | bytes 262176 | tf_op jit(solution)/shard_map/ppermute | solution.py:325
  12.1 1.3 %deconv_own.1 = (bf16[2,144,1536]{2,1,0:T(8,128)(2,1)S(1)}, bf16[2,2,144,256]{3,2,1,0:T(8,128)(2,1)S(1)}, f32[2,144,256]{2,1,0:T(8,128)S(1)}, f32[2,2,144,256]{3,2,1,0:T(8,128)S(1)}, f32[2,256]{1,0:T(2,128)S(1)}) custom-call(bf16[2,144,512]{2,1,0:T(8,128)(2,1)S(1)} %constant_dynamic-update-slice_fusion.lines_ref, ...), custom_call_target="tpu_custom_call" | custom-call | flops 905969664 | bytes 2097152 | tf_op jit(solution)/shard_map/deconv_own/pallas_call | solution.py:343
  13.3 0.0 copy-start.2
  13.4 0.0 copy-start.4
  13.4 0.0 copy-start.5
  13.4 0.5 %deconv_next.1 = (bf16[2,2,144,256]{3,2,1,0:T(8,128)(2,1)S(1)}, bf16[1,144,1536]{2,1,0:T(8,128)(2,1)S(1)}, f32[8,128]{1,0:T(8,128)S(1)}) custom-call(bf16[2,128,512]{2,1,0:T(8,128)(2,1)S(1)} %collective-permute-done.2.lines_ref.next_ref, bf16[2,16,512]{2,1,0:T(8,128)(2,1)S(1)} %collective-permute-done.3.edge_ref.next_edge_ref, ...), custom_call_target="tpu_custom_call" | custom-call | flops 301989888 | bytes 2097152 | tf_op jit(solution)/shard_map/deconv_next/pallas_call | solution.py:359
  13.9 0.6 %collective-permute-start.5 = (f32[8,128]{1,0:T(8,128)S(1)}, f32[8,128]{1,0:T(8,128)S(1)}, u32[]{:S(2)}, u32[]{:S(2)}) collective-permute-start(f32[8,128]{1,0:T(8,128)S(1)} %get-tuple-element.30), channel_id=1, source_target_pairs={{0,1},{1,0},{2,3},{3,2},{4,5},{5,4},{6,7},{7,6},{8,9},{9,8},{10,11... | collective-permute-start | bytes 12296 | tf_op jit(solution)/shard_map/ppermute | solution.py:287
  14.5 0.8 %collective-permute-done.5 = f32[8,128]{1,0:T(8,128)S(1)} collective-permute-done((f32[8,128]{1,0:T(8,128)S(1)}, f32[8,128]{1,0:T(8,128)S(1)}, u32[]{:S(2)}, u32[]{:S(2)}) %collective-permute-start.5) | collective-permute-done | bytes 4128 | tf_op jit(solution)/shard_map/ppermute | solution.py:287
  15.3 1.8 %collective-permute-start.6 = (f32[8,128]{1,0:T(8,128)S(1)}, f32[8,128]{1,0:T(8,128)S(1)}, u32[]{:S(2)}, u32[]{:S(2)}) collective-permute-start(f32[8,128]{1,0:T(8,128)S(1)} %add.12), channel_id=1, source_target_pairs={{0,4},{2,6},{4,0},{6,2},{8,12},{10,14},{12,8},{14,10},{1,5},{3,7},... | collective-permute-start | bytes 12296 | tf_op jit(solution)/shard_map/ppermute | solution.py:287
  17.1 1.8 %collective-permute-done.6 = f32[8,128]{1,0:T(8,128)S(1)} collective-permute-done((f32[8,128]{1,0:T(8,128)S(1)}, f32[8,128]{1,0:T(8,128)S(1)}, u32[]{:S(2)}, u32[]{:S(2)}) %collective-permute-start.6) | collective-permute-done | bytes 4128 | tf_op jit(solution)/shard_map/ppermute | solution.py:287
  18.9 2.8 %collective-permute-start.7 = (f32[8,128]{1,0:T(8,128)S(1)}, f32[8,128]{1,0:T(8,128)S(1)}, u32[]{:S(2)}, u32[]{:S(2)}) collective-permute-start(f32[8,128]{1,0:T(8,128)S(1)} %add.13), channel_id=1, source_target_pairs={{0,8},{2,10},{4,12},{6,14},{8,0},{10,2},{12,4},{14,6},{1,9},{3,11}... | collective-permute-start | bytes 12296 | tf_op jit(solution)/shard_map/ppermute | solution.py:287
  21.8 1.7 %collective-permute-done.7 = f32[8,128]{1,0:T(8,128)S(1)} collective-permute-done((f32[8,128]{1,0:T(8,128)S(1)}, f32[8,128]{1,0:T(8,128)S(1)}, u32[]{:S(2)}, u32[]{:S(2)}) %collective-permute-start.7) | collective-permute-done | bytes 4128 | tf_op jit(solution)/shard_map/ppermute | solution.py:287
  23.4 2.7 %collective-permute-start.8 = (f32[8,128]{1,0:T(8,128)S(1)}, f32[8,128]{1,0:T(8,128)S(1)}, u32[]{:S(2)}, u32[]{:S(2)}) collective-permute-start(f32[8,128]{1,0:T(8,128)S(1)} %add.14), channel_id=1, source_target_pairs={{0,2},{2,0},{4,6},{6,4},{8,10},{10,8},{12,14},{14,12},{1,3},{3,1},... | collective-permute-start | bytes 12296 | tf_op jit(solution)/shard_map/ppermute | solution.py:287
  26.2 1.2 %deconv_halo.1.halo_ref = bf16[4,2,144,256]{3,2,1,0:T(8,128)(2,1)S(1)} custom-call(bf16[2,144,512]{2,1,0:T(8,128)(2,1)S(1)} %collective-permute-done.4.above_ref, bf16[2,128,512]{2,1,0:T(8,128)(2,1)S(1)} %collective-permute-done.2.lines_ref.next_ref, bf16[2,16,512]{2,1,0:T(8,128)(2,1)S(1)} %collective-permute-done.3.edge_ref.next_edge_ref, ...), custom_call_target="tpu_custom_call" | custom-call | flops 1207959552 | bytes 2097152 | tf_op jit(solution)/shard_map/deconv_halo/pallas_call | solution.py:367
  27.4 0.3 %collective-permute-done.8 = f32[8,128]{1,0:T(8,128)S(1)} collective-permute-done((f32[8,128]{1,0:T(8,128)S(1)}, f32[8,128]{1,0:T(8,128)S(1)}, u32[]{:S(2)}, u32[]{:S(2)}) %collective-permute-start.8) | collective-permute-done | bytes 4128 | tf_op jit(solution)/shard_map/ppermute | solution.py:287
  27.8 4.8 %convs.1 = bf16[4,256,256]{2,1,0:T(8,128)(2,1)} custom-call(bf16[2,2,144,256]{3,2,1,0:T(8,128)(2,1)S(1)} %get-tuple-element.23.u_ref, bf16[2,2,144,256]{3,2,1,0:T(8,128)(2,1)S(1)} %get-tuple-element.26.u_next_ref, bf16[4,2,144,256]{3,2,1,0:T(8,128)(2,1)S(1)} %deconv_halo.1.halo_ref, f32[8,128]{1,0:T(8,128)S(1)} %add.15.stats_ref, ...), custom_call_target="tpu_custom_call" | custom-call | flops 5000000000 | bytes 2097152 | tf_op jit(solution)/shard_map/convs/pallas_call | solution.py:378
  (24 shorter events, 0.1 us)
Async XLA Ops:
  0.0 12.1 %collective-permute-start.1 = (bf16[4,4,512,128]{3,2,1,0:T(8,128)(2,1)}, bf16[4,4,512,128]{3,2,1,0:T(8,128)(2,1)S(1)}, u32[]{:S(2)}, u32[]{:S(2)}) collective-permute-start(bf16[4,4,512,128]{3,2,1,0:T(8,128)(2,1)} %param.9), channel_id=1, source_target_pairs={{0,1},{1,0},{2,3},{3,2},{4,5},{5,4},{6,7},{7,6},{8,9},{9,8},{10,11... | collective-permute-start | bytes 6291464 | tf_op jit(solution)/shard_map/ppermute | solution.py:334
  0.5 11.6 %collective-permute-start.2 = (bf16[2,128,512]{2,1,0:T(8,128)(2,1)}, bf16[2,128,512]{2,1,0:T(8,128)(2,1)S(1)}, u32[]{:S(2)}, u32[]{:S(2)}) collective-permute-start(bf16[2,128,512]{2,1,0:T(8,128)(2,1)} %image_ref.1), channel_id=1, source_target_pairs={{2,0},{4,2},{6,4},{8,6},{10,8},{12,10},{14,12},{3,1},{5,3},{7,5},{... | collective-permute-start | bytes 786440 | tf_op jit(solution)/shard_map/ppermute | solution.py:325
  2.8 2.3 %collective-permute-start = (bf16[2,16,512]{2,1,0:T(8,128)(2,1)S(1)}, bf16[2,16,512]{2,1,0:T(8,128)(2,1)S(1)}, u32[]{:S(2)}, u32[]{:S(2)}) collective-permute-start(bf16[2,16,512]{2,1,0:T(8,128)(2,1)S(1)} %get-tuple-element.20), channel_id=1, source_target_pairs={{0,1},{1,0},{2,3},{3,2},{4,5},{5,4},{6,7},{7,6},{8,9},{9,8},{10,11... | collective-permute-start | bytes 98312 | tf_op jit(solution)/shard_map/ppermute | solution.py:333
  2.9 24.8 %collective-permute-start.10 = (bf16[3,3,256,128]{3,2,1,0:T(8,128)(2,1)}, bf16[3,3,256,128]{3,2,1,0:T(8,128)(2,1)S(1)}, u32[]{:S(2)}, u32[]{:S(2)}) collective-permute-start(bf16[3,3,256,128]{3,2,1,0:T(8,128)(2,1)} %own_w2.1), channel_id=1, source_target_pairs={{0,1},{1,0},{2,3},{3,2},{4,5},{5,4},{6,7},{7,6},{8,9},{9,8},{10,11... | collective-permute-start | bytes 1769480 | tf_op jit(solution)/shard_map/ppermute | solution.py:336
  3.4 24.4 %collective-permute-start.9 = (bf16[3,3,256,128]{3,2,1,0:T(8,128)(2,1)}, bf16[3,3,256,128]{3,2,1,0:T(8,128)(2,1)S(1)}, u32[]{:S(2)}, u32[]{:S(2)}) collective-permute-start(bf16[3,3,256,128]{3,2,1,0:T(8,128)(2,1)} %own_w1.1), channel_id=1, source_target_pairs={{0,1},{1,0},{2,3},{3,2},{4,5},{5,4},{6,7},{7,6},{8,9},{9,8},{10,11... | collective-permute-start | bytes 1769480 | tf_op jit(solution)/shard_map/ppermute | solution.py:335
  5.1 21.1 %collective-permute-start.4 = (bf16[2,144,512]{2,1,0:T(8,128)(2,1)S(1)}, bf16[2,144,512]{2,1,0:T(8,128)(2,1)S(1)}, u32[]{:S(2)}, u32[]{:S(2)}) collective-permute-start(bf16[2,144,512]{2,1,0:T(8,128)(2,1)S(1)} %constant_dynamic-update-slice_fusion.lines_ref), channel_id=1, source_target_pairs={{0,2},{2,4},{4,6},{6,8},{8,10},{10,12},{12,14},{1,3},{3,5},{5,7},{... | collective-permute-start | bytes 884744 | tf_op jit(solution)/shard_map/ppermute | solution.py:341
  12.1 1.3 %collective-permute-start.3 = (bf16[2,16,512]{2,1,0:T(8,128)(2,1)S(1)}, bf16[2,16,512]{2,1,0:T(8,128)(2,1)S(1)}, u32[]{:S(2)}, u32[]{:S(2)}) collective-permute-start(bf16[2,16,512]{2,1,0:T(8,128)(2,1)S(1)} %next_edges.1), channel_id=1, source_target_pairs={{0,1},{1,0},{2,3},{3,2},{4,5},{5,4},{6,7},{7,6},{8,9},{9,8},{10,11... | collective-permute-start | bytes 98312 | tf_op jit(solution)/shard_map/ppermute | solution.py:358
  13.3 8.4 %copy-start.2 = (f32[256]{0:T(256)S(1)}, f32[256]{0:T(256)}, u32[]{:S(2)}) copy-start(f32[256]{0:T(256)} %param.15) | copy-start | bytes 3076
  13.3 8.4 %copy-start.3 = (f32[256]{0:T(256)S(1)}, f32[256]{0:T(256)}, u32[]{:S(2)}) copy-start(f32[256]{0:T(256)} %param.13) | copy-start | bytes 3076
  13.4 8.4 %copy-start.4 = (f32[256]{0:T(256)S(1)}, f32[256]{0:T(256)}, u32[]{:S(2)}) copy-start(f32[256]{0:T(256)} %param.11) | copy-start | bytes 3076
  13.4 8.4 %copy-start.5 = (f32[256]{0:T(256)S(1)}, f32[256]{0:T(256)}, u32[]{:S(2)}) copy-start(f32[256]{0:T(256)} %param.10) | copy-start | bytes 3076
  13.9 1.4 %collective-permute-start.5 = (f32[8,128]{1,0:T(8,128)S(1)}, f32[8,128]{1,0:T(8,128)S(1)}, u32[]{:S(2)}, u32[]{:S(2)}) collective-permute-start(f32[8,128]{1,0:T(8,128)S(1)} %get-tuple-element.30), channel_id=1, source_target_pairs={{0,1},{1,0},{2,3},{3,2},{4,5},{5,4},{6,7},{7,6},{8,9},{9,8},{10,11... | collective-permute-start | bytes 12296 | tf_op jit(solution)/shard_map/ppermute | solution.py:287
  15.3 3.6 %collective-permute-start.6 = (f32[8,128]{1,0:T(8,128)S(1)}, f32[8,128]{1,0:T(8,128)S(1)}, u32[]{:S(2)}, u32[]{:S(2)}) collective-permute-start(f32[8,128]{1,0:T(8,128)S(1)} %add.12), channel_id=1, source_target_pairs={{0,4},{2,6},{4,0},{6,2},{8,12},{10,14},{12,8},{14,10},{1,5},{3,7},... | collective-permute-start | bytes 12296 | tf_op jit(solution)/shard_map/ppermute | solution.py:287
  18.9 4.5 %collective-permute-start.7 = (f32[8,128]{1,0:T(8,128)S(1)}, f32[8,128]{1,0:T(8,128)S(1)}, u32[]{:S(2)}, u32[]{:S(2)}) collective-permute-start(f32[8,128]{1,0:T(8,128)S(1)} %add.13), channel_id=1, source_target_pairs={{0,8},{2,10},{4,12},{6,14},{8,0},{10,2},{12,4},{14,6},{1,9},{3,11}... | collective-permute-start | bytes 12296 | tf_op jit(solution)/shard_map/ppermute | solution.py:287
  23.4 4.3 %collective-permute-start.8 = (f32[8,128]{1,0:T(8,128)S(1)}, f32[8,128]{1,0:T(8,128)S(1)}, u32[]{:S(2)}, u32[]{:S(2)}) collective-permute-start(f32[8,128]{1,0:T(8,128)S(1)} %add.14), channel_id=1, source_target_pairs={{0,2},{2,0},{4,6},{6,4},{8,10},{10,8},{12,14},{14,12},{1,3},{3,1},... | collective-permute-start | bytes 12296 | tf_op jit(solution)/shard_map/ppermute | solution.py:287
  26.2 1.6 %copy-start = (bf16[3,3,256,128]{3,2,1,0:T(8,128)(2,1)S(1)}, bf16[3,3,256,128]{3,2,1,0:T(8,128)(2,1)}, u32[]{:S(2)}) copy-start(bf16[3,3,256,128]{3,2,1,0:T(8,128)(2,1)} %own_w1.1) | copy-start | bytes 1769476
  26.2 1.6 %copy-start.1 = (bf16[3,3,256,128]{3,2,1,0:T(8,128)(2,1)S(1)}, bf16[3,3,256,128]{3,2,1,0:T(8,128)(2,1)}, u32[]{:S(2)}) copy-start(bf16[3,3,256,128]{3,2,1,0:T(8,128)(2,1)} %own_w2.1) | copy-start | bytes 1769476

commit v14 on v13

--- a/solution.py
+++ b/solution.py
@@ -14,8 +14,7 @@
 VMEM_BYTES = 24 * 2**20
 
 
-def silu(v):
-    h = 0.5 * v
+def silu_of_half(h):
     return h + h * jnp.tanh(h)
 
 
@@ -204,19 +203,22 @@
     mean = group_sum(sums, width_group) / count
     spread = group_sum(squares, width_group) / count - mean * mean
     scale = lax.rsqrt(spread + 1e-05) * params_ref[0:1]
-    shift = own_first(params_ref[1:2] - mean * scale)
-    scale = own_first(scale)
-
-    mask = edge_mask(width)
+    shift = own_first(0.5 * (params_ref[1:2] - mean * scale))
+    scale = own_first(0.5 * scale)
+    bias1 = own_first(0.5 * params_ref[2:3])
+    bias2 = own_first(params_ref[3:4])
+
+    edge_seen = edge_mask(width)[width:]
     place = lax.axis_index("rows")
     last = lax.axis_size("rows") - 1
 
-    def inside(row, beyond):
+    def masked(row, beyond, value):
+        value = jnp.concatenate([value[:width], jnp.where(edge_seen, value[width:], 0.0)], axis=0)
         if row < beyond:
-            return mask & (place > 0)
+            return jnp.where(place > 0, value, 0.0)
         if row >= lines - 2 * HALO + beyond:
-            return mask & (place < last)
-        return mask
+            return jnp.where(place < last, value, 0.0)
+        return value
 
     def hidden(row):
         if row < 3:
@@ -227,38 +229,44 @@
             source = u_next_ref.at[row - 3 - early]
         else:
             source = halo_ref.at[3]
-        seen = inside(row, HALO)
         fill(
             g,
             row,
-            *[jnp.where(seen, silu(source[phase].astype(jnp.float32) * scale + shift), 0.0) for phase in range(2)],
+            *[
+                masked(row, HALO, silu_of_half(source[phase].astype(jnp.float32) * scale + shift))
+                for phase in range(2)
+            ],
         )
 
-    def conv(source, start, size, cells, phase, own, other, bias):
-        acc = bias
+    def dots(source, start, size, cells, phase, own, other):
+        total = None
         for a in range(3):
-            acc = acc + jnp.dot(
+            term = jnp.dot(
                 source[start + a : start + a + size, 0:cells, phase * cout : (phase + 3) * cout].reshape(
                     size * cells, 3 * cout
                 ),
                 kernel_row(a, own, other),
                 preferred_element_type=jnp.float32,
             )
-        return acc.reshape(size, cells, cout)
+            total = term if total is None else total + term
+        return total.reshape(size, cells, cout)
 
     chunk = 2
-    bias1 = own_first(params_ref[2:3])
-    bias2 = own_first(params_ref[3:4])
 
     def first(start):
-        results = [silu(conv(g, start, chunk, total, phase, own_w1, other_w1, bias1)) for phase in range(2)]
+        return [dots(g, start, chunk, total, phase, own_w1, other_w1) for phase in range(2)]
+
+    def activate(start, results):
         for row in range(chunk):
-            seen = inside(start + row, 1)
-            fill(act, start + row, *[jnp.where(seen, r[row], 0.0) for r in results])
+            fill(
+                act,
+                start + row,
+                *[masked(start + row, 1, silu_of_half(0.5 * r[row] + bias1)) for r in results],
+            )
 
     def second(start):
         for phase in range(2):
-            acc = conv(act, start, chunk, width, phase, own_w2, other_w2, bias2)
+            acc = dots(act, start, chunk, width, phase, own_w2, other_w2) + bias2
             for row in range(chunk):
                 for side in range(2):
                     mixed[side, start + row, pl.ds(phase, width, stride=2), :] = acc[
@@ -268,14 +276,16 @@
             out_ref[row, :, pl.ds(own_at, half)] = mixed[0, row].astype(jnp.bfloat16)
             out_ref[row, :, pl.ds(other_at, half)] = mixed[1, row].astype(jnp.bfloat16)
 
-    for row in range(chunk):
+    for row in range(2 * chunk):
         hidden(row)
     for start in range(0, lines - 2, chunk):
-        for row in range(start + chunk, start + 2 * chunk):
+        results = first(start)
+        for row in range(start + 2 * chunk, min(start + 3 * chunk, lines)):
             hidden(row)
-        first(start)
-        if start >= chunk:
-            second(start - chunk)
+        if start >= 2 * chunk:
+            second(start - 2 * chunk)
+        activate(start, results)
+    second(lines - 4 - chunk)
 
 
 def total_over(block, axis):

time: 32.8 us -> 32.7 us (level)
  no operation moved by 1% of the time
where the time goes in v14:
time: 32.7 us; the launch traced here: 32.5 us
  starting transfers between devices  15.7 us (48%)
  Pallas kernels  10.4 us (32%)
  waiting for transfers between devices  6.11 us (19%)
    ppermute x4, starting transfers between devices, total_over(): lax.ppermute(block, axis, [(i, i ^ step) for i in range(size)])  7.9 us
    ppermute x1, starting transfers between devices, local(): above = lax.ppermute(lines, 'rows', to_next)  5.46 us
    pallas_call x1, Pallas kernels, local(): call(functools.partial(conv_kernel, count), [vmem] * 9, [((2 * rows, 2 *...  4.68 us
    ppermute x4, waiting for transfers between devices, total_over(): lax.ppermute(block, axis, [(i, i ^ step) for i in range(size)])  4.63 us
    pallas_call x1, Pallas kernels, local(): call(near_kernel, [hbm], [(shape_w, bf16)], [pltpu.SemaphoreType.DMA(())]...  1.6 us
    ppermute x1, waiting for transfers between devices, local(): following = lax.ppermute(image, 'rows', to_previous)  1.46 us
    ppermute x1, starting transfers between devices, local(): following = lax.ppermute(image, 'rows', to_previous)  1.28 us
    pallas_call x1, Pallas kernels, local(): call(own_kernel, [vmem] * 3, [((rows, total, 3 * cin), bf16), ((2 * rows...  1.26 us
  transfers between devices with their start and end apart: 11, of which 5 were waited for; matrix products, arithmetic and copies ran while one was open for 0% of the time, Pallas kernels for 17%

profile of v14, /device:TPU:0, one launch (start us, length us, event | category | flops | bytes accessed | tf_op | source)
XLA Modules:
  0.0 32.5 jit_solution(1050798613423221196)
XLA Ops:
  0.0 0.5 %collective-permute-start.1 = (bf16[4,4,512,128]{3,2,1,0:T(8,128)(2,1)}, bf16[4,4,512,128]{3,2,1,0:T(8,128)(2,1)S(1)}, u32[]{:S(2)}, u32[]{:S(2)}) collective-permute-start(bf16[4,4,512,128]{3,2,1,0:T(8,128)(2,1)} %param.9), channel_id=1, source_target_pairs={{0,1},{1,0},{2,3},{3,2},{4,5},{5,4},{6,7},{7,6},{8,9},{9,8},{10,11... | collective-permute-start | bytes 6291464 | tf_op jit(solution)/shard_map/ppermute | solution.py:344
  0.5 1.3 %collective-permute-start.2 = (bf16[2,128,512]{2,1,0:T(8,128)(2,1)}, bf16[2,128,512]{2,1,0:T(8,128)(2,1)S(1)}, u32[]{:S(2)}, u32[]{:S(2)}) collective-permute-start(bf16[2,128,512]{2,1,0:T(8,128)(2,1)} %image_ref.1), channel_id=1, source_target_pairs={{2,0},{4,2},{6,4},{8,6},{10,8},{12,10},{14,12},{3,1},{5,3},{7,5},{... | collective-permute-start | bytes 786440 | tf_op jit(solution)/shard_map/ppermute | solution.py:335
  1.7 1.1 %cut.1 = (bf16[2,128,512]{2,1,0:T(8,128)(2,1)S(1)}, bf16[2,16,512]{2,1,0:T(8,128)(2,1)S(1)}) custom-call(bf16[2,128,512]{2,1,0:T(8,128)(2,1)} %image_ref.1), custom_call_target="tpu_custom_call" | custom-call | bytes 2097152 | tf_op jit(solution)/shard_map/cut/pallas_call | solution.py:336
  2.8 0.1 collective-permute-start
  2.9 0.5 %collective-permute-start.10 = (bf16[3,3,256,128]{3,2,1,0:T(8,128)(2,1)}, bf16[3,3,256,128]{3,2,1,0:T(8,128)(2,1)S(1)}, u32[]{:S(2)}, u32[]{:S(2)}) collective-permute-start(bf16[3,3,256,128]{3,2,1,0:T(8,128)(2,1)} %own_w2.1), channel_id=1, source_target_pairs={{0,1},{1,0},{2,3},{3,2},{4,5},{5,4},{6,7},{7,6},{8,9},{9,8},{10,11... | collective-permute-start | bytes 1769480 | tf_op jit(solution)/shard_map/ppermute | solution.py:346
  3.4 0.1 collective-permute-start.9
  3.5 1.6 %near_weights.1.own_w = bf16[4,2,2,512,128]{4,3,2,1,0:T(8,128)(2,1)S(1)} custom-call(bf16[4,2,2,512,128]{4,3,2,1,0:T(8,128)(2,1)} %bitcast.9), custom_call_target="tpu_custom_call" | custom-call | bytes 2097152 | tf_op jit(solution)/shard_map/near_weights/pallas_call | solution.py:347
  5.1 5.5 %collective-permute-start.4 = (bf16[2,144,512]{2,1,0:T(8,128)(2,1)S(1)}, bf16[2,144,512]{2,1,0:T(8,128)(2,1)S(1)}, u32[]{:S(2)}, u32[]{:S(2)}) collective-permute-start(bf16[2,144,512]{2,1,0:T(8,128)(2,1)S(1)} %constant_dynamic-update-slice_fusion.lines_ref), channel_id=1, source_target_pairs={{0,2},{2,4},{4,6},{6,8},{8,10},{10,12},{12,14},{1,3},{3,5},{5,7},{... | collective-permute-start | bytes 884744 | tf_op jit(solution)/shard_map/ppermute | solution.py:351
  10.6 1.5 %collective-permute-done.2.lines_ref.next_ref = bf16[2,128,512]{2,1,0:T(8,128)(2,1)S(1)} collective-permute-done((bf16[2,128,512]{2,1,0:T(8,128)(2,1)}, bf16[2,128,512]{2,1,0:T(8,128)(2,1)S(1)}, u32[]{:S(2)}, u32[]{:S(2)}) %collective-permute-start.2) | collective-permute-done | bytes 262176 | tf_op jit(solution)/shard_map/ppermute | solution.py:335
  12.1 1.3 %deconv_own.1 = (bf16[2,144,1536]{2,1,0:T(8,128)(2,1)S(1)}, bf16[2,2,144,256]{3,2,1,0:T(8,128)(2,1)S(1)}, f32[2,144,256]{2,1,0:T(8,128)S(1)}, f32[2,2,144,256]{3,2,1,0:T(8,128)S(1)}, f32[2,256]{1,0:T(2,128)S(1)}) custom-call(bf16[2,144,512]{2,1,0:T(8,128)(2,1)S(1)} %constant_dynamic-update-slice_fusion.lines_ref, ...), custom_call_target="tpu_custom_call" | custom-call | flops 905969664 | bytes 2097152 | tf_op jit(solution)/shard_map/deconv_own/pallas_call | solution.py:353
  13.3 0.0 copy-start.2
  13.4 0.0 copy-start.4
  13.4 0.0 copy-start.5
  13.4 0.5 %deconv_next.1 = (bf16[2,2,144,256]{3,2,1,0:T(8,128)(2,1)S(1)}, bf16[1,144,1536]{2,1,0:T(8,128)(2,1)S(1)}, f32[8,128]{1,0:T(8,128)S(1)}) custom-call(bf16[2,128,512]{2,1,0:T(8,128)(2,1)S(1)} %collective-permute-done.2.lines_ref.next_ref, bf16[2,16,512]{2,1,0:T(8,128)(2,1)S(1)} %collective-permute-done.3.edge_ref.next_edge_ref, ...), custom_call_target="tpu_custom_call" | custom-call | flops 301989888 | bytes 2097152 | tf_op jit(solution)/shard_map/deconv_next/pallas_call | solution.py:369
  13.9 0.6 %collective-permute-start.5 = (f32[8,128]{1,0:T(8,128)S(1)}, f32[8,128]{1,0:T(8,128)S(1)}, u32[]{:S(2)}, u32[]{:S(2)}) collective-permute-start(f32[8,128]{1,0:T(8,128)S(1)} %get-tuple-element.30), channel_id=1, source_target_pairs={{0,1},{1,0},{2,3},{3,2},{4,5},{5,4},{6,7},{7,6},{8,9},{9,8},{10,11... | collective-permute-start | bytes 12296 | tf_op jit(solution)/shard_map/ppermute | solution.py:297
  14.5 0.8 %collective-permute-done.5 = f32[8,128]{1,0:T(8,128)S(1)} collective-permute-done((f32[8,128]{1,0:T(8,128)S(1)}, f32[8,128]{1,0:T(8,128)S(1)}, u32[]{:S(2)}, u32[]{:S(2)}) %collective-permute-start.5) | collective-permute-done | bytes 4128 | tf_op jit(solution)/shard_map/ppermute | solution.py:297
  15.3 1.8 %collective-permute-start.6 = (f32[8,128]{1,0:T(8,128)S(1)}, f32[8,128]{1,0:T(8,128)S(1)}, u32[]{:S(2)}, u32[]{:S(2)}) collective-permute-start(f32[8,128]{1,0:T(8,128)S(1)} %add.12), channel_id=1, source_target_pairs={{0,4},{2,6},{4,0},{6,2},{8,12},{10,14},{12,8},{14,10},{1,5},{3,7},... | collective-permute-start | bytes 12296 | tf_op jit(solution)/shard_map/ppermute | solution.py:297
  17.1 1.8 %collective-permute-done.6 = f32[8,128]{1,0:T(8,128)S(1)} collective-permute-done((f32[8,128]{1,0:T(8,128)S(1)}, f32[8,128]{1,0:T(8,128)S(1)}, u32[]{:S(2)}, u32[]{:S(2)}) %collective-permute-start.6) | collective-permute-done | bytes 4128 | tf_op jit(solution)/shard_map/ppermute | solution.py:297
  18.9 2.8 %collective-permute-start.7 = (f32[8,128]{1,0:T(8,128)S(1)}, f32[8,128]{1,0:T(8,128)S(1)}, u32[]{:S(2)}, u32[]{:S(2)}) collective-permute-start(f32[8,128]{1,0:T(8,128)S(1)} %add.13), channel_id=1, source_target_pairs={{0,8},{2,10},{4,12},{6,14},{8,0},{10,2},{12,4},{14,6},{1,9},{3,11}... | collective-permute-start | bytes 12296 | tf_op jit(solution)/shard_map/ppermute | solution.py:297
  21.8 1.7 %collective-permute-done.7 = f32[8,128]{1,0:T(8,128)S(1)} collective-permute-done((f32[8,128]{1,0:T(8,128)S(1)}, f32[8,128]{1,0:T(8,128)S(1)}, u32[]{:S(2)}, u32[]{:S(2)}) %collective-permute-start.7) | collective-permute-done | bytes 4128 | tf_op jit(solution)/shard_map/ppermute | solution.py:297
  23.4 2.7 %collective-permute-start.8 = (f32[8,128]{1,0:T(8,128)S(1)}, f32[8,128]{1,0:T(8,128)S(1)}, u32[]{:S(2)}, u32[]{:S(2)}) collective-permute-start(f32[8,128]{1,0:T(8,128)S(1)} %add.14), channel_id=1, source_target_pairs={{0,2},{2,0},{4,6},{6,4},{8,10},{10,8},{12,14},{14,12},{1,3},{3,1},... | collective-permute-start | bytes 12296 | tf_op jit(solution)/shard_map/ppermute | solution.py:297
  26.2 1.2 %deconv_halo.1.halo_ref = bf16[4,2,144,256]{3,2,1,0:T(8,128)(2,1)S(1)} custom-call(bf16[2,144,512]{2,1,0:T(8,128)(2,1)S(1)} %collective-permute-done.4.above_ref, bf16[2,128,512]{2,1,0:T(8,128)(2,1)S(1)} %collective-permute-done.2.lines_ref.next_ref, bf16[2,16,512]{2,1,0:T(8,128)(2,1)S(1)} %collective-permute-done.3.edge_ref.next_edge_ref, ...), custom_call_target="tpu_custom_call" | custom-call | flops 1207959552 | bytes 2097152 | tf_op jit(solution)/shard_map/deconv_halo/pallas_call | solution.py:377
  27.4 0.3 %collective-permute-done.8 = f32[8,128]{1,0:T(8,128)S(1)} collective-permute-done((f32[8,128]{1,0:T(8,128)S(1)}, f32[8,128]{1,0:T(8,128)S(1)}, u32[]{:S(2)}, u32[]{:S(2)}) %collective-permute-start.8) | collective-permute-done | bytes 4128 | tf_op jit(solution)/shard_map/ppermute | solution.py:297
  27.8 4.7 %convs.1 = bf16[4,256,256]{2,1,0:T(8,128)(2,1)} custom-call(bf16[2,2,144,256]{3,2,1,0:T(8,128)(2,1)S(1)} %get-tuple-element.23.u_ref, bf16[2,2,144,256]{3,2,1,0:T(8,128)(2,1)S(1)} %get-tuple-element.26.u_next_ref, bf16[4,2,144,256]{3,2,1,0:T(8,128)(2,1)S(1)} %deconv_halo.1.halo_ref, f32[8,128]{1,0:T(8,128)S(1)} %add.15.stats_ref, ...), custom_call_target="tpu_custom_call" | custom-call | flops 5000000000 | bytes 2097152 | tf_op jit(solution)/shard_map/convs/pallas_call | solution.py:388
  (24 shorter events, 0.1 us)
Async XLA Ops:
  0.0 12.1 %collective-permute-start.1 = (bf16[4,4,512,128]{3,2,1,0:T(8,128)(2,1)}, bf16[4,4,512,128]{3,2,1,0:T(8,128)(2,1)S(1)}, u32[]{:S(2)}, u32[]{:S(2)}) collective-permute-start(bf16[4,4,512,128]{3,2,1,0:T(8,128)(2,1)} %param.9), channel_id=1, source_target_pairs={{0,1},{1,0},{2,3},{3,2},{4,5},{5,4},{6,7},{7,6},{8,9},{9,8},{10,11... | collective-permute-start | bytes 6291464 | tf_op jit(solution)/shard_map/ppermute | solution.py:344
  0.5 11.6 %collective-permute-start.2 = (bf16[2,128,512]{2,1,0:T(8,128)(2,1)}, bf16[2,128,512]{2,1,0:T(8,128)(2,1)S(1)}, u32[]{:S(2)}, u32[]{:S(2)}) collective-permute-start(bf16[2,128,512]{2,1,0:T(8,128)(2,1)} %image_ref.1), channel_id=1, source_target_pairs={{2,0},{4,2},{6,4},{8,6},{10,8},{12,10},{14,12},{3,1},{5,3},{7,5},{... | collective-permute-start | bytes 786440 | tf_op jit(solution)/shard_map/ppermute | solution.py:335
  2.8 2.3 %collective-permute-start = (bf16[2,16,512]{2,1,0:T(8,128)(2,1)S(1)}, bf16[2,16,512]{2,1,0:T(8,128)(2,1)S(1)}, u32[]{:S(2)}, u32[]{:S(2)}) collective-permute-start(bf16[2,16,512]{2,1,0:T(8,128)(2,1)S(1)} %get-tuple-element.20), channel_id=1, source_target_pairs={{0,1},{1,0},{2,3},{3,2},{4,5},{5,4},{6,7},{7,6},{8,9},{9,8},{10,11... | collective-permute-start | bytes 98312 | tf_op jit(solution)/shard_map/ppermute | solution.py:343
  2.9 24.8 %collective-permute-start.10 = (bf16[3,3,256,128]{3,2,1,0:T(8,128)(2,1)}, bf16[3,3,256,128]{3,2,1,0:T(8,128)(2,1)S(1)}, u32[]{:S(2)}, u32[]{:S(2)}) collective-permute-start(bf16[3,3,256,128]{3,2,1,0:T(8,128)(2,1)} %own_w2.1), channel_id=1, source_target_pairs={{0,1},{1,0},{2,3},{3,2},{4,5},{5,4},{6,7},{7,6},{8,9},{9,8},{10,11... | collective-permute-start | bytes 1769480 | tf_op jit(solution)/shard_map/ppermute | solution.py:346
  3.4 24.4 %collective-permute-start.9 = (bf16[3,3,256,128]{3,2,1,0:T(8,128)(2,1)}, bf16[3,3,256,128]{3,2,1,0:T(8,128)(2,1)S(1)}, u32[]{:S(2)}, u32[]{:S(2)}) collective-permute-start(bf16[3,3,256,128]{3,2,1,0:T(8,128)(2,1)} %own_w1.1), channel_id=1, source_target_pairs={{0,1},{1,0},{2,3},{3,2},{4,5},{5,4},{6,7},{7,6},{8,9},{9,8},{10,11... | collective-permute-start | bytes 1769480 | tf_op jit(solution)/shard_map/ppermute | solution.py:345
  5.1 21.1 %collective-permute-start.4 = (bf16[2,144,512]{2,1,0:T(8,128)(2,1)S(1)}, bf16[2,144,512]{2,1,0:T(8,128)(2,1)S(1)}, u32[]{:S(2)}, u32[]{:S(2)}) collective-permute-start(bf16[2,144,512]{2,1,0:T(8,128)(2,1)S(1)} %constant_dynamic-update-slice_fusion.lines_ref), channel_id=1, source_target_pairs={{0,2},{2,4},{4,6},{6,8},{8,10},{10,12},{12,14},{1,3},{3,5},{5,7},{... | collective-permute-start | bytes 884744 | tf_op jit(solution)/shard_map/ppermute | solution.py:351
  12.1 1.3 %collective-permute-start.3 = (bf16[2,16,512]{2,1,0:T(8,128)(2,1)S(1)}, bf16[2,16,512]{2,1,0:T(8,128)(2,1)S(1)}, u32[]{:S(2)}, u32[]{:S(2)}) collective-permute-start(bf16[2,16,512]{2,1,0:T(8,128)(2,1)S(1)} %next_edges.1), channel_id=1, source_target_pairs={{0,1},{1,0},{2,3},{3,2},{4,5},{5,4},{6,7},{7,6},{8,9},{9,8},{10,11... | collective-permute-start | bytes 98312 | tf_op jit(solution)/shard_map/ppermute | solution.py:368
  13.3 8.4 %copy-start.2 = (f32[256]{0:T(256)S(1)}, f32[256]{0:T(256)}, u32[]{:S(2)}) copy-start(f32[256]{0:T(256)} %param.15) | copy-start | bytes 3076
  13.3 8.4 %copy-start.3 = (f32[256]{0:T(256)S(1)}, f32[256]{0:T(256)}, u32[]{:S(2)}) copy-start(f32[256]{0:T(256)} %param.13) | copy-start | bytes 3076
  13.4 8.4 %copy-start.4 = (f32[256]{0:T(256)S(1)}, f32[256]{0:T(256)}, u32[]{:S(2)}) copy-start(f32[256]{0:T(256)} %param.11) | copy-start | bytes 3076
  13.4 8.4 %copy-start.5 = (f32[256]{0:T(256)S(1)}, f32[256]{0:T(256)}, u32[]{:S(2)}) copy-start(f32[256]{0:T(256)} %param.10) | copy-start | bytes 3076
  13.9 1.4 %collective-permute-start.5 = (f32[8,128]{1,0:T(8,128)S(1)}, f32[8,128]{1,0:T(8,128)S(1)}, u32[]{:S(2)}, u32[]{:S(2)}) collective-permute-start(f32[8,128]{1,0:T(8,128)S(1)} %get-tuple-element.30), channel_id=1, source_target_pairs={{0,1},{1,0},{2,3},{3,2},{4,5},{5,4},{6,7},{7,6},{8,9},{9,8},{10,11... | collective-permute-start | bytes 12296 | tf_op jit(solution)/shard_map/ppermute | solution.py:297
  15.3 3.6 %collective-permute-start.6 = (f32[8,128]{1,0:T(8,128)S(1)}, f32[8,128]{1,0:T(8,128)S(1)}, u32[]{:S(2)}, u32[]{:S(2)}) collective-permute-start(f32[8,128]{1,0:T(8,128)S(1)} %add.12), channel_id=1, source_target_pairs={{0,4},{2,6},{4,0},{6,2},{8,12},{10,14},{12,8},{14,10},{1,5},{3,7},... | collective-permute-start | bytes 12296 | tf_op jit(solution)/shard_map/ppermute | solution.py:297
  18.9 4.5 %collective-permute-start.7 = (f32[8,128]{1,0:T(8,128)S(1)}, f32[8,128]{1,0:T(8,128)S(1)}, u32[]{:S(2)}, u32[]{:S(2)}) collective-permute-start(f32[8,128]{1,0:T(8,128)S(1)} %add.13), channel_id=1, source_target_pairs={{0,8},{2,10},{4,12},{6,14},{8,0},{10,2},{12,4},{14,6},{1,9},{3,11}... | collective-permute-start | bytes 12296 | tf_op jit(solution)/shard_map/ppermute | solution.py:297
  23.4 4.3 %collective-permute-start.8 = (f32[8,128]{1,0:T(8,128)S(1)}, f32[8,128]{1,0:T(8,128)S(1)}, u32[]{:S(2)}, u32[]{:S(2)}) collective-permute-start(f32[8,128]{1,0:T(8,128)S(1)} %add.14), channel_id=1, source_target_pairs={{0,2},{2,0},{4,6},{6,4},{8,10},{10,8},{12,14},{14,12},{1,3},{3,1},... | collective-permute-start | bytes 12296 | tf_op jit(solution)/shard_map/ppermute | solution.py:297
  26.2 1.6 %copy-start = (bf16[3,3,256,128]{3,2,1,0:T(8,128)(2,1)S(1)}, bf16[3,3,256,128]{3,2,1,0:T(8,128)(2,1)}, u32[]{:S(2)}) copy-start(bf16[3,3,256,128]{3,2,1,0:T(8,128)(2,1)} %own_w1.1) | copy-start | bytes 1769476
  26.2 1.6 %copy-start.1 = (bf16[3,3,256,128]{3,2,1,0:T(8,128)(2,1)S(1)}, bf16[3,3,256,128]{3,2,1,0:T(8,128)(2,1)}, u32[]{:S(2)}) copy-start(bf16[3,3,256,128]{3,2,1,0:T(8,128)(2,1)} %own_w2.1) | copy-start | bytes 1769476

commit v15 on v14

--- a/solution.py
+++ b/solution.py
@@ -40,29 +40,16 @@
         copy.wait()
 
 
-def pick_kernel(lines_ref, edges_ref):
-    width = lines_ref.shape[1]
-    at_left = lax.axis_index("fsdp") == 0
-
-    @pl.when(at_left)
-    def _():
-        edges_ref[...] = lines_ref[:, width - EDGE :]
-
-    @pl.when(jnp.logical_not(at_left))
-    def _():
-        edges_ref[...] = lines_ref[:, :EDGE]
-
-
 def near_kernel(weight_ref, near_ref, sem):
     copy = pltpu.make_async_copy(weight_ref, near_ref, sem)
     copy.start()
     copy.wait()
 
 
-def spread_line(out, main, edge):
+def spread_line(out, main, edge, inside=True):
     width, cin = main.shape
     line = jnp.concatenate([main.astype(jnp.float32), edge.astype(jnp.float32)], axis=0)
-    line = jnp.where(edge_mask(width), line, 0.0)
+    line = jnp.where(edge_mask(width) & inside, line, 0.0)
     out[:, 0:cin] = pltpu.roll(line, width + EDGE - 1, 0).astype(jnp.bfloat16)
     out[:, cin : 2 * cin] = line.astype(jnp.bfloat16)
     out[:, 2 * cin : 3 * cin] = pltpu.roll(line, 1, 0).astype(jnp.bfloat16)
@@ -90,45 +77,53 @@
     )
 
 
-def own_kernel(lines_ref, own_w, other_w, xs_ref, u_ref, part_ref, tail_ref, sums_ref):
+def sides():
+    place = lax.axis_index("rows")
+    return lax.axis_index("fsdp"), place > 0, place < lax.axis_size("rows") - 1
+
+
+def own_kernel(lines_ref, own_w, other_w, u_ref, shares_ref, sums_ref, xs_ref):
     rows, total, _ = lines_ref.shape
     width = total - EDGE
     for row in range(rows):
         spread_line(xs_ref.at[row], lines_ref[row, :width], lines_ref[row, width:])
-    first_here = lax.axis_index("rows") == 0
+    column, above, below = sides()
     sums = jnp.zeros((2, u_ref.shape[-1]), jnp.float32)
     for phase in range(2):
-        dot = functools.partial(tap_dot, phase=phase, own_w=own_w, other_w=other_w)
-        upper = dot(xs_ref[...], kr=1)
-        lower = dot(xs_ref[...], kr=3)
-        part_ref[phase] = upper[0]
-        tail_ref[phase, 1] = lower[rows - 1]
-        even = [(upper[row + 1] + lower[row]).astype(jnp.bfloat16) for row in range(rows - 1)]
-        upper = dot(xs_ref[...], kr=2)
-        lower = dot(xs_ref[1:], kr=0)
-        tail_ref[phase, 0] = upper[rows - 1]
-        odd = [(upper[row] + lower[row]).astype(jnp.bfloat16) for row in range(rows - 1)]
+        terms = [tap_dot(xs_ref[...], phase, kr, own_w, other_w) for kr in range(4)]
+        shares_ref[0, 0, phase] = terms[0][0]
+        shares_ref[0, 1, phase] = terms[1][0]
+        shares_ref[1, 0, phase] = terms[2][rows - 1]
+        shares_ref[1, 1, phase] = terms[3][rows - 1]
         for row in range(rows - 1):
-            u_ref[2 * row, phase] = odd[row]
-            u_ref[2 * row + 1, phase] = even[row]
-            sums += add_sums(odd[row], width) + add_sums(even[row], width)
-        sums += jnp.where(first_here, add_sums(part_ref[phase].astype(jnp.bfloat16), width), 0.0)
+            odd = (terms[2][row] + terms[0][row + 1]).astype(jnp.bfloat16)
+            even = (terms[3][row] + terms[1][row + 1]).astype(jnp.bfloat16)
+            u_ref[2 * row, phase] = odd
+            u_ref[2 * row + 1, phase] = even
+            sums += add_sums(odd, width) + add_sums(even, width)
+        bottom = add_sums(shares_ref[1, 0, phase].astype(jnp.bfloat16), width)
+        top = add_sums(shares_ref[0, 1, phase].astype(jnp.bfloat16), width)
+        sums += jnp.where((column == 0) & jnp.logical_not(below), bottom, 0.0)
+        sums += jnp.where((column == 1) & jnp.logical_not(above), top, 0.0)
     sums_ref[...] = sums
 
 
-def next_kernel(next_ref, edge_ref, tail_ref, sums_ref, own_w, other_w, u_ref, xs_ref, stats_ref):
-    width = next_ref.shape[1]
-    last_here = lax.axis_index("rows") == lax.axis_size("rows") - 1
-    spread_line(xs_ref.at[0], next_ref[0], edge_ref[0])
-    column = lax.axis_index("fsdp")
+def first_kernel(first_ref, shares_ref, sums_ref, own_w, other_w, u_ref, xs_ref, stats_ref):
+    width = first_ref.shape[1] - EDGE
+    column, above, below = sides()
+    near = 1 - column
+    inside = jnp.where(column == 0, above, below)
+    spread_line(xs_ref.at[0], first_ref[near, :width], first_ref[near, width:], inside)
     sums = sums_ref[...]
     for phase in range(2):
-        dot = functools.partial(tap_dot, phase=phase, own_w=own_w, other_w=other_w)
-        odd = (tail_ref[phase, 0] + dot(xs_ref[...], kr=0)[0]).astype(jnp.bfloat16)
-        even = (tail_ref[phase, 1] + dot(xs_ref[...], kr=1)[0]).astype(jnp.bfloat16)
+        odd = tap_dot(xs_ref[...], phase, 2 - 2 * column, own_w, other_w)[0]
+        odd = (shares_ref[column, 0, phase] + odd).astype(jnp.bfloat16)
+        even = tap_dot(xs_ref[...], phase, 3 - 2 * column, own_w, other_w)[0]
+        even = (shares_ref[column, 1, phase] + even).astype(jnp.bfloat16)
         u_ref[0, phase] = odd
         u_ref[1, phase] = even
-        sums += add_sums(odd, width) + jnp.where(last_here, 0.0, add_sums(even, width))
+        sums += jnp.where((column == 1) | above, add_sums(odd, width), 0.0)
+        sums += jnp.where((column == 0) | below, add_sums(even, width), 0.0)
     half = sums.shape[1] // 2
     halves = []
     for row in range(2):
@@ -137,18 +132,38 @@
     stats_ref[...] = jnp.concatenate(halves + [jnp.zeros((4, half), jnp.float32)], axis=0)
 
 
-def halo_kernel(above_ref, next_ref, next_edge_ref, xs_ref, xs_next_ref, part_ref, own_w, other_w, u_ref, xs_above, xs_below):
-    width = next_ref.shape[1]
-    for row in range(HALO):
-        spread_line(xs_above.at[row], above_ref[row, :width], above_ref[row, width:])
-    spread_line(xs_below.at[0], next_ref[1], next_edge_ref[1])
+def halo_kernel(
+    second_ref, first_ref, xs_near_ref, shares_ref, u_own_ref, u_first_ref, own_w, other_w, u_ref, xs_far, xs_second
+):
+    width = first_ref.shape[1] - EDGE
+    early = u_own_ref.shape[0]
+    column, above, below = sides()
+    inside = jnp.where(column == 0, above, below)
+    inside_second = jnp.where(column == 0, below, above)
+    end = u_ref.shape[0] - 1
+    first_at = jnp.where(column == 0, 1, end - 2)
+    second_at = jnp.where(column == 0, end - 2, 1)
+    first_end = column * end
+    second_end = (1 - column) * end
+    spread_line(xs_far.at[0], first_ref[column, :width], first_ref[column, width:], inside)
+    for n in range(HALO):
+        line = jnp.where(column == 0, n, 1 - n)
+        spread_line(xs_second.at[n], second_ref[line, :width], second_ref[line, width:], inside_second)
+    for row in range(early):
+        u_ref[3 + row] = u_own_ref[row]
+    for row in range(2):
+        u_ref[first_at + row] = u_first_ref[row]
     for phase in range(2):
-        dot = functools.partial(tap_dot, phase=phase, own_w=own_w, other_w=other_w)
-        outer = dot(xs_above[...], kr=3)
-        u_ref[0, phase] = (outer[0] + dot(xs_above[1:2], kr=1)[0]).astype(jnp.bfloat16)
-        u_ref[2, phase] = (outer[1] + part_ref[phase]).astype(jnp.bfloat16)
-        u_ref[1, phase] = (dot(xs_above[1:2], kr=2)[0] + dot(xs_ref[0:1], kr=0)[0]).astype(jnp.bfloat16)
-        u_ref[3, phase] = (dot(xs_next_ref[...], kr=2)[0] + dot(xs_below[...], kr=0)[0]).astype(jnp.bfloat16)
+
+        def dot(lines, kr):
+            return tap_dot(lines, phase, kr, own_w, other_w)[0]
+
+        near, far = xs_second[0:1], xs_second[1:2]
+        far_row = dot(xs_near_ref[...], 1 + column) + dot(xs_far[...], 3 - 3 * column)
+        u_ref[first_end, phase] = far_row.astype(jnp.bfloat16)
+        u_ref[second_at, phase] = (shares_ref[1 - column, 0, phase] + dot(near, 2 * column)).astype(jnp.bfloat16)
+        u_ref[second_at + 1, phase] = (shares_ref[1 - column, 1, phase] + dot(near, 1 + 2 * column)).astype(jnp.bfloat16)
+        u_ref[second_end, phase] = (dot(near, 2 - column) + dot(far, 3 * column)).astype(jnp.bfloat16)
 
 
 def group_sum(v, width):
@@ -172,11 +187,9 @@
 
 
 def conv_kernel(
-    count, u_ref, u_next_ref, halo_ref, stats_ref, params_ref, own_w1, other_w1, own_w2, other_w2, out_ref, g, act, mixed
+    count, u_ref, stats_ref, params_ref, own_w1, other_w1, own_w2, other_w2, out_ref, g, act, mixed
 ):
-    early, _, total, cout = u_ref.shape
-    main = early + u_next_ref.shape[0]
-    lines = main + 2 * HALO
+    lines, _, total, cout = u_ref.shape
     width = total - EDGE
     half = own_w1.shape[-1]
     column = lax.axis_index("fsdp")
@@ -221,19 +234,11 @@
         return value
 
     def hidden(row):
-        if row < 3:
-            source = halo_ref.at[row]
-        elif row < 3 + early:
-            source = u_ref.at[row - 3]
-        elif row < 3 + main:
-            source = u_next_ref.at[row - 3 - early]
-        else:
-            source = halo_ref.at[3]
         fill(
             g,
             row,
             *[
-                masked(row, HALO, silu_of_half(source[phase].astype(jnp.float32) * scale + shift))
+                masked(row, HALO, silu_of_half(u_ref[row, phase].astype(jnp.float32) * scale + shift))
                 for phase in range(2)
             ],
         )
@@ -288,14 +293,13 @@
     second(lines - 4 - chunk)
 
 
-def total_over(block, axis):
-    size = lax.axis_size(axis)
-    if size & (size - 1):
-        return lax.psum(block, axis)
+def total_over(block, last):
+    size = lax.axis_size("rows")
+    assert size & (size - 1) == 0
     steps = [2**n for n in range(size.bit_length() - 1)]
     for step in steps[1:] + steps[:1]:
-        block = block + lax.ppermute(block, axis, [(i, i ^ step) for i in range(size)])
-    return block
+        block = block + lax.ppermute(block, "rows", [(i, i ^ step) for i in range(size)])
+    return block + lax.ppermute(after(block, last), "fsdp", [(0, 1), (1, 0)])
 
 
 def after(value, *others):
@@ -311,8 +315,10 @@
     n_rows = lax.axis_size("rows")
     count = float(2 * rows * n_rows * 2 * width * columns * (cout // NORM_GROUPS))
     swap = [(0, 1), (1, 0)]
-    to_next = [(i, i + 1) for i in range(n_rows - 1)]
-    to_previous = [(i + 1, i) for i in range(n_rows - 1)]
+    ends = range(n_rows - 1)
+    bottom = 2 * n_rows - 1
+    to_first = [(2 * i, 2 * i + 2) for i in ends] + [(2 * i + 3, 2 * i + 1) for i in ends] + [(bottom - 1, bottom), (1, 0)]
+    to_second = [(2 * i + 2, 2 * i) for i in ends] + [(2 * i + 1, 2 * i + 3) for i in ends] + [(bottom, bottom - 1), (0, 1)]
     total = width + EDGE
     hbm = pl.BlockSpec(memory_space=pltpu.HBM)
     vmem = pl.BlockSpec(memory_space=pltpu.VMEM)
@@ -332,7 +338,7 @@
 
     in_hbm = functools.partial(pltpu.with_memory_space_constraint, memory_space=pltpu.HBM)
     shape_w = (taps, taps // 2, 2, cin, lanes)
-    following = lax.ppermute(image, "rows", to_previous)
+    both = ("rows", "fsdp")
     near, edges = call(
         cut_kernel,
         [hbm],
@@ -341,53 +347,51 @@
         "cut",
     )(in_hbm(image))
     edge = lax.ppermute(edges, "fsdp", swap)
-    other_w = lax.ppermute(deconv_weight, "fsdp", swap).reshape(shape_w)
-    first_other = lax.ppermute(after(first_weight, edges), "fsdp", swap)
-    second_other = lax.ppermute(after(second_weight, edges), "fsdp", swap)
+    lines = jnp.concatenate([near, edge], axis=1)
+    first = lax.ppermute(lines, both, to_first)
+    other_w = lax.ppermute(after(deconv_weight, edge), "fsdp", swap).reshape(shape_w)
+    first_other = lax.ppermute(after(first_weight, edge), "fsdp", swap)
+    second_other = lax.ppermute(after(second_weight, edge), "fsdp", swap)
     (own_w,) = call(near_kernel, [hbm], [(shape_w, bf16)], [pltpu.SemaphoreType.DMA(())], "near_weights")(
         in_hbm(after(deconv_weight, edges).reshape(shape_w))
     )
-    lines = jnp.concatenate([after(near, own_w), edge], axis=1)
-    above = lax.ppermute(lines, "rows", to_next)
     u_line = (2, total, cout)
-    xs, u, part, tail, sums = call(
+    spread = (1, total, 3 * cin)
+    u_own, shares, sums = call(
         own_kernel,
         [vmem] * 3,
         [
-            ((rows, total, 3 * cin), bf16),
             ((2 * rows - 2, *u_line), bf16),
-            (u_line, f32),
-            ((2, *u_line), f32),
+            ((2, 2, *u_line), f32),
             ((2, cout), f32),
         ],
+        [pltpu.VMEM((rows, total, 3 * cin), bf16)],
+        "deconv_own",
+        flops=2 * 2 * (2 * rows) * total * 4 * cin * cout,
+    )(lines, own_w, other_w)
+    second = lax.ppermute(after(lines, first, sums), both, to_second)
+    u_first, xs_near, stats = call(
+        first_kernel,
+        [vmem] * 5,
+        [((2, *u_line), bf16), (spread, bf16), ((8, cout // 2), f32)],
         [],
-        "deconv_own",
-        flops=2 * 2 * (2 * rows - 1) * total * 4 * cin * cout,
-    )(lines, own_w, other_w)
-    (next_edges,) = call(pick_kernel, [vmem], [((rows, EDGE, cin), bf16)], [], "next_edges")(following)
-    next_edge = lax.ppermute(next_edges, "fsdp", swap)
-    u_next, xs_next, stats = call(
-        next_kernel,
-        [vmem] * 6,
-        [((2, *u_line), bf16), ((1, total, 3 * cin), bf16), ((8, cout // 2), f32)],
-        [],
-        "deconv_next",
+        "deconv_first",
         flops=2 * 2 * total * 4 * cin * cout,
-    )(following, next_edge, tail, sums, own_w, other_w)
-    (halo,) = call(
+    )(first, shares, sums, own_w, other_w)
+    (u,) = call(
         halo_kernel,
         [vmem] * 8,
-        [((4, *u_line), bf16)],
-        [pltpu.VMEM((HALO, total, 3 * cin), bf16), pltpu.VMEM((1, total, 3 * cin), bf16)],
+        [((2 * rows + 2 * HALO, *u_line), bf16)],
+        [pltpu.VMEM(spread, bf16), pltpu.VMEM((HALO, *spread[1:]), bf16)],
         "deconv_halo",
-        flops=2 * 2 * 4 * total * 4 * cin * cout,
-    )(above, following, next_edge, xs, xs_next, part, own_w, other_w)
-
-    totals = total_over(total_over(stats, "fsdp"), "rows")
+        flops=2 * 2 * 3 * total * 4 * cin * cout,
+    )(second, first, xs_near, shares, u_own, u_first, own_w, other_w)
+
+    totals = total_over(stats, u)
     params = jnp.stack([norm_gain, norm_shift, first_bias, second_bias])
     (out,) = call(
         functools.partial(conv_kernel, count),
-        [vmem] * 9,
+        [vmem] * 7,
         [((2 * rows, 2 * width, cout), bf16)],
         [
             pltpu.VMEM((2 * rows + 2 * HALO, total, 4 * cout), bf16),
@@ -396,7 +400,7 @@
         ],
         "convs",
         flops=5 * 10**9,
-    )(u, u_next, halo, totals, params, first_weight, first_other, second_weight, second_other)
+    )(u, totals, params, first_weight, first_other, second_weight, second_other)
     return out
 
 

time: 32.7 us -> 37.3 us (1.14)
  waiting for transfers between devices: 6.11 us -> 16 us
  starting transfers between devices: 15.7 us -> 10.5 us
    ppermute x10 -> x9, waiting for transfers between devices: 6.11 us -> 15.1 us  [the longest x3 10 us: total_over(): lax.ppermute(block, 'rows', [(i, i ^ step) for i in range(size)])]
    ppermute x10 -> x9, starting transfers between devices: 15.6 us -> 9.95 us  [the longest x3 6.31 us: total_over(): lax.ppermute(block, 'rows', [(i, i ^ step) for i in range(size)])]
    ppermute x1, waiting for transfers between devices: 0.01 us -> 0.86 us  [local(): edge = lax.ppermute(edges, 'fsdp', swap)]
    ppermute x1, starting transfers between devices: 0.12 us -> 0.52 us  [local(): edge = lax.ppermute(edges, 'fsdp', swap)]
    pallas_call x5 -> x4, Pallas kernels: 7.71 us -> 7.68 us  [the longest x1 4.63 us: local(): call(functools.partial(conv_kernel, count), [vmem] * 7, [((2 * rows, 2 *...]
  transfers between devices with their start and end apart: 11 -> 10, of which waited for: 5 -> 6; matrix products, arithmetic and copies ran while one was open for 0% -> 0% of each run, Pallas kernels for 17% -> 13%
where the time goes in v15:
time: 37.3 us; the launch traced here: 37.1 us
  waiting for transfers between devices  16 us (43%)
  starting transfers between devices  10.5 us (28%)
  Pallas kernels  10.4 us (28%)
    ppermute x3, waiting for transfers between devices, total_over(): lax.ppermute(block, 'rows', [(i, i ^ step) for i in range(size)])  10 us
    ppermute x3, starting transfers between devices, total_over(): lax.ppermute(block, 'rows', [(i, i ^ step) for i in range(size)])  6.31 us
    pallas_call x1, Pallas kernels, local(): call(functools.partial(conv_kernel, count), [vmem] * 7, [((2 * rows, 2 *...  4.63 us
    ppermute x1, waiting for transfers between devices, local(): first = lax.ppermute(lines, both, to_first)  3.98 us
    ppermute x1, starting transfers between devices, local(): first = lax.ppermute(lines, both, to_first)  2.73 us
    pallas_call x1, Pallas kernels, local(): call(near_kernel, [hbm], [(shape_w, bf16)], [pltpu.SemaphoreType.DMA(())]...  1.69 us
    pallas_call x1, Pallas kernels, local(): call(own_kernel, [vmem] * 3, [((2 * rows - 2, *u_line), bf16), ((2, 2, *u...  1.4 us
    pallas_call x1, Pallas kernels, local(): call(halo_kernel, [vmem] * 8, [((2 * rows + 2 * HALO, *u_line), bf16)], [...  1.13 us
  transfers between devices with their start and end apart: 10, of which 6 were waited for; matrix products, arithmetic and copies ran while one was open for 0% of the time, Pallas kernels for 13%

profile of v15, /device:TPU:0, one launch (start us, length us, event | category | flops | bytes accessed | tf_op | source)
XLA Modules:
  0.0 37.1 jit_solution(9812639741009198720)
XLA Ops:
  0.0 1.0 %cut.1 = (bf16[2,128,512]{2,1,0:T(8,128)(2,1)S(1)}, bf16[2,16,512]{2,1,0:T(8,128)(2,1)S(1)}) custom-call(bf16[2,128,512]{2,1,0:T(8,128)(2,1)} %image_ref.1), custom_call_target="tpu_custom_call" | custom-call | bytes 2097152 | tf_op jit(solution)/shard_map/cut/pallas_call | solution.py:342
  1.1 0.5 %collective-permute-start = (bf16[2,16,512]{2,1,0:T(8,128)(2,1)S(1)}, bf16[2,16,512]{2,1,0:T(8,128)(2,1)S(1)}, u32[]{:S(2)}, u32[]{:S(2)}) collective-permute-start(bf16[2,16,512]{2,1,0:T(8,128)(2,1)S(1)} %get-tuple-element.20), channel_id=1, source_target_pairs={{0,1},{1,0},{2,3},{3,2},{4,5},{5,4},{6,7},{7,6},{8,9},{9,8},{10,11... | collective-permute-start | bytes 98312 | tf_op jit(solution)/shard_map/ppermute | solution.py:349
  1.6 0.9 %collective-permute-done = bf16[2,16,512]{2,1,0:T(8,128)(2,1)S(1)} collective-permute-done((bf16[2,16,512]{2,1,0:T(8,128)(2,1)S(1)}, bf16[2,16,512]{2,1,0:T(8,128)(2,1)S(1)}, u32[]{:S(2)}, u32[]{:S(2)}) %collective-permute-start) | collective-permute-done | bytes 32800 | tf_op jit(solution)/shard_map/ppermute | solution.py:349
  2.4 0.3 collective-permute-start.2
  2.8 2.7 %collective-permute-start.1 = (bf16[2,144,512]{2,1,0:T(8,128)(2,1)S(1)}, bf16[2,144,512]{2,1,0:T(8,128)(2,1)S(1)}, u32[]{:S(2)}, u32[]{:S(2)}) collective-permute-start(bf16[2,144,512]{2,1,0:T(8,128)(2,1)S(1)} %constant_dynamic-update-slice_fusion.lines_ref), channel_id=1, source_target_pairs={{0,2},{2,4},{4,6},{6,8},{8,10},{10,12},{12,14},{3,1},{5,3},{7,5},{... | collective-permute-start | bytes 884744 | tf_op jit(solution)/shard_map/ppermute | solution.py:351
  5.6 1.7 %near_weights.1.own_w = bf16[4,2,2,512,128]{4,3,2,1,0:T(8,128)(2,1)S(1)} custom-call(bf16[4,2,2,512,128]{4,3,2,1,0:T(8,128)(2,1)} %bitcast.9), custom_call_target="tpu_custom_call" | custom-call | bytes 2097152 | tf_op jit(solution)/shard_map/near_weights/pallas_call | solution.py:355
  7.3 0.1 collective-permute-start.8
  7.3 0.1 copy-done.1
  7.4 0.4 %collective-permute-start.9 = (bf16[3,3,256,128]{3,2,1,0:T(8,128)(2,1)S(1)}, bf16[3,3,256,128]{3,2,1,0:T(8,128)(2,1)S(1)}, u32[]{:S(2)}, u32[]{:S(2)}) collective-permute-start(bf16[3,3,256,128]{3,2,1,0:T(8,128)(2,1)S(1)} %copy-done.1), channel_id=1, source_target_pairs={{0,1},{1,0},{2,3},{3,2},{4,5},{5,4},{6,7},{7,6},{8,9},{9,8},{10,11... | collective-permute-start | bytes 1769480 | tf_op jit(solution)/shard_map/ppermute | solution.py:354
  7.8 1.4 %deconv_own.1 = (bf16[2,2,144,256]{3,2,1,0:T(8,128)(2,1)S(1)}, f32[2,2,2,144,256]{4,3,2,1,0:T(8,128)S(1)}, f32[2,256]{1,0:T(2,128)S(1)}) custom-call(bf16[2,144,512]{2,1,0:T(8,128)(2,1)S(1)} %constant_dynamic-update-slice_fusion.lines_ref, bf16[4,2,2,512,128]{4,3,2,1,0:T(8,128)(2,1)S(1)} %near_weights.1.own_w, bf16[4,2,2,512,128]{4,3,2,1,0:T(8,128)(2,1)S(1)} %bitcast.6), custom_call_target="tpu_custom_call" | custom-call | flops 1207959552 | bytes 2097152 | tf_op jit(solution)/shard_map/deconv_own/pallas_call | solution.py:360
  9.3 4.0 %collective-permute-done.1.first_ref = bf16[2,144,512]{2,1,0:T(8,128)(2,1)S(1)} collective-permute-done((bf16[2,144,512]{2,1,0:T(8,128)(2,1)S(1)}, bf16[2,144,512]{2,1,0:T(8,128)(2,1)S(1)}, u32[]{:S(2)}, u32[]{:S(2)}) %collective-permute-start.1) | collective-permute-done | bytes 294944 | tf_op jit(solution)/shard_map/ppermute | solution.py:351
  13.2 0.5 %deconv_first.1 = (bf16[2,2,144,256]{3,2,1,0:T(8,128)(2,1)S(1)}, bf16[1,144,1536]{2,1,0:T(8,128)(2,1)S(1)}, f32[8,128]{1,0:T(8,128)S(1)}) custom-call(bf16[2,144,512]{2,1,0:T(8,128)(2,1)S(1)} %collective-permute-done.1.first_ref, f32[2,2,2,144,256]{4,3,2,1,0:T(8,128)S(1)} %get-tuple-element.25.shares_ref, f32[2,256]{1,0:T(2,128)S(1)} %get-tuple-element.23.sums_ref, ...), custom_call_target="tpu_custom_call" | custom-call | flops 301989888 | bytes 2097152 | tf_op jit(solution)/shard_map/deconv_first/pallas_call | solution.py:373
  13.8 4.0 %collective-permute-start.4 = (f32[8,128]{1,0:T(8,128)S(1)}, f32[8,128]{1,0:T(8,128)S(1)}, u32[]{:S(2)}, u32[]{:S(2)}) collective-permute-start(f32[8,128]{1,0:T(8,128)S(1)} %get-tuple-element.29), channel_id=1, source_target_pairs={{0,4},{2,6},{4,0},{6,2},{8,12},{10,14},{12,8},{14,10},{1,5},{3,7},... | collective-permute-start | bytes 12296 | tf_op jit(solution)/shard_map/ppermute | solution.py:301
  17.8 4.2 %collective-permute-done.4 = f32[8,128]{1,0:T(8,128)S(1)} collective-permute-done((f32[8,128]{1,0:T(8,128)S(1)}, f32[8,128]{1,0:T(8,128)S(1)}, u32[]{:S(2)}, u32[]{:S(2)}) %collective-permute-start.4) | collective-permute-done | bytes 4128 | tf_op jit(solution)/shard_map/ppermute | solution.py:301
  22.0 2.3 %collective-permute-start.5 = (f32[8,128]{1,0:T(8,128)S(1)}, f32[8,128]{1,0:T(8,128)S(1)}, u32[]{:S(2)}, u32[]{:S(2)}) collective-permute-start(f32[8,128]{1,0:T(8,128)S(1)} %add.12), channel_id=1, source_target_pairs={{0,8},{2,10},{4,12},{6,14},{8,0},{10,2},{12,4},{14,6},{1,9},{3,11}... | collective-permute-start | bytes 12296 | tf_op jit(solution)/shard_map/ppermute | solution.py:301
  24.3 2.2 %collective-permute-done.5 = f32[8,128]{1,0:T(8,128)S(1)} collective-permute-done((f32[8,128]{1,0:T(8,128)S(1)}, f32[8,128]{1,0:T(8,128)S(1)}, u32[]{:S(2)}, u32[]{:S(2)}) %collective-permute-start.5) | collective-permute-done | bytes 4128 | tf_op jit(solution)/shard_map/ppermute | solution.py:301
  26.5 3.6 %collective-permute-done.6 = f32[8,128]{1,0:T(8,128)S(1)} collective-permute-done((f32[8,128]{1,0:T(8,128)S(1)}, f32[8,128]{1,0:T(8,128)S(1)}, u32[]{:S(2)}, u32[]{:S(2)}) %collective-permute-start.6) | collective-permute-done | bytes 4128 | tf_op jit(solution)/shard_map/ppermute | solution.py:301
  30.1 0.0 copy-start.3
  30.1 0.0 copy-start.4
  30.1 0.0 copy-start.5
  30.1 1.1 %deconv_halo.1.u_ref = bf16[8,2,144,256]{3,2,1,0:T(8,128)(2,1)S(1)} custom-call(bf16[2,144,512]{2,1,0:T(8,128)(2,1)S(1)} %collective-permute-done.3.second_ref, bf16[2,144,512]{2,1,0:T(8,128)(2,1)S(1)} %collective-permute-done.1.first_ref, bf16[1,144,1536]{2,1,0:T(8,128)(2,1)S(1)} %get-tuple-element.26.xs_near_ref, ...), custom_call_target="tpu_custom_call" | custom-call | flops 905969664 | bytes 2097152 | tf_op jit(solution)/shard_map/deconv_halo/pallas_call | solution.py:381
  31.3 0.1 collective-permute-start.7
  31.4 1.1 %collective-permute-done.7 = f32[8,128]{1,0:T(8,128)S(1)} collective-permute-done((f32[8,128]{1,0:T(8,128)S(1)}, f32[8,128]{1,0:T(8,128)S(1)}, u32[]{:S(2)}, u32[]{:S(2)}) %collective-permute-start.7) | collective-permute-done | bytes 4128 | tf_op jit(solution)/shard_map/ppermute | solution.py:302
  32.5 4.6 %convs.1 = bf16[4,256,256]{2,1,0:T(8,128)(2,1)} custom-call(bf16[8,2,144,256]{3,2,1,0:T(8,128)(2,1)S(1)} %deconv_halo.1.u_ref, f32[8,128]{1,0:T(8,128)S(1)} %add.15.stats_ref, f32[4,256]{1,0:T(4,128)S(1)} %pad_maximum_fusion.params_ref, bf16[3,3,256,128]{3,2,1,0:T(8,128)(2,1)S(1)} %copy-done, bf16[3,3,256,128]{3,2,1,0:T(8,128)(2,1)S(1)} %collective-permute-done.8.other_w1, ...), custom_call_target="tpu_custom_call" | custom-call | flops 5000000000 | bytes 2097152 | tf_op jit(solution)/shard_map/convs/pallas_call | solution.py:392
  (21 shorter events, 0.1 us)
Async XLA Ops:
  1.1 1.4 %collective-permute-start = (bf16[2,16,512]{2,1,0:T(8,128)(2,1)S(1)}, bf16[2,16,512]{2,1,0:T(8,128)(2,1)S(1)}, u32[]{:S(2)}, u32[]{:S(2)}) collective-permute-start(bf16[2,16,512]{2,1,0:T(8,128)(2,1)S(1)} %get-tuple-element.20), channel_id=1, source_target_pairs={{0,1},{1,0},{2,3},{3,2},{4,5},{5,4},{6,7},{7,6},{8,9},{9,8},{10,11... | collective-permute-start | bytes 98312 | tf_op jit(solution)/shard_map/ppermute | solution.py:349
  2.4 5.4 %collective-permute-start.2 = (bf16[4,4,512,128]{3,2,1,0:T(8,128)(2,1)}, bf16[4,4,512,128]{3,2,1,0:T(8,128)(2,1)S(1)}, u32[]{:S(2)}, u32[]{:S(2)}) collective-permute-start(bf16[4,4,512,128]{3,2,1,0:T(8,128)(2,1)} %param.9), channel_id=1, source_target_pairs={{0,1},{1,0},{2,3},{3,2},{4,5},{5,4},{6,7},{7,6},{8,9},{9,8},{10,11... | collective-permute-start | bytes 6291464 | tf_op jit(solution)/shard_map/ppermute | solution.py:352
  2.8 10.4 %collective-permute-start.1 = (bf16[2,144,512]{2,1,0:T(8,128)(2,1)S(1)}, bf16[2,144,512]{2,1,0:T(8,128)(2,1)S(1)}, u32[]{:S(2)}, u32[]{:S(2)}) collective-permute-start(bf16[2,144,512]{2,1,0:T(8,128)(2,1)S(1)} %constant_dynamic-update-slice_fusion.lines_ref), channel_id=1, source_target_pairs={{0,2},{2,4},{4,6},{6,8},{8,10},{10,12},{12,14},{3,1},{5,3},{7,5},{... | collective-permute-start | bytes 884744 | tf_op jit(solution)/shard_map/ppermute | solution.py:351
  5.5 1.7 %copy-start = (bf16[3,3,256,128]{3,2,1,0:T(8,128)(2,1)S(1)}, bf16[3,3,256,128]{3,2,1,0:T(8,128)(2,1)}, u32[]{:S(2)}) copy-start(bf16[3,3,256,128]{3,2,1,0:T(8,128)(2,1)} %own_w1.1) | copy-start | bytes 1769476
  5.5 1.9 %copy-start.1 = (bf16[3,3,256,128]{3,2,1,0:T(8,128)(2,1)S(1)}, bf16[3,3,256,128]{3,2,1,0:T(8,128)(2,1)}, u32[]{:S(2)}) copy-start(bf16[3,3,256,128]{3,2,1,0:T(8,128)(2,1)} %own_w2.1) | copy-start | bytes 1769476
  7.3 25.2 %collective-permute-start.8 = (bf16[3,3,256,128]{3,2,1,0:T(8,128)(2,1)S(1)}, bf16[3,3,256,128]{3,2,1,0:T(8,128)(2,1)S(1)}, u32[]{:S(2)}, u32[]{:S(2)}) collective-permute-start(bf16[3,3,256,128]{3,2,1,0:T(8,128)(2,1)S(1)} %copy-done), channel_id=1, source_target_pairs={{0,1},{1,0},{2,3},{3,2},{4,5},{5,4},{6,7},{7,6},{8,9},{9,8},{10,11... | collective-permute-start | bytes 1769480 | tf_op jit(solution)/shard_map/ppermute | solution.py:353
  7.4 25.1 %collective-permute-start.9 = (bf16[3,3,256,128]{3,2,1,0:T(8,128)(2,1)S(1)}, bf16[3,3,256,128]{3,2,1,0:T(8,128)(2,1)S(1)}, u32[]{:S(2)}, u32[]{:S(2)}) collective-permute-start(bf16[3,3,256,128]{3,2,1,0:T(8,128)(2,1)S(1)} %copy-done.1), channel_id=1, source_target_pairs={{0,1},{1,0},{2,3},{3,2},{4,5},{5,4},{6,7},{7,6},{8,9},{9,8},{10,11... | collective-permute-start | bytes 1769480 | tf_op jit(solution)/shard_map/ppermute | solution.py:354
  13.2 16.9 %collective-permute-start.3 = (bf16[2,144,512]{2,1,0:T(8,128)(2,1)S(1)}, bf16[2,144,512]{2,1,0:T(8,128)(2,1)S(1)}, u32[]{:S(2)}, u32[]{:S(2)}) collective-permute-start(bf16[2,144,512]{2,1,0:T(8,128)(2,1)S(1)} %constant_dynamic-update-slice_fusion.lines_ref), channel_id=1, source_target_pairs={{2,0},{4,2},{6,4},{8,6},{10,8},{12,10},{14,12},{1,3},{3,5},{5,7},{... | collective-permute-start | bytes 884744 | tf_op jit(solution)/shard_map/ppermute | solution.py:372
  13.8 8.2 %collective-permute-start.4 = (f32[8,128]{1,0:T(8,128)S(1)}, f32[8,128]{1,0:T(8,128)S(1)}, u32[]{:S(2)}, u32[]{:S(2)}) collective-permute-start(f32[8,128]{1,0:T(8,128)S(1)} %get-tuple-element.29), channel_id=1, source_target_pairs={{0,4},{2,6},{4,0},{6,2},{8,12},{10,14},{12,8},{14,10},{1,5},{3,7},... | collective-permute-start | bytes 12296 | tf_op jit(solution)/shard_map/ppermute | solution.py:301
  22.0 4.5 %collective-permute-start.5 = (f32[8,128]{1,0:T(8,128)S(1)}, f32[8,128]{1,0:T(8,128)S(1)}, u32[]{:S(2)}, u32[]{:S(2)}) collective-permute-start(f32[8,128]{1,0:T(8,128)S(1)} %add.12), channel_id=1, source_target_pairs={{0,8},{2,10},{4,12},{6,14},{8,0},{10,2},{12,4},{14,6},{1,9},{3,11}... | collective-permute-start | bytes 12296 | tf_op jit(solution)/shard_map/ppermute | solution.py:301
  26.5 3.6 %collective-permute-start.6 = (f32[8,128]{1,0:T(8,128)S(1)}, f32[8,128]{1,0:T(8,128)S(1)}, u32[]{:S(2)}, u32[]{:S(2)}) collective-permute-start(f32[8,128]{1,0:T(8,128)S(1)} %add.13), channel_id=1, source_target_pairs={{0,2},{2,0},{4,6},{6,4},{8,10},{10,8},{12,14},{14,12},{1,3},{3,1},... | collective-permute-start | bytes 12296 | tf_op jit(solution)/shard_map/ppermute | solution.py:301
  30.1 1.3 %copy-start.2 = (f32[256]{0:T(256)S(1)}, f32[256]{0:T(256)}, u32[]{:S(2)}) copy-start(f32[256]{0:T(256)} %param.15) | copy-start | bytes 3076
  30.1 1.3 %copy-start.3 = (f32[256]{0:T(256)S(1)}, f32[256]{0:T(256)}, u32[]{:S(2)}) copy-start(f32[256]{0:T(256)} %param.13) | copy-start | bytes 3076
  30.1 1.3 %copy-start.4 = (f32[256]{0:T(256)S(1)}, f32[256]{0:T(256)}, u32[]{:S(2)}) copy-start(f32[256]{0:T(256)} %param.11) | copy-start | bytes 3076
  30.1 1.3 %copy-start.5 = (f32[256]{0:T(256)S(1)}, f32[256]{0:T(256)}, u32[]{:S(2)}) copy-start(f32[256]{0:T(256)} %param.10) | copy-start | bytes 3076
  31.3 1.2 %collective-permute-start.7 = (f32[8,128]{1,0:T(8,128)S(1)}, f32[8,128]{1,0:T(8,128)S(1)}, u32[]{:S(2)}, u32[]{:S(2)}) collective-permute-start(f32[8,128]{1,0:T(8,128)S(1)} %add.14), channel_id=1, source_target_pairs={{0,1},{1,0},{2,3},{3,2},{4,5},{5,4},{6,7},{7,6},{8,9},{9,8},{10,11... | collective-permute-start | bytes 12296 | tf_op jit(solution)/shard_map/ppermute | solution.py:302

commit v16 on v14

--- a/solution.py
+++ b/solution.py
@@ -187,10 +187,18 @@
         low, high = row[:, :half], row[:, half:]
         return jnp.concatenate([jnp.where(column == 0, low, high), jnp.where(column == 0, high, low)], axis=1)
 
-    def kernel_row(a, own, other):
+    def kernel(own, other):
         return jnp.concatenate(
             [
-                jnp.concatenate([ref[a, b, pl.ds(at, half), :] for b in range(3) for at in (own_at, other_at)], axis=0)
+                jnp.concatenate(
+                    [
+                        ref[a, b, pl.ds(at, half), :]
+                        for a in range(3)
+                        for b in range(3)
+                        for at in (own_at, other_at)
+                    ],
+                    axis=0,
+                )
                 for ref in (own, other)
             ],
             axis=1,
@@ -239,17 +247,14 @@
         )
 
     def dots(source, start, size, cells, phase, own, other):
-        total = None
-        for a in range(3):
-            term = jnp.dot(
-                source[start + a : start + a + size, 0:cells, phase * cout : (phase + 3) * cout].reshape(
-                    size * cells, 3 * cout
-                ),
-                kernel_row(a, own, other),
-                preferred_element_type=jnp.float32,
+        taps = [
+            source[start + a : start + a + size, 0:cells, phase * cout : (phase + 3) * cout].reshape(
+                size * cells, 3 * cout
             )
-            total = term if total is None else total + term
-        return total.reshape(size, cells, cout)
+            for a in range(3)
+        ]
+        out = jnp.dot(jnp.concatenate(taps, axis=1), kernel(own, other), preferred_element_type=jnp.float32)
+        return out.reshape(size, cells, cout)
 
     chunk = 2
 

time: 32.7 us -> 32.7 us (level)
  no operation moved by 1% of the time
where the time goes in v16:
time: 32.7 us; the launch traced here: 32.5 us
  starting transfers between devices  15.7 us (48%)
  Pallas kernels  10.4 us (32%)
  waiting for transfers between devices  6.11 us (19%)
    ppermute x4, starting transfers between devices, total_over(): lax.ppermute(block, axis, [(i, i ^ step) for i in range(size)])  7.9 us
    ppermute x1, starting transfers between devices, local(): above = lax.ppermute(lines, 'rows', to_next)  5.46 us
    pallas_call x1, Pallas kernels, local(): call(functools.partial(conv_kernel, count), [vmem] * 9, [((2 * rows, 2 *...  4.68 us
    ppermute x4, waiting for transfers between devices, total_over(): lax.ppermute(block, axis, [(i, i ^ step) for i in range(size)])  4.63 us
    pallas_call x1, Pallas kernels, local(): call(near_kernel, [hbm], [(shape_w, bf16)], [pltpu.SemaphoreType.DMA(())]...  1.6 us
    ppermute x1, waiting for transfers between devices, local(): following = lax.ppermute(image, 'rows', to_previous)  1.46 us
    ppermute x1, starting transfers between devices, local(): following = lax.ppermute(image, 'rows', to_previous)  1.28 us
    pallas_call x1, Pallas kernels, local(): call(own_kernel, [vmem] * 3, [((rows, total, 3 * cin), bf16), ((2 * rows...  1.26 us
  transfers between devices with their start and end apart: 11, of which 5 were waited for; matrix products, arithmetic and copies ran while one was open for 0% of the time, Pallas kernels for 17%

profile of v16, /device:TPU:0, one launch (start us, length us, event | category | flops | bytes accessed | tf_op | source)
XLA Modules:
  0.0 32.5 jit_solution(1175974616098932109)
XLA Ops:
  0.0 0.5 %collective-permute-start.1 = (bf16[4,4,512,128]{3,2,1,0:T(8,128)(2,1)}, bf16[4,4,512,128]{3,2,1,0:T(8,128)(2,1)S(1)}, u32[]{:S(2)}, u32[]{:S(2)}) collective-permute-start(bf16[4,4,512,128]{3,2,1,0:T(8,128)(2,1)} %param.9), channel_id=1, source_target_pairs={{0,1},{1,0},{2,3},{3,2},{4,5},{5,4},{6,7},{7,6},{8,9},{9,8},{10,11... | collective-permute-start | bytes 6291464 | tf_op jit(solution)/shard_map/ppermute | solution.py:349
  0.5 1.3 %collective-permute-start.2 = (bf16[2,128,512]{2,1,0:T(8,128)(2,1)}, bf16[2,128,512]{2,1,0:T(8,128)(2,1)S(1)}, u32[]{:S(2)}, u32[]{:S(2)}) collective-permute-start(bf16[2,128,512]{2,1,0:T(8,128)(2,1)} %image_ref.1), channel_id=1, source_target_pairs={{2,0},{4,2},{6,4},{8,6},{10,8},{12,10},{14,12},{3,1},{5,3},{7,5},{... | collective-permute-start | bytes 786440 | tf_op jit(solution)/shard_map/ppermute | solution.py:340
  1.7 1.1 %cut.1 = (bf16[2,128,512]{2,1,0:T(8,128)(2,1)S(1)}, bf16[2,16,512]{2,1,0:T(8,128)(2,1)S(1)}) custom-call(bf16[2,128,512]{2,1,0:T(8,128)(2,1)} %image_ref.1), custom_call_target="tpu_custom_call" | custom-call | bytes 2097152 | tf_op jit(solution)/shard_map/cut/pallas_call | solution.py:341
  2.8 0.1 collective-permute-start
  2.9 0.5 %collective-permute-start.10 = (bf16[3,3,256,128]{3,2,1,0:T(8,128)(2,1)}, bf16[3,3,256,128]{3,2,1,0:T(8,128)(2,1)S(1)}, u32[]{:S(2)}, u32[]{:S(2)}) collective-permute-start(bf16[3,3,256,128]{3,2,1,0:T(8,128)(2,1)} %own_w2.1), channel_id=1, source_target_pairs={{0,1},{1,0},{2,3},{3,2},{4,5},{5,4},{6,7},{7,6},{8,9},{9,8},{10,11... | collective-permute-start | bytes 1769480 | tf_op jit(solution)/shard_map/ppermute | solution.py:351
  3.4 0.1 collective-permute-start.9
  3.5 1.6 %near_weights.1.own_w = bf16[4,2,2,512,128]{4,3,2,1,0:T(8,128)(2,1)S(1)} custom-call(bf16[4,2,2,512,128]{4,3,2,1,0:T(8,128)(2,1)} %bitcast.9), custom_call_target="tpu_custom_call" | custom-call | bytes 2097152 | tf_op jit(solution)/shard_map/near_weights/pallas_call | solution.py:352
  5.1 5.5 %collective-permute-start.4 = (bf16[2,144,512]{2,1,0:T(8,128)(2,1)S(1)}, bf16[2,144,512]{2,1,0:T(8,128)(2,1)S(1)}, u32[]{:S(2)}, u32[]{:S(2)}) collective-permute-start(bf16[2,144,512]{2,1,0:T(8,128)(2,1)S(1)} %constant_dynamic-update-slice_fusion.lines_ref), channel_id=1, source_target_pairs={{0,2},{2,4},{4,6},{6,8},{8,10},{10,12},{12,14},{1,3},{3,5},{5,7},{... | collective-permute-start | bytes 884744 | tf_op jit(solution)/shard_map/ppermute | solution.py:356
  10.6 1.5 %collective-permute-done.2.lines_ref.next_ref = bf16[2,128,512]{2,1,0:T(8,128)(2,1)S(1)} collective-permute-done((bf16[2,128,512]{2,1,0:T(8,128)(2,1)}, bf16[2,128,512]{2,1,0:T(8,128)(2,1)S(1)}, u32[]{:S(2)}, u32[]{:S(2)}) %collective-permute-start.2) | collective-permute-done | bytes 262176 | tf_op jit(solution)/shard_map/ppermute | solution.py:340
  12.1 1.3 %deconv_own.1 = (bf16[2,144,1536]{2,1,0:T(8,128)(2,1)S(1)}, bf16[2,2,144,256]{3,2,1,0:T(8,128)(2,1)S(1)}, f32[2,144,256]{2,1,0:T(8,128)S(1)}, f32[2,2,144,256]{3,2,1,0:T(8,128)S(1)}, f32[2,256]{1,0:T(2,128)S(1)}) custom-call(bf16[2,144,512]{2,1,0:T(8,128)(2,1)S(1)} %constant_dynamic-update-slice_fusion.lines_ref, ...), custom_call_target="tpu_custom_call" | custom-call | flops 905969664 | bytes 2097152 | tf_op jit(solution)/shard_map/deconv_own/pallas_call | solution.py:358
  13.3 0.0 copy-start.2
  13.4 0.0 copy-start.4
  13.4 0.0 copy-start.5
  13.4 0.5 %deconv_next.1 = (bf16[2,2,144,256]{3,2,1,0:T(8,128)(2,1)S(1)}, bf16[1,144,1536]{2,1,0:T(8,128)(2,1)S(1)}, f32[8,128]{1,0:T(8,128)S(1)}) custom-call(bf16[2,128,512]{2,1,0:T(8,128)(2,1)S(1)} %collective-permute-done.2.lines_ref.next_ref, bf16[2,16,512]{2,1,0:T(8,128)(2,1)S(1)} %collective-permute-done.3.edge_ref.next_edge_ref, ...), custom_call_target="tpu_custom_call" | custom-call | flops 301989888 | bytes 2097152 | tf_op jit(solution)/shard_map/deconv_next/pallas_call | solution.py:374
  13.9 0.6 %collective-permute-start.5 = (f32[8,128]{1,0:T(8,128)S(1)}, f32[8,128]{1,0:T(8,128)S(1)}, u32[]{:S(2)}, u32[]{:S(2)}) collective-permute-start(f32[8,128]{1,0:T(8,128)S(1)} %get-tuple-element.30), channel_id=1, source_target_pairs={{0,1},{1,0},{2,3},{3,2},{4,5},{5,4},{6,7},{7,6},{8,9},{9,8},{10,11... | collective-permute-start | bytes 12296 | tf_op jit(solution)/shard_map/ppermute | solution.py:302
  14.5 0.8 %collective-permute-done.5 = f32[8,128]{1,0:T(8,128)S(1)} collective-permute-done((f32[8,128]{1,0:T(8,128)S(1)}, f32[8,128]{1,0:T(8,128)S(1)}, u32[]{:S(2)}, u32[]{:S(2)}) %collective-permute-start.5) | collective-permute-done | bytes 4128 | tf_op jit(solution)/shard_map/ppermute | solution.py:302
  15.3 1.8 %collective-permute-start.6 = (f32[8,128]{1,0:T(8,128)S(1)}, f32[8,128]{1,0:T(8,128)S(1)}, u32[]{:S(2)}, u32[]{:S(2)}) collective-permute-start(f32[8,128]{1,0:T(8,128)S(1)} %add.12), channel_id=1, source_target_pairs={{0,4},{2,6},{4,0},{6,2},{8,12},{10,14},{12,8},{14,10},{1,5},{3,7},... | collective-permute-start | bytes 12296 | tf_op jit(solution)/shard_map/ppermute | solution.py:302
  17.1 1.8 %collective-permute-done.6 = f32[8,128]{1,0:T(8,128)S(1)} collective-permute-done((f32[8,128]{1,0:T(8,128)S(1)}, f32[8,128]{1,0:T(8,128)S(1)}, u32[]{:S(2)}, u32[]{:S(2)}) %collective-permute-start.6) | collective-permute-done | bytes 4128 | tf_op jit(solution)/shard_map/ppermute | solution.py:302
  18.9 2.8 %collective-permute-start.7 = (f32[8,128]{1,0:T(8,128)S(1)}, f32[8,128]{1,0:T(8,128)S(1)}, u32[]{:S(2)}, u32[]{:S(2)}) collective-permute-start(f32[8,128]{1,0:T(8,128)S(1)} %add.13), channel_id=1, source_target_pairs={{0,8},{2,10},{4,12},{6,14},{8,0},{10,2},{12,4},{14,6},{1,9},{3,11}... | collective-permute-start | bytes 12296 | tf_op jit(solution)/shard_map/ppermute | solution.py:302
  21.8 1.7 %collective-permute-done.7 = f32[8,128]{1,0:T(8,128)S(1)} collective-permute-done((f32[8,128]{1,0:T(8,128)S(1)}, f32[8,128]{1,0:T(8,128)S(1)}, u32[]{:S(2)}, u32[]{:S(2)}) %collective-permute-start.7) | collective-permute-done | bytes 4128 | tf_op jit(solution)/shard_map/ppermute | solution.py:302
  23.4 2.7 %collective-permute-start.8 = (f32[8,128]{1,0:T(8,128)S(1)}, f32[8,128]{1,0:T(8,128)S(1)}, u32[]{:S(2)}, u32[]{:S(2)}) collective-permute-start(f32[8,128]{1,0:T(8,128)S(1)} %add.14), channel_id=1, source_target_pairs={{0,2},{2,0},{4,6},{6,4},{8,10},{10,8},{12,14},{14,12},{1,3},{3,1},... | collective-permute-start | bytes 12296 | tf_op jit(solution)/shard_map/ppermute | solution.py:302
  26.2 1.2 %deconv_halo.1.halo_ref = bf16[4,2,144,256]{3,2,1,0:T(8,128)(2,1)S(1)} custom-call(bf16[2,144,512]{2,1,0:T(8,128)(2,1)S(1)} %collective-permute-done.4.above_ref, bf16[2,128,512]{2,1,0:T(8,128)(2,1)S(1)} %collective-permute-done.2.lines_ref.next_ref, bf16[2,16,512]{2,1,0:T(8,128)(2,1)S(1)} %collective-permute-done.3.edge_ref.next_edge_ref, ...), custom_call_target="tpu_custom_call" | custom-call | flops 1207959552 | bytes 2097152 | tf_op jit(solution)/shard_map/deconv_halo/pallas_call | solution.py:382
  27.4 0.3 %collective-permute-done.8 = f32[8,128]{1,0:T(8,128)S(1)} collective-permute-done((f32[8,128]{1,0:T(8,128)S(1)}, f32[8,128]{1,0:T(8,128)S(1)}, u32[]{:S(2)}, u32[]{:S(2)}) %collective-permute-start.8) | collective-permute-done | bytes 4128 | tf_op jit(solution)/shard_map/ppermute | solution.py:302
  27.8 4.7 %convs.1 = bf16[4,256,256]{2,1,0:T(8,128)(2,1)} custom-call(bf16[2,2,144,256]{3,2,1,0:T(8,128)(2,1)S(1)} %get-tuple-element.23.u_ref, bf16[2,2,144,256]{3,2,1,0:T(8,128)(2,1)S(1)} %get-tuple-element.26.u_next_ref, bf16[4,2,144,256]{3,2,1,0:T(8,128)(2,1)S(1)} %deconv_halo.1.halo_ref, f32[8,128]{1,0:T(8,128)S(1)} %add.15.stats_ref, ...), custom_call_target="tpu_custom_call" | custom-call | flops 5000000000 | bytes 2097152 | tf_op jit(solution)/shard_map/convs/pallas_call | solution.py:393
  (24 shorter events, 0.1 us)
Async XLA Ops:
  0.0 12.1 %collective-permute-start.1 = (bf16[4,4,512,128]{3,2,1,0:T(8,128)(2,1)}, bf16[4,4,512,128]{3,2,1,0:T(8,128)(2,1)S(1)}, u32[]{:S(2)}, u32[]{:S(2)}) collective-permute-start(bf16[4,4,512,128]{3,2,1,0:T(8,128)(2,1)} %param.9), channel_id=1, source_target_pairs={{0,1},{1,0},{2,3},{3,2},{4,5},{5,4},{6,7},{7,6},{8,9},{9,8},{10,11... | collective-permute-start | bytes 6291464 | tf_op jit(solution)/shard_map/ppermute | solution.py:349
  0.5 11.6 %collective-permute-start.2 = (bf16[2,128,512]{2,1,0:T(8,128)(2,1)}, bf16[2,128,512]{2,1,0:T(8,128)(2,1)S(1)}, u32[]{:S(2)}, u32[]{:S(2)}) collective-permute-start(bf16[2,128,512]{2,1,0:T(8,128)(2,1)} %image_ref.1), channel_id=1, source_target_pairs={{2,0},{4,2},{6,4},{8,6},{10,8},{12,10},{14,12},{3,1},{5,3},{7,5},{... | collective-permute-start | bytes 786440 | tf_op jit(solution)/shard_map/ppermute | solution.py:340
  2.8 2.3 %collective-permute-start = (bf16[2,16,512]{2,1,0:T(8,128)(2,1)S(1)}, bf16[2,16,512]{2,1,0:T(8,128)(2,1)S(1)}, u32[]{:S(2)}, u32[]{:S(2)}) collective-permute-start(bf16[2,16,512]{2,1,0:T(8,128)(2,1)S(1)} %get-tuple-element.20), channel_id=1, source_target_pairs={{0,1},{1,0},{2,3},{3,2},{4,5},{5,4},{6,7},{7,6},{8,9},{9,8},{10,11... | collective-permute-start | bytes 98312 | tf_op jit(solution)/shard_map/ppermute | solution.py:348
  2.9 24.8 %collective-permute-start.10 = (bf16[3,3,256,128]{3,2,1,0:T(8,128)(2,1)}, bf16[3,3,256,128]{3,2,1,0:T(8,128)(2,1)S(1)}, u32[]{:S(2)}, u32[]{:S(2)}) collective-permute-start(bf16[3,3,256,128]{3,2,1,0:T(8,128)(2,1)} %own_w2.1), channel_id=1, source_target_pairs={{0,1},{1,0},{2,3},{3,2},{4,5},{5,4},{6,7},{7,6},{8,9},{9,8},{10,11... | collective-permute-start | bytes 1769480 | tf_op jit(solution)/shard_map/ppermute | solution.py:351
  3.4 24.4 %collective-permute-start.9 = (bf16[3,3,256,128]{3,2,1,0:T(8,128)(2,1)}, bf16[3,3,256,128]{3,2,1,0:T(8,128)(2,1)S(1)}, u32[]{:S(2)}, u32[]{:S(2)}) collective-permute-start(bf16[3,3,256,128]{3,2,1,0:T(8,128)(2,1)} %own_w1.1), channel_id=1, source_target_pairs={{0,1},{1,0},{2,3},{3,2},{4,5},{5,4},{6,7},{7,6},{8,9},{9,8},{10,11... | collective-permute-start | bytes 1769480 | tf_op jit(solution)/shard_map/ppermute | solution.py:350
  5.1 21.1 %collective-permute-start.4 = (bf16[2,144,512]{2,1,0:T(8,128)(2,1)S(1)}, bf16[2,144,512]{2,1,0:T(8,128)(2,1)S(1)}, u32[]{:S(2)}, u32[]{:S(2)}) collective-permute-start(bf16[2,144,512]{2,1,0:T(8,128)(2,1)S(1)} %constant_dynamic-update-slice_fusion.lines_ref), channel_id=1, source_target_pairs={{0,2},{2,4},{4,6},{6,8},{8,10},{10,12},{12,14},{1,3},{3,5},{5,7},{... | collective-permute-start | bytes 884744 | tf_op jit(solution)/shard_map/ppermute | solution.py:356
  12.1 1.3 %collective-permute-start.3 = (bf16[2,16,512]{2,1,0:T(8,128)(2,1)S(1)}, bf16[2,16,512]{2,1,0:T(8,128)(2,1)S(1)}, u32[]{:S(2)}, u32[]{:S(2)}) collective-permute-start(bf16[2,16,512]{2,1,0:T(8,128)(2,1)S(1)} %next_edges.1), channel_id=1, source_target_pairs={{0,1},{1,0},{2,3},{3,2},{4,5},{5,4},{6,7},{7,6},{8,9},{9,8},{10,11... | collective-permute-start | bytes 98312 | tf_op jit(solution)/shard_map/ppermute | solution.py:373
  13.3 8.4 %copy-start.2 = (f32[256]{0:T(256)S(1)}, f32[256]{0:T(256)}, u32[]{:S(2)}) copy-start(f32[256]{0:T(256)} %param.15) | copy-start | bytes 3076
  13.3 8.4 %copy-start.3 = (f32[256]{0:T(256)S(1)}, f32[256]{0:T(256)}, u32[]{:S(2)}) copy-start(f32[256]{0:T(256)} %param.13) | copy-start | bytes 3076
  13.4 8.4 %copy-start.4 = (f32[256]{0:T(256)S(1)}, f32[256]{0:T(256)}, u32[]{:S(2)}) copy-start(f32[256]{0:T(256)} %param.11) | copy-start | bytes 3076
  13.4 8.4 %copy-start.5 = (f32[256]{0:T(256)S(1)}, f32[256]{0:T(256)}, u32[]{:S(2)}) copy-start(f32[256]{0:T(256)} %param.10) | copy-start | bytes 3076
  13.9 1.4 %collective-permute-start.5 = (f32[8,128]{1,0:T(8,128)S(1)}, f32[8,128]{1,0:T(8,128)S(1)}, u32[]{:S(2)}, u32[]{:S(2)}) collective-permute-start(f32[8,128]{1,0:T(8,128)S(1)} %get-tuple-element.30), channel_id=1, source_target_pairs={{0,1},{1,0},{2,3},{3,2},{4,5},{5,4},{6,7},{7,6},{8,9},{9,8},{10,11... | collective-permute-start | bytes 12296 | tf_op jit(solution)/shard_map/ppermute | solution.py:302
  15.3 3.6 %collective-permute-start.6 = (f32[8,128]{1,0:T(8,128)S(1)}, f32[8,128]{1,0:T(8,128)S(1)}, u32[]{:S(2)}, u32[]{:S(2)}) collective-permute-start(f32[8,128]{1,0:T(8,128)S(1)} %add.12), channel_id=1, source_target_pairs={{0,4},{2,6},{4,0},{6,2},{8,12},{10,14},{12,8},{14,10},{1,5},{3,7},... | collective-permute-start | bytes 12296 | tf_op jit(solution)/shard_map/ppermute | solution.py:302
  18.9 4.5 %collective-permute-start.7 = (f32[8,128]{1,0:T(8,128)S(1)}, f32[8,128]{1,0:T(8,128)S(1)}, u32[]{:S(2)}, u32[]{:S(2)}) collective-permute-start(f32[8,128]{1,0:T(8,128)S(1)} %add.13), channel_id=1, source_target_pairs={{0,8},{2,10},{4,12},{6,14},{8,0},{10,2},{12,4},{14,6},{1,9},{3,11}... | collective-permute-start | bytes 12296 | tf_op jit(solution)/shard_map/ppermute | solution.py:302
  23.4 4.3 %collective-permute-start.8 = (f32[8,128]{1,0:T(8,128)S(1)}, f32[8,128]{1,0:T(8,128)S(1)}, u32[]{:S(2)}, u32[]{:S(2)}) collective-permute-start(f32[8,128]{1,0:T(8,128)S(1)} %add.14), channel_id=1, source_target_pairs={{0,2},{2,0},{4,6},{6,4},{8,10},{10,8},{12,14},{14,12},{1,3},{3,1},... | collective-permute-start | bytes 12296 | tf_op jit(solution)/shard_map/ppermute | solution.py:302
  26.2 1.6 %copy-start = (bf16[3,3,256,128]{3,2,1,0:T(8,128)(2,1)S(1)}, bf16[3,3,256,128]{3,2,1,0:T(8,128)(2,1)}, u32[]{:S(2)}) copy-start(bf16[3,3,256,128]{3,2,1,0:T(8,128)(2,1)} %own_w1.1) | copy-start | bytes 1769476
  26.2 1.6 %copy-start.1 = (bf16[3,3,256,128]{3,2,1,0:T(8,128)(2,1)S(1)}, bf16[3,3,256,128]{3,2,1,0:T(8,128)(2,1)}, u32[]{:S(2)}) copy-start(bf16[3,3,256,128]{3,2,1,0:T(8,128)(2,1)} %own_w2.1) | copy-start | bytes 1769476

commit v17 on v16

--- a/solution.py
+++ b/solution.py
@@ -256,41 +256,36 @@
         out = jnp.dot(jnp.concatenate(taps, axis=1), kernel(own, other), preferred_element_type=jnp.float32)
         return out.reshape(size, cells, cout)
 
-    chunk = 2
-
-    def first(start):
-        return [dots(g, start, chunk, total, phase, own_w1, other_w1) for phase in range(2)]
-
-    def activate(start, results):
-        for row in range(chunk):
-            fill(
-                act,
-                start + row,
-                *[masked(start + row, 1, silu_of_half(0.5 * r[row] + bias1)) for r in results],
-            )
-
-    def second(start):
+    def first(row):
+        return [dots(g, row, 1, total, phase, own_w1, other_w1)[0] for phase in range(2)]
+
+    def activate(row, results):
+        fill(act, row, *[masked(row, 1, silu_of_half(0.5 * r + bias1)) for r in results])
+
+    def second(row):
         for phase in range(2):
-            acc = dots(act, start, chunk, width, phase, own_w2, other_w2) + bias2
-            for row in range(chunk):
-                for side in range(2):
-                    mixed[side, start + row, pl.ds(phase, width, stride=2), :] = acc[
-                        row, :, side * half : (side + 1) * half
-                    ]
-        for row in range(start, start + chunk):
-            out_ref[row, :, pl.ds(own_at, half)] = mixed[0, row].astype(jnp.bfloat16)
-            out_ref[row, :, pl.ds(other_at, half)] = mixed[1, row].astype(jnp.bfloat16)
-
-    for row in range(2 * chunk):
+            acc = dots(act, row, 1, width, phase, own_w2, other_w2)[0] + bias2
+            for side in range(2):
+                mixed[side, row, pl.ds(phase, width, stride=2), :] = acc[:, side * half : (side + 1) * half]
+        out_ref[row, :, pl.ds(own_at, half)] = mixed[0, row].astype(jnp.bfloat16)
+        out_ref[row, :, pl.ds(other_at, half)] = mixed[1, row].astype(jnp.bfloat16)
+
+    for row in range(3):
         hidden(row)
-    for start in range(0, lines - 2, chunk):
-        results = first(start)
-        for row in range(start + 2 * chunk, min(start + 3 * chunk, lines)):
-            hidden(row)
-        if start >= 2 * chunk:
-            second(start - 2 * chunk)
-        activate(start, results)
-    second(lines - 4 - chunk)
+    results = None
+    for row in range(lines - 2):
+        latest = first(row)
+        if row >= 4:
+            second(row - 4)
+        if row + 3 < lines:
+            hidden(row + 3)
+        if row >= 1:
+            activate(row - 1, results)
+        results = latest
+    if lines >= 6:
+        second(lines - 6)
+    activate(lines - 3, results)
+    second(lines - 5)
 
 
 def total_over(block, axis):

time: 32.7 us -> 32.7 us (level)
  no operation moved by 1% of the time
where the time goes in v17:
time: 32.7 us; the launch traced here: 32.5 us
  starting transfers between devices  15.7 us (48%)
  Pallas kernels  10.4 us (32%)
  waiting for transfers between devices  6.11 us (19%)
    ppermute x4, starting transfers between devices, total_over(): lax.ppermute(block, axis, [(i, i ^ step) for i in range(size)])  7.9 us
    ppermute x1, starting transfers between devices, local(): above = lax.ppermute(lines, 'rows', to_next)  5.46 us
    pallas_call x1, Pallas kernels, local(): call(functools.partial(conv_kernel, count), [vmem] * 9, [((2 * rows, 2 *...  4.71 us
    ppermute x4, waiting for transfers between devices, total_over(): lax.ppermute(block, axis, [(i, i ^ step) for i in range(size)])  4.63 us
    pallas_call x1, Pallas kernels, local(): call(near_kernel, [hbm], [(shape_w, bf16)], [pltpu.SemaphoreType.DMA(())]...  1.6 us
    ppermute x1, waiting for transfers between devices, local(): following = lax.ppermute(image, 'rows', to_previous)  1.46 us
    ppermute x1, starting transfers between devices, local(): following = lax.ppermute(image, 'rows', to_previous)  1.28 us
    pallas_call x1, Pallas kernels, local(): call(own_kernel, [vmem] * 3, [((rows, total, 3 * cin), bf16), ((2 * rows...  1.26 us
  transfers between devices with their start and end apart: 11, of which 5 were waited for; matrix products, arithmetic and copies ran while one was open for 0% of the time, Pallas kernels for 17%

profile of v17, /device:TPU:0, one launch (start us, length us, event | category | flops | bytes accessed | tf_op | source)
XLA Modules:
  0.0 32.5 jit_solution(1188115094603214648)
XLA Ops:
  0.0 0.5 %collective-permute-start.1 = (bf16[4,4,512,128]{3,2,1,0:T(8,128)(2,1)}, bf16[4,4,512,128]{3,2,1,0:T(8,128)(2,1)S(1)}, u32[]{:S(2)}, u32[]{:S(2)}) collective-permute-start(bf16[4,4,512,128]{3,2,1,0:T(8,128)(2,1)} %param.9), channel_id=1, source_target_pairs={{0,1},{1,0},{2,3},{3,2},{4,5},{5,4},{6,7},{7,6},{8,9},{9,8},{10,11... | collective-permute-start | bytes 6291464 | tf_op jit(solution)/shard_map/ppermute | solution.py:344
  0.5 1.3 %collective-permute-start.2 = (bf16[2,128,512]{2,1,0:T(8,128)(2,1)}, bf16[2,128,512]{2,1,0:T(8,128)(2,1)S(1)}, u32[]{:S(2)}, u32[]{:S(2)}) collective-permute-start(bf16[2,128,512]{2,1,0:T(8,128)(2,1)} %image_ref.1), channel_id=1, source_target_pairs={{2,0},{4,2},{6,4},{8,6},{10,8},{12,10},{14,12},{3,1},{5,3},{7,5},{... | collective-permute-start | bytes 786440 | tf_op jit(solution)/shard_map/ppermute | solution.py:335
  1.7 1.1 %cut.1 = (bf16[2,128,512]{2,1,0:T(8,128)(2,1)S(1)}, bf16[2,16,512]{2,1,0:T(8,128)(2,1)S(1)}) custom-call(bf16[2,128,512]{2,1,0:T(8,128)(2,1)} %image_ref.1), custom_call_target="tpu_custom_call" | custom-call | bytes 2097152 | tf_op jit(solution)/shard_map/cut/pallas_call | solution.py:336
  2.8 0.1 collective-permute-start
  2.9 0.5 %collective-permute-start.10 = (bf16[3,3,256,128]{3,2,1,0:T(8,128)(2,1)}, bf16[3,3,256,128]{3,2,1,0:T(8,128)(2,1)S(1)}, u32[]{:S(2)}, u32[]{:S(2)}) collective-permute-start(bf16[3,3,256,128]{3,2,1,0:T(8,128)(2,1)} %own_w2.1), channel_id=1, source_target_pairs={{0,1},{1,0},{2,3},{3,2},{4,5},{5,4},{6,7},{7,6},{8,9},{9,8},{10,11... | collective-permute-start | bytes 1769480 | tf_op jit(solution)/shard_map/ppermute | solution.py:346
  3.4 0.1 collective-permute-start.9
  3.5 1.6 %near_weights.1.own_w = bf16[4,2,2,512,128]{4,3,2,1,0:T(8,128)(2,1)S(1)} custom-call(bf16[4,2,2,512,128]{4,3,2,1,0:T(8,128)(2,1)} %bitcast.9), custom_call_target="tpu_custom_call" | custom-call | bytes 2097152 | tf_op jit(solution)/shard_map/near_weights/pallas_call | solution.py:347
  5.1 5.5 %collective-permute-start.4 = (bf16[2,144,512]{2,1,0:T(8,128)(2,1)S(1)}, bf16[2,144,512]{2,1,0:T(8,128)(2,1)S(1)}, u32[]{:S(2)}, u32[]{:S(2)}) collective-permute-start(bf16[2,144,512]{2,1,0:T(8,128)(2,1)S(1)} %constant_dynamic-update-slice_fusion.lines_ref), channel_id=1, source_target_pairs={{0,2},{2,4},{4,6},{6,8},{8,10},{10,12},{12,14},{1,3},{3,5},{5,7},{... | collective-permute-start | bytes 884744 | tf_op jit(solution)/shard_map/ppermute | solution.py:351
  10.6 1.5 %collective-permute-done.2.lines_ref.next_ref = bf16[2,128,512]{2,1,0:T(8,128)(2,1)S(1)} collective-permute-done((bf16[2,128,512]{2,1,0:T(8,128)(2,1)}, bf16[2,128,512]{2,1,0:T(8,128)(2,1)S(1)}, u32[]{:S(2)}, u32[]{:S(2)}) %collective-permute-start.2) | collective-permute-done | bytes 262176 | tf_op jit(solution)/shard_map/ppermute | solution.py:335
  12.1 1.3 %deconv_own.1 = (bf16[2,144,1536]{2,1,0:T(8,128)(2,1)S(1)}, bf16[2,2,144,256]{3,2,1,0:T(8,128)(2,1)S(1)}, f32[2,144,256]{2,1,0:T(8,128)S(1)}, f32[2,2,144,256]{3,2,1,0:T(8,128)S(1)}, f32[2,256]{1,0:T(2,128)S(1)}) custom-call(bf16[2,144,512]{2,1,0:T(8,128)(2,1)S(1)} %constant_dynamic-update-slice_fusion.lines_ref, ...), custom_call_target="tpu_custom_call" | custom-call | flops 905969664 | bytes 2097152 | tf_op jit(solution)/shard_map/deconv_own/pallas_call | solution.py:353
  13.3 0.0 copy-start.2
  13.4 0.0 copy-start.4
  13.4 0.0 copy-start.5
  13.4 0.5 %deconv_next.1 = (bf16[2,2,144,256]{3,2,1,0:T(8,128)(2,1)S(1)}, bf16[1,144,1536]{2,1,0:T(8,128)(2,1)S(1)}, f32[8,128]{1,0:T(8,128)S(1)}) custom-call(bf16[2,128,512]{2,1,0:T(8,128)(2,1)S(1)} %collective-permute-done.2.lines_ref.next_ref, bf16[2,16,512]{2,1,0:T(8,128)(2,1)S(1)} %collective-permute-done.3.edge_ref.next_edge_ref, ...), custom_call_target="tpu_custom_call" | custom-call | flops 301989888 | bytes 2097152 | tf_op jit(solution)/shard_map/deconv_next/pallas_call | solution.py:369
  13.9 0.6 %collective-permute-start.5 = (f32[8,128]{1,0:T(8,128)S(1)}, f32[8,128]{1,0:T(8,128)S(1)}, u32[]{:S(2)}, u32[]{:S(2)}) collective-permute-start(f32[8,128]{1,0:T(8,128)S(1)} %get-tuple-element.30), channel_id=1, source_target_pairs={{0,1},{1,0},{2,3},{3,2},{4,5},{5,4},{6,7},{7,6},{8,9},{9,8},{10,11... | collective-permute-start | bytes 12296 | tf_op jit(solution)/shard_map/ppermute | solution.py:297
  14.5 0.8 %collective-permute-done.5 = f32[8,128]{1,0:T(8,128)S(1)} collective-permute-done((f32[8,128]{1,0:T(8,128)S(1)}, f32[8,128]{1,0:T(8,128)S(1)}, u32[]{:S(2)}, u32[]{:S(2)}) %collective-permute-start.5) | collective-permute-done | bytes 4128 | tf_op jit(solution)/shard_map/ppermute | solution.py:297
  15.3 1.8 %collective-permute-start.6 = (f32[8,128]{1,0:T(8,128)S(1)}, f32[8,128]{1,0:T(8,128)S(1)}, u32[]{:S(2)}, u32[]{:S(2)}) collective-permute-start(f32[8,128]{1,0:T(8,128)S(1)} %add.12), channel_id=1, source_target_pairs={{0,4},{2,6},{4,0},{6,2},{8,12},{10,14},{12,8},{14,10},{1,5},{3,7},... | collective-permute-start | bytes 12296 | tf_op jit(solution)/shard_map/ppermute | solution.py:297
  17.1 1.8 %collective-permute-done.6 = f32[8,128]{1,0:T(8,128)S(1)} collective-permute-done((f32[8,128]{1,0:T(8,128)S(1)}, f32[8,128]{1,0:T(8,128)S(1)}, u32[]{:S(2)}, u32[]{:S(2)}) %collective-permute-start.6) | collective-permute-done | bytes 4128 | tf_op jit(solution)/shard_map/ppermute | solution.py:297
  18.9 2.8 %collective-permute-start.7 = (f32[8,128]{1,0:T(8,128)S(1)}, f32[8,128]{1,0:T(8,128)S(1)}, u32[]{:S(2)}, u32[]{:S(2)}) collective-permute-start(f32[8,128]{1,0:T(8,128)S(1)} %add.13), channel_id=1, source_target_pairs={{0,8},{2,10},{4,12},{6,14},{8,0},{10,2},{12,4},{14,6},{1,9},{3,11}... | collective-permute-start | bytes 12296 | tf_op jit(solution)/shard_map/ppermute | solution.py:297
  21.8 1.7 %collective-permute-done.7 = f32[8,128]{1,0:T(8,128)S(1)} collective-permute-done((f32[8,128]{1,0:T(8,128)S(1)}, f32[8,128]{1,0:T(8,128)S(1)}, u32[]{:S(2)}, u32[]{:S(2)}) %collective-permute-start.7) | collective-permute-done | bytes 4128 | tf_op jit(solution)/shard_map/ppermute | solution.py:297
  23.4 2.7 %collective-permute-start.8 = (f32[8,128]{1,0:T(8,128)S(1)}, f32[8,128]{1,0:T(8,128)S(1)}, u32[]{:S(2)}, u32[]{:S(2)}) collective-permute-start(f32[8,128]{1,0:T(8,128)S(1)} %add.14), channel_id=1, source_target_pairs={{0,2},{2,0},{4,6},{6,4},{8,10},{10,8},{12,14},{14,12},{1,3},{3,1},... | collective-permute-start | bytes 12296 | tf_op jit(solution)/shard_map/ppermute | solution.py:297
  26.2 1.2 %deconv_halo.1.halo_ref = bf16[4,2,144,256]{3,2,1,0:T(8,128)(2,1)S(1)} custom-call(bf16[2,144,512]{2,1,0:T(8,128)(2,1)S(1)} %collective-permute-done.4.above_ref, bf16[2,128,512]{2,1,0:T(8,128)(2,1)S(1)} %collective-permute-done.2.lines_ref.next_ref, bf16[2,16,512]{2,1,0:T(8,128)(2,1)S(1)} %collective-permute-done.3.edge_ref.next_edge_ref, ...), custom_call_target="tpu_custom_call" | custom-call | flops 1207959552 | bytes 2097152 | tf_op jit(solution)/shard_map/deconv_halo/pallas_call | solution.py:377
  27.4 0.3 %collective-permute-done.8 = f32[8,128]{1,0:T(8,128)S(1)} collective-permute-done((f32[8,128]{1,0:T(8,128)S(1)}, f32[8,128]{1,0:T(8,128)S(1)}, u32[]{:S(2)}, u32[]{:S(2)}) %collective-permute-start.8) | collective-permute-done | bytes 4128 | tf_op jit(solution)/shard_map/ppermute | solution.py:297
  27.8 4.7 %convs.1 = bf16[4,256,256]{2,1,0:T(8,128)(2,1)} custom-call(bf16[2,2,144,256]{3,2,1,0:T(8,128)(2,1)S(1)} %get-tuple-element.23.u_ref, bf16[2,2,144,256]{3,2,1,0:T(8,128)(2,1)S(1)} %get-tuple-element.26.u_next_ref, bf16[4,2,144,256]{3,2,1,0:T(8,128)(2,1)S(1)} %deconv_halo.1.halo_ref, f32[8,128]{1,0:T(8,128)S(1)} %add.15.stats_ref, ...), custom_call_target="tpu_custom_call" | custom-call | flops 5000000000 | bytes 2097152 | tf_op jit(solution)/shard_map/convs/pallas_call | solution.py:388
  (24 shorter events, 0.1 us)
Async XLA Ops:
  0.0 12.1 %collective-permute-start.1 = (bf16[4,4,512,128]{3,2,1,0:T(8,128)(2,1)}, bf16[4,4,512,128]{3,2,1,0:T(8,128)(2,1)S(1)}, u32[]{:S(2)}, u32[]{:S(2)}) collective-permute-start(bf16[4,4,512,128]{3,2,1,0:T(8,128)(2,1)} %param.9), channel_id=1, source_target_pairs={{0,1},{1,0},{2,3},{3,2},{4,5},{5,4},{6,7},{7,6},{8,9},{9,8},{10,11... | collective-permute-start | bytes 6291464 | tf_op jit(solution)/shard_map/ppermute | solution.py:344
  0.5 11.6 %collective-permute-start.2 = (bf16[2,128,512]{2,1,0:T(8,128)(2,1)}, bf16[2,128,512]{2,1,0:T(8,128)(2,1)S(1)}, u32[]{:S(2)}, u32[]{:S(2)}) collective-permute-start(bf16[2,128,512]{2,1,0:T(8,128)(2,1)} %image_ref.1), channel_id=1, source_target_pairs={{2,0},{4,2},{6,4},{8,6},{10,8},{12,10},{14,12},{3,1},{5,3},{7,5},{... | collective-permute-start | bytes 786440 | tf_op jit(solution)/shard_map/ppermute | solution.py:335
  2.8 2.3 %collective-permute-start = (bf16[2,16,512]{2,1,0:T(8,128)(2,1)S(1)}, bf16[2,16,512]{2,1,0:T(8,128)(2,1)S(1)}, u32[]{:S(2)}, u32[]{:S(2)}) collective-permute-start(bf16[2,16,512]{2,1,0:T(8,128)(2,1)S(1)} %get-tuple-element.20), channel_id=1, source_target_pairs={{0,1},{1,0},{2,3},{3,2},{4,5},{5,4},{6,7},{7,6},{8,9},{9,8},{10,11... | collective-permute-start | bytes 98312 | tf_op jit(solution)/shard_map/ppermute | solution.py:343
  2.9 24.8 %collective-permute-start.10 = (bf16[3,3,256,128]{3,2,1,0:T(8,128)(2,1)}, bf16[3,3,256,128]{3,2,1,0:T(8,128)(2,1)S(1)}, u32[]{:S(2)}, u32[]{:S(2)}) collective-permute-start(bf16[3,3,256,128]{3,2,1,0:T(8,128)(2,1)} %own_w2.1), channel_id=1, source_target_pairs={{0,1},{1,0},{2,3},{3,2},{4,5},{5,4},{6,7},{7,6},{8,9},{9,8},{10,11... | collective-permute-start | bytes 1769480 | tf_op jit(solution)/shard_map/ppermute | solution.py:346
  3.4 24.4 %collective-permute-start.9 = (bf16[3,3,256,128]{3,2,1,0:T(8,128)(2,1)}, bf16[3,3,256,128]{3,2,1,0:T(8,128)(2,1)S(1)}, u32[]{:S(2)}, u32[]{:S(2)}) collective-permute-start(bf16[3,3,256,128]{3,2,1,0:T(8,128)(2,1)} %own_w1.1), channel_id=1, source_target_pairs={{0,1},{1,0},{2,3},{3,2},{4,5},{5,4},{6,7},{7,6},{8,9},{9,8},{10,11... | collective-permute-start | bytes 1769480 | tf_op jit(solution)/shard_map/ppermute | solution.py:345
  5.1 21.1 %collective-permute-start.4 = (bf16[2,144,512]{2,1,0:T(8,128)(2,1)S(1)}, bf16[2,144,512]{2,1,0:T(8,128)(2,1)S(1)}, u32[]{:S(2)}, u32[]{:S(2)}) collective-permute-start(bf16[2,144,512]{2,1,0:T(8,128)(2,1)S(1)} %constant_dynamic-update-slice_fusion.lines_ref), channel_id=1, source_target_pairs={{0,2},{2,4},{4,6},{6,8},{8,10},{10,12},{12,14},{1,3},{3,5},{5,7},{... | collective-permute-start | bytes 884744 | tf_op jit(solution)/shard_map/ppermute | solution.py:351
  12.1 1.3 %collective-permute-start.3 = (bf16[2,16,512]{2,1,0:T(8,128)(2,1)S(1)}, bf16[2,16,512]{2,1,0:T(8,128)(2,1)S(1)}, u32[]{:S(2)}, u32[]{:S(2)}) collective-permute-start(bf16[2,16,512]{2,1,0:T(8,128)(2,1)S(1)} %next_edges.1), channel_id=1, source_target_pairs={{0,1},{1,0},{2,3},{3,2},{4,5},{5,4},{6,7},{7,6},{8,9},{9,8},{10,11... | collective-permute-start | bytes 98312 | tf_op jit(solution)/shard_map/ppermute | solution.py:368
  13.3 8.4 %copy-start.2 = (f32[256]{0:T(256)S(1)}, f32[256]{0:T(256)}, u32[]{:S(2)}) copy-start(f32[256]{0:T(256)} %param.15) | copy-start | bytes 3076
  13.3 8.4 %copy-start.3 = (f32[256]{0:T(256)S(1)}, f32[256]{0:T(256)}, u32[]{:S(2)}) copy-start(f32[256]{0:T(256)} %param.13) | copy-start | bytes 3076
  13.4 8.4 %copy-start.4 = (f32[256]{0:T(256)S(1)}, f32[256]{0:T(256)}, u32[]{:S(2)}) copy-start(f32[256]{0:T(256)} %param.11) | copy-start | bytes 3076
  13.4 8.4 %copy-start.5 = (f32[256]{0:T(256)S(1)}, f32[256]{0:T(256)}, u32[]{:S(2)}) copy-start(f32[256]{0:T(256)} %param.10) | copy-start | bytes 3076
  13.9 1.4 %collective-permute-start.5 = (f32[8,128]{1,0:T(8,128)S(1)}, f32[8,128]{1,0:T(8,128)S(1)}, u32[]{:S(2)}, u32[]{:S(2)}) collective-permute-start(f32[8,128]{1,0:T(8,128)S(1)} %get-tuple-element.30), channel_id=1, source_target_pairs={{0,1},{1,0},{2,3},{3,2},{4,5},{5,4},{6,7},{7,6},{8,9},{9,8},{10,11... | collective-permute-start | bytes 12296 | tf_op jit(solution)/shard_map/ppermute | solution.py:297
  15.3 3.6 %collective-permute-start.6 = (f32[8,128]{1,0:T(8,128)S(1)}, f32[8,128]{1,0:T(8,128)S(1)}, u32[]{:S(2)}, u32[]{:S(2)}) collective-permute-start(f32[8,128]{1,0:T(8,128)S(1)} %add.12), channel_id=1, source_target_pairs={{0,4},{2,6},{4,0},{6,2},{8,12},{10,14},{12,8},{14,10},{1,5},{3,7},... | collective-permute-start | bytes 12296 | tf_op jit(solution)/shard_map/ppermute | solution.py:297
  18.9 4.5 %collective-permute-start.7 = (f32[8,128]{1,0:T(8,128)S(1)}, f32[8,128]{1,0:T(8,128)S(1)}, u32[]{:S(2)}, u32[]{:S(2)}) collective-permute-start(f32[8,128]{1,0:T(8,128)S(1)} %add.13), channel_id=1, source_target_pairs={{0,8},{2,10},{4,12},{6,14},{8,0},{10,2},{12,4},{14,6},{1,9},{3,11}... | collective-permute-start | bytes 12296 | tf_op jit(solution)/shard_map/ppermute | solution.py:297
  23.4 4.3 %collective-permute-start.8 = (f32[8,128]{1,0:T(8,128)S(1)}, f32[8,128]{1,0:T(8,128)S(1)}, u32[]{:S(2)}, u32[]{:S(2)}) collective-permute-start(f32[8,128]{1,0:T(8,128)S(1)} %add.14), channel_id=1, source_target_pairs={{0,2},{2,0},{4,6},{6,4},{8,10},{10,8},{12,14},{14,12},{1,3},{3,1},... | collective-permute-start | bytes 12296 | tf_op jit(solution)/shard_map/ppermute | solution.py:297
  26.2 1.6 %copy-start = (bf16[3,3,256,128]{3,2,1,0:T(8,128)(2,1)S(1)}, bf16[3,3,256,128]{3,2,1,0:T(8,128)(2,1)}, u32[]{:S(2)}) copy-start(bf16[3,3,256,128]{3,2,1,0:T(8,128)(2,1)} %own_w1.1) | copy-start | bytes 1769476
  26.2 1.6 %copy-start.1 = (bf16[3,3,256,128]{3,2,1,0:T(8,128)(2,1)S(1)}, bf16[3,3,256,128]{3,2,1,0:T(8,128)(2,1)}, u32[]{:S(2)}) copy-start(bf16[3,3,256,128]{3,2,1,0:T(8,128)(2,1)} %own_w2.1) | copy-start | bytes 1769476

commit v18 on v14

--- a/solution.py
+++ b/solution.py
@@ -163,12 +163,24 @@
     return v
 
 
-def fill(ref, row, even, odd):
-    total, channels = even.shape
-    ref[row, :, 0:channels] = pltpu.roll(odd, 1, 0).astype(jnp.bfloat16)
-    ref[row, :, channels : 2 * channels] = even.astype(jnp.bfloat16)
-    ref[row, :, 2 * channels : 3 * channels] = odd.astype(jnp.bfloat16)
-    ref[row, :, 3 * channels : 4 * channels] = pltpu.roll(even, total - 1, 0).astype(jnp.bfloat16)
+def fill(ref, row, phase, lane, value):
+    total, size = value.shape
+    channels = ref.shape[-1] // 4
+    own, shifted, by = ((1, 3, total - 1), (2, 0, 1))[phase]
+    ref[row, :, own * channels + lane : own * channels + lane + size] = value.astype(jnp.bfloat16)
+    ref[row, :, shifted * channels + lane : shifted * channels + lane + size] = pltpu.roll(value, by, 0).astype(
+        jnp.bfloat16
+    )
+
+
+def weave(dots, rest):
+    done = 0
+    for n, dot in enumerate(dots):
+        dot()
+        upto = len(rest) * (n + 1) // len(dots)
+        for step in rest[done:upto]:
+            step()
+        done = upto
 
 
 def conv_kernel(
@@ -220,6 +232,8 @@
             return jnp.where(place < last, value, 0.0)
         return value
 
+    quarters = [(phase, lane) for phase in range(2) for lane in range(0, cout, half)]
+
     def hidden(row):
         if row < 3:
             source = halo_ref.at[row]
@@ -229,63 +243,62 @@
             source = u_next_ref.at[row - 3 - early]
         else:
             source = halo_ref.at[3]
-        fill(
-            g,
-            row,
-            *[
-                masked(row, HALO, silu_of_half(source[phase].astype(jnp.float32) * scale + shift))
-                for phase in range(2)
-            ],
-        )
-
-    def dots(source, start, size, cells, phase, own, other):
-        total = None
-        for a in range(3):
+
+        def step(phase, lane):
+            part = slice(lane, lane + half)
+            value = source[phase, :, part].astype(jnp.float32) * scale[:, part] + shift[:, part]
+            fill(g, row, phase, lane, masked(row, HALO, silu_of_half(value)))
+
+        return [functools.partial(step, *quarter) for quarter in quarters]
+
+    def activate(row, results):
+        def step(phase, lane):
+            part = slice(lane, lane + half)
+            value = silu_of_half(0.5 * results[phase][:, part] + bias1[:, part])
+            fill(act, row, phase, lane, masked(row, 1, value))
+
+        return [functools.partial(step, *quarter) for quarter in quarters]
+
+    def store(row, results):
+        def step(phase, lane):
+            part = slice(lane, lane + half)
+            mixed[lane // half, row, pl.ds(phase, width, stride=2), :] = results[phase][:, part] + bias2[:, part]
+
+        def last():
+            out_ref[row, :, pl.ds(own_at, half)] = mixed[0, row].astype(jnp.bfloat16)
+            out_ref[row, :, pl.ds(other_at, half)] = mixed[1, row].astype(jnp.bfloat16)
+
+        return [functools.partial(step, *quarter) for quarter in quarters] + [last]
+
+    def dots(source, row, cells, own, other, results):
+        def step(phase, a):
             term = jnp.dot(
-                source[start + a : start + a + size, 0:cells, phase * cout : (phase + 3) * cout].reshape(
-                    size * cells, 3 * cout
-                ),
+                source[row + a, 0:cells, phase * cout : (phase + 3) * cout],
                 kernel_row(a, own, other),
                 preferred_element_type=jnp.float32,
             )
-            total = term if total is None else total + term
-        return total.reshape(size, cells, cout)
-
-    chunk = 2
-
-    def first(start):
-        return [dots(g, start, chunk, total, phase, own_w1, other_w1) for phase in range(2)]
-
-    def activate(start, results):
-        for row in range(chunk):
-            fill(
-                act,
-                start + row,
-                *[masked(start + row, 1, silu_of_half(0.5 * r[row] + bias1)) for r in results],
-            )
-
-    def second(start):
-        for phase in range(2):
-            acc = dots(act, start, chunk, width, phase, own_w2, other_w2) + bias2
-            for row in range(chunk):
-                for side in range(2):
-                    mixed[side, start + row, pl.ds(phase, width, stride=2), :] = acc[
-                        row, :, side * half : (side + 1) * half
-                    ]
-        for row in range(start, start + chunk):
-            out_ref[row, :, pl.ds(own_at, half)] = mixed[0, row].astype(jnp.bfloat16)
-            out_ref[row, :, pl.ds(other_at, half)] = mixed[1, row].astype(jnp.bfloat16)
-
-    for row in range(2 * chunk):
-        hidden(row)
-    for start in range(0, lines - 2, chunk):
-        results = first(start)
-        for row in range(start + 2 * chunk, min(start + 3 * chunk, lines)):
-            hidden(row)
-        if start >= 2 * chunk:
-            second(start - 2 * chunk)
-        activate(start, results)
-    second(lines - 4 - chunk)
+            results[phase] = term if a == 0 else results[phase] + term
+
+        return [functools.partial(step, phase, a) for phase in range(2) for a in range(3)]
+
+    for row in range(3):
+        for step in hidden(row):
+            step()
+    ones = [{} for _ in range(lines - 2)]
+    twos = [{} for _ in range(lines - 4)]
+    for row in range(lines + 1):
+        work, rest = [], []
+        if row < lines - 2:
+            work += dots(g, row, total, own_w1, other_w1, ones[row])
+        if 4 <= row < lines:
+            work += dots(act, row - 4, width, own_w2, other_w2, twos[row - 4])
+        if row + 3 < lines:
+            rest += hidden(row + 3)
+        if 1 <= row < lines - 1:
+            rest += activate(row - 1, ones[row - 1])
+        if row >= 5:
+            rest += store(row - 5, twos[row - 5])
+        weave(work or [lambda: None], rest)
 
 
 def total_over(block, axis):

time: 32.7 us -> 32.9 us (level)
  no operation moved by 1% of the time
where the time goes in v18:
time: 32.9 us; the launch traced here: 32.7 us
  starting transfers between devices  15.7 us (48%)
  Pallas kernels  10.6 us (32%)
  waiting for transfers between devices  6.11 us (19%)
    ppermute x4, starting transfers between devices, total_over(): lax.ppermute(block, axis, [(i, i ^ step) for i in range(size)])  7.9 us
    ppermute x1, starting transfers between devices, local(): above = lax.ppermute(lines, 'rows', to_next)  5.46 us
    pallas_call x1, Pallas kernels, local(): call(functools.partial(conv_kernel, count), [vmem] * 9, [((2 * rows, 2 *...  4.93 us
    ppermute x4, waiting for transfers between devices, total_over(): lax.ppermute(block, axis, [(i, i ^ step) for i in range(size)])  4.63 us
    pallas_call x1, Pallas kernels, local(): call(near_kernel, [hbm], [(shape_w, bf16)], [pltpu.SemaphoreType.DMA(())]...  1.6 us
    ppermute x1, waiting for transfers between devices, local(): following = lax.ppermute(image, 'rows', to_previous)  1.46 us
    ppermute x1, starting transfers between devices, local(): following = lax.ppermute(image, 'rows', to_previous)  1.28 us
    pallas_call x1, Pallas kernels, local(): call(own_kernel, [vmem] * 3, [((rows, total, 3 * cin), bf16), ((2 * rows...  1.26 us
  transfers between devices with their start and end apart: 11, of which 5 were waited for; matrix products, arithmetic and copies ran while one was open for 0% of the time, Pallas kernels for 17%

profile of v18, /device:TPU:0, one launch (start us, length us, event | category | flops | bytes accessed | tf_op | source)
XLA Modules:
  0.0 32.7 jit_solution(3772065138491077718)
XLA Ops:
  0.0 0.5 %collective-permute-start.1 = (bf16[4,4,512,128]{3,2,1,0:T(8,128)(2,1)}, bf16[4,4,512,128]{3,2,1,0:T(8,128)(2,1)S(1)}, u32[]{:S(2)}, u32[]{:S(2)}) collective-permute-start(bf16[4,4,512,128]{3,2,1,0:T(8,128)(2,1)} %param.9), channel_id=1, source_target_pairs={{0,1},{1,0},{2,3},{3,2},{4,5},{5,4},{6,7},{7,6},{8,9},{9,8},{10,11... | collective-permute-start | bytes 6291464 | tf_op jit(solution)/shard_map/ppermute | solution.py:357
  0.5 1.3 %collective-permute-start.2 = (bf16[2,128,512]{2,1,0:T(8,128)(2,1)}, bf16[2,128,512]{2,1,0:T(8,128)(2,1)S(1)}, u32[]{:S(2)}, u32[]{:S(2)}) collective-permute-start(bf16[2,128,512]{2,1,0:T(8,128)(2,1)} %image_ref.1), channel_id=1, source_target_pairs={{2,0},{4,2},{6,4},{8,6},{10,8},{12,10},{14,12},{3,1},{5,3},{7,5},{... | collective-permute-start | bytes 786440 | tf_op jit(solution)/shard_map/ppermute | solution.py:348
  1.7 1.1 %cut.1 = (bf16[2,128,512]{2,1,0:T(8,128)(2,1)S(1)}, bf16[2,16,512]{2,1,0:T(8,128)(2,1)S(1)}) custom-call(bf16[2,128,512]{2,1,0:T(8,128)(2,1)} %image_ref.1), custom_call_target="tpu_custom_call" | custom-call | bytes 2097152 | tf_op jit(solution)/shard_map/cut/pallas_call | solution.py:349
  2.8 0.1 collective-permute-start
  2.9 0.5 %collective-permute-start.10 = (bf16[3,3,256,128]{3,2,1,0:T(8,128)(2,1)}, bf16[3,3,256,128]{3,2,1,0:T(8,128)(2,1)S(1)}, u32[]{:S(2)}, u32[]{:S(2)}) collective-permute-start(bf16[3,3,256,128]{3,2,1,0:T(8,128)(2,1)} %own_w2.1), channel_id=1, source_target_pairs={{0,1},{1,0},{2,3},{3,2},{4,5},{5,4},{6,7},{7,6},{8,9},{9,8},{10,11... | collective-permute-start | bytes 1769480 | tf_op jit(solution)/shard_map/ppermute | solution.py:359
  3.4 0.1 collective-permute-start.9
  3.5 1.6 %near_weights.1.own_w = bf16[4,2,2,512,128]{4,3,2,1,0:T(8,128)(2,1)S(1)} custom-call(bf16[4,2,2,512,128]{4,3,2,1,0:T(8,128)(2,1)} %bitcast.9), custom_call_target="tpu_custom_call" | custom-call | bytes 2097152 | tf_op jit(solution)/shard_map/near_weights/pallas_call | solution.py:360
  5.1 5.5 %collective-permute-start.4 = (bf16[2,144,512]{2,1,0:T(8,128)(2,1)S(1)}, bf16[2,144,512]{2,1,0:T(8,128)(2,1)S(1)}, u32[]{:S(2)}, u32[]{:S(2)}) collective-permute-start(bf16[2,144,512]{2,1,0:T(8,128)(2,1)S(1)} %constant_dynamic-update-slice_fusion.lines_ref), channel_id=1, source_target_pairs={{0,2},{2,4},{4,6},{6,8},{8,10},{10,12},{12,14},{1,3},{3,5},{5,7},{... | collective-permute-start | bytes 884744 | tf_op jit(solution)/shard_map/ppermute | solution.py:364
  10.6 1.5 %collective-permute-done.2.lines_ref.next_ref = bf16[2,128,512]{2,1,0:T(8,128)(2,1)S(1)} collective-permute-done((bf16[2,128,512]{2,1,0:T(8,128)(2,1)}, bf16[2,128,512]{2,1,0:T(8,128)(2,1)S(1)}, u32[]{:S(2)}, u32[]{:S(2)}) %collective-permute-start.2) | collective-permute-done | bytes 262176 | tf_op jit(solution)/shard_map/ppermute | solution.py:348
  12.1 1.3 %deconv_own.1 = (bf16[2,144,1536]{2,1,0:T(8,128)(2,1)S(1)}, bf16[2,2,144,256]{3,2,1,0:T(8,128)(2,1)S(1)}, f32[2,144,256]{2,1,0:T(8,128)S(1)}, f32[2,2,144,256]{3,2,1,0:T(8,128)S(1)}, f32[2,256]{1,0:T(2,128)S(1)}) custom-call(bf16[2,144,512]{2,1,0:T(8,128)(2,1)S(1)} %constant_dynamic-update-slice_fusion.lines_ref, ...), custom_call_target="tpu_custom_call" | custom-call | flops 905969664 | bytes 2097152 | tf_op jit(solution)/shard_map/deconv_own/pallas_call | solution.py:366
  13.3 0.0 copy-start.2
  13.4 0.0 copy-start.4
  13.4 0.0 copy-start.5
  13.4 0.5 %deconv_next.1 = (bf16[2,2,144,256]{3,2,1,0:T(8,128)(2,1)S(1)}, bf16[1,144,1536]{2,1,0:T(8,128)(2,1)S(1)}, f32[8,128]{1,0:T(8,128)S(1)}) custom-call(bf16[2,128,512]{2,1,0:T(8,128)(2,1)S(1)} %collective-permute-done.2.lines_ref.next_ref, bf16[2,16,512]{2,1,0:T(8,128)(2,1)S(1)} %collective-permute-done.3.edge_ref.next_edge_ref, ...), custom_call_target="tpu_custom_call" | custom-call | flops 301989888 | bytes 2097152 | tf_op jit(solution)/shard_map/deconv_next/pallas_call | solution.py:382
  13.9 0.6 %collective-permute-start.5 = (f32[8,128]{1,0:T(8,128)S(1)}, f32[8,128]{1,0:T(8,128)S(1)}, u32[]{:S(2)}, u32[]{:S(2)}) collective-permute-start(f32[8,128]{1,0:T(8,128)S(1)} %get-tuple-element.30), channel_id=1, source_target_pairs={{0,1},{1,0},{2,3},{3,2},{4,5},{5,4},{6,7},{7,6},{8,9},{9,8},{10,11... | collective-permute-start | bytes 12296 | tf_op jit(solution)/shard_map/ppermute | solution.py:310
  14.5 0.8 %collective-permute-done.5 = f32[8,128]{1,0:T(8,128)S(1)} collective-permute-done((f32[8,128]{1,0:T(8,128)S(1)}, f32[8,128]{1,0:T(8,128)S(1)}, u32[]{:S(2)}, u32[]{:S(2)}) %collective-permute-start.5) | collective-permute-done | bytes 4128 | tf_op jit(solution)/shard_map/ppermute | solution.py:310
  15.3 1.8 %collective-permute-start.6 = (f32[8,128]{1,0:T(8,128)S(1)}, f32[8,128]{1,0:T(8,128)S(1)}, u32[]{:S(2)}, u32[]{:S(2)}) collective-permute-start(f32[8,128]{1,0:T(8,128)S(1)} %add.12), channel_id=1, source_target_pairs={{0,4},{2,6},{4,0},{6,2},{8,12},{10,14},{12,8},{14,10},{1,5},{3,7},... | collective-permute-start | bytes 12296 | tf_op jit(solution)/shard_map/ppermute | solution.py:310
  17.1 1.8 %collective-permute-done.6 = f32[8,128]{1,0:T(8,128)S(1)} collective-permute-done((f32[8,128]{1,0:T(8,128)S(1)}, f32[8,128]{1,0:T(8,128)S(1)}, u32[]{:S(2)}, u32[]{:S(2)}) %collective-permute-start.6) | collective-permute-done | bytes 4128 | tf_op jit(solution)/shard_map/ppermute | solution.py:310
  18.9 2.8 %collective-permute-start.7 = (f32[8,128]{1,0:T(8,128)S(1)}, f32[8,128]{1,0:T(8,128)S(1)}, u32[]{:S(2)}, u32[]{:S(2)}) collective-permute-start(f32[8,128]{1,0:T(8,128)S(1)} %add.13), channel_id=1, source_target_pairs={{0,8},{2,10},{4,12},{6,14},{8,0},{10,2},{12,4},{14,6},{1,9},{3,11}... | collective-permute-start | bytes 12296 | tf_op jit(solution)/shard_map/ppermute | solution.py:310
  21.8 1.7 %collective-permute-done.7 = f32[8,128]{1,0:T(8,128)S(1)} collective-permute-done((f32[8,128]{1,0:T(8,128)S(1)}, f32[8,128]{1,0:T(8,128)S(1)}, u32[]{:S(2)}, u32[]{:S(2)}) %collective-permute-start.7) | collective-permute-done | bytes 4128 | tf_op jit(solution)/shard_map/ppermute | solution.py:310
  23.4 2.7 %collective-permute-start.8 = (f32[8,128]{1,0:T(8,128)S(1)}, f32[8,128]{1,0:T(8,128)S(1)}, u32[]{:S(2)}, u32[]{:S(2)}) collective-permute-start(f32[8,128]{1,0:T(8,128)S(1)} %add.14), channel_id=1, source_target_pairs={{0,2},{2,0},{4,6},{6,4},{8,10},{10,8},{12,14},{14,12},{1,3},{3,1},... | collective-permute-start | bytes 12296 | tf_op jit(solution)/shard_map/ppermute | solution.py:310
  26.2 1.2 %deconv_halo.1.halo_ref = bf16[4,2,144,256]{3,2,1,0:T(8,128)(2,1)S(1)} custom-call(bf16[2,144,512]{2,1,0:T(8,128)(2,1)S(1)} %collective-permute-done.4.above_ref, bf16[2,128,512]{2,1,0:T(8,128)(2,1)S(1)} %collective-permute-done.2.lines_ref.next_ref, bf16[2,16,512]{2,1,0:T(8,128)(2,1)S(1)} %collective-permute-done.3.edge_ref.next_edge_ref, ...), custom_call_target="tpu_custom_call" | custom-call | flops 1207959552 | bytes 2097152 | tf_op jit(solution)/shard_map/deconv_halo/pallas_call | solution.py:390
  27.4 0.3 %collective-permute-done.8 = f32[8,128]{1,0:T(8,128)S(1)} collective-permute-done((f32[8,128]{1,0:T(8,128)S(1)}, f32[8,128]{1,0:T(8,128)S(1)}, u32[]{:S(2)}, u32[]{:S(2)}) %collective-permute-start.8) | collective-permute-done | bytes 4128 | tf_op jit(solution)/shard_map/ppermute | solution.py:310
  27.8 4.9 %convs.1 = bf16[4,256,256]{2,1,0:T(8,128)(2,1)} custom-call(bf16[2,2,144,256]{3,2,1,0:T(8,128)(2,1)S(1)} %get-tuple-element.23.u_ref, bf16[2,2,144,256]{3,2,1,0:T(8,128)(2,1)S(1)} %get-tuple-element.26.u_next_ref, bf16[4,2,144,256]{3,2,1,0:T(8,128)(2,1)S(1)} %deconv_halo.1.halo_ref, f32[8,128]{1,0:T(8,128)S(1)} %add.15.stats_ref, ...), custom_call_target="tpu_custom_call" | custom-call | flops 5000000000 | bytes 2097152 | tf_op jit(solution)/shard_map/convs/pallas_call | solution.py:401
  (24 shorter events, 0.1 us)
Async XLA Ops:
  0.0 12.1 %collective-permute-start.1 = (bf16[4,4,512,128]{3,2,1,0:T(8,128)(2,1)}, bf16[4,4,512,128]{3,2,1,0:T(8,128)(2,1)S(1)}, u32[]{:S(2)}, u32[]{:S(2)}) collective-permute-start(bf16[4,4,512,128]{3,2,1,0:T(8,128)(2,1)} %param.9), channel_id=1, source_target_pairs={{0,1},{1,0},{2,3},{3,2},{4,5},{5,4},{6,7},{7,6},{8,9},{9,8},{10,11... | collective-permute-start | bytes 6291464 | tf_op jit(solution)/shard_map/ppermute | solution.py:357
  0.5 11.6 %collective-permute-start.2 = (bf16[2,128,512]{2,1,0:T(8,128)(2,1)}, bf16[2,128,512]{2,1,0:T(8,128)(2,1)S(1)}, u32[]{:S(2)}, u32[]{:S(2)}) collective-permute-start(bf16[2,128,512]{2,1,0:T(8,128)(2,1)} %image_ref.1), channel_id=1, source_target_pairs={{2,0},{4,2},{6,4},{8,6},{10,8},{12,10},{14,12},{3,1},{5,3},{7,5},{... | collective-permute-start | bytes 786440 | tf_op jit(solution)/shard_map/ppermute | solution.py:348
  2.8 2.3 %collective-permute-start = (bf16[2,16,512]{2,1,0:T(8,128)(2,1)S(1)}, bf16[2,16,512]{2,1,0:T(8,128)(2,1)S(1)}, u32[]{:S(2)}, u32[]{:S(2)}) collective-permute-start(bf16[2,16,512]{2,1,0:T(8,128)(2,1)S(1)} %get-tuple-element.20), channel_id=1, source_target_pairs={{0,1},{1,0},{2,3},{3,2},{4,5},{5,4},{6,7},{7,6},{8,9},{9,8},{10,11... | collective-permute-start | bytes 98312 | tf_op jit(solution)/shard_map/ppermute | solution.py:356
  2.9 24.8 %collective-permute-start.10 = (bf16[3,3,256,128]{3,2,1,0:T(8,128)(2,1)}, bf16[3,3,256,128]{3,2,1,0:T(8,128)(2,1)S(1)}, u32[]{:S(2)}, u32[]{:S(2)}) collective-permute-start(bf16[3,3,256,128]{3,2,1,0:T(8,128)(2,1)} %own_w2.1), channel_id=1, source_target_pairs={{0,1},{1,0},{2,3},{3,2},{4,5},{5,4},{6,7},{7,6},{8,9},{9,8},{10,11... | collective-permute-start | bytes 1769480 | tf_op jit(solution)/shard_map/ppermute | solution.py:359
  3.4 24.4 %collective-permute-start.9 = (bf16[3,3,256,128]{3,2,1,0:T(8,128)(2,1)}, bf16[3,3,256,128]{3,2,1,0:T(8,128)(2,1)S(1)}, u32[]{:S(2)}, u32[]{:S(2)}) collective-permute-start(bf16[3,3,256,128]{3,2,1,0:T(8,128)(2,1)} %own_w1.1), channel_id=1, source_target_pairs={{0,1},{1,0},{2,3},{3,2},{4,5},{5,4},{6,7},{7,6},{8,9},{9,8},{10,11... | collective-permute-start | bytes 1769480 | tf_op jit(solution)/shard_map/ppermute | solution.py:358
  5.1 21.1 %collective-permute-start.4 = (bf16[2,144,512]{2,1,0:T(8,128)(2,1)S(1)}, bf16[2,144,512]{2,1,0:T(8,128)(2,1)S(1)}, u32[]{:S(2)}, u32[]{:S(2)}) collective-permute-start(bf16[2,144,512]{2,1,0:T(8,128)(2,1)S(1)} %constant_dynamic-update-slice_fusion.lines_ref), channel_id=1, source_target_pairs={{0,2},{2,4},{4,6},{6,8},{8,10},{10,12},{12,14},{1,3},{3,5},{5,7},{... | collective-permute-start | bytes 884744 | tf_op jit(solution)/shard_map/ppermute | solution.py:364
  12.1 1.3 %collective-permute-start.3 = (bf16[2,16,512]{2,1,0:T(8,128)(2,1)S(1)}, bf16[2,16,512]{2,1,0:T(8,128)(2,1)S(1)}, u32[]{:S(2)}, u32[]{:S(2)}) collective-permute-start(bf16[2,16,512]{2,1,0:T(8,128)(2,1)S(1)} %next_edges.1), channel_id=1, source_target_pairs={{0,1},{1,0},{2,3},{3,2},{4,5},{5,4},{6,7},{7,6},{8,9},{9,8},{10,11... | collective-permute-start | bytes 98312 | tf_op jit(solution)/shard_map/ppermute | solution.py:381
  13.3 8.4 %copy-start.2 = (f32[256]{0:T(256)S(1)}, f32[256]{0:T(256)}, u32[]{:S(2)}) copy-start(f32[256]{0:T(256)} %param.15) | copy-start | bytes 3076
  13.3 8.4 %copy-start.3 = (f32[256]{0:T(256)S(1)}, f32[256]{0:T(256)}, u32[]{:S(2)}) copy-start(f32[256]{0:T(256)} %param.13) | copy-start | bytes 3076
  13.4 8.4 %copy-start.4 = (f32[256]{0:T(256)S(1)}, f32[256]{0:T(256)}, u32[]{:S(2)}) copy-start(f32[256]{0:T(256)} %param.11) | copy-start | bytes 3076
  13.4 8.4 %copy-start.5 = (f32[256]{0:T(256)S(1)}, f32[256]{0:T(256)}, u32[]{:S(2)}) copy-start(f32[256]{0:T(256)} %param.10) | copy-start | bytes 3076
  13.9 1.4 %collective-permute-start.5 = (f32[8,128]{1,0:T(8,128)S(1)}, f32[8,128]{1,0:T(8,128)S(1)}, u32[]{:S(2)}, u32[]{:S(2)}) collective-permute-start(f32[8,128]{1,0:T(8,128)S(1)} %get-tuple-element.30), channel_id=1, source_target_pairs={{0,1},{1,0},{2,3},{3,2},{4,5},{5,4},{6,7},{7,6},{8,9},{9,8},{10,11... | collective-permute-start | bytes 12296 | tf_op jit(solution)/shard_map/ppermute | solution.py:310
  15.3 3.6 %collective-permute-start.6 = (f32[8,128]{1,0:T(8,128)S(1)}, f32[8,128]{1,0:T(8,128)S(1)}, u32[]{:S(2)}, u32[]{:S(2)}) collective-permute-start(f32[8,128]{1,0:T(8,128)S(1)} %add.12), channel_id=1, source_target_pairs={{0,4},{2,6},{4,0},{6,2},{8,12},{10,14},{12,8},{14,10},{1,5},{3,7},... | collective-permute-start | bytes 12296 | tf_op jit(solution)/shard_map/ppermute | solution.py:310
  18.9 4.5 %collective-permute-start.7 = (f32[8,128]{1,0:T(8,128)S(1)}, f32[8,128]{1,0:T(8,128)S(1)}, u32[]{:S(2)}, u32[]{:S(2)}) collective-permute-start(f32[8,128]{1,0:T(8,128)S(1)} %add.13), channel_id=1, source_target_pairs={{0,8},{2,10},{4,12},{6,14},{8,0},{10,2},{12,4},{14,6},{1,9},{3,11}... | collective-permute-start | bytes 12296 | tf_op jit(solution)/shard_map/ppermute | solution.py:310
  23.4 4.3 %collective-permute-start.8 = (f32[8,128]{1,0:T(8,128)S(1)}, f32[8,128]{1,0:T(8,128)S(1)}, u32[]{:S(2)}, u32[]{:S(2)}) collective-permute-start(f32[8,128]{1,0:T(8,128)S(1)} %add.14), channel_id=1, source_target_pairs={{0,2},{2,0},{4,6},{6,4},{8,10},{10,8},{12,14},{14,12},{1,3},{3,1},... | collective-permute-start | bytes 12296 | tf_op jit(solution)/shard_map/ppermute | solution.py:310
  26.2 1.6 %copy-start = (bf16[3,3,256,128]{3,2,1,0:T(8,128)(2,1)S(1)}, bf16[3,3,256,128]{3,2,1,0:T(8,128)(2,1)}, u32[]{:S(2)}) copy-start(bf16[3,3,256,128]{3,2,1,0:T(8,128)(2,1)} %own_w1.1) | copy-start | bytes 1769476
  26.2 1.6 %copy-start.1 = (bf16[3,3,256,128]{3,2,1,0:T(8,128)(2,1)S(1)}, bf16[3,3,256,128]{3,2,1,0:T(8,128)(2,1)}, u32[]{:S(2)}) copy-start(bf16[3,3,256,128]{3,2,1,0:T(8,128)(2,1)} %own_w2.1) | copy-start | bytes 1769476

commit v19 on v14

--- a/solution.py
+++ b/solution.py
@@ -59,10 +59,10 @@
     copy.wait()
 
 
-def spread_line(out, main, edge):
+def spread_line(out, main, edge, inside=True):
     width, cin = main.shape
     line = jnp.concatenate([main.astype(jnp.float32), edge.astype(jnp.float32)], axis=0)
-    line = jnp.where(edge_mask(width), line, 0.0)
+    line = jnp.where(edge_mask(width) & inside, line, 0.0)
     out[:, 0:cin] = pltpu.roll(line, width + EDGE - 1, 0).astype(jnp.bfloat16)
     out[:, cin : 2 * cin] = line.astype(jnp.bfloat16)
     out[:, 2 * cin : 3 * cin] = pltpu.roll(line, 1, 0).astype(jnp.bfloat16)
@@ -119,7 +119,7 @@
 def next_kernel(next_ref, edge_ref, tail_ref, sums_ref, own_w, other_w, u_ref, xs_ref, stats_ref):
     width = next_ref.shape[1]
     last_here = lax.axis_index("rows") == lax.axis_size("rows") - 1
-    spread_line(xs_ref.at[0], next_ref[0], edge_ref[0])
+    spread_line(xs_ref.at[0], next_ref[0], edge_ref[0], jnp.logical_not(last_here))
     column = lax.axis_index("fsdp")
     sums = sums_ref[...]
     for phase in range(2):
@@ -141,7 +141,8 @@
     width = next_ref.shape[1]
     for row in range(HALO):
         spread_line(xs_above.at[row], above_ref[row, :width], above_ref[row, width:])
-    spread_line(xs_below.at[0], next_ref[1], next_edge_ref[1])
+    more_below = lax.axis_index("rows") < lax.axis_size("rows") - 1
+    spread_line(xs_below.at[0], next_ref[1], next_edge_ref[1], more_below)
     for phase in range(2):
         dot = functools.partial(tap_dot, phase=phase, own_w=own_w, other_w=other_w)
         outer = dot(xs_above[...], kr=3)
@@ -312,7 +313,7 @@
     count = float(2 * rows * n_rows * 2 * width * columns * (cout // NORM_GROUPS))
     swap = [(0, 1), (1, 0)]
     to_next = [(i, i + 1) for i in range(n_rows - 1)]
-    to_previous = [(i + 1, i) for i in range(n_rows - 1)]
+    to_previous = [((i + 1) % n_rows, i) for i in range(n_rows)]
     total = width + EDGE
     hbm = pl.BlockSpec(memory_space=pltpu.HBM)
     vmem = pl.BlockSpec(memory_space=pltpu.VMEM)

time: 32.7 us -> 32.5 us (level)
  starting transfers between devices: 15.7 us -> 10.4 us
  waiting for transfers between devices: 6.11 us -> 11.3 us
    ppermute x4, starting transfers between devices: 7.9 us -> 2.33 us  [total_over(): lax.ppermute(block, axis, [(i, i ^ step) for i in range(size)])]
    ppermute x4, waiting for transfers between devices: 4.63 us -> 9.51 us  [total_over(): lax.ppermute(block, axis, [(i, i ^ step) for i in range(size)])]
    ppermute x1, starting transfers between devices: 1.28 us -> 5.55 us  [local(): following = lax.ppermute(image, 'rows', to_previous)]
    ppermute x1, starting transfers between devices: 5.46 us -> 1.31 us  [local(): above = lax.ppermute(lines, 'rows', to_next)]
  transfers between devices with their start and end apart: 11 -> 11, of which waited for: 5 -> 5; matrix products, arithmetic and copies ran while one was open for 0% -> 0% of each run, Pallas kernels for 17% -> 18%
where the time goes in v19:
time: 32.5 us; the launch traced here: 32.3 us
  waiting for transfers between devices  11.3 us (35%)
  starting transfers between devices  10.4 us (32%)
  Pallas kernels  10.4 us (32%)
    ppermute x4, waiting for transfers between devices, total_over(): lax.ppermute(block, axis, [(i, i ^ step) for i in range(size)])  9.51 us
    ppermute x1, starting transfers between devices, local(): following = lax.ppermute(image, 'rows', to_previous)  5.55 us
    pallas_call x1, Pallas kernels, local(): call(functools.partial(conv_kernel, count), [vmem] * 9, [((2 * rows, 2 *...  4.68 us
    ppermute x4, starting transfers between devices, total_over(): lax.ppermute(block, axis, [(i, i ^ step) for i in range(size)])  2.33 us
    ppermute x1, waiting for transfers between devices, local(): following = lax.ppermute(image, 'rows', to_previous)  1.73 us
    pallas_call x1, Pallas kernels, local(): call(near_kernel, [hbm], [(shape_w, bf16)], [pltpu.SemaphoreType.DMA(())]...  1.6 us
    ppermute x1, starting transfers between devices, local(): above = lax.ppermute(lines, 'rows', to_next)  1.31 us
    pallas_call x1, Pallas kernels, local(): call(own_kernel, [vmem] * 3, [((rows, total, 3 * cin), bf16), ((2 * rows...  1.26 us
  transfers between devices with their start and end apart: 11, of which 5 were waited for; matrix products, arithmetic and copies ran while one was open for 0% of the time, Pallas kernels for 18%

profile of v19, /device:TPU:0, one launch (start us, length us, event | category | flops | bytes accessed | tf_op | source)
XLA Modules:
  0.0 32.3 jit_solution(17763365345451891853)
XLA Ops:
  0.0 0.5 %collective-permute-start.1 = (bf16[4,4,512,128]{3,2,1,0:T(8,128)(2,1)}, bf16[4,4,512,128]{3,2,1,0:T(8,128)(2,1)S(1)}, u32[]{:S(2)}, u32[]{:S(2)}) collective-permute-start(bf16[4,4,512,128]{3,2,1,0:T(8,128)(2,1)} %param.9), channel_id=1, source_target_pairs={{0,1},{1,0},{2,3},{3,2},{4,5},{5,4},{6,7},{7,6},{8,9},{9,8},{10,11... | collective-permute-start | bytes 6291464 | tf_op jit(solution)/shard_map/ppermute | solution.py:345
  0.5 5.6 %collective-permute-start.2 = (bf16[2,128,512]{2,1,0:T(8,128)(2,1)}, bf16[2,128,512]{2,1,0:T(8,128)(2,1)S(1)}, u32[]{:S(2)}, u32[]{:S(2)}) collective-permute-start(bf16[2,128,512]{2,1,0:T(8,128)(2,1)} %image_ref.1), channel_id=1, source_target_pairs={{2,0},{4,2},{6,4},{8,6},{10,8},{12,10},{14,12},{0,14},{3,1},{5,3},... | collective-permute-start | bytes 786440 | tf_op jit(solution)/shard_map/ppermute | solution.py:336
  6.0 1.0 %cut.1 = (bf16[2,128,512]{2,1,0:T(8,128)(2,1)S(1)}, bf16[2,16,512]{2,1,0:T(8,128)(2,1)S(1)}) custom-call(bf16[2,128,512]{2,1,0:T(8,128)(2,1)} %image_ref.1), custom_call_target="tpu_custom_call" | custom-call | bytes 2097152 | tf_op jit(solution)/shard_map/cut/pallas_call | solution.py:337
  7.1 0.3 collective-permute-start
  7.3 0.3 collective-permute-start.10
  7.6 0.2 collective-permute-start.9
  7.9 1.6 %near_weights.1.own_w = bf16[4,2,2,512,128]{4,3,2,1,0:T(8,128)(2,1)S(1)} custom-call(bf16[4,2,2,512,128]{4,3,2,1,0:T(8,128)(2,1)} %bitcast.9), custom_call_target="tpu_custom_call" | custom-call | bytes 2097152 | tf_op jit(solution)/shard_map/near_weights/pallas_call | solution.py:348
  9.5 1.3 %collective-permute-start.4 = (bf16[2,144,512]{2,1,0:T(8,128)(2,1)S(1)}, bf16[2,144,512]{2,1,0:T(8,128)(2,1)S(1)}, u32[]{:S(2)}, u32[]{:S(2)}) collective-permute-start(bf16[2,144,512]{2,1,0:T(8,128)(2,1)S(1)} %constant_dynamic-update-slice_fusion.lines_ref), channel_id=1, source_target_pairs={{0,2},{2,4},{4,6},{6,8},{8,10},{10,12},{12,14},{1,3},{3,5},{5,7},{... | collective-permute-start | bytes 884744 | tf_op jit(solution)/shard_map/ppermute | solution.py:352
  10.8 1.7 %collective-permute-done.2.lines_ref.next_ref = bf16[2,128,512]{2,1,0:T(8,128)(2,1)S(1)} collective-permute-done((bf16[2,128,512]{2,1,0:T(8,128)(2,1)}, bf16[2,128,512]{2,1,0:T(8,128)(2,1)S(1)}, u32[]{:S(2)}, u32[]{:S(2)}) %collective-permute-start.2) | collective-permute-done | bytes 262176 | tf_op jit(solution)/shard_map/ppermute | solution.py:336
  12.6 1.3 %deconv_own.1 = (bf16[2,144,1536]{2,1,0:T(8,128)(2,1)S(1)}, bf16[2,2,144,256]{3,2,1,0:T(8,128)(2,1)S(1)}, f32[2,144,256]{2,1,0:T(8,128)S(1)}, f32[2,2,144,256]{3,2,1,0:T(8,128)S(1)}, f32[2,256]{1,0:T(2,128)S(1)}) custom-call(bf16[2,144,512]{2,1,0:T(8,128)(2,1)S(1)} %constant_dynamic-update-slice_fusion.lines_ref, ...), custom_call_target="tpu_custom_call" | custom-call | flops 905969664 | bytes 2097152 | tf_op jit(solution)/shard_map/deconv_own/pallas_call | solution.py:354
  13.9 0.0 copy-start.2
  13.9 0.0 copy-start.3
  13.9 0.0 copy-start.4
  13.9 0.0 copy-start.5
  13.9 0.5 %deconv_next.1 = (bf16[2,2,144,256]{3,2,1,0:T(8,128)(2,1)S(1)}, bf16[1,144,1536]{2,1,0:T(8,128)(2,1)S(1)}, f32[8,128]{1,0:T(8,128)S(1)}) custom-call(bf16[2,128,512]{2,1,0:T(8,128)(2,1)S(1)} %collective-permute-done.2.lines_ref.next_ref, bf16[2,16,512]{2,1,0:T(8,128)(2,1)S(1)} %collective-permute-done.3.edge_ref.next_edge_ref, ...), custom_call_target="tpu_custom_call" | custom-call | flops 301989888 | bytes 2097152 | tf_op jit(solution)/shard_map/deconv_next/pallas_call | solution.py:370
  14.4 0.6 %collective-permute-start.5 = (f32[8,128]{1,0:T(8,128)S(1)}, f32[8,128]{1,0:T(8,128)S(1)}, u32[]{:S(2)}, u32[]{:S(2)}) collective-permute-start(f32[8,128]{1,0:T(8,128)S(1)} %get-tuple-element.30), channel_id=1, source_target_pairs={{0,1},{1,0},{2,3},{3,2},{4,5},{5,4},{6,7},{7,6},{8,9},{9,8},{10,11... | collective-permute-start | bytes 12296 | tf_op jit(solution)/shard_map/ppermute | solution.py:298
  15.0 0.8 %collective-permute-done.5 = f32[8,128]{1,0:T(8,128)S(1)} collective-permute-done((f32[8,128]{1,0:T(8,128)S(1)}, f32[8,128]{1,0:T(8,128)S(1)}, u32[]{:S(2)}, u32[]{:S(2)}) %collective-permute-start.5) | collective-permute-done | bytes 4128 | tf_op jit(solution)/shard_map/ppermute | solution.py:298
  15.8 3.6 %collective-permute-done.6 = f32[8,128]{1,0:T(8,128)S(1)} collective-permute-done((f32[8,128]{1,0:T(8,128)S(1)}, f32[8,128]{1,0:T(8,128)S(1)}, u32[]{:S(2)}, u32[]{:S(2)}) %collective-permute-start.6) | collective-permute-done | bytes 4128 | tf_op jit(solution)/shard_map/ppermute | solution.py:298
  19.5 0.4 %collective-permute-start.7 = (f32[8,128]{1,0:T(8,128)S(1)}, f32[8,128]{1,0:T(8,128)S(1)}, u32[]{:S(2)}, u32[]{:S(2)}) collective-permute-start(f32[8,128]{1,0:T(8,128)S(1)} %add.13), channel_id=1, source_target_pairs={{0,8},{2,10},{4,12},{6,14},{8,0},{10,2},{12,4},{14,6},{1,9},{3,11}... | collective-permute-start | bytes 12296 | tf_op jit(solution)/shard_map/ppermute | solution.py:298
  19.9 4.1 %collective-permute-done.7 = f32[8,128]{1,0:T(8,128)S(1)} collective-permute-done((f32[8,128]{1,0:T(8,128)S(1)}, f32[8,128]{1,0:T(8,128)S(1)}, u32[]{:S(2)}, u32[]{:S(2)}) %collective-permute-start.7) | collective-permute-done | bytes 4128 | tf_op jit(solution)/shard_map/ppermute | solution.py:298
  24.0 1.3 %collective-permute-start.8 = (f32[8,128]{1,0:T(8,128)S(1)}, f32[8,128]{1,0:T(8,128)S(1)}, u32[]{:S(2)}, u32[]{:S(2)}) collective-permute-start(f32[8,128]{1,0:T(8,128)S(1)} %add.14), channel_id=1, source_target_pairs={{0,2},{2,0},{4,6},{6,4},{8,10},{10,8},{12,14},{14,12},{1,3},{3,1},... | collective-permute-start | bytes 12296 | tf_op jit(solution)/shard_map/ppermute | solution.py:298
  25.3 1.2 %deconv_halo.1.halo_ref = bf16[4,2,144,256]{3,2,1,0:T(8,128)(2,1)S(1)} custom-call(bf16[2,144,512]{2,1,0:T(8,128)(2,1)S(1)} %collective-permute-done.4.above_ref, bf16[2,128,512]{2,1,0:T(8,128)(2,1)S(1)} %collective-permute-done.2.lines_ref.next_ref, bf16[2,16,512]{2,1,0:T(8,128)(2,1)S(1)} %collective-permute-done.3.edge_ref.next_edge_ref, ...), custom_call_target="tpu_custom_call" | custom-call | flops 1207959552 | bytes 2097152 | tf_op jit(solution)/shard_map/deconv_halo/pallas_call | solution.py:378
  26.6 1.0 %collective-permute-done.8 = f32[8,128]{1,0:T(8,128)S(1)} collective-permute-done((f32[8,128]{1,0:T(8,128)S(1)}, f32[8,128]{1,0:T(8,128)S(1)}, u32[]{:S(2)}, u32[]{:S(2)}) %collective-permute-start.8) | collective-permute-done | bytes 4128 | tf_op jit(solution)/shard_map/ppermute | solution.py:298
  27.6 4.7 %convs.1 = bf16[4,256,256]{2,1,0:T(8,128)(2,1)} custom-call(bf16[2,2,144,256]{3,2,1,0:T(8,128)(2,1)S(1)} %get-tuple-element.23.u_ref, bf16[2,2,144,256]{3,2,1,0:T(8,128)(2,1)S(1)} %get-tuple-element.26.u_next_ref, bf16[4,2,144,256]{3,2,1,0:T(8,128)(2,1)S(1)} %deconv_halo.1.halo_ref, f32[8,128]{1,0:T(8,128)S(1)} %add.15.stats_ref, ...), custom_call_target="tpu_custom_call" | custom-call | flops 5000000000 | bytes 2097152 | tf_op jit(solution)/shard_map/convs/pallas_call | solution.py:389
  (24 shorter events, 0.1 us)
Async XLA Ops:
  0.0 12.6 %collective-permute-start.1 = (bf16[4,4,512,128]{3,2,1,0:T(8,128)(2,1)}, bf16[4,4,512,128]{3,2,1,0:T(8,128)(2,1)S(1)}, u32[]{:S(2)}, u32[]{:S(2)}) collective-permute-start(bf16[4,4,512,128]{3,2,1,0:T(8,128)(2,1)} %param.9), channel_id=1, source_target_pairs={{0,1},{1,0},{2,3},{3,2},{4,5},{5,4},{6,7},{7,6},{8,9},{9,8},{10,11... | collective-permute-start | bytes 6291464 | tf_op jit(solution)/shard_map/ppermute | solution.py:345
  0.5 12.1 %collective-permute-start.2 = (bf16[2,128,512]{2,1,0:T(8,128)(2,1)}, bf16[2,128,512]{2,1,0:T(8,128)(2,1)S(1)}, u32[]{:S(2)}, u32[]{:S(2)}) collective-permute-start(bf16[2,128,512]{2,1,0:T(8,128)(2,1)} %image_ref.1), channel_id=1, source_target_pairs={{2,0},{4,2},{6,4},{8,6},{10,8},{12,10},{14,12},{0,14},{3,1},{5,3},... | collective-permute-start | bytes 786440 | tf_op jit(solution)/shard_map/ppermute | solution.py:336
  7.1 2.4 %collective-permute-start = (bf16[2,16,512]{2,1,0:T(8,128)(2,1)S(1)}, bf16[2,16,512]{2,1,0:T(8,128)(2,1)S(1)}, u32[]{:S(2)}, u32[]{:S(2)}) collective-permute-start(bf16[2,16,512]{2,1,0:T(8,128)(2,1)S(1)} %get-tuple-element.20), channel_id=1, source_target_pairs={{0,1},{1,0},{2,3},{3,2},{4,5},{5,4},{6,7},{7,6},{8,9},{9,8},{10,11... | collective-permute-start | bytes 98312 | tf_op jit(solution)/shard_map/ppermute | solution.py:344
  7.3 20.2 %collective-permute-start.10 = (bf16[3,3,256,128]{3,2,1,0:T(8,128)(2,1)}, bf16[3,3,256,128]{3,2,1,0:T(8,128)(2,1)S(1)}, u32[]{:S(2)}, u32[]{:S(2)}) collective-permute-start(bf16[3,3,256,128]{3,2,1,0:T(8,128)(2,1)} %own_w2.1), channel_id=1, source_target_pairs={{0,1},{1,0},{2,3},{3,2},{4,5},{5,4},{6,7},{7,6},{8,9},{9,8},{10,11... | collective-permute-start | bytes 1769480 | tf_op jit(solution)/shard_map/ppermute | solution.py:347
  7.6 19.9 %collective-permute-start.9 = (bf16[3,3,256,128]{3,2,1,0:T(8,128)(2,1)}, bf16[3,3,256,128]{3,2,1,0:T(8,128)(2,1)S(1)}, u32[]{:S(2)}, u32[]{:S(2)}) collective-permute-start(bf16[3,3,256,128]{3,2,1,0:T(8,128)(2,1)} %own_w1.1), channel_id=1, source_target_pairs={{0,1},{1,0},{2,3},{3,2},{4,5},{5,4},{6,7},{7,6},{8,9},{9,8},{10,11... | collective-permute-start | bytes 1769480 | tf_op jit(solution)/shard_map/ppermute | solution.py:346
  9.5 15.8 %collective-permute-start.4 = (bf16[2,144,512]{2,1,0:T(8,128)(2,1)S(1)}, bf16[2,144,512]{2,1,0:T(8,128)(2,1)S(1)}, u32[]{:S(2)}, u32[]{:S(2)}) collective-permute-start(bf16[2,144,512]{2,1,0:T(8,128)(2,1)S(1)} %constant_dynamic-update-slice_fusion.lines_ref), channel_id=1, source_target_pairs={{0,2},{2,4},{4,6},{6,8},{8,10},{10,12},{12,14},{1,3},{3,5},{5,7},{... | collective-permute-start | bytes 884744 | tf_op jit(solution)/shard_map/ppermute | solution.py:352
  12.6 1.3 %collective-permute-start.3 = (bf16[2,16,512]{2,1,0:T(8,128)(2,1)S(1)}, bf16[2,16,512]{2,1,0:T(8,128)(2,1)S(1)}, u32[]{:S(2)}, u32[]{:S(2)}) collective-permute-start(bf16[2,16,512]{2,1,0:T(8,128)(2,1)S(1)} %next_edges.1), channel_id=1, source_target_pairs={{0,1},{1,0},{2,3},{3,2},{4,5},{5,4},{6,7},{7,6},{8,9},{9,8},{10,11... | collective-permute-start | bytes 98312 | tf_op jit(solution)/shard_map/ppermute | solution.py:369
  13.9 6.0 %copy-start.2 = (f32[256]{0:T(256)S(1)}, f32[256]{0:T(256)}, u32[]{:S(2)}) copy-start(f32[256]{0:T(256)} %param.15) | copy-start | bytes 3076
  13.9 6.0 %copy-start.3 = (f32[256]{0:T(256)S(1)}, f32[256]{0:T(256)}, u32[]{:S(2)}) copy-start(f32[256]{0:T(256)} %param.13) | copy-start | bytes 3076
  13.9 6.0 %copy-start.4 = (f32[256]{0:T(256)S(1)}, f32[256]{0:T(256)}, u32[]{:S(2)}) copy-start(f32[256]{0:T(256)} %param.11) | copy-start | bytes 3076
  13.9 6.0 %copy-start.5 = (f32[256]{0:T(256)S(1)}, f32[256]{0:T(256)}, u32[]{:S(2)}) copy-start(f32[256]{0:T(256)} %param.10) | copy-start | bytes 3076
  14.4 1.4 %collective-permute-start.5 = (f32[8,128]{1,0:T(8,128)S(1)}, f32[8,128]{1,0:T(8,128)S(1)}, u32[]{:S(2)}, u32[]{:S(2)}) collective-permute-start(f32[8,128]{1,0:T(8,128)S(1)} %get-tuple-element.30), channel_id=1, source_target_pairs={{0,1},{1,0},{2,3},{3,2},{4,5},{5,4},{6,7},{7,6},{8,9},{9,8},{10,11... | collective-permute-start | bytes 12296 | tf_op jit(solution)/shard_map/ppermute | solution.py:298
  15.8 3.6 %collective-permute-start.6 = (f32[8,128]{1,0:T(8,128)S(1)}, f32[8,128]{1,0:T(8,128)S(1)}, u32[]{:S(2)}, u32[]{:S(2)}) collective-permute-start(f32[8,128]{1,0:T(8,128)S(1)} %add.12), channel_id=1, source_target_pairs={{0,4},{2,6},{4,0},{6,2},{8,12},{10,14},{12,8},{14,10},{1,5},{3,7},... | collective-permute-start | bytes 12296 | tf_op jit(solution)/shard_map/ppermute | solution.py:298
  19.5 4.5 %collective-permute-start.7 = (f32[8,128]{1,0:T(8,128)S(1)}, f32[8,128]{1,0:T(8,128)S(1)}, u32[]{:S(2)}, u32[]{:S(2)}) collective-permute-start(f32[8,128]{1,0:T(8,128)S(1)} %add.13), channel_id=1, source_target_pairs={{0,8},{2,10},{4,12},{6,14},{8,0},{10,2},{12,4},{14,6},{1,9},{3,11}... | collective-permute-start | bytes 12296 | tf_op jit(solution)/shard_map/ppermute | solution.py:298
  24.0 3.6 %collective-permute-start.8 = (f32[8,128]{1,0:T(8,128)S(1)}, f32[8,128]{1,0:T(8,128)S(1)}, u32[]{:S(2)}, u32[]{:S(2)}) collective-permute-start(f32[8,128]{1,0:T(8,128)S(1)} %add.14), channel_id=1, source_target_pairs={{0,2},{2,0},{4,6},{6,4},{8,10},{10,8},{12,14},{14,12},{1,3},{3,1},... | collective-permute-start | bytes 12296 | tf_op jit(solution)/shard_map/ppermute | solution.py:298
  25.3 2.3 %copy-start = (bf16[3,3,256,128]{3,2,1,0:T(8,128)(2,1)S(1)}, bf16[3,3,256,128]{3,2,1,0:T(8,128)(2,1)}, u32[]{:S(2)}) copy-start(bf16[3,3,256,128]{3,2,1,0:T(8,128)(2,1)} %own_w1.1) | copy-start | bytes 1769476
  25.3 2.3 %copy-start.1 = (bf16[3,3,256,128]{3,2,1,0:T(8,128)(2,1)S(1)}, bf16[3,3,256,128]{3,2,1,0:T(8,128)(2,1)}, u32[]{:S(2)}) copy-start(bf16[3,3,256,128]{3,2,1,0:T(8,128)(2,1)} %own_w2.1) | copy-start | bytes 1769476

commit v20 on v19

--- a/solution.py
+++ b/solution.py
@@ -294,7 +294,7 @@
     if size & (size - 1):
         return lax.psum(block, axis)
     steps = [2**n for n in range(size.bit_length() - 1)]
-    for step in steps[1:] + steps[:1]:
+    for step in steps[1:2] + steps[:1] + steps[2:]:
         block = block + lax.ppermute(block, axis, [(i, i ^ step) for i in range(size)])
     return block
 

time: 32.5 us -> 32.5 us (level)
  waiting for transfers between devices: 11.3 us -> 10.5 us
  starting transfers between devices: 10.4 us -> 11.2 us
    ppermute x4, waiting for transfers between devices: 9.51 us -> 8.78 us  [total_over(): lax.ppermute(block, axis, [(i, i ^ step) for i in range(size)])]
    ppermute x4, starting transfers between devices: 2.33 us -> 3.05 us  [total_over(): lax.ppermute(block, axis, [(i, i ^ step) for i in range(size)])]
where the time goes in v20:
time: 32.5 us; the launch traced here: 32.3 us
  starting transfers between devices  11.2 us (34%)
  waiting for transfers between devices  10.5 us (32%)
  Pallas kernels  10.4 us (32%)
    ppermute x4, waiting for transfers between devices, total_over(): lax.ppermute(block, axis, [(i, i ^ step) for i in range(size)])  8.78 us
    ppermute x1, starting transfers between devices, local(): following = lax.ppermute(image, 'rows', to_previous)  5.55 us
    pallas_call x1, Pallas kernels, local(): call(functools.partial(conv_kernel, count), [vmem] * 9, [((2 * rows, 2 *...  4.68 us
    ppermute x4, starting transfers between devices, total_over(): lax.ppermute(block, axis, [(i, i ^ step) for i in range(size)])  3.05 us
    ppermute x1, waiting for transfers between devices, local(): following = lax.ppermute(image, 'rows', to_previous)  1.73 us
    pallas_call x1, Pallas kernels, local(): call(near_kernel, [hbm], [(shape_w, bf16)], [pltpu.SemaphoreType.DMA(())]...  1.6 us
    ppermute x1, starting transfers between devices, local(): above = lax.ppermute(lines, 'rows', to_next)  1.31 us
    pallas_call x1, Pallas kernels, local(): call(own_kernel, [vmem] * 3, [((rows, total, 3 * cin), bf16), ((2 * rows...  1.26 us
  transfers between devices with their start and end apart: 11, of which 5 were waited for; matrix products, arithmetic and copies ran while one was open for 0% of the time, Pallas kernels for 18%

profile of v20, /device:TPU:0, one launch (start us, length us, event | category | flops | bytes accessed | tf_op | source)
XLA Modules:
  0.0 32.3 jit_solution(5154717201529962677)
XLA Ops:
  0.0 0.5 %collective-permute-start.1 = (bf16[4,4,512,128]{3,2,1,0:T(8,128)(2,1)}, bf16[4,4,512,128]{3,2,1,0:T(8,128)(2,1)S(1)}, u32[]{:S(2)}, u32[]{:S(2)}) collective-permute-start(bf16[4,4,512,128]{3,2,1,0:T(8,128)(2,1)} %param.9), channel_id=1, source_target_pairs={{0,1},{1,0},{2,3},{3,2},{4,5},{5,4},{6,7},{7,6},{8,9},{9,8},{10,11... | collective-permute-start | bytes 6291464 | tf_op jit(solution)/shard_map/ppermute | solution.py:345
  0.5 5.6 %collective-permute-start.2 = (bf16[2,128,512]{2,1,0:T(8,128)(2,1)}, bf16[2,128,512]{2,1,0:T(8,128)(2,1)S(1)}, u32[]{:S(2)}, u32[]{:S(2)}) collective-permute-start(bf16[2,128,512]{2,1,0:T(8,128)(2,1)} %image_ref.1), channel_id=1, source_target_pairs={{2,0},{4,2},{6,4},{8,6},{10,8},{12,10},{14,12},{0,14},{3,1},{5,3},... | collective-permute-start | bytes 786440 | tf_op jit(solution)/shard_map/ppermute | solution.py:336
  6.0 1.0 %cut.1 = (bf16[2,128,512]{2,1,0:T(8,128)(2,1)S(1)}, bf16[2,16,512]{2,1,0:T(8,128)(2,1)S(1)}) custom-call(bf16[2,128,512]{2,1,0:T(8,128)(2,1)} %image_ref.1), custom_call_target="tpu_custom_call" | custom-call | bytes 2097152 | tf_op jit(solution)/shard_map/cut/pallas_call | solution.py:337
  7.1 0.3 collective-permute-start
  7.3 0.3 collective-permute-start.10
  7.6 0.2 collective-permute-start.9
  7.9 1.6 %near_weights.1.own_w = bf16[4,2,2,512,128]{4,3,2,1,0:T(8,128)(2,1)S(1)} custom-call(bf16[4,2,2,512,128]{4,3,2,1,0:T(8,128)(2,1)} %bitcast.9), custom_call_target="tpu_custom_call" | custom-call | bytes 2097152 | tf_op jit(solution)/shard_map/near_weights/pallas_call | solution.py:348
  9.5 1.3 %collective-permute-start.4 = (bf16[2,144,512]{2,1,0:T(8,128)(2,1)S(1)}, bf16[2,144,512]{2,1,0:T(8,128)(2,1)S(1)}, u32[]{:S(2)}, u32[]{:S(2)}) collective-permute-start(bf16[2,144,512]{2,1,0:T(8,128)(2,1)S(1)} %constant_dynamic-update-slice_fusion.lines_ref), channel_id=1, source_target_pairs={{0,2},{2,4},{4,6},{6,8},{8,10},{10,12},{12,14},{1,3},{3,5},{5,7},{... | collective-permute-start | bytes 884744 | tf_op jit(solution)/shard_map/ppermute | solution.py:352
  10.8 1.7 %collective-permute-done.2.lines_ref.next_ref = bf16[2,128,512]{2,1,0:T(8,128)(2,1)S(1)} collective-permute-done((bf16[2,128,512]{2,1,0:T(8,128)(2,1)}, bf16[2,128,512]{2,1,0:T(8,128)(2,1)S(1)}, u32[]{:S(2)}, u32[]{:S(2)}) %collective-permute-start.2) | collective-permute-done | bytes 262176 | tf_op jit(solution)/shard_map/ppermute | solution.py:336
  12.6 1.3 %deconv_own.1 = (bf16[2,144,1536]{2,1,0:T(8,128)(2,1)S(1)}, bf16[2,2,144,256]{3,2,1,0:T(8,128)(2,1)S(1)}, f32[2,144,256]{2,1,0:T(8,128)S(1)}, f32[2,2,144,256]{3,2,1,0:T(8,128)S(1)}, f32[2,256]{1,0:T(2,128)S(1)}) custom-call(bf16[2,144,512]{2,1,0:T(8,128)(2,1)S(1)} %constant_dynamic-update-slice_fusion.lines_ref, ...), custom_call_target="tpu_custom_call" | custom-call | flops 905969664 | bytes 2097152 | tf_op jit(solution)/shard_map/deconv_own/pallas_call | solution.py:354
  13.9 0.0 copy-start.2
  13.9 0.0 copy-start.3
  13.9 0.0 copy-start.4
  13.9 0.0 copy-start.5
  13.9 0.5 %deconv_next.1 = (bf16[2,2,144,256]{3,2,1,0:T(8,128)(2,1)S(1)}, bf16[1,144,1536]{2,1,0:T(8,128)(2,1)S(1)}, f32[8,128]{1,0:T(8,128)S(1)}) custom-call(bf16[2,128,512]{2,1,0:T(8,128)(2,1)S(1)} %collective-permute-done.2.lines_ref.next_ref, bf16[2,16,512]{2,1,0:T(8,128)(2,1)S(1)} %collective-permute-done.3.edge_ref.next_edge_ref, ...), custom_call_target="tpu_custom_call" | custom-call | flops 301989888 | bytes 2097152 | tf_op jit(solution)/shard_map/deconv_next/pallas_call | solution.py:370
  14.4 0.6 %collective-permute-start.5 = (f32[8,128]{1,0:T(8,128)S(1)}, f32[8,128]{1,0:T(8,128)S(1)}, u32[]{:S(2)}, u32[]{:S(2)}) collective-permute-start(f32[8,128]{1,0:T(8,128)S(1)} %get-tuple-element.30), channel_id=1, source_target_pairs={{0,1},{1,0},{2,3},{3,2},{4,5},{5,4},{6,7},{7,6},{8,9},{9,8},{10,11... | collective-permute-start | bytes 12296 | tf_op jit(solution)/shard_map/ppermute | solution.py:298
  15.0 0.8 %collective-permute-done.5 = f32[8,128]{1,0:T(8,128)S(1)} collective-permute-done((f32[8,128]{1,0:T(8,128)S(1)}, f32[8,128]{1,0:T(8,128)S(1)}, u32[]{:S(2)}, u32[]{:S(2)}) %collective-permute-start.5) | collective-permute-done | bytes 4128 | tf_op jit(solution)/shard_map/ppermute | solution.py:298
  15.8 3.6 %collective-permute-done.6 = f32[8,128]{1,0:T(8,128)S(1)} collective-permute-done((f32[8,128]{1,0:T(8,128)S(1)}, f32[8,128]{1,0:T(8,128)S(1)}, u32[]{:S(2)}, u32[]{:S(2)}) %collective-permute-start.6) | collective-permute-done | bytes 4128 | tf_op jit(solution)/shard_map/ppermute | solution.py:298
  19.5 0.2 collective-permute-start.7
  19.7 3.3 %collective-permute-done.7 = f32[8,128]{1,0:T(8,128)S(1)} collective-permute-done((f32[8,128]{1,0:T(8,128)S(1)}, f32[8,128]{1,0:T(8,128)S(1)}, u32[]{:S(2)}, u32[]{:S(2)}) %collective-permute-start.7) | collective-permute-done | bytes 4128 | tf_op jit(solution)/shard_map/ppermute | solution.py:298
  23.1 2.2 %collective-permute-start.8 = (f32[8,128]{1,0:T(8,128)S(1)}, f32[8,128]{1,0:T(8,128)S(1)}, u32[]{:S(2)}, u32[]{:S(2)}) collective-permute-start(f32[8,128]{1,0:T(8,128)S(1)} %add.14), channel_id=1, source_target_pairs={{0,8},{2,10},{4,12},{6,14},{8,0},{10,2},{12,4},{14,6},{1,9},{3,11}... | collective-permute-start | bytes 12296 | tf_op jit(solution)/shard_map/ppermute | solution.py:298
  25.3 1.2 %deconv_halo.1.halo_ref = bf16[4,2,144,256]{3,2,1,0:T(8,128)(2,1)S(1)} custom-call(bf16[2,144,512]{2,1,0:T(8,128)(2,1)S(1)} %collective-permute-done.4.above_ref, bf16[2,128,512]{2,1,0:T(8,128)(2,1)S(1)} %collective-permute-done.2.lines_ref.next_ref, bf16[2,16,512]{2,1,0:T(8,128)(2,1)S(1)} %collective-permute-done.3.edge_ref.next_edge_ref, ...), custom_call_target="tpu_custom_call" | custom-call | flops 1207959552 | bytes 2097152 | tf_op jit(solution)/shard_map/deconv_halo/pallas_call | solution.py:378
  26.6 1.0 %collective-permute-done.8 = f32[8,128]{1,0:T(8,128)S(1)} collective-permute-done((f32[8,128]{1,0:T(8,128)S(1)}, f32[8,128]{1,0:T(8,128)S(1)}, u32[]{:S(2)}, u32[]{:S(2)}) %collective-permute-start.8) | collective-permute-done | bytes 4128 | tf_op jit(solution)/shard_map/ppermute | solution.py:298
  27.6 4.7 %convs.1 = bf16[4,256,256]{2,1,0:T(8,128)(2,1)} custom-call(bf16[2,2,144,256]{3,2,1,0:T(8,128)(2,1)S(1)} %get-tuple-element.23.u_ref, bf16[2,2,144,256]{3,2,1,0:T(8,128)(2,1)S(1)} %get-tuple-element.26.u_next_ref, bf16[4,2,144,256]{3,2,1,0:T(8,128)(2,1)S(1)} %deconv_halo.1.halo_ref, f32[8,128]{1,0:T(8,128)S(1)} %add.15.stats_ref, ...), custom_call_target="tpu_custom_call" | custom-call | flops 5000000000 | bytes 2097152 | tf_op jit(solution)/shard_map/convs/pallas_call | solution.py:389
  (24 shorter events, 0.1 us)
Async XLA Ops:
  0.0 12.6 %collective-permute-start.1 = (bf16[4,4,512,128]{3,2,1,0:T(8,128)(2,1)}, bf16[4,4,512,128]{3,2,1,0:T(8,128)(2,1)S(1)}, u32[]{:S(2)}, u32[]{:S(2)}) collective-permute-start(bf16[4,4,512,128]{3,2,1,0:T(8,128)(2,1)} %param.9), channel_id=1, source_target_pairs={{0,1},{1,0},{2,3},{3,2},{4,5},{5,4},{6,7},{7,6},{8,9},{9,8},{10,11... | collective-permute-start | bytes 6291464 | tf_op jit(solution)/shard_map/ppermute | solution.py:345
  0.5 12.1 %collective-permute-start.2 = (bf16[2,128,512]{2,1,0:T(8,128)(2,1)}, bf16[2,128,512]{2,1,0:T(8,128)(2,1)S(1)}, u32[]{:S(2)}, u32[]{:S(2)}) collective-permute-start(bf16[2,128,512]{2,1,0:T(8,128)(2,1)} %image_ref.1), channel_id=1, source_target_pairs={{2,0},{4,2},{6,4},{8,6},{10,8},{12,10},{14,12},{0,14},{3,1},{5,3},... | collective-permute-start | bytes 786440 | tf_op jit(solution)/shard_map/ppermute | solution.py:336
  7.1 2.4 %collective-permute-start = (bf16[2,16,512]{2,1,0:T(8,128)(2,1)S(1)}, bf16[2,16,512]{2,1,0:T(8,128)(2,1)S(1)}, u32[]{:S(2)}, u32[]{:S(2)}) collective-permute-start(bf16[2,16,512]{2,1,0:T(8,128)(2,1)S(1)} %get-tuple-element.20), channel_id=1, source_target_pairs={{0,1},{1,0},{2,3},{3,2},{4,5},{5,4},{6,7},{7,6},{8,9},{9,8},{10,11... | collective-permute-start | bytes 98312 | tf_op jit(solution)/shard_map/ppermute | solution.py:344
  7.3 20.2 %collective-permute-start.10 = (bf16[3,3,256,128]{3,2,1,0:T(8,128)(2,1)}, bf16[3,3,256,128]{3,2,1,0:T(8,128)(2,1)S(1)}, u32[]{:S(2)}, u32[]{:S(2)}) collective-permute-start(bf16[3,3,256,128]{3,2,1,0:T(8,128)(2,1)} %own_w2.1), channel_id=1, source_target_pairs={{0,1},{1,0},{2,3},{3,2},{4,5},{5,4},{6,7},{7,6},{8,9},{9,8},{10,11... | collective-permute-start | bytes 1769480 | tf_op jit(solution)/shard_map/ppermute | solution.py:347
  7.6 19.9 %collective-permute-start.9 = (bf16[3,3,256,128]{3,2,1,0:T(8,128)(2,1)}, bf16[3,3,256,128]{3,2,1,0:T(8,128)(2,1)S(1)}, u32[]{:S(2)}, u32[]{:S(2)}) collective-permute-start(bf16[3,3,256,128]{3,2,1,0:T(8,128)(2,1)} %own_w1.1), channel_id=1, source_target_pairs={{0,1},{1,0},{2,3},{3,2},{4,5},{5,4},{6,7},{7,6},{8,9},{9,8},{10,11... | collective-permute-start | bytes 1769480 | tf_op jit(solution)/shard_map/ppermute | solution.py:346
  9.5 15.8 %collective-permute-start.4 = (bf16[2,144,512]{2,1,0:T(8,128)(2,1)S(1)}, bf16[2,144,512]{2,1,0:T(8,128)(2,1)S(1)}, u32[]{:S(2)}, u32[]{:S(2)}) collective-permute-start(bf16[2,144,512]{2,1,0:T(8,128)(2,1)S(1)} %constant_dynamic-update-slice_fusion.lines_ref), channel_id=1, source_target_pairs={{0,2},{2,4},{4,6},{6,8},{8,10},{10,12},{12,14},{1,3},{3,5},{5,7},{... | collective-permute-start | bytes 884744 | tf_op jit(solution)/shard_map/ppermute | solution.py:352
  12.6 1.3 %collective-permute-start.3 = (bf16[2,16,512]{2,1,0:T(8,128)(2,1)S(1)}, bf16[2,16,512]{2,1,0:T(8,128)(2,1)S(1)}, u32[]{:S(2)}, u32[]{:S(2)}) collective-permute-start(bf16[2,16,512]{2,1,0:T(8,128)(2,1)S(1)} %next_edges.1), channel_id=1, source_target_pairs={{0,1},{1,0},{2,3},{3,2},{4,5},{5,4},{6,7},{7,6},{8,9},{9,8},{10,11... | collective-permute-start | bytes 98312 | tf_op jit(solution)/shard_map/ppermute | solution.py:369
  13.9 5.8 %copy-start.2 = (f32[256]{0:T(256)S(1)}, f32[256]{0:T(256)}, u32[]{:S(2)}) copy-start(f32[256]{0:T(256)} %param.15) | copy-start | bytes 3076
  13.9 5.8 %copy-start.3 = (f32[256]{0:T(256)S(1)}, f32[256]{0:T(256)}, u32[]{:S(2)}) copy-start(f32[256]{0:T(256)} %param.13) | copy-start | bytes 3076
  13.9 5.8 %copy-start.4 = (f32[256]{0:T(256)S(1)}, f32[256]{0:T(256)}, u32[]{:S(2)}) copy-start(f32[256]{0:T(256)} %param.11) | copy-start | bytes 3076
  13.9 5.8 %copy-start.5 = (f32[256]{0:T(256)S(1)}, f32[256]{0:T(256)}, u32[]{:S(2)}) copy-start(f32[256]{0:T(256)} %param.10) | copy-start | bytes 3076
  14.4 1.4 %collective-permute-start.5 = (f32[8,128]{1,0:T(8,128)S(1)}, f32[8,128]{1,0:T(8,128)S(1)}, u32[]{:S(2)}, u32[]{:S(2)}) collective-permute-start(f32[8,128]{1,0:T(8,128)S(1)} %get-tuple-element.30), channel_id=1, source_target_pairs={{0,1},{1,0},{2,3},{3,2},{4,5},{5,4},{6,7},{7,6},{8,9},{9,8},{10,11... | collective-permute-start | bytes 12296 | tf_op jit(solution)/shard_map/ppermute | solution.py:298
  15.8 3.6 %collective-permute-start.6 = (f32[8,128]{1,0:T(8,128)S(1)}, f32[8,128]{1,0:T(8,128)S(1)}, u32[]{:S(2)}, u32[]{:S(2)}) collective-permute-start(f32[8,128]{1,0:T(8,128)S(1)} %add.12), channel_id=1, source_target_pairs={{0,4},{2,6},{4,0},{6,2},{8,12},{10,14},{12,8},{14,10},{1,5},{3,7},... | collective-permute-start | bytes 12296 | tf_op jit(solution)/shard_map/ppermute | solution.py:298
  19.5 3.6 %collective-permute-start.7 = (f32[8,128]{1,0:T(8,128)S(1)}, f32[8,128]{1,0:T(8,128)S(1)}, u32[]{:S(2)}, u32[]{:S(2)}) collective-permute-start(f32[8,128]{1,0:T(8,128)S(1)} %add.13), channel_id=1, source_target_pairs={{0,2},{2,0},{4,6},{6,4},{8,10},{10,8},{12,14},{14,12},{1,3},{3,1},... | collective-permute-start | bytes 12296 | tf_op jit(solution)/shard_map/ppermute | solution.py:298
  23.1 4.5 %collective-permute-start.8 = (f32[8,128]{1,0:T(8,128)S(1)}, f32[8,128]{1,0:T(8,128)S(1)}, u32[]{:S(2)}, u32[]{:S(2)}) collective-permute-start(f32[8,128]{1,0:T(8,128)S(1)} %add.14), channel_id=1, source_target_pairs={{0,8},{2,10},{4,12},{6,14},{8,0},{10,2},{12,4},{14,6},{1,9},{3,11}... | collective-permute-start | bytes 12296 | tf_op jit(solution)/shard_map/ppermute | solution.py:298
  25.3 2.3 %copy-start = (bf16[3,3,256,128]{3,2,1,0:T(8,128)(2,1)S(1)}, bf16[3,3,256,128]{3,2,1,0:T(8,128)(2,1)}, u32[]{:S(2)}) copy-start(bf16[3,3,256,128]{3,2,1,0:T(8,128)(2,1)} %own_w1.1) | copy-start | bytes 1769476
  25.3 2.3 %copy-start.1 = (bf16[3,3,256,128]{3,2,1,0:T(8,128)(2,1)S(1)}, bf16[3,3,256,128]{3,2,1,0:T(8,128)(2,1)}, u32[]{:S(2)}) copy-start(bf16[3,3,256,128]{3,2,1,0:T(8,128)(2,1)} %own_w2.1) | copy-start | bytes 1769476
